TPU v7x, 128 devices: a whole 4x4x4 slice. The times are simulated.
128 devices in a mesh: row: 16 (over x, y), col: 8 (over z, core).
Axes of the slice: x: 4, y: 4, z: 4, core: 2. Of those that a mesh axis runs over, the one named last changes fastest.
Arguments:
- source1: float32 [2, 64, 48, 128], P(None, 'row', 'col'), may hold values from -6 to 6
- source2: float32 [2, 64, 48, 128], P(None, 'row', 'col'), may hold values from -6 to 6
- coupling: float32 [2, 64, 48], P(None, 'row', 'col'), may hold values from -1.5 to 1.5
- factor1: float32 [2, 3072, 3072], P(None, 'row', 'col'), may hold values from -0.0546875 to 0.0546875
- factor2: float32 [2, 3072, 3072], P(None, 'row', 'col'), may hold values from -0.0546875 to 0.0546875
- diag_inv: float32 [2, 768, 3072], P(None, None, 'row'), may hold values from -0.15625 to 0.15625
- front_order: int32 [3072], replicated, may hold values from 0 to 3071, each once
Outputs:
- solution1: float32 [2, 64, 48, 128], P(None, 'row', 'col')
- forward2: float32 [2, 3072, 128], P(None, 'row')
Inputs may be any that keep to these rules, and one draw needn't show every extreme that they name: `front_order`: a permutation of the patch's 3072 cells.
All inputs are finite; a program needn't handle non-finite values.
Results may differ from a plain program's by a relative error of at most 0.00012.
Values sent between devices are 32-bit elements; how exact they have to be, the bound alone decides.
No kernel may reach another device: no remote copies, remote signals or barrier semaphores. Data moves between devices by JAX's collectives and lax.ppermute only.
A program may use at most 64 MiB of HBM per device.

v0:
```python
import jax
import jax.numpy as jnp
from jax import lax
from jax.sharding import PartitionSpec as P

GROUP = 4


def complex_product(matrix, vector):
    highest = lax.Precision.HIGHEST
    real_part = jnp.dot(
        matrix[0], vector[0], precision=highest, preferred_element_type=jnp.float32
    ) - jnp.dot(matrix[1], vector[1], precision=highest, preferred_element_type=jnp.float32)
    imag_part = jnp.dot(
        matrix[0], vector[1], precision=highest, preferred_element_type=jnp.float32
    ) + jnp.dot(matrix[1], vector[0], precision=highest, preferred_element_type=jnp.float32)
    return jnp.stack([real_part, imag_part])


def gather_front(plane, positions):
    gathered = lax.all_gather(plane, ("row", "col"), axis=1, tiled=True)
    flat_cells = gathered.reshape(gathered.shape[0], -1, gathered.shape[-1])
    return jnp.take(flat_cells, positions, axis=1)


def sweep(factor_row, rhs_front, inverse, backward, row_id, col_id, row_count, col_count):
    slab_rows = factor_row.shape[1]
    block_count = row_count // GROUP
    block_rows = slab_rows * GROUP
    piece_cols = factor_row.shape[2] // block_count
    vec_count = rhs_front.shape[-1]
    zeros_block = jnp.zeros((2, block_rows, vec_count), jnp.float32)
    sub_index = row_id % GROUP
    owner_block = row_id // GROUP

    def local_product(vector):
        picked = vector.reshape(2, block_count, col_count, piece_cols, vec_count)
        picked = lax.dynamic_index_in_dim(picked, col_id, 2, keepdims=False)
        return complex_product(factor_row, picked.reshape(2, block_count * piece_cols, vec_count))

    def place(slab):
        return lax.dynamic_update_slice_in_dim(zeros_block, slab, sub_index * slab_rows, 1)

    def one_turn(turn_index, vector):
        current = block_count - 1 - turn_index if backward else turn_index
        is_owner = owner_block == current
        rhs_block = lax.dynamic_slice_in_dim(rhs_front, current * block_rows, block_rows, 1)
        rhs_slab = lax.dynamic_slice_in_dim(
            rhs_front, current * block_rows + sub_index * slab_rows, slab_rows, 1
        )

        def owned_part():
            product = local_product(vector)
            if backward:
                lead_flag = jnp.where(col_id == 0, 1.0, 0.0).astype(jnp.float32)
                return complex_product(inverse, lead_flag * rhs_slab - product)
            return place(-product)

        summed = lax.psum(lax.cond(is_owner, owned_part, lambda: zeros_block), ("row", "col"))
        solved = summed if backward else rhs_block + summed
        return lax.dynamic_update_slice_in_dim(vector, solved, current * block_rows, 1)

    return lax.fori_loop(0, block_count, one_turn, jnp.zeros_like(rhs_front))


def on_device(source1, source2, coupling, factor1, factor2, diag_inv, front_order):
    row_count = lax.axis_size("row")
    col_count = lax.axis_size("col")
    row_id = lax.axis_index("row")
    col_id = lax.axis_index("col")
    cells_y = source1.shape[1]
    cells_x = source1.shape[2]
    width_x = cells_x * col_count
    order_size = front_order.shape[0]
    cell_y = front_order // width_x
    cell_x = front_order % width_x
    positions = (
        (cell_y // cells_y * col_count + cell_x // cells_x) * cells_y + cell_y % cells_y
    ) * cells_x + cell_x % cells_x
    b_first = gather_front(source1, positions)
    y_first = sweep(factor1, b_first, diag_inv, False, row_id, col_id, row_count, col_count)
    x_first = sweep(factor1, y_first, diag_inv, True, row_id, col_id, row_count, col_count)
    slots = (
        jnp.zeros((order_size,), jnp.int32)
        .at[front_order]
        .set(jnp.arange(order_size, dtype=jnp.int32))
    )
    local_y = row_id * cells_y + jnp.arange(cells_y, dtype=jnp.int32)
    local_x = col_id * cells_x + jnp.arange(cells_x, dtype=jnp.int32)
    own_cells = (local_y[:, None] * width_x + local_x[None, :]).reshape(-1)
    own_rows = jnp.take(slots, own_cells)
    solution1 = jnp.take(x_first, own_rows, axis=1).reshape(2, cells_y, cells_x, x_first.shape[-1])
    link_real = coupling[0][:, :, None]
    link_imag = coupling[1][:, :, None]
    next_real = source2[0] - (link_real * solution1[0] - link_imag * solution1[1])
    next_imag = source2[1] - (link_real * solution1[1] + link_imag * solution1[0])
    next_rhs = jnp.stack([next_real, next_imag])
    b_second = gather_front(next_rhs, positions)
    y_second = sweep(factor2, b_second, diag_inv, False, row_id, col_id, row_count, col_count)
    slab_rows = factor2.shape[1]
    forward2 = lax.dynamic_slice_in_dim(y_second, row_id * slab_rows, slab_rows, 1)
    return (solution1, forward2)


def solution(mesh):
    in_specs = (
        P(None, "row", "col", None),
        P(None, "row", "col", None),
        P(None, "row", "col"),
        P(None, "row", "col"),
        P(None, "row", "col"),
        P(None, None, "row"),
        P(),
    )
    out_specs = (P(None, "row", "col", None), P(None, "row", None))
    return jax.shard_map(
        on_device, mesh=mesh, in_specs=in_specs, out_specs=out_specs, check_vma=False
    )
```

profile of v0, /device:TPU:4, one launch (start us, length us, event | category | flops | bytes accessed | tf_op | source)
XLA Modules:
  0.0 2077.2 jit_solution(16511209209430467342)
XLA Ops:
  7.2 1.4 copy.28
  8.9 1.7 copy.30
  11.4 11.8 scatter_custom_fusion
  24.1 54.2 %all-gather.3.cloned.1.call-done = f32[2,512,6,128]{3,0,2,1:T(2,128)} async-done(((f32[2,4,6,128]{3,0,2,1:T(2,128)}), f32[2,512,6,128]{3,0,2,1:T(2,128)}) %all-gather.3.cloned.1.call-update) | async-done | bytes 3145744 | tf_op jit(solution)/shard_map/all_gather | solution.py:21
  78.3 23.4 %gather_fusion.2 = f32[3072,2,128]{2,1,0:T(2,128)} fusion(f32[2,3072,128]{2,0,1:T(2,128)} %bitcast.140, s32[3072]{0:T(1024)S(1)} %broadcast_clamp_fusion), kind=kCustom, calls=%fused_computation.clone | custom fusion | bytes 6303744 | tf_op jit(solution)/shard_map/jit(_take)/gather | solution.py:23
  101.7 12.7 select_bitcast_fusion.1
  114.4 1.8 broadcast.203.clone.1
  116.3 609.2 %while.41 = (s32[]{:T(128)}, f32[2,3072,128]{2,1,0:T(8,128)}, f32[2,3072,128]{2,0,1:T(2,128)}, s32[]{:T(128)}, s32[]{:T(128)}, /*index=5*/f32[2,192,384]{2,1,0:T...) while((s32[]{:T(128)}, f32[2,3072,128]{2,1,0:T(8,128)}, ...), condition=%wide.region_5.7_spmd, body=%wide.region_1.6_spmd.sunk | while | flops 453525504 | bytes 13173101 | solution.py:63
  118.4 148.6 %all-reduce.4.cloned.1.call-done = f32[2,768,128]{2,1,0:T(8,128)} async-done(((f32[2,768,128]{2,1,0:T(8,128)}), f32[2,768,128]{2,1,0:T(8,128)}) %all-reduce.4.cloned.1.call-update) | async-done | bytes 786448 | tf_op jit(solution)/shard_map/while/body/eval_jaxpr/psum | solution.py:59
  267.0 2.1 fusion.84
  271.3 148.1 %all-reduce.4.cloned.1.call-done = f32[2,768,128]{2,1,0:T(8,128)} async-done(((f32[2,768,128]{2,1,0:T(8,128)}), f32[2,768,128]{2,1,0:T(8,128)}) %all-reduce.4.cloned.1.call-update) | async-done | bytes 786448 | tf_op jit(solution)/shard_map/while/body/eval_jaxpr/psum | solution.py:59
  419.3 2.1 fusion.84
  421.4 4.4 conditional.6
  425.8 1.2 constant_dynamic-slice_fusion.11
  427.0 144.3 %all-reduce.4.cloned.1.call-done = f32[2,768,128]{2,1,0:T(8,128)} async-done(((f32[2,768,128]{2,1,0:T(8,128)}), f32[2,768,128]{2,1,0:T(8,128)}) %all-reduce.4.cloned.1.call-update) | async-done | bytes 786448 | tf_op jit(solution)/shard_map/while/body/eval_jaxpr/psum | solution.py:59
  571.3 2.1 fusion.84
  574.4 1.2 constant_dynamic-slice_fusion.11
  575.6 147.8 %all-reduce.4.cloned.1.call-done = f32[2,768,128]{2,1,0:T(8,128)} async-done(((f32[2,768,128]{2,1,0:T(8,128)}), f32[2,768,128]{2,1,0:T(8,128)}) %all-reduce.4.cloned.1.call-update) | async-done | bytes 786448 | tf_op jit(solution)/shard_map/while/body/eval_jaxpr/psum | solution.py:59
  723.4 2.1 fusion.84
  725.5 1.9 broadcast.203.clone
  727.3 621.2 %while.42 = (s32[]{:T(128)}, f32[2,3072,128]{2,1,0:T(8,128)}, s32[]{:T(128)}, s32[]{:T(128)}, s32[]{:T(128)}, /*index=5*/f32[2,3072,128]{2,1,0:T(8,128)}, f32[2,...) while((s32[]{:T(128)}, f32[2,3072,128]{2,1,0:T(8,128)}, ...), condition=%wide.region_10.12_spmd, body=%wide.region_6.11_spmd.sunk | while | flops 1359740928 | bytes 19268016 | solution.py:63
  728.6 152.6 %all-reduce.6.cloned.1.call-done = f32[2,768,128]{2,1,0:T(8,128)} async-done(((f32[2,768,128]{2,1,0:T(8,128)}), f32[2,768,128]{2,1,0:T(8,128)}) %all-reduce.6.cloned.1.call-update) | async-done | bytes 786448 | tf_op jit(solution)/shard_map/while/body/eval_jaxpr/psum | solution.py:59
  881.2 2.1 constant_dynamic-update-slice_fusion.2
  883.3 7.8 conditional.7
  892.3 144.8 %all-reduce.6.cloned.1.call-done = f32[2,768,128]{2,1,0:T(8,128)} async-done(((f32[2,768,128]{2,1,0:T(8,128)}), f32[2,768,128]{2,1,0:T(8,128)}) %all-reduce.6.cloned.1.call-update) | async-done | bytes 786448 | tf_op jit(solution)/shard_map/while/body/eval_jaxpr/psum | solution.py:59
  1037.1 2.1 constant_dynamic-update-slice_fusion.2
  1040.4 151.2 %all-reduce.6.cloned.1.call-done = f32[2,768,128]{2,1,0:T(8,128)} async-done(((f32[2,768,128]{2,1,0:T(8,128)}), f32[2,768,128]{2,1,0:T(8,128)}) %all-reduce.6.cloned.1.call-update) | async-done | bytes 786448 | tf_op jit(solution)/shard_map/while/body/eval_jaxpr/psum | solution.py:59
  1191.6 2.1 constant_dynamic-update-slice_fusion.2
  1195.0 151.5 %all-reduce.6.cloned.1.call-done = f32[2,768,128]{2,1,0:T(8,128)} async-done(((f32[2,768,128]{2,1,0:T(8,128)}), f32[2,768,128]{2,1,0:T(8,128)}) %all-reduce.6.cloned.1.call-update) | async-done | bytes 786448 | tf_op jit(solution)/shard_map/while/body/eval_jaxpr/psum | solution.py:59
  1346.5 2.1 constant_dynamic-update-slice_fusion.2
  1348.6 7.1 copy.31
  1355.7 2.5 gather_fusion.1
  1359.9 61.9 %all-gather.5.cloned.1.call-done = f32[2,512,6,128]{3,0,2,1:T(2,128)} async-done(((f32[2,4,6,128]{3,0,2,1:T(2,128)}), f32[2,512,6,128]{3,0,2,1:T(2,128)}) %all-gather.5.cloned.1.call-update) | async-done | bytes 3145744 | tf_op jit(solution)/shard_map/all_gather | solution.py:21
  1421.9 23.4 %gather_fusion.3 = f32[3072,2,128]{2,1,0:T(2,128)} fusion(f32[2,3072,128]{2,0,1:T(2,128)} %bitcast.141, s32[3072]{0:T(1024)S(1)} %broadcast_clamp_fusion), kind=kCustom, calls=%fused_computation.1.clone | custom fusion | bytes 6303744 | tf_op jit(solution)/shard_map/jit(_take)/gather | solution.py:23
  1445.3 12.7 select_bitcast_fusion
  1458.0 1.8 broadcast.203
  1459.9 609.2 %while.43 = (s32[]{:T(128)}, f32[2,3072,128]{2,1,0:T(8,128)}, f32[2,3072,128]{2,0,1:T(2,128)}, s32[]{:T(128)}, s32[]{:T(128)}, /*index=5*/f32[2,192,384]{2,1,0:T...) while((s32[]{:T(128)}, f32[2,3072,128]{2,1,0:T(8,128)}, ...), condition=%wide.region_15.17_spmd, body=%wide.region_11.16_spmd.sunk | while | flops 453525504 | bytes 13173101 | solution.py:63
  1460.8 1.2 constant_dynamic-slice_fusion.12
  1462.0 148.6 %all-reduce.8.cloned.1.call-done = f32[2,768,128]{2,1,0:T(8,128)} async-done(((f32[2,768,128]{2,1,0:T(8,128)}), f32[2,768,128]{2,1,0:T(8,128)}) %all-reduce.8.cloned.1.call-update) | async-done | bytes 786448 | tf_op jit(solution)/shard_map/while/body/eval_jaxpr/psum | solution.py:59
  1610.6 2.1 fusion.85
  1614.9 147.8 %all-reduce.8.cloned.1.call-done = f32[2,768,128]{2,1,0:T(8,128)} async-done(((f32[2,768,128]{2,1,0:T(8,128)}), f32[2,768,128]{2,1,0:T(8,128)}) %all-reduce.8.cloned.1.call-update) | async-done | bytes 786448 | tf_op jit(solution)/shard_map/while/body/eval_jaxpr/psum | solution.py:59
  1762.6 2.1 fusion.85
  1764.7 4.4 conditional.8
  1770.3 144.6 %all-reduce.8.cloned.1.call-done = f32[2,768,128]{2,1,0:T(8,128)} async-done(((f32[2,768,128]{2,1,0:T(8,128)}), f32[2,768,128]{2,1,0:T(8,128)}) %all-reduce.8.cloned.1.call-update) | async-done | bytes 786448 | tf_op jit(solution)/shard_map/while/body/eval_jaxpr/psum | solution.py:59
  1915.0 2.1 fusion.85
  1919.2 147.8 %all-reduce.8.cloned.1.call-done = f32[2,768,128]{2,1,0:T(8,128)} async-done(((f32[2,768,128]{2,1,0:T(8,128)}), f32[2,768,128]{2,1,0:T(8,128)}) %all-reduce.8.cloned.1.call-update) | async-done | bytes 786448 | tf_op jit(solution)/shard_map/while/body/eval_jaxpr/psum | solution.py:59
  2067.0 2.1 fusion.85
  2069.1 1.6 constant_dynamic-slice_fusion.8
  (115 shorter events, 42.5 us)
Async XLA Ops:
  7.2 16.8 copy-start.2
  7.2 16.8 copy-start.4
  7.2 16.9 copy-start.3
  7.2 71.1 %all-gather.3.cloned.1.call-start = ((), (), s32[]{:S(2)}) async-start(), calls=%async_computation | async-start | bytes 3170304 | tf_op jit(solution)/shard_map/all_gather | solution.py:21
  114.4 1.8 copy-start
  116.3 150.7 %all-reduce.4.cloned.1.call-start = ((), (), s32[]{:S(2)}) async-start(), calls=%async_computation.2 | async-start | bytes 1572864 | tf_op jit(solution)/shard_map/while/body/eval_jaxpr/psum | solution.py:59
  269.1 150.2 %all-reduce.4.cloned.1.call-start = ((), (), s32[]{:S(2)}) async-start(), calls=%async_computation.2 | async-start | bytes 1572864 | tf_op jit(solution)/shard_map/while/body/eval_jaxpr/psum | solution.py:59
  421.4 149.9 %all-reduce.4.cloned.1.call-start = ((), (), s32[]{:S(2)}) async-start(), calls=%async_computation.2 | async-start | bytes 1572864 | tf_op jit(solution)/shard_map/while/body/eval_jaxpr/psum | solution.py:59
  573.4 149.9 %all-reduce.4.cloned.1.call-start = ((), (), s32[]{:S(2)}) async-start(), calls=%async_computation.2 | async-start | bytes 1572864 | tf_op jit(solution)/shard_map/while/body/eval_jaxpr/psum | solution.py:59
  727.3 153.9 %all-reduce.6.cloned.1.call-start = ((), (), s32[]{:S(2)}) async-start(), calls=%async_computation.3 | async-start | bytes 1572864 | tf_op jit(solution)/shard_map/while/body/eval_jaxpr/psum | solution.py:59
  883.3 153.8 %all-reduce.6.cloned.1.call-start = ((), (), s32[]{:S(2)}) async-start(), calls=%async_computation.3 | async-start | bytes 1572864 | tf_op jit(solution)/shard_map/while/body/eval_jaxpr/psum | solution.py:59
  1039.1 152.5 %all-reduce.6.cloned.1.call-start = ((), (), s32[]{:S(2)}) async-start(), calls=%async_computation.3 | async-start | bytes 1572864 | tf_op jit(solution)/shard_map/while/body/eval_jaxpr/psum | solution.py:59
  1193.7 152.8 %all-reduce.6.cloned.1.call-start = ((), (), s32[]{:S(2)}) async-start(), calls=%async_computation.3 | async-start | bytes 1572864 | tf_op jit(solution)/shard_map/while/body/eval_jaxpr/psum | solution.py:59
  1348.6 73.3 %all-gather.5.cloned.1.call-start = ((), (), s32[]{:S(2)}) async-start(), calls=%async_computation.1 | async-start | bytes 3170304 | tf_op jit(solution)/shard_map/all_gather | solution.py:21
  1458.0 1.8 copy-start.1
  1459.9 150.7 %all-reduce.8.cloned.1.call-start = ((), (), s32[]{:S(2)}) async-start(), calls=%async_computation.4 | async-start | bytes 1572864 | tf_op jit(solution)/shard_map/while/body/eval_jaxpr/psum | solution.py:59
  1612.7 149.9 %all-reduce.8.cloned.1.call-start = ((), (), s32[]{:S(2)}) async-start(), calls=%async_computation.4 | async-start | bytes 1572864 | tf_op jit(solution)/shard_map/while/body/eval_jaxpr/psum | solution.py:59
  1764.7 150.2 %all-reduce.8.cloned.1.call-start = ((), (), s32[]{:S(2)}) async-start(), calls=%async_computation.4 | async-start | bytes 1572864 | tf_op jit(solution)/shard_map/while/body/eval_jaxpr/psum | solution.py:59
  1917.1 149.9 %all-reduce.8.cloned.1.call-start = ((), (), s32[]{:S(2)}) async-start(), calls=%async_computation.4 | async-start | bytes 1572864 | tf_op jit(solution)/shard_map/while/body/eval_jaxpr/psum | solution.py:59
Sparse Core Ops, SparseCore 0:
  11.6 66.6 all-gather.2
  121.7 145.1 all-reduce.3
  274.6 144.7 all-reduce.3
  426.6 144.7 all-reduce.3
  578.6 144.7 all-reduce.3
  732.5 148.6 all-reduce.5
  892.4 144.6 all-reduce.5
  1044.6 146.9 all-reduce.5
  1199.2 147.2 all-reduce.5
  1359.2 62.6 all-gather.4
  1465.4 145.1 all-reduce.7
  1617.9 144.7 all-reduce.7
  1770.2 144.7 all-reduce.7
  1922.2 144.7 all-reduce.7
where the time goes:
time: 2080 us
  waiting for transfers between devices  1890 us (91%)
  local copies, waits for them, and re-layouts  113 us (5%)
  other arithmetic  46.5 us (2%)
    psum x12, waiting for transfers between devices, one_turn(): lax.psum(lax.cond(is_owner, owned_part, lambda: zeros_block), ('row', 'co...  1780 us
    all_gather x2, waiting for transfers between devices, gather_front(): gathered = lax.all_gather(plane, ('row', 'col'), axis=1, tiled=True)  116 us
    gather x2, local copies, waits for them, and re-layouts, gather_front(): return jnp.take(flat_cells, positions, axis=1)  46.9 us
  transfers between devices with their start and end apart: 14, of which 14 were waited for; matrix products, arithmetic and copies ran while one was open for 1% of the time, Pallas kernels for 0%

commit v1 on v0

v1 whole, which is shorter than its diff:
```python
import functools

import jax
import jax.numpy as jnp
from jax import lax
from jax.experimental import pallas as pl
from jax.experimental.pallas import tpu as pltpu
from jax.sharding import PartitionSpec as P

GROUP = 4
CHUNK = 16
ROWS = 2 * CHUNK
SLAB = 192
BLOCK = 768
PIECE = 96
CELLS = 24
VMEM = 40 * 1024 * 1024

SDS = jax.ShapeDtypeStruct
f32 = jnp.float32


def split(value):
    high = value.astype(jnp.bfloat16)
    return high, (value - high.astype(f32)).astype(jnp.bfloat16)


def complex_dot(vector, weight):
    half = weight.shape[1] // 2
    weight_high, weight_low = split(weight)
    high, low = split(vector)
    both = jnp.dot(
        jnp.concatenate([high, low], axis=0), weight_high, preferred_element_type=f32
    )
    total = both[:ROWS] + both[ROWS:] + jnp.dot(high, weight_low, preferred_element_type=f32)
    real = total[:CHUNK, :half] - total[CHUNK:, half:]
    imag = total[:CHUNK, half:] + total[CHUNK:, :half]
    return jnp.concatenate([real, imag], axis=0)


def block_weight(ref, at=0):
    return ref[:, at].reshape(BLOCK, 2 * SLAB)


def slabs_dot(refs, weight_ref, q, keep=None):
    total = None
    for d, ref in enumerate(refs):
        source = lax.rem(q - d + GROUP, GROUP)
        slab = ref[...]
        if keep is not None:
            keep[source] = slab
        weight = weight_ref[pl.ds(2 * source, 2), 0].reshape(SLAB, 2 * SLAB)
        part = complex_dot(slab, weight)
        total = part if total is None else total + part
    return total


def add_refs(refs):
    total = refs[0][...]
    for ref in refs[1:]:
        total = total + ref[...]
    return total


def call(body, out_shape, inputs, blocks=None, scratch=()):
    blocks = blocks or {}
    specs = []
    for at, value in enumerate(inputs):
        if at in blocks:
            specs.append(blocks[at])
        elif value.dtype == jnp.int32:
            specs.append(pl.BlockSpec(memory_space=pltpu.SMEM))
        else:
            specs.append(pl.BlockSpec(value.shape, lambda i, n=value.ndim: (0,) * n))
    outs = tuple(
        pl.BlockSpec(shape.shape, lambda i, n=len(shape.shape): (0,) * n) for shape in out_shape
    )
    return pl.pallas_call(
        body,
        grid=(1,),
        in_specs=specs,
        out_specs=outs,
        out_shape=tuple(out_shape),
        scratch_shapes=scratch,
        compiler_params=pltpu.CompilerParams(vmem_limit_bytes=VMEM),
    )(*inputs)


def factor_block(block):
    return pl.BlockSpec((8, 1, PIECE, 2 * SLAB), lambda i: (0, block, 0, 0))


def pack_kernel(first_ref, second_ref, link_ref, out_ref):
    lane = lax.broadcasted_iota(jnp.int32, (6, 128), 1)
    for y in range(4):
        parts = [first_ref[0, y], first_ref[1, y], second_ref[0, y], second_ref[1, y]]
        links = jnp.where(lane < 96, link_ref[0, y], link_ref[1, y])
        for c in range(8):
            row = links
            for at, part in enumerate(parts):
                shift = (16 * at - 16 * c) % 128
                moved = pltpu.roll(part, shift, 1) if shift else part
                row = jnp.where((lane >= 16 * at) & (lane < 16 * at + 16), moved, row)
            out_ref[c, 6 * y : 6 * y + 6, :] = row


def front_kernel(where_ref, cells_ref, rhs_ref, link_ref, rows_ref):
    def some(step, carry):
        for u in range(16):
            at = step * 16 + u
            rows_ref[pl.ds(at, 1), :] = cells_ref[pl.ds(where_ref[at], 1), :]
        return carry

    lax.fori_loop(0, 64, some, 0)
    for part in range(8):
        turned = rows_ref[128 * part : 128 * part + 128, :].T
        rhs_ref[:, 128 * part : 128 * part + 128] = turned[:64]
        link_ref[0:8, 128 * part : 128 * part + 128] = turned[64:72]
        link_ref[8:16, 128 * part : 128 * part + 128] = turned[96:104]


def start_kernel(place_ref, rhs_ref, weight_ref, acc_ref):
    product = complex_dot(rhs_ref[0:ROWS, 0:BLOCK], block_weight(weight_ref))
    slab = rhs_ref[0:ROWS, BLOCK : BLOCK + SLAB]
    acc_ref[...] = jnp.where(place_ref[0] > 0, slab - product, slab)


def forward_one_kernel(place_ref, acc_ref, y0, y1, y2, y3, weight_ref, out_ref, keep_ref):
    q = place_ref[1]
    out_ref[...] = acc_ref[...] - slabs_dot([y0, y1, y2, y3], weight_ref, q, keep_ref)


def sent_dot(sent_ref, weight_ref):
    total = None
    for s in range(GROUP):
        weight = weight_ref[2 * s : 2 * s + 2, 0].reshape(SLAB, 2 * SLAB)
        part = complex_dot(sent_ref[s], weight)
        total = part if total is None else total + part
    return total


def forward_two_kernel(
    place_ref, acc_ref, y0, y1, y2, y3, sent_ref, weight2_ref, weight1_ref, inverse_ref, out_ref, part_ref
):
    q = place_ref[1]
    solved = (
        acc_ref[...]
        - slabs_dot([y0, y1, y2, y3], weight2_ref, q)
        - sent_dot(sent_ref, weight1_ref)
    )
    out_ref[...] = solved
    part_ref[...] = complex_dot(solved, inverse_ref[...])


def back_three_kernel(acc_ref, p0, p1, p2, p3, weight_ref, inverse_ref, x_ref, out_ref, part_ref):
    x = add_refs([p0, p1, p2, p3])
    x_ref[...] = x
    acc = acc_ref[...] - complex_dot(x, block_weight(weight_ref))
    out_ref[...] = acc
    part_ref[...] = complex_dot(acc, inverse_ref[...])


def back_two_kernel(
    acc_ref, p0, p1, p2, p3, x3_ref, weight2_ref, weight3_ref, inverse_ref, x_ref, out_ref, part_ref
):
    x = add_refs([p0, p1, p2, p3])
    x_ref[0] = x
    x_ref[1] = x3_ref[...]
    acc = (
        acc_ref[...]
        - complex_dot(x3_ref[...], block_weight(weight3_ref))
        - complex_dot(x, block_weight(weight2_ref))
    )
    out_ref[...] = acc
    part_ref[...] = complex_dot(acc, inverse_ref[...])


def back_one_kernel(
    acc_ref, p0, p1, p2, p3, later_ref, weight1_ref, weight2_ref, weight3_ref, inverse_ref, x_ref, part_ref
):
    x = add_refs([p0, p1, p2, p3])
    x_ref[0] = x
    x_ref[1] = later_ref[0]
    acc = (
        acc_ref[...]
        - complex_dot(later_ref[1], block_weight(weight3_ref))
        - complex_dot(later_ref[0], block_weight(weight2_ref))
        - complex_dot(x, block_weight(weight1_ref))
    )
    part_ref[...] = complex_dot(acc, inverse_ref[...])


def coupled(rhs, link_real, link_imag, x):
    real = rhs[:CHUNK] - (link_real * x[:CHUNK] - link_imag * x[CHUNK:])
    imag = rhs[CHUNK:] - (link_real * x[CHUNK:] + link_imag * x[:CHUNK])
    return jnp.concatenate([real, imag], axis=0)


def second_block(rhs_ref, link_ref, x):
    return coupled(
        rhs_ref[ROWS : 2 * ROWS, 0:BLOCK], link_ref[0:1, 0:BLOCK], link_ref[8:9, 0:BLOCK], x
    )


def second_slab(rhs_ref, link_ref, x, q):
    own = x[:, 0:SLAB]
    for s in range(1, GROUP):
        own = jnp.where(q == s, x[:, SLAB * s : SLAB * s + SLAB], own)
    end = BLOCK + SLAB
    return coupled(
        rhs_ref[ROWS : 2 * ROWS, BLOCK:end], link_ref[0:1, BLOCK:end], link_ref[8:9, BLOCK:end], own
    )


def couple_kernel(
    place_ref, rhs_ref, link_ref, p0, p1, p2, p3, x1_ref, x2_ref, x3_ref, weight_ref, x0_ref, slab_ref, out_ref
):
    plane, q = place_ref[0], place_ref[1]
    x0 = add_refs([p0, p1, p2, p3])
    x0_ref[0] = x0
    x0_ref[1] = x1_ref[...]
    own = jnp.where(plane == 1, x1_ref[...], jnp.where(plane == 2, x2_ref[...], x3_ref[...]))
    slab = second_slab(rhs_ref, link_ref, own, q)
    slab_ref[...] = slab
    out_ref[...] = slab - complex_dot(second_block(rhs_ref, link_ref, x0), block_weight(weight_ref))


def second_one_kernel(
    place_ref,
    rhs_ref,
    link_ref,
    slab_ref,
    x0_ref,
    f0,
    f1,
    f2,
    f3,
    weight0_ref,
    weight1_ref,
    out_ref,
    keep_ref,
):
    plane, q = place_ref[0], place_ref[1]
    x0 = x0_ref[...]
    first = second_slab(rhs_ref, link_ref, x0, q)
    product = complex_dot(second_block(rhs_ref, link_ref, x0), block_weight(weight0_ref))
    later = slab_ref[...] - product - slabs_dot([f0, f1, f2, f3], weight1_ref, q, keep_ref)
    out_ref[...] = jnp.where(plane == 0, first, later)


def cells_kernel(where_ref, x0_ref, x1_ref, x2_ref, x3_ref, out_ref, front_ref, rows_ref):
    for k, ref in enumerate((x0_ref, x1_ref, x2_ref, x3_ref)):
        for part in range(6):
            at = BLOCK * k + 128 * part
            piece = ref[:, 128 * part : 128 * part + 128]
            wide = jnp.concatenate([piece, jnp.zeros((128 - ROWS, 128), f32)], axis=0)
            front_ref[at : at + 128, :] = wide.T
    rows_ref[...] = jnp.zeros_like(rows_ref)
    for c in range(8):
        for u in range(CELLS):
            rows_ref[64 + u : 65 + u, :] = front_ref[pl.ds(where_ref[CELLS * c + u], 1), :]
        out_ref[c] = rows_ref[...].T[:ROWS]


def second_two_kernel(
    place_ref, acc_ref, f0, f1, f2, f3, sent_ref, cells_ref, weight2_ref, weight1_ref, out_ref
):
    q = place_ref[1]
    solved = (
        acc_ref[...]
        - slabs_dot([f0, f1, f2, f3], weight2_ref, q)
        - sent_dot(sent_ref, weight1_ref)
    )
    lane = lax.broadcasted_iota(jnp.int32, (ROWS, 128), 1)
    tail = jnp.concatenate([solved[:, 128:], jnp.zeros((ROWS, 64), f32)], axis=1)
    for c in range(8):
        out_ref[c, :, 0:128] = solved[:, 0:128]
        out_ref[c, :, 128:256] = jnp.where(lane < 64, tail, cells_ref[c])


def out_kernel(got_ref, solution_ref, forward_ref):
    for part in range(2):
        wide = got_ref[:, CHUNK * part : CHUNK * part + CHUNK, :].reshape(128, 256)
        forward_ref[part, 0:128, :] = wide[:, 0:128].T
        turned = wide[:, 128:256].T
        forward_ref[part, 128:SLAB, :] = turned[0:64]
        for y in range(4):
            solution_ref[part, y] = turned[64 + 6 * y : 70 + 6 * y]


def plane_send(value, source, target, turn=0):
    pairs = [
        (GROUP * source + q, GROUP * target + (q + turn) % GROUP) for q in range(GROUP)
    ]
    return lax.ppermute(value, "row", pairs)


def plane_spread(value, source, target):
    return [plane_send(value, source, target, d) for d in range(GROUP)]


def on_device(source1, source2, coupling, factor1, factor2, diag_inv, front_order):
    row_id = lax.axis_index("row")
    col_id = lax.axis_index("col")
    place = jnp.stack([row_id // GROUP, row_id % GROUP]).astype(jnp.int32)

    def gather_factor(factor):
        turned = factor.reshape(2 * SLAB, 4 * PIECE).T
        return lax.all_gather(turned, "col").reshape(8, 4, PIECE, 2 * SLAB)

    matrix1 = gather_factor(factor1)

    links = jnp.broadcast_to(coupling[..., None], coupling.shape + (128,))
    (packed,) = call(pack_kernel, [SDS((8, CELLS, 128), f32)], [source1, source2, links])
    packed = jnp.broadcast_to(packed[None], (16, 8, CELLS, 128)).reshape(128, CELLS, 128)
    cells = lax.all_to_all(packed, ("row", "col"), 0, 0).reshape(128 * CELLS, 128)

    cell_y = front_order // 48
    cell_x = front_order % 48
    place_of = ((cell_y // 4) * 8 + cell_x // 6) * CELLS + (cell_y % 4) * 6 + cell_x % 6
    own = lax.dynamic_slice_in_dim(place_of, row_id * SLAB, SLAB)
    where = jnp.concatenate([place_of[:BLOCK], own, jnp.zeros((64,), jnp.int32)])
    rhs, link = call(
        front_kernel,
        [SDS((64, 1024), f32), SDS((16, 1024), f32)],
        [where, cells],
        scratch=[pltpu.VMEM((1024, 128), f32)],
    )
    factor2, diag_inv, cells = lax.optimization_barrier((factor2, diag_inv, cells))
    matrix2 = gather_factor(factor2)
    inverse = diag_inv.reshape(2 * BLOCK, SLAB).T

    slab_shape = SDS((ROWS, SLAB), f32)
    block_shape = SDS((ROWS, BLOCK), f32)
    sent_shape = SDS((GROUP, ROWS, SLAB), f32)

    (acc,) = call(start_kernel, [slab_shape], [place, rhs, matrix1], {2: factor_block(0)})
    got = plane_spread(acc, 1, 2)
    acc, kept = call(
        forward_one_kernel,
        [slab_shape, sent_shape],
        [place, acc, *got, matrix1],
        {6: factor_block(1)},
    )
    got = plane_spread(acc, 2, 3)
    sent = plane_send(kept, 2, 3)
    acc, part = call(
        forward_two_kernel,
        [slab_shape, block_shape],
        [place, acc, *got, sent, matrix1, matrix1, inverse],
        {7: factor_block(2), 8: factor_block(1)},
    )
    got = plane_spread(part, 3, 2)
    x3, acc, part = call(
        back_three_kernel,
        [block_shape, slab_shape, block_shape],
        [acc, *got, matrix1, inverse],
        {5: factor_block(3)},
    )
    got = plane_spread(part, 2, 1)
    x3_one = plane_send(x3, 2, 1)
    x3_three = plane_send(x3, 2, 3)
    x23, acc, part = call(
        back_two_kernel,
        [SDS((2, ROWS, BLOCK), f32), slab_shape, block_shape],
        [acc, *got, x3_one, matrix1, matrix1, inverse],
        {6: factor_block(2), 7: factor_block(3)},
    )
    got = plane_spread(part, 1, 0)
    x23_zero = plane_send(x23, 1, 0)
    x2_two = plane_send(x23[0], 1, 2)
    x12, part = call(
        back_one_kernel,
        [SDS((2, ROWS, BLOCK), f32), block_shape],
        [acc, *got, x23_zero, matrix1, matrix1, matrix1, inverse],
        {6: factor_block(1), 7: factor_block(2), 8: factor_block(3)},
    )
    got = plane_spread(part, 0, 1)
    x1_one = plane_send(x12[0], 0, 1)
    x12_three = plane_send(x12, 0, 3)
    x3_all = x3 + x3_one + x3_three + x23_zero[1]
    x2_all = x23[0] + x23_zero[0] + x2_two + x12_three[1]
    x1_some = x12[0] + x1_one + x12_three[0]
    x01, slab, acc = call(
        couple_kernel,
        [SDS((2, ROWS, BLOCK), f32), slab_shape, slab_shape],
        [place, rhs, link, *got, x1_some, x2_all, x3_all, matrix2],
        {10: factor_block(0)},
    )
    got = plane_spread(acc, 1, 2)
    x01_two = plane_send(x01, 1, 2)
    x0_three = plane_send(x01[0], 1, 3)
    x0_zero = plane_send(x01[0], 1, 0)
    x0_all = x01[0] + x01_two[0] + x0_three + x0_zero
    x1_all = x1_some + x01_two[1]
    acc, kept = call(
        second_one_kernel,
        [slab_shape, sent_shape],
        [place, rhs, link, slab, x0_all, *got, matrix2, matrix2],
        {9: factor_block(0), 10: factor_block(1)},
    )
    got = plane_spread(acc, 2, 3)
    sent = plane_send(kept, 2, 3)

    at = jnp.arange(SLAB, dtype=jnp.int32)
    own_c, own_y, own_x = at // CELLS, at % CELLS // 6, at % 6
    own_cells = (row_id * 4 + own_y) * 48 + own_c * 6 + own_x
    hits = front_order[None, :] == own_cells[:, None]
    slots = jnp.sum(jnp.where(hits, jnp.arange(4 * BLOCK, dtype=jnp.int32)[None, :], 0), axis=1)
    (mine,) = call(
        cells_kernel,
        [SDS((8, ROWS, 128), f32)],
        [slots, x0_all, x1_all, x2_all, x3_all],
        scratch=[pltpu.VMEM((4 * BLOCK, 128), f32), pltpu.VMEM((128, 128), f32)],
    )
    (last,) = call(
        second_two_kernel,
        [SDS((8, ROWS, 256), f32)],
        [place, acc, *got, sent, mine, matrix2, matrix2],
        {8: factor_block(2), 9: factor_block(1)},
    )
    arrived = lax.all_to_all(last, "col", 0, 0)
    return call(
        out_kernel, [SDS((2, 4, 6, 128), f32), SDS((2, SLAB, 128), f32)], [arrived]
    )


def solution(mesh):
    in_specs = (
        P(None, "row", "col", None),
        P(None, "row", "col", None),
        P(None, "row", "col"),
        P(None, "row", "col"),
        P(None, "row", "col"),
        P(None, None, "row"),
        P(),
    )
    out_specs = (P(None, "row", "col", None), P(None, "row", None))
    return jax.shard_map(
        on_device, mesh=mesh, in_specs=in_specs, out_specs=out_specs, check_vma=False
    )
```

time: 2080 us -> 197 us (0.09)
  waiting for transfers between devices: 1890 us -> 61.4 us
  local copies, waits for them, and re-layouts: 113 us -> 11.1 us
  starting transfers between devices: 0.07 us -> 48.5 us
  other arithmetic: 46.5 us -> 0.78 us
  blocking collectives: 0 us -> 43.9 us
    psum x12 -> x0, waiting for transfers between devices: 1780 us -> none  [one_turn(): lax.psum(lax.cond(is_owner, owned_part, lambda: zeros_block), ('row', 'co...]
    all_gather x2, waiting for transfers between devices: 116 us -> 14.6 us  [gather_factor(): return lax.all_gather(turned, 'col').reshape(8, 4, PIECE, 2 * SLAB)]
    gather x5 -> x0, local copies, waits for them, and re-layouts: 50.1 us -> none  [the longest x2 46.9 us: gather_front(): return jnp.take(flat_cells, positions, axis=1)]
    ppermute x0 -> x43, starting transfers between devices: none -> 48.4 us  [plane_send(): return lax.ppermute(value, 'row', pairs)]
    ppermute x0 -> x43, waiting for transfers between devices: none -> 46.8 us  [plane_send(): return lax.ppermute(value, 'row', pairs)]
    all_to_all x0 -> x2, blocking collectives: none -> 43.9 us  [the longest x1 33.6 us: on_device(): lax.all_to_all(packed, ('row', 'col'), 0, 0).reshape(128 * CELLS, 128)]
    select_n x7 -> x0, other arithmetic: 26.3 us -> none  [the longest x2 25.4 us: gather_front(): return jnp.take(flat_cells, positions, axis=1)]
  transfers between devices with their start and end apart: 14 -> 45, of which waited for: 14 -> 20; matrix products, arithmetic and copies ran while one was open for 1% -> 2% of each run, Pallas kernels for 0% -> 5%
where the time goes in v1:
time: 197 us; the launch traced here: 195 us
  waiting for transfers between devices  61.4 us (31%)
  starting transfers between devices  48.5 us (25%)
  blocking collectives  43.9 us (22%)
  between operations  14.7 us (7%)
  Pallas kernels  14.5 us (7%)
  local copies, waits for them, and re-layouts  11.1 us (6%)
    ppermute x43, starting transfers between devices, plane_send(): return lax.ppermute(value, 'row', pairs)  48.4 us
    ppermute x43, waiting for transfers between devices, plane_send(): return lax.ppermute(value, 'row', pairs)  46.8 us
    all_to_all x1, blocking collectives, on_device(): lax.all_to_all(packed, ('row', 'col'), 0, 0).reshape(128 * CELLS, 128)  33.6 us
    all_gather x2, waiting for transfers between devices, gather_factor(): return lax.all_gather(turned, 'col').reshape(8, 4, PIECE, 2 * SLAB)  14.6 us
    pallas_call x13, Pallas kernels, call(): pl.pallas_call(body, grid=(1,), in_specs=specs, out_specs=outs, out_shape...  14.5 us
    all_to_all x1, blocking collectives, on_device(): arrived = lax.all_to_all(last, 'col', 0, 0)  10.3 us
    unnamed x16, local copies, waits for them, and re-layouts  6.18 us
  transfers between devices with their start and end apart: 45, of which 20 were waited for; matrix products, arithmetic and copies ran while one was open for 2% of the time, Pallas kernels for 5%

profile of v1, /device:TPU:4, one launch (start us, length us, event | category | flops | bytes accessed | tf_op | source)
XLA Modules:
  0.0 194.9 jit_solution(3719187303092356944)
XLA Ops:
  7.2 2.1 %copy.17 = f32[384,384]{0,1:T(8,128)} copy(f32[384,384]{1,0:T(8,128)} %bitcast.82) | data formatting | bytes 1179648 | tf_op jit(solution)/shard_map/reshape | solution.py:308
  12.0 33.6 %all_to_all.10 = f32[128,24,128]{2,1,0:T(8,128)S(1)} all-to-all(f32[128,24,128]{2,1,0:T(8,128)S(1)} %bitcast.78), channel_id=1, replica_groups=mesh['row'=16,'col'=8] {'row','col'}, dimensions={0} | all-to-all | bytes 3145728 | tf_op jit(solution)/shard_map/all_to_all | solution.py:316
  47.0 1.9 shard_map.87
  48.9 14.5 %all-gather.5.cloned.1.call-done = f32[3072,384]{1,0:T(8,128)} async-done(((f32[384,384]{1,0:T(8,128)}), f32[3072,384]{1,0:T(8,128)}) %all-gather.5.cloned.1.call-update) | async-done | bytes 4718608 | tf_op jit(solution)/shard_map/all_gather | solution.py:309
  63.4 2.3 %copy-done = f32[3072,384]{1,0:T(8,128)S(1)} copy-done((f32[3072,384]{1,0:T(8,128)S(1)}, f32[3072,384]{1,0:T(8,128)}, u32[]{:S(2)}) %copy-start) | copy-done | bytes 4718616
  66.8 1.4 collective-permute-start
  68.2 1.3 collective-permute-start.1
  69.5 1.3 collective-permute-start.2
  70.8 1.3 collective-permute-start.3
  72.7 3.5 %collective-permute-done.1.y1 = f32[32,192]{1,0:T(8,128)S(1)} collective-permute-done((f32[32,192]{1,0:T(8,128)S(1)}, f32[32,192]{1,0:T(8,128)S(1)}, u32[]{:S(2)}, u32[]{:S(2)}) %collective-permute-start.1) | collective-permute-done | bytes 24608 | tf_op jit(solution)/shard_map/ppermute | solution.py:295
  76.2 2.2 %collective-permute-done.2.y2 = f32[32,192]{1,0:T(8,128)S(1)} collective-permute-done((f32[32,192]{1,0:T(8,128)S(1)}, f32[32,192]{1,0:T(8,128)S(1)}, u32[]{:S(2)}, u32[]{:S(2)}) %collective-permute-start.2) | collective-permute-done | bytes 24608 | tf_op jit(solution)/shard_map/ppermute | solution.py:295
  81.4 1.3 collective-permute-start.4
  82.7 1.3 collective-permute-start.5
  84.0 1.3 collective-permute-start.6
  85.3 1.3 collective-permute-start.7
  88.2 1.6 shard_map.90
  89.9 1.3 collective-permute-start.9
  91.2 1.3 collective-permute-start.10
  92.5 1.3 collective-permute-start.11
  93.8 1.3 collective-permute-start.12
  95.1 1.9 collective-permute-done.9.p0
  97.0 4.5 %collective-permute-done.10.p1 = f32[32,768]{1,0:T(8,128)S(1)} collective-permute-done((f32[32,768]{1,0:T(8,128)S(1)}, f32[32,768]{1,0:T(8,128)S(1)}, u32[]{:S(2)}, u32[]{:S(2)}) %collective-permute-start.10) | collective-permute-done | bytes 98336 | tf_op jit(solution)/shard_map/ppermute | solution.py:295
  101.5 2.1 %collective-permute-done.11.p2 = f32[32,768]{1,0:T(8,128)S(1)} collective-permute-done((f32[32,768]{1,0:T(8,128)S(1)}, f32[32,768]{1,0:T(8,128)S(1)}, u32[]{:S(2)}, u32[]{:S(2)}) %collective-permute-start.11) | collective-permute-done | bytes 98336 | tf_op jit(solution)/shard_map/ppermute | solution.py:295
  104.4 1.3 collective-permute-start.13
  105.7 1.3 collective-permute-start.14
  107.0 1.3 collective-permute-start.15
  108.3 1.3 collective-permute-start.16
  109.6 1.3 collective-permute-start.17
  111.0 2.1 %collective-permute-done.15.p2 = f32[32,768]{1,0:T(8,128)S(1)} collective-permute-done((f32[32,768]{1,0:T(8,128)S(1)}, f32[32,768]{1,0:T(8,128)S(1)}, u32[]{:S(2)}, u32[]{:S(2)}) %collective-permute-start.15) | collective-permute-done | bytes 98336 | tf_op jit(solution)/shard_map/ppermute | solution.py:295
  119.6 1.3 collective-permute-start.30
  120.9 1.3 collective-permute-start.29
  122.2 1.3 shard_map.93
  126.3 3.4 %collective-permute-done.29 = f32[32,768]{1,0:T(8,128)S(1)} collective-permute-done((f32[32,768]{1,0:T(8,128)S(1)}, f32[32,768]{1,0:T(8,128)S(1)}, u32[]{:S(2)}, u32[]{:S(2)}) %collective-permute-start.29) | collective-permute-done | bytes 98336 | tf_op jit(solution)/shard_map/ppermute | solution.py:295
  131.3 2.3 %copy-done.2 = f32[3072,384]{1,0:T(8,128)S(1)} copy-done((f32[3072,384]{1,0:T(8,128)S(1)}, f32[3072,384]{1,0:T(8,128)}, u32[]{:S(2)}) %copy-start.2) | copy-done | bytes 4718616
  134.6 1.4 collective-permute-start.31
  137.4 1.3 collective-permute-start.34
  138.7 1.3 collective-permute-start.35
  140.0 1.3 collective-permute-start.36
  141.3 1.3 collective-permute-start.37
  142.6 14.8 %collective-permute-done.31 = f32[2,32,768]{2,1,0:T(8,128)S(1)} collective-permute-done((f32[2,32,768]{2,1,0:T(8,128)S(1)}, f32[2,32,768]{2,1,0:T(8,128)S(1)}, u32[]{:S(2)}, u32[]{:S(2)}) %collective-permute-start.31) | collective-permute-done | bytes 196640 | tf_op jit(solution)/shard_map/ppermute | solution.py:295
  157.5 1.9 collective-permute-done.34.f0
  159.5 3.8 %collective-permute-done.35.f1 = f32[32,192]{1,0:T(8,128)S(1)} collective-permute-done((f32[32,192]{1,0:T(8,128)S(1)}, f32[32,192]{1,0:T(8,128)S(1)}, u32[]{:S(2)}, u32[]{:S(2)}) %collective-permute-start.35) | collective-permute-done | bytes 24608 | tf_op jit(solution)/shard_map/ppermute | solution.py:295
  166.7 1.3 collective-permute-start.39
  168.0 1.3 collective-permute-start.40
  169.3 1.9 collective-permute-start.41
  171.2 1.3 collective-permute-start.42
  175.0 1.3 shard_map.97
  176.4 10.3 %all_to_all.11.got_ref = f32[8,32,256]{2,1,0:T(8,128)S(1)} all-to-all(f32[8,32,256]{2,1,0:T(8,128)S(1)} %shard_map.97), channel_id=1, replica_groups=mesh['row'=16,'col'=8] {'col'}, dimensions={0} | all-to-all | bytes 524288 | tf_op jit(solution)/shard_map/all_to_all | solution.py:422
  (94 shorter events, 31.3 us)
Async XLA Ops:
  7.2 56.3 %all-gather.5.cloned.1.call-start = ((), (), s32[]{:S(2)}) async-start(), calls=%async_computation.2 | async-start | bytes 5308416 | tf_op jit(solution)/shard_map/all_gather | solution.py:309
  9.4 121.9 %all-gather.7.cloned.1.call-start = ((), (), s32[]{:S(2)}) async-start(), calls=%async_computation.3 | async-start | bytes 5308416 | tf_op jit(solution)/shard_map/all_gather | solution.py:309
  11.8 33.8 %copy-start.5 = (f32[2,192,384]{2,1,0:T(8,128)S(1)}, f32[2,192,384]{2,1,0:T(8,128)}, u32[]{:S(2)}) copy-start(f32[2,192,384]{2,1,0:T(8,128)} %param.11) | copy-start | bytes 1769476
  12.0 34.7 %copy-start.6 = (s32[3072]{0:T(1024)S(1)}, s32[3072]{0:T(1024)}, u32[]{:S(2)}) copy-start(s32[3072]{0:T(1024)} %param.13) | copy-start | bytes 36868
  66.8 5.9 %collective-permute-start = (f32[32,192]{1,0:T(8,128)S(1)}, f32[32,192]{1,0:T(8,128)S(1)}, u32[]{:S(2)}, u32[]{:S(2)}) collective-permute-start(f32[32,192]{1,0:T(8,128)S(1)} %shard_map.88.acc_ref), channel_id=1, source_target_pairs={{32,64},{40,72},{48,80},{56,88},{33,65},{41,73},{49,81},{57,89},{3... | collective-permute-start | bytes 73736 | tf_op jit(solution)/shard_map/ppermute | solution.py:295
  68.2 8.0 %collective-permute-start.1 = (f32[32,192]{1,0:T(8,128)S(1)}, f32[32,192]{1,0:T(8,128)S(1)}, u32[]{:S(2)}, u32[]{:S(2)}) collective-permute-start(f32[32,192]{1,0:T(8,128)S(1)} %shard_map.88.acc_ref), channel_id=1, source_target_pairs={{32,72},{40,80},{48,88},{56,64},{33,73},{41,81},{49,89},{57,65},{3... | collective-permute-start | bytes 73736 | tf_op jit(solution)/shard_map/ppermute | solution.py:295
  69.5 8.9 %collective-permute-start.2 = (f32[32,192]{1,0:T(8,128)S(1)}, f32[32,192]{1,0:T(8,128)S(1)}, u32[]{:S(2)}, u32[]{:S(2)}) collective-permute-start(f32[32,192]{1,0:T(8,128)S(1)} %shard_map.88.acc_ref), channel_id=1, source_target_pairs={{32,80},{40,88},{48,64},{56,72},{33,81},{41,89},{49,65},{57,73},{3... | collective-permute-start | bytes 73736 | tf_op jit(solution)/shard_map/ppermute | solution.py:295
  70.8 8.3 %collective-permute-start.3 = (f32[32,192]{1,0:T(8,128)S(1)}, f32[32,192]{1,0:T(8,128)S(1)}, u32[]{:S(2)}, u32[]{:S(2)}) collective-permute-start(f32[32,192]{1,0:T(8,128)S(1)} %shard_map.88.acc_ref), channel_id=1, source_target_pairs={{32,88},{40,64},{48,72},{56,80},{33,89},{41,65},{49,73},{57,81},{3... | collective-permute-start | bytes 73736 | tf_op jit(solution)/shard_map/ppermute | solution.py:295
  80.1 8.1 %collective-permute-start.8 = (f32[4,32,192]{2,1,0:T(8,128)S(1)}, f32[4,32,192]{2,1,0:T(8,128)S(1)}, u32[]{:S(2)}, u32[]{:S(2)}) collective-permute-start(f32[4,32,192]{2,1,0:T(8,128)S(1)} %get-tuple-element.26), channel_id=1, source_target_pairs={{64,96},{72,104},{80,112},{88,120},{65,97},{73,105},{81,113},{89,1... | collective-permute-start | bytes 294920 | tf_op jit(solution)/shard_map/ppermute | solution.py:295
  81.4 5.4 %collective-permute-start.4 = (f32[32,192]{1,0:T(8,128)S(1)}, f32[32,192]{1,0:T(8,128)S(1)}, u32[]{:S(2)}, u32[]{:S(2)}) collective-permute-start(f32[32,192]{1,0:T(8,128)S(1)} %get-tuple-element.25.acc_ref), channel_id=1, source_target_pairs={{64,96},{72,104},{80,112},{88,120},{65,97},{73,105},{81,113},{89,1... | collective-permute-start | bytes 73736 | tf_op jit(solution)/shard_map/ppermute | solution.py:295
  82.7 4.1 %collective-permute-start.5 = (f32[32,192]{1,0:T(8,128)S(1)}, f32[32,192]{1,0:T(8,128)S(1)}, u32[]{:S(2)}, u32[]{:S(2)}) collective-permute-start(f32[32,192]{1,0:T(8,128)S(1)} %get-tuple-element.25.acc_ref), channel_id=1, source_target_pairs={{64,104},{72,112},{80,120},{88,96},{65,105},{73,113},{81,121},{89,... | collective-permute-start | bytes 73736 | tf_op jit(solution)/shard_map/ppermute | solution.py:295
  84.0 3.1 %collective-permute-start.6 = (f32[32,192]{1,0:T(8,128)S(1)}, f32[32,192]{1,0:T(8,128)S(1)}, u32[]{:S(2)}, u32[]{:S(2)}) collective-permute-start(f32[32,192]{1,0:T(8,128)S(1)} %get-tuple-element.25.acc_ref), channel_id=1, source_target_pairs={{64,112},{72,120},{80,96},{88,104},{65,113},{73,121},{81,97},{89,1... | collective-permute-start | bytes 73736 | tf_op jit(solution)/shard_map/ppermute | solution.py:295
  85.3 2.9 %collective-permute-start.7 = (f32[32,192]{1,0:T(8,128)S(1)}, f32[32,192]{1,0:T(8,128)S(1)}, u32[]{:S(2)}, u32[]{:S(2)}) collective-permute-start(f32[32,192]{1,0:T(8,128)S(1)} %get-tuple-element.25.acc_ref), channel_id=1, source_target_pairs={{64,120},{72,96},{80,104},{88,112},{65,121},{73,97},{81,105},{89,1... | collective-permute-start | bytes 73736 | tf_op jit(solution)/shard_map/ppermute | solution.py:295
  89.9 7.1 %collective-permute-start.9 = (f32[32,768]{1,0:T(8,128)S(1)}, f32[32,768]{1,0:T(8,128)S(1)}, u32[]{:S(2)}, u32[]{:S(2)}) collective-permute-start(f32[32,768]{1,0:T(8,128)S(1)} %get-tuple-element.29), channel_id=1, source_target_pairs={{96,64},{104,72},{112,80},{120,88},{97,65},{105,73},{113,81},{121,... | collective-permute-start | bytes 294920 | tf_op jit(solution)/shard_map/ppermute | solution.py:295
  91.2 10.4 %collective-permute-start.10 = (f32[32,768]{1,0:T(8,128)S(1)}, f32[32,768]{1,0:T(8,128)S(1)}, u32[]{:S(2)}, u32[]{:S(2)}) collective-permute-start(f32[32,768]{1,0:T(8,128)S(1)} %get-tuple-element.29), channel_id=1, source_target_pairs={{96,72},{104,80},{112,88},{120,64},{97,73},{105,81},{113,89},{121,... | collective-permute-start | bytes 294920 | tf_op jit(solution)/shard_map/ppermute | solution.py:295
  92.5 11.2 %collective-permute-start.11 = (f32[32,768]{1,0:T(8,128)S(1)}, f32[32,768]{1,0:T(8,128)S(1)}, u32[]{:S(2)}, u32[]{:S(2)}) collective-permute-start(f32[32,768]{1,0:T(8,128)S(1)} %get-tuple-element.29), channel_id=1, source_target_pairs={{96,80},{104,88},{112,64},{120,72},{97,81},{105,89},{113,65},{121,... | collective-permute-start | bytes 294920 | tf_op jit(solution)/shard_map/ppermute | solution.py:295
  93.8 9.9 %collective-permute-start.12 = (f32[32,768]{1,0:T(8,128)S(1)}, f32[32,768]{1,0:T(8,128)S(1)}, u32[]{:S(2)}, u32[]{:S(2)}) collective-permute-start(f32[32,768]{1,0:T(8,128)S(1)} %get-tuple-element.29), channel_id=1, source_target_pairs={{96,88},{104,64},{112,72},{120,80},{97,89},{105,65},{113,73},{121,... | collective-permute-start | bytes 294920 | tf_op jit(solution)/shard_map/ppermute | solution.py:295
  104.4 6.5 %collective-permute-start.13 = (f32[32,768]{1,0:T(8,128)S(1)}, f32[32,768]{1,0:T(8,128)S(1)}, u32[]{:S(2)}, u32[]{:S(2)}) collective-permute-start(f32[32,768]{1,0:T(8,128)S(1)} %get-tuple-element.31), channel_id=1, source_target_pairs={{64,32},{72,40},{80,48},{88,56},{65,33},{73,41},{81,49},{89,57},{6... | collective-permute-start | bytes 294920 | tf_op jit(solution)/shard_map/ppermute | solution.py:295
  105.7 5.3 %collective-permute-start.14 = (f32[32,768]{1,0:T(8,128)S(1)}, f32[32,768]{1,0:T(8,128)S(1)}, u32[]{:S(2)}, u32[]{:S(2)}) collective-permute-start(f32[32,768]{1,0:T(8,128)S(1)} %get-tuple-element.31), channel_id=1, source_target_pairs={{64,40},{72,48},{80,56},{88,32},{65,41},{73,49},{81,57},{89,33},{6... | collective-permute-start | bytes 294920 | tf_op jit(solution)/shard_map/ppermute | solution.py:295
  107.0 6.1 %collective-permute-start.15 = (f32[32,768]{1,0:T(8,128)S(1)}, f32[32,768]{1,0:T(8,128)S(1)}, u32[]{:S(2)}, u32[]{:S(2)}) collective-permute-start(f32[32,768]{1,0:T(8,128)S(1)} %get-tuple-element.31), channel_id=1, source_target_pairs={{64,48},{72,56},{80,32},{88,40},{65,49},{73,57},{81,33},{89,41},{6... | collective-permute-start | bytes 294920 | tf_op jit(solution)/shard_map/ppermute | solution.py:295
  108.3 5.8 %collective-permute-start.16 = (f32[32,768]{1,0:T(8,128)S(1)}, f32[32,768]{1,0:T(8,128)S(1)}, u32[]{:S(2)}, u32[]{:S(2)}) collective-permute-start(f32[32,768]{1,0:T(8,128)S(1)} %get-tuple-element.31), channel_id=1, source_target_pairs={{64,56},{72,32},{80,40},{88,48},{65,57},{73,33},{81,41},{89,49},{6... | collective-permute-start | bytes 294920 | tf_op jit(solution)/shard_map/ppermute | solution.py:295
  109.6 5.5 %collective-permute-start.17 = (f32[32,768]{1,0:T(8,128)S(1)}, f32[32,768]{1,0:T(8,128)S(1)}, u32[]{:S(2)}, u32[]{:S(2)}) collective-permute-start(f32[32,768]{1,0:T(8,128)S(1)} %get-tuple-element.32), channel_id=1, source_target_pairs={{64,32},{72,40},{80,48},{88,56},{65,33},{73,41},{81,49},{89,57},{6... | collective-permute-start | bytes 294920 | tf_op jit(solution)/shard_map/ppermute | solution.py:295
  116.1 3.4 %collective-permute-start.18 = (f32[32,768]{1,0:T(8,128)S(1)}, f32[32,768]{1,0:T(8,128)S(1)}, u32[]{:S(2)}, u32[]{:S(2)}) collective-permute-start(f32[32,768]{1,0:T(8,128)S(1)} %get-tuple-element.34), channel_id=1, source_target_pairs={{32,0},{40,8},{48,16},{56,24},{33,1},{41,9},{49,17},{57,25},{34,2}... | collective-permute-start | bytes 294920 | tf_op jit(solution)/shard_map/ppermute | solution.py:295
  116.8 4.0 %collective-permute-start.19 = (f32[32,768]{1,0:T(8,128)S(1)}, f32[32,768]{1,0:T(8,128)S(1)}, u32[]{:S(2)}, u32[]{:S(2)}) collective-permute-start(f32[32,768]{1,0:T(8,128)S(1)} %get-tuple-element.34), channel_id=1, source_target_pairs={{32,8},{40,16},{48,24},{56,0},{33,9},{41,17},{49,25},{57,1},{34,10... | collective-permute-start | bytes 294920 | tf_op jit(solution)/shard_map/ppermute | solution.py:295
  117.5 4.7 %collective-permute-start.20 = (f32[32,768]{1,0:T(8,128)S(1)}, f32[32,768]{1,0:T(8,128)S(1)}, u32[]{:S(2)}, u32[]{:S(2)}) collective-permute-start(f32[32,768]{1,0:T(8,128)S(1)} %get-tuple-element.34), channel_id=1, source_target_pairs={{32,16},{40,24},{48,0},{56,8},{33,17},{41,25},{49,1},{57,9},{34,18... | collective-permute-start | bytes 294920 | tf_op jit(solution)/shard_map/ppermute | solution.py:295
  118.2 4.0 %collective-permute-start.21 = (f32[32,768]{1,0:T(8,128)S(1)}, f32[32,768]{1,0:T(8,128)S(1)}, u32[]{:S(2)}, u32[]{:S(2)}) collective-permute-start(f32[32,768]{1,0:T(8,128)S(1)} %get-tuple-element.34), channel_id=1, source_target_pairs={{32,24},{40,0},{48,8},{56,16},{33,25},{41,1},{49,9},{57,17},{34,26... | collective-permute-start | bytes 294920 | tf_op jit(solution)/shard_map/ppermute | solution.py:295
  118.8 3.3 %collective-permute-start.22 = (f32[2,32,768]{2,1,0:T(8,128)S(1)}, f32[2,32,768]{2,1,0:T(8,128)S(1)}, u32[]{:S(2)}, u32[]{:S(2)}) collective-permute-start(f32[2,32,768]{2,1,0:T(8,128)S(1)} %get-tuple-element.35), channel_id=1, source_target_pairs={{32,0},{40,8},{48,16},{56,24},{33,1},{41,9},{49,17},{57,25},{34,2}... | collective-permute-start | bytes 589832 | tf_op jit(solution)/shard_map/ppermute | solution.py:295
  119.6 6.1 %collective-permute-start.30 = (f32[32,768]{1,0:T(8,128)S(1)}, f32[32,768]{1,0:T(8,128)S(1)}, u32[]{:S(2)}, u32[]{:S(2)}) collective-permute-start(f32[32,768]{1,0:T(8,128)S(1)} %get-tuple-element.32), channel_id=1, source_target_pairs={{64,96},{72,104},{80,112},{88,120},{65,97},{73,105},{81,113},{89,1... | collective-permute-start | bytes 294920 | tf_op jit(solution)/shard_map/ppermute | solution.py:295
  120.9 8.9 %collective-permute-start.29 = (f32[32,768]{1,0:T(8,128)S(1)}, f32[32,768]{1,0:T(8,128)S(1)}, u32[]{:S(2)}, u32[]{:S(2)}) collective-permute-start(f32[32,768]{1,0:T(8,128)S(1)} %slice_bitcast_fusion.7), channel_id=1, source_target_pairs={{32,64},{40,72},{48,80},{56,88},{33,65},{41,73},{49,81},{57,89},{3... | collective-permute-start | bytes 294920 | tf_op jit(solution)/shard_map/ppermute | solution.py:295
  123.6 7.5 %collective-permute-start.28 = (f32[2,32,768]{2,1,0:T(8,128)S(1)}, f32[2,32,768]{2,1,0:T(8,128)S(1)}, u32[]{:S(2)}, u32[]{:S(2)}) collective-permute-start(f32[2,32,768]{2,1,0:T(8,128)S(1)} %get-tuple-element.37), channel_id=1, source_target_pairs={{0,96},{8,104},{16,112},{24,120},{1,97},{9,105},{17,113},{25,121},... | collective-permute-start | bytes 589832 | tf_op jit(solution)/shard_map/ppermute | solution.py:295
  124.3 6.1 %collective-permute-start.27 = (f32[32,768]{1,0:T(8,128)S(1)}, f32[32,768]{1,0:T(8,128)S(1)}, u32[]{:S(2)}, u32[]{:S(2)}) collective-permute-start(f32[32,768]{1,0:T(8,128)S(1)} %slice_bitcast_fusion.8), channel_id=1, source_target_pairs={{0,32},{8,40},{16,48},{24,56},{1,33},{9,41},{17,49},{25,57},{2,34}... | collective-permute-start | bytes 294920 | tf_op jit(solution)/shard_map/ppermute | solution.py:295
  124.9 6.2 %collective-permute-start.23 = (f32[32,768]{1,0:T(8,128)S(1)}, f32[32,768]{1,0:T(8,128)S(1)}, u32[]{:S(2)}, u32[]{:S(2)}) collective-permute-start(f32[32,768]{1,0:T(8,128)S(1)} %get-tuple-element.36), channel_id=1, source_target_pairs={{0,32},{8,40},{16,48},{24,56},{1,33},{9,41},{17,49},{25,57},{2,34}... | collective-permute-start | bytes 294920 | tf_op jit(solution)/shard_map/ppermute | solution.py:295
  125.6 5.6 %collective-permute-start.24 = (f32[32,768]{1,0:T(8,128)S(1)}, f32[32,768]{1,0:T(8,128)S(1)}, u32[]{:S(2)}, u32[]{:S(2)}) collective-permute-start(f32[32,768]{1,0:T(8,128)S(1)} %get-tuple-element.36), channel_id=1, source_target_pairs={{0,40},{8,48},{16,56},{24,32},{1,41},{9,49},{17,57},{25,33},{2,42}... | collective-permute-start | bytes 294920 | tf_op jit(solution)/shard_map/ppermute | solution.py:295
  129.7 1.5 collective-permute-start.25
  130.4 0.8 collective-permute-start.26
  133.6 30.5 %copy-start.3 = (f32[3072,384]{1,0:T(8,128)S(1)}, f32[3072,384]{1,0:T(8,128)}, u32[]{:S(2)}) copy-start(f32[3072,384]{1,0:T(8,128)} %all-gather.7.cloned.1.call-done) | copy-start | bytes 14155780
  134.6 22.9 %collective-permute-start.31 = (f32[2,32,768]{2,1,0:T(8,128)S(1)}, f32[2,32,768]{2,1,0:T(8,128)S(1)}, u32[]{:S(2)}, u32[]{:S(2)}) collective-permute-start(f32[2,32,768]{2,1,0:T(8,128)S(1)} %get-tuple-element.40), channel_id=1, source_target_pairs={{32,64},{40,72},{48,80},{56,88},{33,65},{41,73},{49,81},{57,89},{3... | collective-permute-start | bytes 589832 | tf_op jit(solution)/shard_map/ppermute | solution.py:295
  136.0 4.0 %collective-permute-start.33 = (f32[32,768]{1,0:T(8,128)S(1)}, f32[32,768]{1,0:T(8,128)S(1)}, u32[]{:S(2)}, u32[]{:S(2)}) collective-permute-start(f32[32,768]{1,0:T(8,128)S(1)} %slice_bitcast_fusion.6), channel_id=1, source_target_pairs={{32,0},{40,8},{48,16},{56,24},{33,1},{41,9},{49,17},{57,25},{34,2}... | collective-permute-start | bytes 294920 | tf_op jit(solution)/shard_map/ppermute | solution.py:295
  136.7 4.6 %collective-permute-start.32 = (f32[32,768]{1,0:T(8,128)S(1)}, f32[32,768]{1,0:T(8,128)S(1)}, u32[]{:S(2)}, u32[]{:S(2)}) collective-permute-start(f32[32,768]{1,0:T(8,128)S(1)} %slice_bitcast_fusion.6), channel_id=1, source_target_pairs={{32,96},{40,104},{48,112},{56,120},{33,97},{41,105},{49,113},{57,1... | collective-permute-start | bytes 294920 | tf_op jit(solution)/shard_map/ppermute | solution.py:295
  137.4 22.0 %collective-permute-start.34 = (f32[32,192]{1,0:T(8,128)S(1)}, f32[32,192]{1,0:T(8,128)S(1)}, u32[]{:S(2)}, u32[]{:S(2)}) collective-permute-start(f32[32,192]{1,0:T(8,128)S(1)} %get-tuple-element.41), channel_id=1, source_target_pairs={{32,64},{40,72},{48,80},{56,88},{33,65},{41,73},{49,81},{57,89},{3... | collective-permute-start | bytes 73736 | tf_op jit(solution)/shard_map/ppermute | solution.py:295
  138.7 24.6 %collective-permute-start.35 = (f32[32,192]{1,0:T(8,128)S(1)}, f32[32,192]{1,0:T(8,128)S(1)}, u32[]{:S(2)}, u32[]{:S(2)}) collective-permute-start(f32[32,192]{1,0:T(8,128)S(1)} %get-tuple-element.41), channel_id=1, source_target_pairs={{32,72},{40,80},{48,88},{56,64},{33,73},{41,81},{49,89},{57,65},{3... | collective-permute-start | bytes 73736 | tf_op jit(solution)/shard_map/ppermute | solution.py:295
  140.0 23.9 %collective-permute-start.36 = (f32[32,192]{1,0:T(8,128)S(1)}, f32[32,192]{1,0:T(8,128)S(1)}, u32[]{:S(2)}, u32[]{:S(2)}) collective-permute-start(f32[32,192]{1,0:T(8,128)S(1)} %get-tuple-element.41), channel_id=1, source_target_pairs={{32,80},{40,88},{48,64},{56,72},{33,81},{41,89},{49,65},{57,73},{3... | collective-permute-start | bytes 73736 | tf_op jit(solution)/shard_map/ppermute | solution.py:295
  141.3 22.8 %collective-permute-start.37 = (f32[32,192]{1,0:T(8,128)S(1)}, f32[32,192]{1,0:T(8,128)S(1)}, u32[]{:S(2)}, u32[]{:S(2)}) collective-permute-start(f32[32,192]{1,0:T(8,128)S(1)} %get-tuple-element.41), channel_id=1, source_target_pairs={{32,88},{40,64},{48,72},{56,80},{33,89},{41,65},{49,73},{57,81},{3... | collective-permute-start | bytes 73736 | tf_op jit(solution)/shard_map/ppermute | solution.py:295
  165.4 8.9 %collective-permute-start.38 = (f32[32,192]{1,0:T(8,128)S(1)}, f32[32,192]{1,0:T(8,128)S(1)}, u32[]{:S(2)}, u32[]{:S(2)}) collective-permute-start(f32[32,192]{1,0:T(8,128)S(1)} %get-tuple-element.42.acc_ref), channel_id=1, source_target_pairs={{64,96},{72,104},{80,112},{88,120},{65,97},{73,105},{81,113},{89,1... | collective-permute-start | bytes 73736 | tf_op jit(solution)/shard_map/ppermute | solution.py:295
  166.7 7.6 %collective-permute-start.39 = (f32[32,192]{1,0:T(8,128)S(1)}, f32[32,192]{1,0:T(8,128)S(1)}, u32[]{:S(2)}, u32[]{:S(2)}) collective-permute-start(f32[32,192]{1,0:T(8,128)S(1)} %get-tuple-element.42.acc_ref), channel_id=1, source_target_pairs={{64,104},{72,112},{80,120},{88,96},{65,105},{73,113},{81,121},{89,... | collective-permute-start | bytes 73736 | tf_op jit(solution)/shard_map/ppermute | solution.py:295
  168.0 6.3 %collective-permute-start.40 = (f32[32,192]{1,0:T(8,128)S(1)}, f32[32,192]{1,0:T(8,128)S(1)}, u32[]{:S(2)}, u32[]{:S(2)}) collective-permute-start(f32[32,192]{1,0:T(8,128)S(1)} %get-tuple-element.42.acc_ref), channel_id=1, source_target_pairs={{64,112},{72,120},{80,96},{88,104},{65,113},{73,121},{81,97},{89,1... | collective-permute-start | bytes 73736 | tf_op jit(solution)/shard_map/ppermute | solution.py:295
  169.3 5.0 %collective-permute-start.41 = (f32[32,192]{1,0:T(8,128)S(1)}, f32[32,192]{1,0:T(8,128)S(1)}, u32[]{:S(2)}, u32[]{:S(2)}) collective-permute-start(f32[32,192]{1,0:T(8,128)S(1)} %get-tuple-element.42.acc_ref), channel_id=1, source_target_pairs={{64,120},{72,96},{80,104},{88,112},{65,121},{73,97},{81,105},{89,1... | collective-permute-start | bytes 73736 | tf_op jit(solution)/shard_map/ppermute | solution.py:295
  171.2 3.8 %collective-permute-start.42 = (f32[4,32,192]{2,1,0:T(8,128)S(1)}, f32[4,32,192]{2,1,0:T(8,128)S(1)}, u32[]{:S(2)}, u32[]{:S(2)}) collective-permute-start(f32[4,32,192]{2,1,0:T(8,128)S(1)} %get-tuple-element.43), channel_id=1, source_target_pairs={{64,96},{72,104},{80,112},{88,120},{65,97},{73,105},{81,113},{89,1... | collective-permute-start | bytes 294920 | tf_op jit(solution)/shard_map/ppermute | solution.py:295
  (4 other events, 37.8 us)
Sparse Core Ops, SparseCore 0:
  9.7 53.7 all-gather.4
  65.1 34.1 all-gather.6

commit v2 on v1

v2 whole, which is shorter than its diff:
```python
import functools

import jax
import jax.numpy as jnp
from jax import lax
from jax.experimental import pallas as pl
from jax.experimental.pallas import tpu as pltpu
from jax.sharding import PartitionSpec as P

GROUP = 4
CHUNK = 16
ROWS = 2 * CHUNK
SLAB = 192
BLOCK = 768
PIECE = 96
CELLS = 24
VMEM = 40 * 1024 * 1024

SDS = jax.ShapeDtypeStruct
f32 = jnp.float32


def split(value):
    high = value.astype(jnp.bfloat16)
    return high, (value - high.astype(f32)).astype(jnp.bfloat16)


def complex_dot(vector, weight):
    half = weight.shape[1] // 2
    weight_high, weight_low = split(weight)
    high, low = split(vector)
    both = jnp.dot(
        jnp.concatenate([high, low], axis=0), weight_high, preferred_element_type=f32
    )
    total = both[:ROWS] + both[ROWS:] + jnp.dot(high, weight_low, preferred_element_type=f32)
    real = total[:CHUNK, :half] - total[CHUNK:, half:]
    imag = total[:CHUNK, half:] + total[CHUNK:, :half]
    return jnp.concatenate([real, imag], axis=0)


def block_weight(ref):
    return ref[...].reshape(BLOCK, 2 * SLAB)


def slabs_dot(slabs, weight_ref, q, keep=None):
    total = None
    for d, slab in enumerate(slabs):
        source = lax.rem(q - d + GROUP, GROUP)
        if keep is not None:
            keep[source] = slab
        weight = weight_ref[pl.ds(2 * source, 2)].reshape(SLAB, 2 * SLAB)
        part = complex_dot(slab, weight)
        total = part if total is None else total + part
    return total


def sent_dot(sent_ref, weight_ref):
    total = None
    for s in range(GROUP):
        weight = weight_ref[2 * s : 2 * s + 2].reshape(SLAB, 2 * SLAB)
        part = complex_dot(sent_ref[s], weight)
        total = part if total is None else total + part
    return total


def add_refs(refs):
    total = refs[0][...]
    for ref in refs[1:]:
        total = total + ref[...]
    return total


def call(body, out_shape, inputs, scratch=()):
    specs = []
    for value in inputs:
        if value.dtype == jnp.int32:
            specs.append(pl.BlockSpec(memory_space=pltpu.SMEM))
        else:
            specs.append(pl.BlockSpec(value.shape, lambda i, n=value.ndim: (0,) * n))
    outs = tuple(
        pl.BlockSpec(shape.shape, lambda i, n=len(shape.shape): (0,) * n) for shape in out_shape
    )
    return pl.pallas_call(
        body,
        grid=(1,),
        in_specs=specs,
        out_specs=outs,
        out_shape=tuple(out_shape),
        scratch_shapes=scratch,
        compiler_params=pltpu.CompilerParams(vmem_limit_bytes=VMEM),
    )(*inputs)


def pack_kernel(first_ref, second_ref, link_ref, out_ref):
    lane = lax.broadcasted_iota(jnp.int32, (6, 128), 1)
    for y in range(2):
        parts = []
        for half in range(2):
            for ref in (first_ref, second_ref):
                parts += [ref[0, y + 2 * half], ref[1, y + 2 * half]]
        for c in range(8):
            row = jnp.zeros((6, 128), f32)
            for at, part in enumerate(parts):
                shift = (16 * at - 16 * c) % 128
                moved = pltpu.roll(part, shift, 1) if shift else part
                row = jnp.where((lane >= 16 * at) & (lane < 16 * at + 16), moved, row)
            out_ref[c, 6 * y : 6 * y + 6, :] = row
    for c in range(8):
        out_ref[c, 12:16, :] = jnp.broadcast_to(link_ref[...], (4, 128))


def front_kernel(where_ref, cells_ref, mark_ref, rhs_ref, link_ref, rows_ref, links_ref):
    def some(step, carry):
        for u in range(16):
            at = step * 16 + u
            source = where_ref[at]
            rows_ref[pl.ds(at, 1), :] = cells_ref[pl.ds(source, 1), :]
            links_ref[pl.ds(at, 1), :] = cells_ref[pl.ds(source // 16 * 16 + 15, 1), :]
        return carry

    lax.fori_loop(0, 64, some, 0)
    lane = lax.broadcasted_iota(jnp.int32, (32, 128), 0).astype(f32)
    for part in range(8):
        at = slice(128 * part, 128 * part + 128)
        turned = rows_ref[at, :].T
        upper = mark_ref[0:1, at] > 0.5
        rhs_ref[:, at] = jnp.where(upper, turned[64:128], turned[0:64])
        turned = links_ref[at, :].T
        own = mark_ref[1:2, at] == lane
        real = jnp.sum(jnp.where(own, turned[0:32], 0.0), axis=0, keepdims=True)
        imag = jnp.sum(jnp.where(own, turned[32:64], 0.0), axis=0, keepdims=True)
        link_ref[0:8, at] = jnp.broadcast_to(real, (8, 128))
        link_ref[8:16, at] = jnp.broadcast_to(imag, (8, 128))


def start_kernel(place_ref, rhs_ref, weight_ref, acc_ref):
    product = complex_dot(rhs_ref[0:ROWS, 0:BLOCK], block_weight(weight_ref))
    slab = rhs_ref[0:ROWS, BLOCK : BLOCK + SLAB]
    acc_ref[...] = jnp.where(place_ref[0] > 0, slab - product, slab)


def forward_one_kernel(place_ref, acc_ref, y0, y1, y2, y3, weight_ref, out_ref, keep_ref):
    slabs = [y0[...], y1[...], y2[...], y3[...]]
    acc = acc_ref[...] - slabs_dot(slabs, weight_ref, place_ref[1], keep_ref)
    out_ref[...] = acc
    keep_ref[GROUP] = acc


def forward_two_kernel(
    place_ref, acc_ref, sent_ref, y1, y2, y3, weight2_ref, weight1_ref, inverse_ref, out_ref, part_ref
):
    slabs = [sent_ref[GROUP], y1[...], y2[...], y3[...]]
    solved = (
        acc_ref[...]
        - slabs_dot(slabs, weight2_ref, place_ref[1])
        - sent_dot(sent_ref, weight1_ref)
    )
    out_ref[...] = solved
    part_ref[...] = complex_dot(solved, inverse_ref[...])


def back_three_kernel(
    acc_ref, p0, p1, p2, p3, weight_ref, inverse_ref, x_ref, acc_out_ref, part_ref, pair_ref
):
    x = add_refs([p0, p1, p2, p3])
    acc = acc_ref[...] - complex_dot(x, block_weight(weight_ref))
    part = complex_dot(acc, inverse_ref[...])
    x_ref[...] = x
    acc_out_ref[...] = acc
    part_ref[...] = part
    pair_ref[0] = part
    pair_ref[1] = x


def back_two_kernel(
    acc_ref, got_ref, p1, p2, p3, weight2_ref, weight3_ref, inverse_ref, x_ref, acc_out_ref, part_ref, pair_ref
):
    x = add_refs([got_ref.at[0], p1, p2, p3])
    acc = (
        acc_ref[...]
        - complex_dot(got_ref[1], block_weight(weight3_ref))
        - complex_dot(x, block_weight(weight2_ref))
    )
    part = complex_dot(acc, inverse_ref[...])
    x_ref[...] = x
    acc_out_ref[...] = acc
    part_ref[...] = part
    pair_ref[0] = part
    pair_ref[1] = x


def back_one_kernel(
    acc_ref,
    x3_ref,
    got_ref,
    p1,
    p2,
    p3,
    weight1_ref,
    weight2_ref,
    weight3_ref,
    inverse_ref,
    both_ref,
    part_ref,
    pair_ref,
):
    x = add_refs([got_ref.at[0], p1, p2, p3])
    acc = (
        acc_ref[...]
        - complex_dot(x3_ref[...], block_weight(weight3_ref))
        - complex_dot(got_ref[1], block_weight(weight2_ref))
        - complex_dot(x, block_weight(weight1_ref))
    )
    part = complex_dot(acc, inverse_ref[...])
    both_ref[0] = x
    both_ref[1] = got_ref[1]
    part_ref[...] = part
    pair_ref[0] = part
    pair_ref[1] = x


def coupled(rhs, link_real, link_imag, x):
    real = rhs[:CHUNK] - (link_real * x[:CHUNK] - link_imag * x[CHUNK:])
    imag = rhs[CHUNK:] - (link_real * x[CHUNK:] + link_imag * x[:CHUNK])
    return jnp.concatenate([real, imag], axis=0)


def second_block(rhs_ref, link_ref, x):
    return coupled(
        rhs_ref[ROWS : 2 * ROWS, 0:BLOCK], link_ref[0:1, 0:BLOCK], link_ref[8:9, 0:BLOCK], x
    )


def second_slab(rhs_ref, link_ref, x, q):
    own = x[:, 0:SLAB]
    for s in range(1, GROUP):
        own = jnp.where(q == s, x[:, SLAB * s : SLAB * s + SLAB], own)
    end = BLOCK + SLAB
    return coupled(
        rhs_ref[ROWS : 2 * ROWS, BLOCK:end], link_ref[0:1, BLOCK:end], link_ref[8:9, BLOCK:end], own
    )


def couple_kernel(
    place_ref,
    rhs_ref,
    link_ref,
    got_ref,
    p1,
    p2,
    p3,
    x2_ref,
    x3_ref,
    weight_ref,
    x0_ref,
    x1_ref,
    slab_ref,
    out_ref,
    send_ref,
):
    plane, q = place_ref[0], place_ref[1]
    x0 = add_refs([got_ref.at[0], p1, p2, p3])
    x1 = got_ref[1]
    own = jnp.where(plane == 1, x1, jnp.where(plane == 2, x2_ref[...], x3_ref[...]))
    slab = second_slab(rhs_ref, link_ref, own, q)
    solved = slab - complex_dot(second_block(rhs_ref, link_ref, x0), block_weight(weight_ref))
    x0_ref[...] = x0
    x1_ref[...] = x1
    slab_ref[...] = slab
    out_ref[...] = solved
    send_ref[:, 0:BLOCK] = x0
    send_ref[:, BLOCK : BLOCK + SLAB] = solved
    send_ref[:, BLOCK + SLAB :] = jnp.zeros((ROWS, 64), f32)


def second_one_kernel(
    place_ref,
    rhs_ref,
    link_ref,
    slab_ref,
    x0_own,
    x0_zero,
    x0_three,
    got_ref,
    f1,
    f2,
    f3,
    weight0_ref,
    weight1_ref,
    out_ref,
    keep_ref,
    x0_ref,
):
    plane, q = place_ref[0], place_ref[1]
    x0 = x0_own[...] + x0_zero[...] + x0_three[...] + got_ref[:, 0:BLOCK]
    x0_ref[...] = x0
    first = second_slab(rhs_ref, link_ref, x0, q)
    slabs = [got_ref[:, BLOCK : BLOCK + SLAB], f1[...], f2[...], f3[...]]
    product = complex_dot(second_block(rhs_ref, link_ref, x0), block_weight(weight0_ref))
    later = slab_ref[...] - product - slabs_dot(slabs, weight1_ref, q, keep_ref)
    solved = jnp.where(plane == 0, first, later)
    out_ref[...] = solved
    keep_ref[GROUP] = solved


def cells_kernel(
    where_ref,
    x0_ref,
    both_zero,
    x1_one,
    x1_two,
    both_three,
    x2_one,
    x2_two,
    x3_zero,
    pair_one,
    x3_two,
    x3_three,
    out_ref,
    front_ref,
    rows_ref,
):
    blocks = (
        x0_ref[...],
        both_zero[0] + x1_one[...] + x1_two[...] + both_three[0],
        both_zero[1] + x2_one[...] + x2_two[...] + both_three[1],
        x3_zero[...] + pair_one[1] + x3_two[...] + x3_three[...],
    )
    for k, x in enumerate(blocks):
        for part in range(6):
            at = BLOCK * k + 128 * part
            piece = x[:, 128 * part : 128 * part + 128]
            wide = jnp.concatenate([piece, jnp.zeros((128 - ROWS, 128), f32)], axis=0)
            front_ref[at : at + 128, :] = wide.T
    rows_ref[...] = jnp.zeros_like(rows_ref)
    for c in range(8):
        for u in range(CELLS):
            rows_ref[64 + u : 65 + u, :] = front_ref[pl.ds(where_ref[CELLS * c + u], 1), :]
        out_ref[c] = rows_ref[...].T[:ROWS]


def second_two_kernel(
    place_ref, acc_ref, sent_ref, f1, f2, f3, cells_ref, weight2_ref, weight1_ref, out_ref
):
    slabs = [sent_ref[GROUP], f1[...], f2[...], f3[...]]
    solved = (
        acc_ref[...]
        - slabs_dot(slabs, weight2_ref, place_ref[1])
        - sent_dot(sent_ref, weight1_ref)
    )
    lane = lax.broadcasted_iota(jnp.int32, (ROWS, 128), 1)
    tail = jnp.concatenate([solved[:, 128:], jnp.zeros((ROWS, 64), f32)], axis=1)
    for c in range(8):
        out_ref[c, :, 0:128] = solved[:, 0:128]
        out_ref[c, :, 128:256] = jnp.where(lane < 64, tail, cells_ref[c])


def out_kernel(got_ref, solution_ref, forward_ref):
    for part in range(2):
        wide = got_ref[:, CHUNK * part : CHUNK * part + CHUNK, :].reshape(128, 256)
        forward_ref[part, 0:128, :] = wide[:, 0:128].T
        turned = wide[:, 128:256].T
        forward_ref[part, 128:SLAB, :] = turned[0:64]
        for y in range(4):
            solution_ref[part, y] = turned[64 + 6 * y : 70 + 6 * y]


def plane_send(value, source, target, turn=0):
    pairs = [
        (GROUP * source + q, GROUP * target + (q + turn) % GROUP) for q in range(GROUP)
    ]
    return lax.ppermute(value, "row", pairs)


def plane_spread(value, source, target, first=None):
    return [
        plane_send(value if first is None or d else first, source, target, d)
        for d in range(GROUP)
    ]


def after(value, arrived):
    return lax.optimization_barrier((value, arrived))[0]


def on_device(source1, source2, coupling, factor1, factor2, diag_inv, front_order):
    row_id = lax.axis_index("row")
    col_id = lax.axis_index("col")
    place = jnp.stack([row_id // GROUP, row_id % GROUP]).astype(jnp.int32)

    def gather_blocks(turned, first, count):
        piece = turned[PIECE * first : PIECE * (first + count)]
        whole = lax.all_gather(piece, "col").reshape(8, count, PIECE, 2 * SLAB)
        return [whole[:, at] for at in range(count)]

    turned1 = factor1.reshape(2 * SLAB, 4 * PIECE).T
    matrix1 = gather_blocks(turned1, 0, 1)

    links = jnp.pad(coupling.reshape(2, CELLS), ((0, 0), (0, 32 - CELLS))).reshape(1, 64)
    links = jnp.pad(links, ((0, 0), (0, 64)))
    (packed,) = call(pack_kernel, [SDS((8, 16, 128), f32)], [source1, source2, links])
    turned1, packed = lax.optimization_barrier((turned1, packed))
    matrix1 += gather_blocks(turned1, 1, 1)
    matrix1 += gather_blocks(turned1, 2, 1)
    matrix1 += gather_blocks(turned1, 3, 1)
    packed = jnp.broadcast_to(packed[None], (16, 8, 16, 128)).reshape(128, 16, 128)
    cells = lax.all_to_all(packed, ("row", "col"), 0, 0).reshape(128 * 16, 128)

    cell_y = front_order // 48
    cell_x = front_order % 48
    place_of = ((cell_y // 4) * 8 + cell_x // 6) * 16 + (cell_y % 2) * 6 + cell_x % 6
    upper = (cell_y % 4) // 2
    inner = (cell_y % 4) * 6 + cell_x % 6
    every = jnp.stack([place_of, upper, inner])
    own = lax.dynamic_slice_in_dim(every, row_id * SLAB, SLAB, 1)
    every = jnp.concatenate([every[:, :BLOCK], own, jnp.zeros((3, 64), jnp.int32)], axis=1)
    rhs, link = call(
        front_kernel,
        [SDS((64, 1024), f32), SDS((16, 1024), f32)],
        [every[0], cells, every[1:].astype(f32)],
        scratch=[pltpu.VMEM((1024, 128), f32), pltpu.VMEM((1024, 128), f32)],
    )
    factor2, diag_inv, cells = lax.optimization_barrier((factor2, diag_inv, cells))
    turned2 = factor2.reshape(2 * SLAB, 4 * PIECE).T
    matrix2 = gather_blocks(turned2, 0, 3)
    inverse = diag_inv.reshape(2 * BLOCK, SLAB).T

    slab_shape = SDS((ROWS, SLAB), f32)
    block_shape = SDS((ROWS, BLOCK), f32)
    pair_shape = SDS((2, ROWS, BLOCK), f32)
    sent_shape = SDS((GROUP + 1, ROWS, SLAB), f32)

    (acc,) = call(start_kernel, [slab_shape], [place, rhs, matrix1[0]])
    got = plane_spread(acc, 1, 2)
    acc, kept = call(
        forward_one_kernel, [slab_shape, sent_shape], [place, acc, *got, matrix1[1]]
    )
    got = plane_spread(acc, 2, 3, kept)
    acc, part = call(
        forward_two_kernel,
        [slab_shape, block_shape],
        [place, acc, *got, matrix1[2], matrix1[1], inverse],
    )
    got = plane_spread(part, 3, 2)
    x3_two, acc, part, pair = call(
        back_three_kernel,
        [block_shape, slab_shape, block_shape, pair_shape],
        [acc, *got, matrix1[3], inverse],
    )
    got = plane_spread(part, 2, 1, pair)
    pair_one = got[0]
    x3_three = plane_send(after(x3_two, got[1]), 2, 3)
    x2_one, acc, part, pair = call(
        back_two_kernel,
        [block_shape, slab_shape, block_shape, pair_shape],
        [acc, *got, matrix1[2], matrix1[3], inverse],
    )
    matrix2, part, pair = lax.optimization_barrier((matrix2, part, pair))
    got = plane_spread(part, 1, 0, pair)
    x3_zero = plane_send(x3_three, 3, 0)
    x2_two = plane_send(after(x2_one, got[1]), 1, 2)
    both_zero, part, pair = call(
        back_one_kernel,
        [pair_shape, block_shape, pair_shape],
        [acc, x3_zero, *got, matrix1[1], matrix1[2], matrix1[3], inverse],
    )
    got = plane_spread(part, 0, 1, pair)
    both_three = plane_send(after(both_zero, got[1]), 0, 3)
    x0_one, x1_one, slab, acc, send = call(
        couple_kernel,
        [block_shape, block_shape, slab_shape, slab_shape, SDS((ROWS, 1024), f32)],
        [place, rhs, link, *got, x2_two, x3_three, matrix2[0]],
    )
    got = plane_spread(acc, 1, 2, send)
    x0_zero = plane_send(after(x0_one, got[1]), 1, 0)
    x0_three = plane_send(after(x0_one, got[1]), 1, 3)
    x1_two = plane_send(after(x1_one, got[2]), 1, 2)
    acc, kept, x0_all = call(
        second_one_kernel,
        [slab_shape, sent_shape, block_shape],
        [place, rhs, link, slab, x0_one, x0_zero, x0_three, *got, matrix2[0], matrix2[1]],
    )
    got = plane_spread(acc, 2, 3, kept)

    at = jnp.arange(SLAB, dtype=jnp.int32)
    own_c, own_y, own_x = at // CELLS, at % CELLS // 6, at % 6
    own_cells = (row_id * 4 + own_y) * 48 + own_c * 6 + own_x
    hits = front_order[None, :] == own_cells[:, None]
    slots = jnp.sum(jnp.where(hits, jnp.arange(4 * BLOCK, dtype=jnp.int32)[None, :], 0), axis=1)
    (mine,) = call(
        cells_kernel,
        [SDS((8, ROWS, 128), f32)],
        [
            slots,
            x0_all,
            both_zero,
            x1_one,
            x1_two,
            both_three,
            x2_one,
            x2_two,
            x3_zero,
            pair_one,
            x3_two,
            x3_three,
        ],
        scratch=[pltpu.VMEM((4 * BLOCK, 128), f32), pltpu.VMEM((128, 128), f32)],
    )
    (last,) = call(
        second_two_kernel,
        [SDS((8, ROWS, 256), f32)],
        [place, acc, *got, mine, matrix2[2], matrix2[1]],
    )
    arrived = lax.all_to_all(last, "col", 0, 0)
    return call(
        out_kernel, [SDS((2, 4, 6, 128), f32), SDS((2, SLAB, 128), f32)], [arrived]
    )


def solution(mesh):
    in_specs = (
        P(None, "row", "col", None),
        P(None, "row", "col", None),
        P(None, "row", "col"),
        P(None, "row", "col"),
        P(None, "row", "col"),
        P(None, None, "row"),
        P(),
    )
    out_specs = (P(None, "row", "col", None), P(None, "row", None))
    return jax.shard_map(
        on_device, mesh=mesh, in_specs=in_specs, out_specs=out_specs, check_vma=False
    )
```

time: 197 us -> 239 us (1.21)
  waiting for transfers between devices: 61.4 us -> 85.5 us
  starting transfers between devices: 48.5 us -> 56.5 us
  local copies, waits for them, and re-layouts: 11.1 us -> 18.8 us
  Pallas kernels: 14.5 us -> 22.1 us
  blocking collectives: 43.9 us -> 38.1 us
    all_gather x2 -> x5, waiting for transfers between devices: 14.6 us -> 56.9 us  [gather_blocks(): whole = lax.all_gather(piece, 'col').reshape(8, count, PIECE, 2 * SLAB)]
    ppermute x43 -> x39, waiting for transfers between devices: 46.8 us -> 27.3 us  [plane_send(): return lax.ppermute(value, 'row', pairs)]
    ppermute x43 -> x39, starting transfers between devices: 48.4 us -> 56.3 us  [plane_send(): return lax.ppermute(value, 'row', pairs)]
    pallas_call x13, Pallas kernels: 14.5 us -> 22.1 us  [call(): pl.pallas_call(body, grid=(1,), in_specs=specs, out_specs=outs, out_shape...]
    all_to_all x1, blocking collectives: 33.6 us -> 27.9 us  [on_device(): cells = lax.all_to_all(packed, ('row', 'col'), 0, 0).reshape(128 * 16, 128)]
    squeeze x3 -> x1, local copies, waits for them, and re-layouts: 0.03 us -> 3.38 us  [gather_blocks(): return [whole[:, at] for at in range(count)]]
    unnamed x16 -> x70, local copies, waits for them, and re-layouts: 6.18 us -> 9.11 us
    slice x1 -> x5, local copies, waits for them, and re-layouts: 0.01 us -> 2.48 us  [the longest x3 2.47 us: gather_blocks(): piece = turned[PIECE * first:PIECE * (first + count)]]
  transfers between devices with their start and end apart: 45 -> 44, of which waited for: 20 -> 11; matrix products, arithmetic and copies ran while one was open for 2% -> 3% of each run, Pallas kernels for 5% -> 8%
where the time goes in v2:
time: 239 us; the launch traced here: 236 us
  waiting for transfers between devices  85.5 us (36%)
  starting transfers between devices  56.5 us (24%)
  blocking collectives  38.1 us (16%)
  Pallas kernels  22.1 us (9%)
  local copies, waits for them, and re-layouts  18.8 us (8%)
  between operations  14.7 us (6%)
    all_gather x5, waiting for transfers between devices, gather_blocks(): whole = lax.all_gather(piece, 'col').reshape(8, count, PIECE, 2 * SLAB)  56.9 us
    ppermute x39, starting transfers between devices, plane_send(): return lax.ppermute(value, 'row', pairs)  56.3 us
    all_to_all x1, blocking collectives, on_device(): cells = lax.all_to_all(packed, ('row', 'col'), 0, 0).reshape(128 * 16, 128)  27.9 us
    ppermute x39, waiting for transfers between devices, plane_send(): return lax.ppermute(value, 'row', pairs)  27.3 us
    pallas_call x13, Pallas kernels, call(): pl.pallas_call(body, grid=(1,), in_specs=specs, out_specs=outs, out_shape...  22.1 us
    all_to_all x1, blocking collectives, on_device(): arrived = lax.all_to_all(last, 'col', 0, 0)  10.2 us
    unnamed x70, local copies, waits for them, and re-layouts  9.11 us
  transfers between devices with their start and end apart: 44, of which 11 were waited for; matrix products, arithmetic and copies ran while one was open for 3% of the time, Pallas kernels for 8%

profile of v2, /device:TPU:4, one launch (start us, length us, event | category | flops | bytes accessed | tf_op | source)
XLA Modules:
  0.0 236.3 jit_solution(16687440373112856150)
XLA Ops:
  7.2 1.3 copy.41
  12.0 27.9 %all_to_all.10 = f32[128,16,128]{2,1,0:T(8,128)S(1)} all-to-all(f32[128,16,128]{2,1,0:T(8,128)S(1)} %bitcast.51), channel_id=1, replica_groups=mesh['row'=16,'col'=8] {'row','col'}, dimensions={0} | all-to-all | bytes 2097152 | tf_op jit(solution)/shard_map/all_to_all | solution.py:407
  41.3 6.9 %shard_map.87 = (f32[64,1024]{1,0:T(8,128)S(1)}, f32[16,1024]{1,0:T(8,128)S(1)}) custom-call(s32[1024]{0:T(1024)S(1)} %bitcast.50, f32[2048,128]{1,0:T(8,128)S(1)} %bitcast.48, f32[2,1024]{1,0:T(2,128)S(1)} %slice_convert_fusion.mark_ref), custom_call_target="tpu_custom_call" | custom-call | tf_op jit(solution)/shard_map/pallas_call | solution.py:83
  48.9 1.4 copy-done.12
  51.3 1.3 collective-permute-start.3
  52.6 1.3 collective-permute-start.2
  53.9 1.3 collective-permute-start.1
  55.2 1.3 collective-permute-start
  56.5 16.6 %all-gather.13.cloned.1.call-done = f32[768,384]{1,0:T(8,128)} async-done(((f32[96,384]{1,0:T(8,128)}), f32[768,384]{1,0:T(8,128)}) %all-gather.13.cloned.1.call-update) | async-done | bytes 1179664 | tf_op jit(solution)/shard_map/all_gather | solution.py:393
  73.1 1.3 copy-done
  75.4 3.1 %collective-permute-start.4 = (f32[5,32,192]{2,1,0:T(8,128)S(1)}, f32[5,32,192]{2,1,0:T(8,128)S(1)}, u32[]{:S(2)}, u32[]{:S(2)}) collective-permute-start(f32[5,32,192]{2,1,0:T(8,128)S(1)} %get-tuple-element.46), channel_id=1, source_target_pairs={{64,96},{72,104},{80,112},{88,120},{65,97},{73,105},{81,113},{89,1... | collective-permute-start | bytes 368648 | tf_op jit(solution)/shard_map/ppermute | solution.py:372
  78.5 3.5 %collective-permute-start.7 = (f32[32,192]{1,0:T(8,128)S(1)}, f32[32,192]{1,0:T(8,128)S(1)}, u32[]{:S(2)}, u32[]{:S(2)}) collective-permute-start(f32[32,192]{1,0:T(8,128)S(1)} %get-tuple-element.45.acc_ref), channel_id=1, source_target_pairs={{64,120},{72,96},{80,104},{88,112},{65,121},{73,97},{81,105},{89,1... | collective-permute-start | bytes 73736 | tf_op jit(solution)/shard_map/ppermute | solution.py:372
  82.0 1.6 collective-permute-start.6
  83.5 1.3 collective-permute-start.5
  84.8 1.5 copy.53
  86.3 12.2 %all-gather.15.cloned.1.call-done = f32[768,384]{1,0:T(8,128)} async-done(((f32[96,384]{1,0:T(8,128)}), f32[768,384]{1,0:T(8,128)}) %all-gather.15.cloned.1.call-update) | async-done | bytes 1179664 | tf_op jit(solution)/shard_map/all_gather | solution.py:393
  99.8 1.6 shard_map.90
  101.5 1.3 collective-permute-start.11
  102.8 1.3 collective-permute-start.10
  104.1 1.3 collective-permute-start.9
  105.4 1.3 collective-permute-start.8
  106.7 17.2 %all-gather.17.cloned.1.call-done = f32[768,384]{1,0:T(8,128)} async-done(((f32[96,384]{1,0:T(8,128)}), f32[768,384]{1,0:T(8,128)}) %all-gather.17.cloned.1.call-update) | async-done | bytes 1179664 | tf_op jit(solution)/shard_map/all_gather | solution.py:393
  125.2 1.3 shard_map.91
  126.5 2.5 %collective-permute-start.12 = (f32[2,32,768]{2,1,0:T(8,128)S(1)}, f32[2,32,768]{2,1,0:T(8,128)S(1)}, u32[]{:S(2)}, u32[]{:S(2)}) collective-permute-start(f32[2,32,768]{2,1,0:T(8,128)S(1)} %get-tuple-element.51), channel_id=1, source_target_pairs={{64,32},{72,40},{80,48},{88,56},{65,33},{73,41},{81,49},{89,57},{6... | collective-permute-start | bytes 589832 | tf_op jit(solution)/shard_map/ppermute | solution.py:372
  128.9 2.2 collective-permute-start.13
  131.2 2.6 %collective-permute-start.15 = (f32[32,768]{1,0:T(8,128)S(1)}, f32[32,768]{1,0:T(8,128)S(1)}, u32[]{:S(2)}, u32[]{:S(2)}) collective-permute-start(f32[32,768]{1,0:T(8,128)S(1)} %get-tuple-element.52), channel_id=1, source_target_pairs={{64,56},{72,32},{80,40},{88,48},{65,57},{73,33},{81,41},{89,49},{6... | collective-permute-start | bytes 294920 | tf_op jit(solution)/shard_map/ppermute | solution.py:372
  133.7 1.6 collective-permute-start.14
  136.3 1.9 collective-permute-start.16
  138.4 1.4 collective-permute-done.14.p2
  144.1 10.9 %all-gather.19.cloned.1.call-done = f32[2304,384]{1,0:T(8,128)} async-done(((f32[288,384]{1,0:T(8,128)}), f32[2304,384]{1,0:T(8,128)}) %all-gather.19.cloned.1.call-update) | async-done | bytes 3538960 | tf_op jit(solution)/shard_map/all_gather | solution.py:393
  155.0 3.4 %slice_bitcast_fusion = (f32[8,96,384]{2,1,0:T(8,128)}, f32[8,96,384]{2,1,0:T(8,128)S(1)}, f32[8,96,384]{2,1,0:T(8,128)S(1)}) fusion(f32[8,3,96,384]{3,2,1,0:T(8,128)} %bitcast.52), kind=kLoop, calls=%fused_computation.1 | loop fusion | bytes 7077888 | tf_op jit(solution)/shard_map/squeeze | solution.py:394
  161.9 1.9 shard_map.93
  165.3 1.3 collective-permute-start.26
  168.7 12.8 %collective-permute-done.26.x2_ref.x2_two = f32[32,768]{1,0:T(8,128)S(1)} collective-permute-done((f32[32,768]{1,0:T(8,128)S(1)}, f32[32,768]{1,0:T(8,128)S(1)}, u32[]{:S(2)}, u32[]{:S(2)}) %collective-permute-start.26) | collective-permute-done | bytes 98336 | tf_op jit(solution)/shard_map/ppermute | solution.py:372
  181.5 2.0 shard_map.94
  183.5 1.3 collective-permute-start.27
  184.7 1.3 collective-permute-start.31
  186.0 1.3 collective-permute-start.30
  187.3 1.3 collective-permute-start.32
  188.6 10.3 %collective-permute-done.27.f1 = f32[32,192]{1,0:T(8,128)S(1)} collective-permute-done((f32[32,192]{1,0:T(8,128)}, f32[32,192]{1,0:T(8,128)S(1)}, u32[]{:S(2)}, u32[]{:S(2)}) %collective-permute-start.27) | collective-permute-done | bytes 24608 | tf_op jit(solution)/shard_map/ppermute | solution.py:372
  201.3 1.3 collective-permute-start.37
  203.9 5.8 %collective-permute-start.36 = (f32[32,192]{1,0:T(8,128)S(1)}, f32[32,192]{1,0:T(8,128)S(1)}, u32[]{:S(2)}, u32[]{:S(2)}) collective-permute-start(f32[32,192]{1,0:T(8,128)S(1)} %get-tuple-element.72.acc_ref), channel_id=1, source_target_pairs={{64,120},{72,96},{80,104},{88,112},{65,121},{73,97},{81,105},{89,1... | collective-permute-start | bytes 73736 | tf_op jit(solution)/shard_map/ppermute | solution.py:372
  209.7 1.6 collective-permute-start.35
  211.3 1.3 collective-permute-start.34
  212.6 1.3 collective-permute-start.33
  214.4 1.8 shard_map.96.cells_ref
  216.8 1.3 shard_map.97
  218.1 10.2 %all_to_all.11.got_ref = f32[8,32,256]{2,1,0:T(8,128)S(1)} all-to-all(f32[8,32,256]{2,1,0:T(8,128)S(1)} %shard_map.97), channel_id=1, replica_groups=mesh['row'=16,'col'=8] {'col'}, dimensions={0} | all-to-all | bytes 524288 | tf_op jit(solution)/shard_map/all_to_all | solution.py:514
  (154 shorter events, 28.3 us)
Async XLA Ops:
  7.2 41.7 %all-gather.11.cloned.1.call-start = ((), (), s32[]{:S(2)}) async-start(), calls=%async_computation.2 | async-start | bytes 1327104 | tf_op jit(solution)/shard_map/all_gather | solution.py:393
  9.2 63.8 %all-gather.13.cloned.1.call-start = ((), (), s32[]{:S(2)}) async-start(), calls=%async_computation.3 | async-start | bytes 1327104 | tf_op jit(solution)/shard_map/all_gather | solution.py:393
  10.5 88.0 %all-gather.15.cloned.1.call-start = ((), (), s32[]{:S(2)}) async-start(), calls=%async_computation.4 | async-start | bytes 1327104 | tf_op jit(solution)/shard_map/all_gather | solution.py:393
  11.3 112.6 %all-gather.17.cloned.1.call-start = ((), (), s32[]{:S(2)}) async-start(), calls=%async_computation.5 | async-start | bytes 1327104 | tf_op jit(solution)/shard_map/all_gather | solution.py:393
  11.8 143.1 %all-gather.19.cloned.1.call-start = ((), (), s32[]{:S(2)}) async-start(), calls=%async_computation.6 | async-start | bytes 3981312 | tf_op jit(solution)/shard_map/all_gather | solution.py:393
  12.0 27.9 %copy-start.29 = (f32[2,192,384]{2,1,0:T(8,128)S(1)}, f32[2,192,384]{2,1,0:T(8,128)}, u32[]{:S(2)}) copy-start(f32[2,192,384]{2,1,0:T(8,128)} %param.11) | copy-start | bytes 1769476
  48.9 26.5 %copy-start.9 = (f32[64,1024]{1,0:T(8,128)}, f32[64,1024]{1,0:T(8,128)S(1)}, u32[]{:S(2)}) copy-start(f32[64,1024]{1,0:T(8,128)S(1)} %get-tuple-element.42.rhs_ref) | copy-start | bytes 786436
  51.3 21.8 %collective-permute-start.3 = (f32[32,192]{1,0:T(8,128)S(1)}, f32[32,192]{1,0:T(8,128)S(1)}, u32[]{:S(2)}, u32[]{:S(2)}) collective-permute-start(f32[32,192]{1,0:T(8,128)S(1)} %shard_map.88.acc_ref), channel_id=1, source_target_pairs={{32,88},{40,64},{48,72},{56,80},{33,89},{41,65},{49,73},{57,81},{3... | collective-permute-start | bytes 73736 | tf_op jit(solution)/shard_map/ppermute | solution.py:372
  52.6 20.5 %collective-permute-start.2 = (f32[32,192]{1,0:T(8,128)S(1)}, f32[32,192]{1,0:T(8,128)S(1)}, u32[]{:S(2)}, u32[]{:S(2)}) collective-permute-start(f32[32,192]{1,0:T(8,128)S(1)} %shard_map.88.acc_ref), channel_id=1, source_target_pairs={{32,80},{40,88},{48,64},{56,72},{33,81},{41,89},{49,65},{57,73},{3... | collective-permute-start | bytes 73736 | tf_op jit(solution)/shard_map/ppermute | solution.py:372
  53.9 19.2 %collective-permute-start.1 = (f32[32,192]{1,0:T(8,128)S(1)}, f32[32,192]{1,0:T(8,128)S(1)}, u32[]{:S(2)}, u32[]{:S(2)}) collective-permute-start(f32[32,192]{1,0:T(8,128)S(1)} %shard_map.88.acc_ref), channel_id=1, source_target_pairs={{32,72},{40,80},{48,88},{56,64},{33,73},{41,81},{49,89},{57,65},{3... | collective-permute-start | bytes 73736 | tf_op jit(solution)/shard_map/ppermute | solution.py:372
  55.2 17.9 %collective-permute-start = (f32[32,192]{1,0:T(8,128)S(1)}, f32[32,192]{1,0:T(8,128)S(1)}, u32[]{:S(2)}, u32[]{:S(2)}) collective-permute-start(f32[32,192]{1,0:T(8,128)S(1)} %shard_map.88.acc_ref), channel_id=1, source_target_pairs={{32,64},{40,72},{48,80},{56,88},{33,65},{41,73},{49,81},{57,89},{3... | collective-permute-start | bytes 73736 | tf_op jit(solution)/shard_map/ppermute | solution.py:372
  75.4 23.2 %collective-permute-start.4 = (f32[5,32,192]{2,1,0:T(8,128)S(1)}, f32[5,32,192]{2,1,0:T(8,128)S(1)}, u32[]{:S(2)}, u32[]{:S(2)}) collective-permute-start(f32[5,32,192]{2,1,0:T(8,128)S(1)} %get-tuple-element.46), channel_id=1, source_target_pairs={{64,96},{72,104},{80,112},{88,120},{65,97},{73,105},{81,113},{89,1... | collective-permute-start | bytes 368648 | tf_op jit(solution)/shard_map/ppermute | solution.py:372
  78.5 20.1 %collective-permute-start.7 = (f32[32,192]{1,0:T(8,128)S(1)}, f32[32,192]{1,0:T(8,128)S(1)}, u32[]{:S(2)}, u32[]{:S(2)}) collective-permute-start(f32[32,192]{1,0:T(8,128)S(1)} %get-tuple-element.45.acc_ref), channel_id=1, source_target_pairs={{64,120},{72,96},{80,104},{88,112},{65,121},{73,97},{81,105},{89,1... | collective-permute-start | bytes 73736 | tf_op jit(solution)/shard_map/ppermute | solution.py:372
  82.0 16.6 %collective-permute-start.6 = (f32[32,192]{1,0:T(8,128)S(1)}, f32[32,192]{1,0:T(8,128)S(1)}, u32[]{:S(2)}, u32[]{:S(2)}) collective-permute-start(f32[32,192]{1,0:T(8,128)S(1)} %get-tuple-element.45.acc_ref), channel_id=1, source_target_pairs={{64,112},{72,120},{80,96},{88,104},{65,113},{73,121},{81,97},{89,1... | collective-permute-start | bytes 73736 | tf_op jit(solution)/shard_map/ppermute | solution.py:372
  83.5 15.0 %collective-permute-start.5 = (f32[32,192]{1,0:T(8,128)S(1)}, f32[32,192]{1,0:T(8,128)S(1)}, u32[]{:S(2)}, u32[]{:S(2)}) collective-permute-start(f32[32,192]{1,0:T(8,128)S(1)} %get-tuple-element.45.acc_ref), channel_id=1, source_target_pairs={{64,104},{72,112},{80,120},{88,96},{65,105},{73,113},{81,121},{89,... | collective-permute-start | bytes 73736 | tf_op jit(solution)/shard_map/ppermute | solution.py:372
  101.5 22.4 %collective-permute-start.11 = (f32[32,768]{1,0:T(8,128)S(1)}, f32[32,768]{1,0:T(8,128)S(1)}, u32[]{:S(2)}, u32[]{:S(2)}) collective-permute-start(f32[32,768]{1,0:T(8,128)S(1)} %get-tuple-element.49), channel_id=1, source_target_pairs={{96,88},{104,64},{112,72},{120,80},{97,89},{105,65},{113,73},{121,... | collective-permute-start | bytes 294920 | tf_op jit(solution)/shard_map/ppermute | solution.py:372
  102.8 21.1 %collective-permute-start.10 = (f32[32,768]{1,0:T(8,128)S(1)}, f32[32,768]{1,0:T(8,128)S(1)}, u32[]{:S(2)}, u32[]{:S(2)}) collective-permute-start(f32[32,768]{1,0:T(8,128)S(1)} %get-tuple-element.49), channel_id=1, source_target_pairs={{96,80},{104,88},{112,64},{120,72},{97,81},{105,89},{113,65},{121,... | collective-permute-start | bytes 294920 | tf_op jit(solution)/shard_map/ppermute | solution.py:372
  104.1 19.8 %collective-permute-start.9 = (f32[32,768]{1,0:T(8,128)S(1)}, f32[32,768]{1,0:T(8,128)S(1)}, u32[]{:S(2)}, u32[]{:S(2)}) collective-permute-start(f32[32,768]{1,0:T(8,128)S(1)} %get-tuple-element.49), channel_id=1, source_target_pairs={{96,72},{104,80},{112,88},{120,64},{97,73},{105,81},{113,89},{121,... | collective-permute-start | bytes 294920 | tf_op jit(solution)/shard_map/ppermute | solution.py:372
  105.4 18.5 %collective-permute-start.8 = (f32[32,768]{1,0:T(8,128)S(1)}, f32[32,768]{1,0:T(8,128)S(1)}, u32[]{:S(2)}, u32[]{:S(2)}) collective-permute-start(f32[32,768]{1,0:T(8,128)S(1)} %get-tuple-element.49), channel_id=1, source_target_pairs={{96,64},{104,72},{112,80},{120,88},{97,65},{105,73},{113,81},{121,... | collective-permute-start | bytes 294920 | tf_op jit(solution)/shard_map/ppermute | solution.py:372
  126.5 13.4 %collective-permute-start.12 = (f32[2,32,768]{2,1,0:T(8,128)S(1)}, f32[2,32,768]{2,1,0:T(8,128)S(1)}, u32[]{:S(2)}, u32[]{:S(2)}) collective-permute-start(f32[2,32,768]{2,1,0:T(8,128)S(1)} %get-tuple-element.51), channel_id=1, source_target_pairs={{64,32},{72,40},{80,48},{88,56},{65,33},{73,41},{81,49},{89,57},{6... | collective-permute-start | bytes 589832 | tf_op jit(solution)/shard_map/ppermute | solution.py:372
  128.9 7.3 %collective-permute-start.13 = (f32[32,768]{1,0:T(8,128)S(1)}, f32[32,768]{1,0:T(8,128)S(1)}, u32[]{:S(2)}, u32[]{:S(2)}) collective-permute-start(f32[32,768]{1,0:T(8,128)S(1)} %get-tuple-element.52), channel_id=1, source_target_pairs={{64,40},{72,48},{80,56},{88,32},{65,41},{73,49},{81,57},{89,33},{6... | collective-permute-start | bytes 294920 | tf_op jit(solution)/shard_map/ppermute | solution.py:372
  131.2 7.2 %collective-permute-start.15 = (f32[32,768]{1,0:T(8,128)S(1)}, f32[32,768]{1,0:T(8,128)S(1)}, u32[]{:S(2)}, u32[]{:S(2)}) collective-permute-start(f32[32,768]{1,0:T(8,128)S(1)} %get-tuple-element.52), channel_id=1, source_target_pairs={{64,56},{72,32},{80,40},{88,48},{65,57},{73,33},{81,41},{89,49},{6... | collective-permute-start | bytes 294920 | tf_op jit(solution)/shard_map/ppermute | solution.py:372
  133.7 6.1 %collective-permute-start.14 = (f32[32,768]{1,0:T(8,128)S(1)}, f32[32,768]{1,0:T(8,128)S(1)}, u32[]{:S(2)}, u32[]{:S(2)}) collective-permute-start(f32[32,768]{1,0:T(8,128)S(1)} %get-tuple-element.52), channel_id=1, source_target_pairs={{64,48},{72,56},{80,32},{88,40},{65,49},{73,57},{81,33},{89,41},{6... | collective-permute-start | bytes 294920 | tf_op jit(solution)/shard_map/ppermute | solution.py:372
  136.3 22.8 %collective-permute-start.16 = (f32[32,768]{1,0:T(8,128)}, f32[32,768]{1,0:T(8,128)}, u32[]{:S(2)}, u32[]{:S(2)}) collective-permute-start(f32[32,768]{1,0:T(8,128)} %get-tuple-element.55.x3_two), channel_id=1, source_target_pairs={{64,96},{72,104},{80,112},{88,120},{65,97},{73,105},{81,113},{89,1... | collective-permute-start | bytes 294920 | tf_op jit(solution)/shard_map/ppermute | solution.py:372
  158.4 3.4 %collective-permute-start.18 = (f32[2,32,768]{2,1,0:T(8,128)S(1)}, f32[2,32,768]{2,1,0:T(8,128)S(1)}, u32[]{:S(2)}, u32[]{:S(2)}) collective-permute-start(f32[2,32,768]{2,1,0:T(8,128)S(1)} %copy-done.26), channel_id=1, source_target_pairs={{32,0},{40,8},{48,16},{56,24},{33,1},{41,9},{49,17},{57,25},{34,2}... | collective-permute-start | bytes 589832 | tf_op jit(solution)/shard_map/ppermute | solution.py:372
  159.1 2.7 %collective-permute-start.17 = (f32[32,768]{1,0:T(8,128)}, f32[32,768]{1,0:T(8,128)S(1)}, u32[]{:S(2)}, u32[]{:S(2)}) collective-permute-start(f32[32,768]{1,0:T(8,128)} %collective-permute-done.16.x3_ref.x3_three), channel_id=1, source_target_pairs={{96,0},{104,8},{112,16},{120,24},{97,1},{105,9},{113,17},{121,25},... | collective-permute-start | bytes 294920 | tf_op jit(solution)/shard_map/ppermute | solution.py:372
  159.8 2.0 collective-permute-start.21
  160.4 1.4 collective-permute-start.20
  161.1 0.7 collective-permute-start.19
  163.8 38.8 %copy-start.11 = (f32[64,1024]{1,0:T(8,128)S(1)}, f32[64,1024]{1,0:T(8,128)}, u32[]{:S(2)}) copy-start(f32[64,1024]{1,0:T(8,128)} %copy-done.9) | copy-start | bytes 786436
  163.8 38.8 %copy-start.19 = (f32[16,1024]{1,0:T(8,128)S(1)}, f32[16,1024]{1,0:T(8,128)}, u32[]{:S(2)}) copy-start(f32[16,1024]{1,0:T(8,128)} %copy-done.17) | copy-start | bytes 196612
  163.8 17.6 %collective-permute-start.22 = (f32[2,32,768]{2,1,0:T(8,128)S(1)}, f32[2,32,768]{2,1,0:T(8,128)S(1)}, u32[]{:S(2)}, u32[]{:S(2)}) collective-permute-start(f32[2,32,768]{2,1,0:T(8,128)S(1)} %get-tuple-element.61), channel_id=1, source_target_pairs={{0,32},{8,40},{16,48},{24,56},{1,33},{9,41},{17,49},{25,57},{2,34}... | collective-permute-start | bytes 589832 | tf_op jit(solution)/shard_map/ppermute | solution.py:372
  164.6 3.3 %collective-permute-start.23 = (f32[32,768]{1,0:T(8,128)S(1)}, f32[32,768]{1,0:T(8,128)S(1)}, u32[]{:S(2)}, u32[]{:S(2)}) collective-permute-start(f32[32,768]{1,0:T(8,128)S(1)} %get-tuple-element.62), channel_id=1, source_target_pairs={{0,40},{8,48},{16,56},{24,32},{1,41},{9,49},{17,57},{25,33},{2,42}... | collective-permute-start | bytes 294920 | tf_op jit(solution)/shard_map/ppermute | solution.py:372
  165.3 16.1 %collective-permute-start.26 = (f32[32,768]{1,0:T(8,128)S(1)}, f32[32,768]{1,0:T(8,128)S(1)}, u32[]{:S(2)}, u32[]{:S(2)}) collective-permute-start(f32[32,768]{1,0:T(8,128)S(1)} %copy-done.21), channel_id=1, source_target_pairs={{32,64},{40,72},{48,80},{56,88},{33,65},{41,73},{49,81},{57,89},{3... | collective-permute-start | bytes 294920 | tf_op jit(solution)/shard_map/ppermute | solution.py:372
  166.6 14.8 %collective-permute-start.25 = (f32[32,768]{1,0:T(8,128)S(1)}, f32[32,768]{1,0:T(8,128)S(1)}, u32[]{:S(2)}, u32[]{:S(2)}) collective-permute-start(f32[32,768]{1,0:T(8,128)S(1)} %get-tuple-element.62), channel_id=1, source_target_pairs={{0,56},{8,32},{16,40},{24,48},{1,57},{9,33},{17,41},{25,49},{2,58}... | collective-permute-start | bytes 294920 | tf_op jit(solution)/shard_map/ppermute | solution.py:372
  167.3 14.2 %collective-permute-start.24 = (f32[32,768]{1,0:T(8,128)S(1)}, f32[32,768]{1,0:T(8,128)S(1)}, u32[]{:S(2)}, u32[]{:S(2)}) collective-permute-start(f32[32,768]{1,0:T(8,128)S(1)} %get-tuple-element.62), channel_id=1, source_target_pairs={{0,48},{8,56},{16,32},{24,40},{1,49},{9,57},{17,33},{25,41},{2,50}... | collective-permute-start | bytes 294920 | tf_op jit(solution)/shard_map/ppermute | solution.py:372
  168.0 44.7 %collective-permute-start.38 = (f32[2,32,768]{2,1,0:T(8,128)}, f32[2,32,768]{2,1,0:T(8,128)S(1)}, u32[]{:S(2)}, u32[]{:S(2)}) collective-permute-start(f32[2,32,768]{2,1,0:T(8,128)} %get-tuple-element.78.both_zero), channel_id=1, source_target_pairs={{0,96},{8,104},{16,112},{24,120},{1,97},{9,105},{17,113},{25,121},... | collective-permute-start | bytes 589832 | tf_op jit(solution)/shard_map/ppermute | solution.py:372
  183.5 15.5 %collective-permute-start.27 = (f32[32,192]{1,0:T(8,128)}, f32[32,192]{1,0:T(8,128)S(1)}, u32[]{:S(2)}, u32[]{:S(2)}) collective-permute-start(f32[32,192]{1,0:T(8,128)} %get-tuple-element.68), channel_id=1, source_target_pairs={{32,72},{40,80},{48,88},{56,64},{33,73},{41,81},{49,89},{57,65},{3... | collective-permute-start | bytes 73736 | tf_op jit(solution)/shard_map/ppermute | solution.py:372
  184.7 15.9 %collective-permute-start.31 = (f32[32,192]{1,0:T(8,128)}, f32[32,192]{1,0:T(8,128)S(1)}, u32[]{:S(2)}, u32[]{:S(2)}) collective-permute-start(f32[32,192]{1,0:T(8,128)} %get-tuple-element.68), channel_id=1, source_target_pairs={{32,80},{40,88},{48,64},{56,72},{33,81},{41,89},{49,65},{57,73},{3... | collective-permute-start | bytes 73736 | tf_op jit(solution)/shard_map/ppermute | solution.py:372
  186.0 16.6 %collective-permute-start.30 = (f32[32,1024]{1,0:T(8,128)S(1)}, f32[32,1024]{1,0:T(8,128)S(1)}, u32[]{:S(2)}, u32[]{:S(2)}) collective-permute-start(f32[32,1024]{1,0:T(8,128)S(1)} %get-tuple-element.70), channel_id=1, source_target_pairs={{32,64},{40,72},{48,80},{56,88},{33,65},{41,73},{49,81},{57,89},{3... | collective-permute-start | bytes 393224 | tf_op jit(solution)/shard_map/ppermute | solution.py:372
  187.3 13.9 %collective-permute-start.32 = (f32[32,192]{1,0:T(8,128)}, f32[32,192]{1,0:T(8,128)S(1)}, u32[]{:S(2)}, u32[]{:S(2)}) collective-permute-start(f32[32,192]{1,0:T(8,128)} %get-tuple-element.68), channel_id=1, source_target_pairs={{32,88},{40,64},{48,72},{56,80},{33,89},{41,65},{49,73},{57,81},{3... | collective-permute-start | bytes 73736 | tf_op jit(solution)/shard_map/ppermute | solution.py:372
  198.9 3.7 %collective-permute-start.29 = (f32[32,768]{1,0:T(8,128)S(1)}, f32[32,768]{1,0:T(8,128)S(1)}, u32[]{:S(2)}, u32[]{:S(2)}) collective-permute-start(f32[32,768]{1,0:T(8,128)S(1)} %get-tuple-element.69.x0_own), channel_id=1, source_target_pairs={{32,96},{40,104},{48,112},{56,120},{33,97},{41,105},{49,113},{57,1... | collective-permute-start | bytes 294920 | tf_op jit(solution)/shard_map/ppermute | solution.py:372
  200.6 2.0 collective-permute-start.28
  201.3 13.1 %collective-permute-start.37 = (f32[32,768]{1,0:T(8,128)S(1)}, f32[32,768]{1,0:T(8,128)S(1)}, u32[]{:S(2)}, u32[]{:S(2)}) collective-permute-start(f32[32,768]{1,0:T(8,128)S(1)} %get-tuple-element.77.x1_one), channel_id=1, source_target_pairs={{32,64},{40,72},{48,80},{56,88},{33,65},{41,73},{49,81},{57,89},{3... | collective-permute-start | bytes 294920 | tf_op jit(solution)/shard_map/ppermute | solution.py:372
  203.9 12.3 %collective-permute-start.36 = (f32[32,192]{1,0:T(8,128)S(1)}, f32[32,192]{1,0:T(8,128)S(1)}, u32[]{:S(2)}, u32[]{:S(2)}) collective-permute-start(f32[32,192]{1,0:T(8,128)S(1)} %get-tuple-element.72.acc_ref), channel_id=1, source_target_pairs={{64,120},{72,96},{80,104},{88,112},{65,121},{73,97},{81,105},{89,1... | collective-permute-start | bytes 73736 | tf_op jit(solution)/shard_map/ppermute | solution.py:372
  209.7 6.5 %collective-permute-start.35 = (f32[32,192]{1,0:T(8,128)S(1)}, f32[32,192]{1,0:T(8,128)S(1)}, u32[]{:S(2)}, u32[]{:S(2)}) collective-permute-start(f32[32,192]{1,0:T(8,128)S(1)} %get-tuple-element.72.acc_ref), channel_id=1, source_target_pairs={{64,112},{72,120},{80,96},{88,104},{65,113},{73,121},{81,97},{89,1... | collective-permute-start | bytes 73736 | tf_op jit(solution)/shard_map/ppermute | solution.py:372
  211.3 4.9 %collective-permute-start.34 = (f32[32,192]{1,0:T(8,128)S(1)}, f32[32,192]{1,0:T(8,128)S(1)}, u32[]{:S(2)}, u32[]{:S(2)}) collective-permute-start(f32[32,192]{1,0:T(8,128)S(1)} %get-tuple-element.72.acc_ref), channel_id=1, source_target_pairs={{64,104},{72,112},{80,120},{88,96},{65,105},{73,113},{81,121},{89,... | collective-permute-start | bytes 73736 | tf_op jit(solution)/shard_map/ppermute | solution.py:372
  212.6 4.1 %collective-permute-start.33 = (f32[5,32,192]{2,1,0:T(8,128)S(1)}, f32[5,32,192]{2,1,0:T(8,128)S(1)}, u32[]{:S(2)}, u32[]{:S(2)}) collective-permute-start(f32[5,32,192]{2,1,0:T(8,128)S(1)} %get-tuple-element.73), channel_id=1, source_target_pairs={{64,96},{72,104},{80,112},{88,120},{65,97},{73,105},{81,113},{89,1... | collective-permute-start | bytes 368648 | tf_op jit(solution)/shard_map/ppermute | solution.py:372
  (30 other events, 173.6 us)
Sparse Core Ops, SparseCore 0:
  10.3 35.4 all-gather.10
  47.5 25.4 all-gather.12
  74.7 23.7 all-gather.14
  100.1 23.7 all-gather.16
  125.4 29.5 all-gather.18

commit v3 on v2

--- a/solution.py
+++ b/solution.py
@@ -38,26 +38,30 @@
     return jnp.concatenate([real, imag], axis=0)
 
 
-def block_weight(ref):
-    return ref[...].reshape(BLOCK, 2 * SLAB)
-
-
-def slabs_dot(slabs, weight_ref, q, keep=None):
+def slot_of(plane, block):
+    return jnp.minimum(jnp.where(plane < block, block - 1, block), GROUP - 2)
+
+
+def block_weight(ref, slot):
+    return ref[:, slot].reshape(BLOCK, 2 * SLAB)
+
+
+def slabs_dot(slabs, weight_ref, slot, q, keep=None):
     total = None
     for d, slab in enumerate(slabs):
         source = lax.rem(q - d + GROUP, GROUP)
         if keep is not None:
             keep[source] = slab
-        weight = weight_ref[pl.ds(2 * source, 2)].reshape(SLAB, 2 * SLAB)
+        weight = weight_ref[pl.ds(2 * source, 2), slot].reshape(SLAB, 2 * SLAB)
         part = complex_dot(slab, weight)
         total = part if total is None else total + part
     return total
 
 
-def sent_dot(sent_ref, weight_ref):
+def sent_dot(sent_ref, weight_ref, slot):
     total = None
     for s in range(GROUP):
-        weight = weight_ref[2 * s : 2 * s + 2].reshape(SLAB, 2 * SLAB)
+        weight = weight_ref[2 * s : 2 * s + 2, slot].reshape(SLAB, 2 * SLAB)
         part = complex_dot(sent_ref[s], weight)
         total = part if total is None else total + part
     return total
@@ -89,6 +93,15 @@
         scratch_shapes=scratch,
         compiler_params=pltpu.CompilerParams(vmem_limit_bytes=VMEM),
     )(*inputs)
+
+
+def turn_first_kernel(place_ref, factor_ref, out_ref, turned_ref):
+    rows = factor_ref[...].reshape(2 * SLAB, 4 * PIECE)
+    for part in range(3):
+        turned_ref[128 * part : 128 * part + 128, :] = rows[:, 128 * part : 128 * part + 128].T
+    for slot in range(GROUP - 1):
+        block = slot + jnp.where(place_ref[0] > slot, 0, 1)
+        out_ref[PIECE * slot : PIECE * slot + PIECE, :] = turned_ref[pl.ds(block * PIECE, PIECE), :]
 
 
 def pack_kernel(first_ref, second_ref, link_ref, out_ref):
@@ -115,7 +128,7 @@
             at = step * 16 + u
             source = where_ref[at]
             rows_ref[pl.ds(at, 1), :] = cells_ref[pl.ds(source, 1), :]
-            links_ref[pl.ds(at, 1), :] = cells_ref[pl.ds(source // 16 * 16 + 15, 1), :]
+            links_ref[pl.ds(at, 1), :] = cells_ref[pl.ds(source | 15, 1), :]
         return carry
 
     lax.fori_loop(0, 64, some, 0)
@@ -134,89 +147,84 @@
 
 
 def start_kernel(place_ref, rhs_ref, weight_ref, acc_ref):
-    product = complex_dot(rhs_ref[0:ROWS, 0:BLOCK], block_weight(weight_ref))
+    slot = slot_of(place_ref[0], 0)
+    product = complex_dot(rhs_ref[0:ROWS, 0:BLOCK], block_weight(weight_ref, slot))
     slab = rhs_ref[0:ROWS, BLOCK : BLOCK + SLAB]
     acc_ref[...] = jnp.where(place_ref[0] > 0, slab - product, slab)
 
 
 def forward_one_kernel(place_ref, acc_ref, y0, y1, y2, y3, weight_ref, out_ref, keep_ref):
     slabs = [y0[...], y1[...], y2[...], y3[...]]
-    acc = acc_ref[...] - slabs_dot(slabs, weight_ref, place_ref[1], keep_ref)
-    out_ref[...] = acc
-    keep_ref[GROUP] = acc
+    slot = slot_of(place_ref[0], 1)
+    out_ref[...] = acc_ref[...] - slabs_dot(slabs, weight_ref, slot, place_ref[1], keep_ref)
 
 
 def forward_two_kernel(
-    place_ref, acc_ref, sent_ref, y1, y2, y3, weight2_ref, weight1_ref, inverse_ref, out_ref, part_ref
-):
-    slabs = [sent_ref[GROUP], y1[...], y2[...], y3[...]]
+    place_ref, acc_ref, sent_ref, y0, y1, y2, y3, weight_ref, inverse_ref, out_ref, part_ref
+):
+    plane, q = place_ref[0], place_ref[1]
+    slabs = [y0[...], y1[...], y2[...], y3[...]]
     solved = (
         acc_ref[...]
-        - slabs_dot(slabs, weight2_ref, place_ref[1])
-        - sent_dot(sent_ref, weight1_ref)
+        - sent_dot(sent_ref, weight_ref, slot_of(plane, 1))
+        - slabs_dot(slabs, weight_ref, slot_of(plane, 2), q)
     )
     out_ref[...] = solved
     part_ref[...] = complex_dot(solved, inverse_ref[...])
 
 
 def back_three_kernel(
-    acc_ref, p0, p1, p2, p3, weight_ref, inverse_ref, x_ref, acc_out_ref, part_ref, pair_ref
+    place_ref, acc_ref, p0, p1, p2, p3, weight_ref, inverse_ref, x_ref, acc_out_ref, part_ref
 ):
     x = add_refs([p0, p1, p2, p3])
-    acc = acc_ref[...] - complex_dot(x, block_weight(weight_ref))
-    part = complex_dot(acc, inverse_ref[...])
+    acc = acc_ref[...] - complex_dot(x, block_weight(weight_ref, slot_of(place_ref[0], 3)))
     x_ref[...] = x
     acc_out_ref[...] = acc
-    part_ref[...] = part
-    pair_ref[0] = part
-    pair_ref[1] = x
+    part_ref[...] = complex_dot(acc, inverse_ref[...])
 
 
 def back_two_kernel(
-    acc_ref, got_ref, p1, p2, p3, weight2_ref, weight3_ref, inverse_ref, x_ref, acc_out_ref, part_ref, pair_ref
-):
-    x = add_refs([got_ref.at[0], p1, p2, p3])
+    place_ref, acc_ref, p0, p1, p2, p3, x3_ref, weight_ref, inverse_ref, x_ref, acc_out_ref, part_ref
+):
+    plane = place_ref[0]
+    x = add_refs([p0, p1, p2, p3])
     acc = (
         acc_ref[...]
-        - complex_dot(got_ref[1], block_weight(weight3_ref))
-        - complex_dot(x, block_weight(weight2_ref))
-    )
-    part = complex_dot(acc, inverse_ref[...])
+        - complex_dot(x3_ref[...], block_weight(weight_ref, slot_of(plane, 3)))
+        - complex_dot(x, block_weight(weight_ref, slot_of(plane, 2)))
+    )
     x_ref[...] = x
     acc_out_ref[...] = acc
-    part_ref[...] = part
-    pair_ref[0] = part
-    pair_ref[1] = x
+    part_ref[...] = complex_dot(acc, inverse_ref[...])
 
 
 def back_one_kernel(
+    place_ref,
     acc_ref,
-    x3_ref,
-    got_ref,
+    p0,
     p1,
     p2,
     p3,
-    weight1_ref,
-    weight2_ref,
-    weight3_ref,
+    x2_ref,
+    x3_ref,
+    weight_ref,
     inverse_ref,
+    x_ref,
     both_ref,
     part_ref,
-    pair_ref,
-):
-    x = add_refs([got_ref.at[0], p1, p2, p3])
+):
+    plane = place_ref[0]
+    x = add_refs([p0, p1, p2, p3])
     acc = (
         acc_ref[...]
-        - complex_dot(x3_ref[...], block_weight(weight3_ref))
-        - complex_dot(got_ref[1], block_weight(weight2_ref))
-        - complex_dot(x, block_weight(weight1_ref))
-    )
-    part = complex_dot(acc, inverse_ref[...])
+        - complex_dot(x3_ref[...], block_weight(weight_ref, slot_of(plane, 3)))
+        - complex_dot(x2_ref[...], block_weight(weight_ref, slot_of(plane, 2)))
+        - complex_dot(x, block_weight(weight_ref, slot_of(plane, 1)))
+    )
+    part_ref[...] = complex_dot(acc, inverse_ref[...])
+    x_ref[...] = x
     both_ref[0] = x
-    both_ref[1] = got_ref[1]
-    part_ref[...] = part
-    pair_ref[0] = part
-    pair_ref[1] = x
+    both_ref[1] = x2_ref[...]
 
 
 def coupled(rhs, link_real, link_imag, x):
@@ -245,32 +253,27 @@
     place_ref,
     rhs_ref,
     link_ref,
-    got_ref,
+    p0,
     p1,
     p2,
     p3,
+    x1_ref,
     x2_ref,
     x3_ref,
     weight_ref,
     x0_ref,
-    x1_ref,
     slab_ref,
     out_ref,
-    send_ref,
 ):
     plane, q = place_ref[0], place_ref[1]
-    x0 = add_refs([got_ref.at[0], p1, p2, p3])
-    x1 = got_ref[1]
-    own = jnp.where(plane == 1, x1, jnp.where(plane == 2, x2_ref[...], x3_ref[...]))
+    x0 = add_refs([p0, p1, p2, p3])
+    own = jnp.where(plane == 1, x1_ref[...], jnp.where(plane == 2, x2_ref[...], x3_ref[...]))
     slab = second_slab(rhs_ref, link_ref, own, q)
-    solved = slab - complex_dot(second_block(rhs_ref, link_ref, x0), block_weight(weight_ref))
     x0_ref[...] = x0
-    x1_ref[...] = x1
     slab_ref[...] = slab
-    out_ref[...] = solved
-    send_ref[:, 0:BLOCK] = x0
-    send_ref[:, BLOCK : BLOCK + SLAB] = solved
-    send_ref[:, BLOCK + SLAB :] = jnp.zeros((ROWS, 64), f32)
+    out_ref[...] = slab - complex_dot(
+        second_block(rhs_ref, link_ref, x0), block_weight(weight_ref, 0)
+    )
 
 
 def second_one_kernel(
@@ -278,29 +281,27 @@
     rhs_ref,
     link_ref,
     slab_ref,
-    x0_own,
+    x0_one,
+    x0_two,
     x0_zero,
     x0_three,
-    got_ref,
+    f0,
     f1,
     f2,
     f3,
-    weight0_ref,
-    weight1_ref,
+    weight_ref,
     out_ref,
     keep_ref,
     x0_ref,
 ):
     plane, q = place_ref[0], place_ref[1]
-    x0 = x0_own[...] + x0_zero[...] + x0_three[...] + got_ref[:, 0:BLOCK]
+    x0 = add_refs([x0_one, x0_two, x0_zero, x0_three])
     x0_ref[...] = x0
     first = second_slab(rhs_ref, link_ref, x0, q)
-    slabs = [got_ref[:, BLOCK : BLOCK + SLAB], f1[...], f2[...], f3[...]]
-    product = complex_dot(second_block(rhs_ref, link_ref, x0), block_weight(weight0_ref))
-    later = slab_ref[...] - product - slabs_dot(slabs, weight1_ref, q, keep_ref)
-    solved = jnp.where(plane == 0, first, later)
-    out_ref[...] = solved
-    keep_ref[GROUP] = solved
+    slabs = [f0[...], f1[...], f2[...], f3[...]]
+    product = complex_dot(second_block(rhs_ref, link_ref, x0), block_weight(weight_ref, 0))
+    later = slab_ref[...] - product - slabs_dot(slabs, weight_ref, 1, q, keep_ref)
+    out_ref[...] = jnp.where(plane == 0, first, later)
 
 
 def cells_kernel(
@@ -313,7 +314,7 @@
     x2_one,
     x2_two,
     x3_zero,
-    pair_one,
+    x3_one,
     x3_two,
     x3_three,
     out_ref,
@@ -324,7 +325,7 @@
         x0_ref[...],
         both_zero[0] + x1_one[...] + x1_two[...] + both_three[0],
         both_zero[1] + x2_one[...] + x2_two[...] + both_three[1],
-        x3_zero[...] + pair_one[1] + x3_two[...] + x3_three[...],
+        x3_zero[...] + x3_one[...] + x3_two[...] + x3_three[...],
     )
     for k, x in enumerate(blocks):
         for part in range(6):
@@ -340,13 +341,13 @@
 
 
 def second_two_kernel(
-    place_ref, acc_ref, sent_ref, f1, f2, f3, cells_ref, weight2_ref, weight1_ref, out_ref
-):
-    slabs = [sent_ref[GROUP], f1[...], f2[...], f3[...]]
+    place_ref, acc_ref, sent_ref, f0, f1, f2, f3, cells_ref, weight_ref, out_ref
+):
+    slabs = [f0[...], f1[...], f2[...], f3[...]]
     solved = (
         acc_ref[...]
-        - slabs_dot(slabs, weight2_ref, place_ref[1])
-        - sent_dot(sent_ref, weight1_ref)
+        - sent_dot(sent_ref, weight_ref, 1)
+        - slabs_dot(slabs, weight_ref, 2, place_ref[1])
     )
     lane = lax.broadcasted_iota(jnp.int32, (ROWS, 128), 1)
     tail = jnp.concatenate([solved[:, 128:], jnp.zeros((ROWS, 64), f32)], axis=1)
@@ -372,11 +373,8 @@
     return lax.ppermute(value, "row", pairs)
 
 
-def plane_spread(value, source, target, first=None):
-    return [
-        plane_send(value if first is None or d else first, source, target, d)
-        for d in range(GROUP)
-    ]
+def plane_spread(value, source, target):
+    return [plane_send(value, source, target, d) for d in range(GROUP)]
 
 
 def after(value, arrived):
@@ -388,23 +386,23 @@
     col_id = lax.axis_index("col")
     place = jnp.stack([row_id // GROUP, row_id % GROUP]).astype(jnp.int32)
 
-    def gather_blocks(turned, first, count):
-        piece = turned[PIECE * first : PIECE * (first + count)]
-        whole = lax.all_gather(piece, "col").reshape(8, count, PIECE, 2 * SLAB)
-        return [whole[:, at] for at in range(count)]
-
-    turned1 = factor1.reshape(2 * SLAB, 4 * PIECE).T
-    matrix1 = gather_blocks(turned1, 0, 1)
+    def gather_blocks(turned):
+        return lax.all_gather(turned, "col").reshape(8, GROUP - 1, PIECE, 2 * SLAB)
+
+    (turned1,) = call(
+        turn_first_kernel,
+        [SDS((3 * PIECE, 2 * SLAB), f32)],
+        [place, factor1],
+        scratch=[pltpu.VMEM((4 * PIECE, 2 * SLAB), f32)],
+    )
+    matrix1 = gather_blocks(turned1)
 
     links = jnp.pad(coupling.reshape(2, CELLS), ((0, 0), (0, 32 - CELLS))).reshape(1, 64)
     links = jnp.pad(links, ((0, 0), (0, 64)))
     (packed,) = call(pack_kernel, [SDS((8, 16, 128), f32)], [source1, source2, links])
-    turned1, packed = lax.optimization_barrier((turned1, packed))
-    matrix1 += gather_blocks(turned1, 1, 1)
-    matrix1 += gather_blocks(turned1, 2, 1)
-    matrix1 += gather_blocks(turned1, 3, 1)
-    packed = jnp.broadcast_to(packed[None], (16, 8, 16, 128)).reshape(128, 16, 128)
-    cells = lax.all_to_all(packed, ("row", "col"), 0, 0).reshape(128 * 16, 128)
+    packed = lax.all_to_all(packed, "col", 0, 0)
+    packed = jnp.broadcast_to(packed[None], (16, 8, 16, 128))
+    cells = lax.all_to_all(packed, "row", 0, 0).reshape(128 * 16, 128)
 
     cell_y = front_order // 48
     cell_x = front_order % 48
@@ -421,66 +419,71 @@
         scratch=[pltpu.VMEM((1024, 128), f32), pltpu.VMEM((1024, 128), f32)],
     )
     factor2, diag_inv, cells = lax.optimization_barrier((factor2, diag_inv, cells))
-    turned2 = factor2.reshape(2 * SLAB, 4 * PIECE).T
-    matrix2 = gather_blocks(turned2, 0, 3)
+    turned2 = factor2[:, :, : 3 * PIECE].reshape(2 * SLAB, 3 * PIECE).T
+    matrix2 = gather_blocks(turned2)
     inverse = diag_inv.reshape(2 * BLOCK, SLAB).T
 
     slab_shape = SDS((ROWS, SLAB), f32)
     block_shape = SDS((ROWS, BLOCK), f32)
     pair_shape = SDS((2, ROWS, BLOCK), f32)
-    sent_shape = SDS((GROUP + 1, ROWS, SLAB), f32)
-
-    (acc,) = call(start_kernel, [slab_shape], [place, rhs, matrix1[0]])
+    sent_shape = SDS((GROUP, ROWS, SLAB), f32)
+
+    (acc,) = call(start_kernel, [slab_shape], [place, rhs, matrix1])
     got = plane_spread(acc, 1, 2)
     acc, kept = call(
-        forward_one_kernel, [slab_shape, sent_shape], [place, acc, *got, matrix1[1]]
-    )
-    got = plane_spread(acc, 2, 3, kept)
+        forward_one_kernel, [slab_shape, sent_shape], [place, acc, *got, matrix1]
+    )
+    got = plane_spread(acc, 2, 3)
+    sent = plane_send(kept, 2, 3)
     acc, part = call(
         forward_two_kernel,
         [slab_shape, block_shape],
-        [place, acc, *got, matrix1[2], matrix1[1], inverse],
+        [place, acc, sent, *got, matrix1, inverse],
     )
     got = plane_spread(part, 3, 2)
-    x3_two, acc, part, pair = call(
+    x3_two, acc, part = call(
         back_three_kernel,
-        [block_shape, slab_shape, block_shape, pair_shape],
-        [acc, *got, matrix1[3], inverse],
-    )
-    got = plane_spread(part, 2, 1, pair)
-    pair_one = got[0]
+        [block_shape, slab_shape, block_shape],
+        [place, acc, *got, matrix1, inverse],
+    )
+    got = plane_spread(part, 2, 1)
+    x3_one = plane_send(x3_two, 2, 1)
     x3_three = plane_send(after(x3_two, got[1]), 2, 3)
-    x2_one, acc, part, pair = call(
+    x2_one, acc, part = call(
         back_two_kernel,
-        [block_shape, slab_shape, block_shape, pair_shape],
-        [acc, *got, matrix1[2], matrix1[3], inverse],
-    )
-    matrix2, part, pair = lax.optimization_barrier((matrix2, part, pair))
-    got = plane_spread(part, 1, 0, pair)
+        [block_shape, slab_shape, block_shape],
+        [place, acc, *got, x3_one, matrix1, inverse],
+    )
+    matrix2, part = lax.optimization_barrier((matrix2, part))
+    got = plane_spread(part, 1, 0)
+    x2_zero = plane_send(x2_one, 1, 0)
     x3_zero = plane_send(x3_three, 3, 0)
     x2_two = plane_send(after(x2_one, got[1]), 1, 2)
-    both_zero, part, pair = call(
+    x1_zero, both_zero, part = call(
         back_one_kernel,
-        [pair_shape, block_shape, pair_shape],
-        [acc, x3_zero, *got, matrix1[1], matrix1[2], matrix1[3], inverse],
-    )
-    got = plane_spread(part, 0, 1, pair)
+        [block_shape, pair_shape, block_shape],
+        [place, acc, *got, x2_zero, x3_zero, matrix1, inverse],
+    )
+    got = plane_spread(part, 0, 1)
+    x1_one = plane_send(x1_zero, 0, 1)
     both_three = plane_send(after(both_zero, got[1]), 0, 3)
-    x0_one, x1_one, slab, acc, send = call(
+    x0_one, slab, acc = call(
         couple_kernel,
-        [block_shape, block_shape, slab_shape, slab_shape, SDS((ROWS, 1024), f32)],
-        [place, rhs, link, *got, x2_two, x3_three, matrix2[0]],
-    )
-    got = plane_spread(acc, 1, 2, send)
+        [block_shape, slab_shape, slab_shape],
+        [place, rhs, link, *got, x1_one, x2_two, x3_three, matrix2],
+    )
+    got = plane_spread(acc, 1, 2)
+    x0_two = plane_send(x0_one, 1, 2)
     x0_zero = plane_send(after(x0_one, got[1]), 1, 0)
     x0_three = plane_send(after(x0_one, got[1]), 1, 3)
     x1_two = plane_send(after(x1_one, got[2]), 1, 2)
     acc, kept, x0_all = call(
         second_one_kernel,
         [slab_shape, sent_shape, block_shape],
-        [place, rhs, link, slab, x0_one, x0_zero, x0_three, *got, matrix2[0], matrix2[1]],
-    )
-    got = plane_spread(acc, 2, 3, kept)
+        [place, rhs, link, slab, x0_one, x0_two, x0_zero, x0_three, *got, matrix2],
+    )
+    got = plane_spread(acc, 2, 3)
+    sent = plane_send(kept, 2, 3)
 
     at = jnp.arange(SLAB, dtype=jnp.int32)
     own_c, own_y, own_x = at // CELLS, at % CELLS // 6, at % 6
@@ -500,7 +503,7 @@
             x2_one,
             x2_two,
             x3_zero,
-            pair_one,
+            x3_one,
             x3_two,
             x3_three,
         ],
@@ -509,7 +512,7 @@
     (last,) = call(
         second_two_kernel,
         [SDS((8, ROWS, 256), f32)],
-        [place, acc, *got, mine, matrix2[2], matrix2[1]],
+        [place, acc, sent, *got, mine, matrix2],
     )
     arrived = lax.all_to_all(last, "col", 0, 0)
     return call(

time: 239 us -> 200 us (0.84)
  waiting for transfers between devices: 85.5 us -> 40.4 us
  blocking collectives: 38.1 us -> 42.6 us
  starting transfers between devices: 56.5 us -> 59.3 us
    all_gather x5 -> x2, waiting for transfers between devices: 56.9 us -> 0.01 us  [gather_blocks(): return lax.all_gather(turned, 'col').reshape(8, GROUP - 1, PIECE, 2 * SLAB)]
    ppermute x39 -> x45, waiting for transfers between devices: 27.3 us -> 40.4 us  [plane_send(): return lax.ppermute(value, 'row', pairs)]
    unnamed x70 -> x66, local copies, waits for them, and re-layouts: 9.11 us -> 14.9 us
    all_to_all x1 -> x2, blocking collectives: 27.9 us -> 32.6 us  [the longest x1 21.9 us: on_device(): cells = lax.all_to_all(packed, 'row', 0, 0).reshape(128 * 16, 128)]
    squeeze x1 -> x0, local copies, waits for them, and re-layouts: 3.38 us -> none  [gather_blocks(): return [whole[:, at] for at in range(count)]]
    ppermute x39 -> x45, starting transfers between devices: 56.3 us -> 59.2 us  [plane_send(): return lax.ppermute(value, 'row', pairs)]
    slice x3 -> x0, local copies, waits for them, and re-layouts: 2.47 us -> none  [gather_blocks(): piece = turned[PIECE * first:PIECE * (first + count)]]
    pallas_call x13 -> x14, Pallas kernels: 22.1 us -> 21.9 us  [call(): pl.pallas_call(body, grid=(1,), in_specs=specs, out_specs=outs, out_shape...]
  transfers between devices with their start and end apart: 44 -> 47, of which waited for: 11 -> 16; matrix products, arithmetic and copies ran while one was open for 3% -> 2% of each run, Pallas kernels for 8% -> 8%
where the time goes in v3:
time: 200 us; the launch traced here: 197 us
  starting transfers between devices  59.3 us (30%)
  blocking collectives  42.6 us (21%)
  waiting for transfers between devices  40.4 us (20%)
  Pallas kernels  21.9 us (11%)
  local copies, waits for them, and re-layouts  17.7 us (9%)
  between operations  14.8 us (7%)
    ppermute x45, starting transfers between devices, plane_send(): return lax.ppermute(value, 'row', pairs)  59.2 us
    ppermute x45, waiting for transfers between devices, plane_send(): return lax.ppermute(value, 'row', pairs)  40.4 us
    pallas_call x14, Pallas kernels, call(): pl.pallas_call(body, grid=(1,), in_specs=specs, out_specs=outs, out_shape...  21.9 us
    all_to_all x1, blocking collectives, on_device(): cells = lax.all_to_all(packed, 'row', 0, 0).reshape(128 * 16, 128)  21.9 us
    unnamed x66, local copies, waits for them, and re-layouts  14.9 us
    all_to_all x1, blocking collectives, on_device(): packed = lax.all_to_all(packed, 'col', 0, 0)  10.7 us
    all_to_all x1, blocking collectives, on_device(): arrived = lax.all_to_all(last, 'col', 0, 0)  9.95 us
  transfers between devices with their start and end apart: 47, of which 16 were waited for; matrix products, arithmetic and copies ran while one was open for 2% of the time, Pallas kernels for 8%

profile of v3, /device:TPU:4, one launch (start us, length us, event | category | flops | bytes accessed | tf_op | source)
XLA Modules:
  0.0 197.5 jit_solution(6128375410076589720)
XLA Ops:
  8.4 1.7 shard_map.88
  12.7 10.7 %all_to_all.15 = f32[8,16,128]{2,1,0:T(8,128)S(1)} all-to-all(f32[8,16,128]{2,1,0:T(8,128)S(1)} %shard_map.86), channel_id=1, replica_groups=mesh['row'=16,'col'=8] {'col'}, dimensions={0} | all-to-all | bytes 131072 | tf_op jit(solution)/shard_map/all_to_all | solution.py:403
  23.5 21.9 %all_to_all.16 = f32[16,8,16,128]{3,2,1,0:T(8,128)S(1)} all-to-all(f32[16,8,16,128]{3,2,1,0:T(8,128)S(1)} %broadcast_in_dim.25), channel_id=1, replica_groups=mesh['row'=16,'col'=8] {'row'}, dimensions={0} | all-to-all | bytes 2097152 | tf_op jit(solution)/shard_map/all_to_all | solution.py:405
  46.8 2.6 %shard_map.87 = (f32[64,1024]{1,0:T(8,128)S(1)}, f32[16,1024]{1,0:T(8,128)S(1)}) custom-call(s32[1024]{0:T(1024)S(1)} %bitcast.30, f32[2048,128]{1,0:T(8,128)S(1)} %bitcast.29, f32[2,1024]{1,0:T(2,128)S(1)} %slice_convert_fusion.mark_ref), custom_call_target="tpu_custom_call" | custom-call | tf_op jit(solution)/shard_map/pallas_call | solution.py:87
  50.7 2.0 %copy-done = f32[2304,384]{1,0:T(8,128)S(1)} copy-done((f32[2304,384]{1,0:T(8,128)S(1)}, f32[2304,384]{1,0:T(8,128)}, u32[]{:S(2)}) %copy-start) | copy-done | bytes 3538968
  54.7 1.6 collective-permute-start
  56.3 1.3 collective-permute-start.1
  57.6 1.3 collective-permute-start.2
  58.9 1.3 collective-permute-start.3
  60.8 3.6 %collective-permute-done.1.y1 = f32[32,192]{1,0:T(8,128)S(1)} collective-permute-done((f32[32,192]{1,0:T(8,128)S(1)}, f32[32,192]{1,0:T(8,128)S(1)}, u32[]{:S(2)}, u32[]{:S(2)}) %collective-permute-start.1) | collective-permute-done | bytes 24608 | tf_op jit(solution)/shard_map/ppermute | solution.py:373
  64.3 1.4 collective-permute-done.2.y2
  68.1 1.3 collective-permute-start.5
  69.4 1.3 collective-permute-start.6
  73.6 1.3 collective-permute-done.8.y3
  74.9 1.6 shard_map.91
  76.6 1.3 collective-permute-start.9
  77.9 1.3 collective-permute-start.10
  79.2 1.3 collective-permute-start.11
  80.5 1.3 collective-permute-start.12
  81.8 2.6 %collective-permute-done.9.p0 = f32[32,768]{1,0:T(8,128)S(1)} collective-permute-done((f32[32,768]{1,0:T(8,128)S(1)}, f32[32,768]{1,0:T(8,128)S(1)}, u32[]{:S(2)}, u32[]{:S(2)}) %collective-permute-start.9) | collective-permute-done | bytes 98336 | tf_op jit(solution)/shard_map/ppermute | solution.py:373
  84.4 3.2 %collective-permute-done.10.p1 = f32[32,768]{1,0:T(8,128)S(1)} collective-permute-done((f32[32,768]{1,0:T(8,128)S(1)}, f32[32,768]{1,0:T(8,128)S(1)}, u32[]{:S(2)}, u32[]{:S(2)}) %collective-permute-start.10) | collective-permute-done | bytes 98336 | tf_op jit(solution)/shard_map/ppermute | solution.py:373
  89.3 1.4 shard_map.92
  90.6 1.3 collective-permute-start.14
  92.0 1.3 collective-permute-start.13
  93.3 1.3 collective-permute-start.15
  94.6 1.3 collective-permute-start.16
  95.9 1.3 collective-permute-start.17
  97.2 1.9 collective-permute-start.23
  101.1 1.6 shard_map.93
  111.4 3.1 %shard_map.94 = (f32[32,768]{1,0:T(8,128)S(1)}, f32[2,32,768]{2,1,0:T(8,128)}, f32[32,768]{1,0:T(8,128)S(1)}) custom-call(s32[2]{0:T(128)S(1)} %pad_add_fusion.1.place_ref, f32[32,192]{1,0:T(8,128)S(1)} %copy-done.27, f32[32,768]{1,0:T(8,128)S(1)} %collective-permute-done.18.p0, f32[32,768]{1,0:T(8,128)S(1)} %collective-permute-done.19.p1, ...), custom_call_target="tpu_custom_call" | custom-call | tf_op jit(solution)/shard_map/pallas_call | solution.py:87
  118.1 1.3 collective-permute-start.30
  119.4 1.4 collective-permute-start.44
  120.8 18.0 %collective-permute-done.30.x2_ref.x2_two = f32[32,768]{1,0:T(8,128)S(1)} collective-permute-done((f32[32,768]{1,0:T(8,128)}, f32[32,768]{1,0:T(8,128)S(1)}, u32[]{:S(2)}, u32[]{:S(2)}) %collective-permute-start.30) | collective-permute-done | bytes 98336 | tf_op jit(solution)/shard_map/ppermute | solution.py:373
  138.8 2.1 %shard_map.95 = (f32[32,768]{1,0:T(8,128)S(1)}, f32[32,192]{1,0:T(8,128)S(1)}, f32[32,192]{1,0:T(8,128)}) custom-call(s32[2]{0:T(128)S(1)} %pad_add_fusion.1.place_ref, f32[64,1024]{1,0:T(8,128)S(1)} %copy-done.8, f32[16,1024]{1,0:T(8,128)S(1)} %copy-done.18, f32[32,768]{1,0:T(8,128)S(1)} %collective-permute-done.25.p0, ...), custom_call_target="tpu_custom_call" | custom-call | tf_op jit(solution)/shard_map/pallas_call | solution.py:87
  143.4 1.3 collective-permute-start.36
  144.7 1.3 collective-permute-start.35
  146.0 1.3 collective-permute-start.37
  147.3 3.0 %collective-permute-done.32.f1 = f32[32,192]{1,0:T(8,128)} collective-permute-done((f32[32,192]{1,0:T(8,128)}, f32[32,192]{1,0:T(8,128)}, u32[]{:S(2)}, u32[]{:S(2)}) %collective-permute-start.32) | collective-permute-done | bytes 24608 | tf_op jit(solution)/shard_map/ppermute | solution.py:373
  153.6 1.3 collective-permute-start.43
  154.9 2.1 %collective-permute-done.31.x0_two = f32[32,768]{1,0:T(8,128)S(1)} collective-permute-done((f32[32,768]{1,0:T(8,128)}, f32[32,768]{1,0:T(8,128)S(1)}, u32[]{:S(2)}, u32[]{:S(2)}) %collective-permute-start.31) | collective-permute-done | bytes 98336 | tf_op jit(solution)/shard_map/ppermute | solution.py:373
  160.5 1.6 shard_map.96
  162.1 6.6 %collective-permute-start.39 = (f32[32,192]{1,0:T(8,128)S(1)}, f32[32,192]{1,0:T(8,128)S(1)}, u32[]{:S(2)}, u32[]{:S(2)}) collective-permute-start(f32[32,192]{1,0:T(8,128)S(1)} %get-tuple-element.56.acc_ref), channel_id=1, source_target_pairs={{64,96},{72,104},{80,112},{88,120},{65,97},{73,105},{81,113},{89,1... | collective-permute-start | bytes 73736 | tf_op jit(solution)/shard_map/ppermute | solution.py:373
  170.0 2.5 %collective-permute-start.41 = (f32[32,192]{1,0:T(8,128)S(1)}, f32[32,192]{1,0:T(8,128)S(1)}, u32[]{:S(2)}, u32[]{:S(2)}) collective-permute-start(f32[32,192]{1,0:T(8,128)S(1)} %get-tuple-element.56.acc_ref), channel_id=1, source_target_pairs={{64,112},{72,120},{80,96},{88,104},{65,113},{73,121},{81,97},{89,1... | collective-permute-start | bytes 73736 | tf_op jit(solution)/shard_map/ppermute | solution.py:373
  172.5 1.6 collective-permute-start.42
  174.1 1.3 collective-permute-start.38
  175.9 1.9 shard_map.97.cells_ref
  177.9 1.3 shard_map.98
  179.3 9.9 %all_to_all.17.got_ref = f32[8,32,256]{2,1,0:T(8,128)S(1)} all-to-all(f32[8,32,256]{2,1,0:T(8,128)S(1)} %shard_map.98), channel_id=1, replica_groups=mesh['row'=16,'col'=8] {'col'}, dimensions={0} | all-to-all | bytes 524288 | tf_op jit(solution)/shard_map/all_to_all | solution.py:517
  (151 shorter events, 42.6 us)
Async XLA Ops:
  7.2 43.6 %all-gather.5.cloned.1.call-start = ((), (), s32[]{:S(2)}) async-start(), calls=%async_computation.3 | async-start | bytes 3981312 | tf_op jit(solution)/shard_map/all_gather | solution.py:390
  10.1 96.5 %all-gather.7.cloned.1.call-start = ((), (), s32[]{:S(2)}) async-start(), calls=%async_computation.4 | async-start | bytes 3981312 | tf_op jit(solution)/shard_map/all_gather | solution.py:390
  54.7 6.1 %collective-permute-start = (f32[32,192]{1,0:T(8,128)S(1)}, f32[32,192]{1,0:T(8,128)S(1)}, u32[]{:S(2)}, u32[]{:S(2)}) collective-permute-start(f32[32,192]{1,0:T(8,128)S(1)} %shard_map.89.acc_ref), channel_id=1, source_target_pairs={{32,64},{40,72},{48,80},{56,88},{33,65},{41,73},{49,81},{57,89},{3... | collective-permute-start | bytes 73736 | tf_op jit(solution)/shard_map/ppermute | solution.py:373
  56.3 8.1 %collective-permute-start.1 = (f32[32,192]{1,0:T(8,128)S(1)}, f32[32,192]{1,0:T(8,128)S(1)}, u32[]{:S(2)}, u32[]{:S(2)}) collective-permute-start(f32[32,192]{1,0:T(8,128)S(1)} %shard_map.89.acc_ref), channel_id=1, source_target_pairs={{32,72},{40,80},{48,88},{56,64},{33,73},{41,81},{49,89},{57,65},{3... | collective-permute-start | bytes 73736 | tf_op jit(solution)/shard_map/ppermute | solution.py:373
  57.6 8.2 %collective-permute-start.2 = (f32[32,192]{1,0:T(8,128)S(1)}, f32[32,192]{1,0:T(8,128)S(1)}, u32[]{:S(2)}, u32[]{:S(2)}) collective-permute-start(f32[32,192]{1,0:T(8,128)S(1)} %shard_map.89.acc_ref), channel_id=1, source_target_pairs={{32,80},{40,88},{48,64},{56,72},{33,81},{41,89},{49,65},{57,73},{3... | collective-permute-start | bytes 73736 | tf_op jit(solution)/shard_map/ppermute | solution.py:373
  58.9 6.9 %collective-permute-start.3 = (f32[32,192]{1,0:T(8,128)S(1)}, f32[32,192]{1,0:T(8,128)S(1)}, u32[]{:S(2)}, u32[]{:S(2)}) collective-permute-start(f32[32,192]{1,0:T(8,128)S(1)} %shard_map.89.acc_ref), channel_id=1, source_target_pairs={{32,88},{40,64},{48,72},{56,80},{33,89},{41,65},{49,73},{57,81},{3... | collective-permute-start | bytes 73736 | tf_op jit(solution)/shard_map/ppermute | solution.py:373
  66.9 8.1 %collective-permute-start.4 = (f32[4,32,192]{2,1,0:T(8,128)S(1)}, f32[4,32,192]{2,1,0:T(8,128)S(1)}, u32[]{:S(2)}, u32[]{:S(2)}) collective-permute-start(f32[4,32,192]{2,1,0:T(8,128)S(1)} %get-tuple-element.35), channel_id=1, source_target_pairs={{64,96},{72,104},{80,112},{88,120},{65,97},{73,105},{81,113},{89,1... | collective-permute-start | bytes 294920 | tf_op jit(solution)/shard_map/ppermute | solution.py:373
  68.1 5.4 %collective-permute-start.5 = (f32[32,192]{1,0:T(8,128)S(1)}, f32[32,192]{1,0:T(8,128)S(1)}, u32[]{:S(2)}, u32[]{:S(2)}) collective-permute-start(f32[32,192]{1,0:T(8,128)S(1)} %get-tuple-element.34.acc_ref), channel_id=1, source_target_pairs={{64,96},{72,104},{80,112},{88,120},{65,97},{73,105},{81,113},{89,1... | collective-permute-start | bytes 73736 | tf_op jit(solution)/shard_map/ppermute | solution.py:373
  69.4 4.1 %collective-permute-start.6 = (f32[32,192]{1,0:T(8,128)S(1)}, f32[32,192]{1,0:T(8,128)S(1)}, u32[]{:S(2)}, u32[]{:S(2)}) collective-permute-start(f32[32,192]{1,0:T(8,128)S(1)} %get-tuple-element.34.acc_ref), channel_id=1, source_target_pairs={{64,104},{72,112},{80,120},{88,96},{65,105},{73,113},{81,121},{89,... | collective-permute-start | bytes 73736 | tf_op jit(solution)/shard_map/ppermute | solution.py:373
  70.7 2.9 %collective-permute-start.7 = (f32[32,192]{1,0:T(8,128)S(1)}, f32[32,192]{1,0:T(8,128)S(1)}, u32[]{:S(2)}, u32[]{:S(2)}) collective-permute-start(f32[32,192]{1,0:T(8,128)S(1)} %get-tuple-element.34.acc_ref), channel_id=1, source_target_pairs={{64,112},{72,120},{80,96},{88,104},{65,113},{73,121},{81,97},{89,1... | collective-permute-start | bytes 73736 | tf_op jit(solution)/shard_map/ppermute | solution.py:373
  72.0 2.9 %collective-permute-start.8 = (f32[32,192]{1,0:T(8,128)S(1)}, f32[32,192]{1,0:T(8,128)S(1)}, u32[]{:S(2)}, u32[]{:S(2)}) collective-permute-start(f32[32,192]{1,0:T(8,128)S(1)} %get-tuple-element.34.acc_ref), channel_id=1, source_target_pairs={{64,120},{72,96},{80,104},{88,112},{65,121},{73,97},{81,105},{89,1... | collective-permute-start | bytes 73736 | tf_op jit(solution)/shard_map/ppermute | solution.py:373
  76.6 7.8 %collective-permute-start.9 = (f32[32,768]{1,0:T(8,128)S(1)}, f32[32,768]{1,0:T(8,128)S(1)}, u32[]{:S(2)}, u32[]{:S(2)}) collective-permute-start(f32[32,768]{1,0:T(8,128)S(1)} %get-tuple-element.38), channel_id=1, source_target_pairs={{96,64},{104,72},{112,80},{120,88},{97,65},{105,73},{113,81},{121,... | collective-permute-start | bytes 294920 | tf_op jit(solution)/shard_map/ppermute | solution.py:373
  77.9 9.7 %collective-permute-start.10 = (f32[32,768]{1,0:T(8,128)S(1)}, f32[32,768]{1,0:T(8,128)S(1)}, u32[]{:S(2)}, u32[]{:S(2)}) collective-permute-start(f32[32,768]{1,0:T(8,128)S(1)} %get-tuple-element.38), channel_id=1, source_target_pairs={{96,72},{104,80},{112,88},{120,64},{97,73},{105,81},{113,89},{121,... | collective-permute-start | bytes 294920 | tf_op jit(solution)/shard_map/ppermute | solution.py:373
  79.2 9.6 %collective-permute-start.11 = (f32[32,768]{1,0:T(8,128)S(1)}, f32[32,768]{1,0:T(8,128)S(1)}, u32[]{:S(2)}, u32[]{:S(2)}) collective-permute-start(f32[32,768]{1,0:T(8,128)S(1)} %get-tuple-element.38), channel_id=1, source_target_pairs={{96,80},{104,88},{112,64},{120,72},{97,81},{105,89},{113,65},{121,... | collective-permute-start | bytes 294920 | tf_op jit(solution)/shard_map/ppermute | solution.py:373
  80.5 8.8 %collective-permute-start.12 = (f32[32,768]{1,0:T(8,128)S(1)}, f32[32,768]{1,0:T(8,128)S(1)}, u32[]{:S(2)}, u32[]{:S(2)}) collective-permute-start(f32[32,768]{1,0:T(8,128)S(1)} %get-tuple-element.38), channel_id=1, source_target_pairs={{96,88},{104,64},{112,72},{120,80},{97,89},{105,65},{113,73},{121,... | collective-permute-start | bytes 294920 | tf_op jit(solution)/shard_map/ppermute | solution.py:373
  90.6 6.5 %collective-permute-start.14 = (f32[32,768]{1,0:T(8,128)S(1)}, f32[32,768]{1,0:T(8,128)S(1)}, u32[]{:S(2)}, u32[]{:S(2)}) collective-permute-start(f32[32,768]{1,0:T(8,128)S(1)} %get-tuple-element.40), channel_id=1, source_target_pairs={{64,40},{72,48},{80,56},{88,32},{65,41},{73,49},{81,57},{89,33},{6... | collective-permute-start | bytes 294920 | tf_op jit(solution)/shard_map/ppermute | solution.py:373
  92.0 7.2 %collective-permute-start.13 = (f32[32,768]{1,0:T(8,128)S(1)}, f32[32,768]{1,0:T(8,128)S(1)}, u32[]{:S(2)}, u32[]{:S(2)}) collective-permute-start(f32[32,768]{1,0:T(8,128)S(1)} %get-tuple-element.40), channel_id=1, source_target_pairs={{64,32},{72,40},{80,48},{88,56},{65,33},{73,41},{81,49},{89,57},{6... | collective-permute-start | bytes 294920 | tf_op jit(solution)/shard_map/ppermute | solution.py:373
  93.3 5.9 %collective-permute-start.15 = (f32[32,768]{1,0:T(8,128)S(1)}, f32[32,768]{1,0:T(8,128)S(1)}, u32[]{:S(2)}, u32[]{:S(2)}) collective-permute-start(f32[32,768]{1,0:T(8,128)S(1)} %get-tuple-element.40), channel_id=1, source_target_pairs={{64,48},{72,56},{80,32},{88,40},{65,49},{73,57},{81,33},{89,41},{6... | collective-permute-start | bytes 294920 | tf_op jit(solution)/shard_map/ppermute | solution.py:373
  94.6 5.5 %collective-permute-start.16 = (f32[32,768]{1,0:T(8,128)S(1)}, f32[32,768]{1,0:T(8,128)S(1)}, u32[]{:S(2)}, u32[]{:S(2)}) collective-permute-start(f32[32,768]{1,0:T(8,128)S(1)} %get-tuple-element.40), channel_id=1, source_target_pairs={{64,56},{72,32},{80,40},{88,48},{65,57},{73,33},{81,41},{89,49},{6... | collective-permute-start | bytes 294920 | tf_op jit(solution)/shard_map/ppermute | solution.py:373
  95.9 5.3 %collective-permute-start.17 = (f32[32,768]{1,0:T(8,128)S(1)}, f32[32,768]{1,0:T(8,128)S(1)}, u32[]{:S(2)}, u32[]{:S(2)}) collective-permute-start(f32[32,768]{1,0:T(8,128)S(1)} %get-tuple-element.47.x3_two), channel_id=1, source_target_pairs={{64,32},{72,40},{80,48},{88,56},{65,33},{73,41},{81,49},{89,57},{6... | collective-permute-start | bytes 294920 | tf_op jit(solution)/shard_map/ppermute | solution.py:373
  97.2 8.1 %collective-permute-start.23 = (f32[32,768]{1,0:T(8,128)S(1)}, f32[32,768]{1,0:T(8,128)}, u32[]{:S(2)}, u32[]{:S(2)}) collective-permute-start(f32[32,768]{1,0:T(8,128)S(1)} %get-tuple-element.47.x3_two), channel_id=1, source_target_pairs={{64,96},{72,104},{80,112},{88,120},{65,97},{73,105},{81,113},{89,1... | collective-permute-start | bytes 294920 | tf_op jit(solution)/shard_map/ppermute | solution.py:373
  104.0 4.6 %collective-permute-start.22 = (f32[32,768]{1,0:T(8,128)}, f32[32,768]{1,0:T(8,128)}, u32[]{:S(2)}, u32[]{:S(2)}) collective-permute-start(f32[32,768]{1,0:T(8,128)} %get-tuple-element.50.x2_one), channel_id=1, source_target_pairs={{32,0},{40,8},{48,16},{56,24},{33,1},{41,9},{49,17},{57,25},{34,2}... | collective-permute-start | bytes 294920 | tf_op jit(solution)/shard_map/ppermute | solution.py:373
  105.3 4.0 %collective-permute-start.24 = (f32[32,768]{1,0:T(8,128)}, f32[32,768]{1,0:T(8,128)}, u32[]{:S(2)}, u32[]{:S(2)}) collective-permute-start(f32[32,768]{1,0:T(8,128)} %collective-permute-done.23.x3_ref.x3_three), channel_id=1, source_target_pairs={{96,0},{104,8},{112,16},{120,24},{97,1},{105,9},{113,17},{121,25},... | collective-permute-start | bytes 294920 | tf_op jit(solution)/shard_map/ppermute | solution.py:373
  106.6 2.7 %collective-permute-start.18 = (f32[32,768]{1,0:T(8,128)}, f32[32,768]{1,0:T(8,128)S(1)}, u32[]{:S(2)}, u32[]{:S(2)}) collective-permute-start(f32[32,768]{1,0:T(8,128)} %copy-done.28), channel_id=1, source_target_pairs={{32,0},{40,8},{48,16},{56,24},{33,1},{41,9},{49,17},{57,25},{34,2}... | collective-permute-start | bytes 294920 | tf_op jit(solution)/shard_map/ppermute | solution.py:373
  107.2 2.1 %collective-permute-start.19 = (f32[32,768]{1,0:T(8,128)}, f32[32,768]{1,0:T(8,128)S(1)}, u32[]{:S(2)}, u32[]{:S(2)}) collective-permute-start(f32[32,768]{1,0:T(8,128)} %copy-done.28), channel_id=1, source_target_pairs={{32,8},{40,16},{48,24},{56,0},{33,9},{41,17},{49,25},{57,1},{34,10... | collective-permute-start | bytes 294920 | tf_op jit(solution)/shard_map/ppermute | solution.py:373
  107.9 1.4 collective-permute-start.20
  108.6 0.7 collective-permute-start.21
  114.5 42.6 %copy-start.3 = (f32[2304,384]{1,0:T(8,128)S(1)}, f32[2304,384]{1,0:T(8,128)}, u32[]{:S(2)}) copy-start(f32[2304,384]{1,0:T(8,128)} %all-gather.7.cloned.1.call-done) | copy-start | bytes 10616836
  114.5 3.6 %collective-permute-start.26 = (f32[32,768]{1,0:T(8,128)S(1)}, f32[32,768]{1,0:T(8,128)S(1)}, u32[]{:S(2)}, u32[]{:S(2)}) collective-permute-start(f32[32,768]{1,0:T(8,128)S(1)} %get-tuple-element.48), channel_id=1, source_target_pairs={{0,40},{8,48},{16,56},{24,32},{1,41},{9,49},{17,57},{25,33},{2,42}... | collective-permute-start | bytes 294920 | tf_op jit(solution)/shard_map/ppermute | solution.py:373
  115.3 4.1 %collective-permute-start.25 = (f32[32,768]{1,0:T(8,128)S(1)}, f32[32,768]{1,0:T(8,128)S(1)}, u32[]{:S(2)}, u32[]{:S(2)}) collective-permute-start(f32[32,768]{1,0:T(8,128)S(1)} %get-tuple-element.48), channel_id=1, source_target_pairs={{0,32},{8,40},{16,48},{24,56},{1,33},{9,41},{17,49},{25,57},{2,34}... | collective-permute-start | bytes 294920 | tf_op jit(solution)/shard_map/ppermute | solution.py:373
  116.1 4.7 %collective-permute-start.27 = (f32[32,768]{1,0:T(8,128)S(1)}, f32[32,768]{1,0:T(8,128)S(1)}, u32[]{:S(2)}, u32[]{:S(2)}) collective-permute-start(f32[32,768]{1,0:T(8,128)S(1)} %get-tuple-element.48), channel_id=1, source_target_pairs={{0,48},{8,56},{16,32},{24,40},{1,49},{9,57},{17,33},{25,41},{2,50}... | collective-permute-start | bytes 294920 | tf_op jit(solution)/shard_map/ppermute | solution.py:373
  116.7 4.0 %collective-permute-start.28 = (f32[32,768]{1,0:T(8,128)S(1)}, f32[32,768]{1,0:T(8,128)S(1)}, u32[]{:S(2)}, u32[]{:S(2)}) collective-permute-start(f32[32,768]{1,0:T(8,128)S(1)} %get-tuple-element.48), channel_id=1, source_target_pairs={{0,56},{8,32},{16,40},{24,48},{1,57},{9,33},{17,41},{25,49},{2,58}... | collective-permute-start | bytes 294920 | tf_op jit(solution)/shard_map/ppermute | solution.py:373
  117.4 3.4 %collective-permute-start.29 = (f32[32,768]{1,0:T(8,128)S(1)}, f32[32,768]{1,0:T(8,128)S(1)}, u32[]{:S(2)}, u32[]{:S(2)}) collective-permute-start(f32[32,768]{1,0:T(8,128)S(1)} %get-tuple-element.49), channel_id=1, source_target_pairs={{0,32},{8,40},{16,48},{24,56},{1,33},{9,41},{17,49},{25,57},{2,34}... | collective-permute-start | bytes 294920 | tf_op jit(solution)/shard_map/ppermute | solution.py:373
  118.1 20.7 %collective-permute-start.30 = (f32[32,768]{1,0:T(8,128)}, f32[32,768]{1,0:T(8,128)S(1)}, u32[]{:S(2)}, u32[]{:S(2)}) collective-permute-start(f32[32,768]{1,0:T(8,128)} %get-tuple-element.50.x2_one), channel_id=1, source_target_pairs={{32,64},{40,72},{48,80},{56,88},{33,65},{41,73},{49,81},{57,89},{3... | collective-permute-start | bytes 294920 | tf_op jit(solution)/shard_map/ppermute | solution.py:373
  119.4 54.7 %collective-permute-start.44 = (f32[2,32,768]{2,1,0:T(8,128)}, f32[2,32,768]{2,1,0:T(8,128)}, u32[]{:S(2)}, u32[]{:S(2)}) collective-permute-start(f32[2,32,768]{2,1,0:T(8,128)} %get-tuple-element.61.both_zero), channel_id=1, source_target_pairs={{0,96},{8,104},{16,112},{24,120},{1,97},{9,105},{17,113},{25,121},... | collective-permute-start | bytes 589832 | tf_op jit(solution)/shard_map/ppermute | solution.py:373
  142.1 8.2 %collective-permute-start.32 = (f32[32,192]{1,0:T(8,128)}, f32[32,192]{1,0:T(8,128)}, u32[]{:S(2)}, u32[]{:S(2)}) collective-permute-start(f32[32,192]{1,0:T(8,128)} %get-tuple-element.54), channel_id=1, source_target_pairs={{32,72},{40,80},{48,88},{56,64},{33,73},{41,81},{49,89},{57,65},{3... | collective-permute-start | bytes 73736 | tf_op jit(solution)/shard_map/ppermute | solution.py:373
  143.4 8.8 %collective-permute-start.36 = (f32[32,192]{1,0:T(8,128)}, f32[32,192]{1,0:T(8,128)}, u32[]{:S(2)}, u32[]{:S(2)}) collective-permute-start(f32[32,192]{1,0:T(8,128)} %get-tuple-element.54), channel_id=1, source_target_pairs={{32,80},{40,88},{48,64},{56,72},{33,81},{41,89},{49,65},{57,73},{3... | collective-permute-start | bytes 73736 | tf_op jit(solution)/shard_map/ppermute | solution.py:373
  144.7 8.2 %collective-permute-start.35 = (f32[32,192]{1,0:T(8,128)}, f32[32,192]{1,0:T(8,128)}, u32[]{:S(2)}, u32[]{:S(2)}) collective-permute-start(f32[32,192]{1,0:T(8,128)} %get-tuple-element.54), channel_id=1, source_target_pairs={{32,64},{40,72},{48,80},{56,88},{33,65},{41,73},{49,81},{57,89},{3... | collective-permute-start | bytes 73736 | tf_op jit(solution)/shard_map/ppermute | solution.py:373
  146.0 7.6 %collective-permute-start.37 = (f32[32,192]{1,0:T(8,128)}, f32[32,192]{1,0:T(8,128)}, u32[]{:S(2)}, u32[]{:S(2)}) collective-permute-start(f32[32,192]{1,0:T(8,128)} %get-tuple-element.54), channel_id=1, source_target_pairs={{32,88},{40,64},{48,72},{56,80},{33,89},{41,65},{49,73},{57,81},{3... | collective-permute-start | bytes 73736 | tf_op jit(solution)/shard_map/ppermute | solution.py:373
  150.3 6.7 %collective-permute-start.31 = (f32[32,768]{1,0:T(8,128)}, f32[32,768]{1,0:T(8,128)S(1)}, u32[]{:S(2)}, u32[]{:S(2)}) collective-permute-start(f32[32,768]{1,0:T(8,128)} %copy-done.22), channel_id=1, source_target_pairs={{32,64},{40,72},{48,80},{56,88},{33,65},{41,73},{49,81},{57,89},{3... | collective-permute-start | bytes 294920 | tf_op jit(solution)/shard_map/ppermute | solution.py:373
  152.2 4.8 %collective-permute-start.33 = (f32[32,768]{1,0:T(8,128)}, f32[32,768]{1,0:T(8,128)S(1)}, u32[]{:S(2)}, u32[]{:S(2)}) collective-permute-start(f32[32,768]{1,0:T(8,128)} %copy-done.22), channel_id=1, source_target_pairs={{32,0},{40,8},{48,16},{56,24},{33,1},{41,9},{49,17},{57,25},{34,2}... | collective-permute-start | bytes 294920 | tf_op jit(solution)/shard_map/ppermute | solution.py:373
  152.9 4.2 %collective-permute-start.34 = (f32[32,768]{1,0:T(8,128)}, f32[32,768]{1,0:T(8,128)S(1)}, u32[]{:S(2)}, u32[]{:S(2)}) collective-permute-start(f32[32,768]{1,0:T(8,128)} %copy-done.22), channel_id=1, source_target_pairs={{32,96},{40,104},{48,112},{56,120},{33,97},{41,105},{49,113},{57,1... | collective-permute-start | bytes 294920 | tf_op jit(solution)/shard_map/ppermute | solution.py:373
  153.6 18.9 %collective-permute-start.43 = (f32[32,768]{1,0:T(8,128)}, f32[32,768]{1,0:T(8,128)S(1)}, u32[]{:S(2)}, u32[]{:S(2)}) collective-permute-start(f32[32,768]{1,0:T(8,128)} %copy-done.13), channel_id=1, source_target_pairs={{32,64},{40,72},{48,80},{56,88},{33,65},{41,73},{49,81},{57,89},{3... | collective-permute-start | bytes 294920 | tf_op jit(solution)/shard_map/ppermute | solution.py:373
  162.1 15.7 %collective-permute-start.39 = (f32[32,192]{1,0:T(8,128)S(1)}, f32[32,192]{1,0:T(8,128)S(1)}, u32[]{:S(2)}, u32[]{:S(2)}) collective-permute-start(f32[32,192]{1,0:T(8,128)S(1)} %get-tuple-element.56.acc_ref), channel_id=1, source_target_pairs={{64,96},{72,104},{80,112},{88,120},{65,97},{73,105},{81,113},{89,1... | collective-permute-start | bytes 73736 | tf_op jit(solution)/shard_map/ppermute | solution.py:373
  168.7 9.1 %collective-permute-start.40 = (f32[32,192]{1,0:T(8,128)S(1)}, f32[32,192]{1,0:T(8,128)S(1)}, u32[]{:S(2)}, u32[]{:S(2)}) collective-permute-start(f32[32,192]{1,0:T(8,128)S(1)} %get-tuple-element.56.acc_ref), channel_id=1, source_target_pairs={{64,104},{72,112},{80,120},{88,96},{65,105},{73,113},{81,121},{89,... | collective-permute-start | bytes 73736 | tf_op jit(solution)/shard_map/ppermute | solution.py:373
  170.0 7.8 %collective-permute-start.41 = (f32[32,192]{1,0:T(8,128)S(1)}, f32[32,192]{1,0:T(8,128)S(1)}, u32[]{:S(2)}, u32[]{:S(2)}) collective-permute-start(f32[32,192]{1,0:T(8,128)S(1)} %get-tuple-element.56.acc_ref), channel_id=1, source_target_pairs={{64,112},{72,120},{80,96},{88,104},{65,113},{73,121},{81,97},{89,1... | collective-permute-start | bytes 73736 | tf_op jit(solution)/shard_map/ppermute | solution.py:373
  172.5 5.3 %collective-permute-start.42 = (f32[32,192]{1,0:T(8,128)S(1)}, f32[32,192]{1,0:T(8,128)S(1)}, u32[]{:S(2)}, u32[]{:S(2)}) collective-permute-start(f32[32,192]{1,0:T(8,128)S(1)} %get-tuple-element.56.acc_ref), channel_id=1, source_target_pairs={{64,120},{72,96},{80,104},{88,112},{65,121},{73,97},{81,105},{89,1... | collective-permute-start | bytes 73736 | tf_op jit(solution)/shard_map/ppermute | solution.py:373
  174.1 3.8 %collective-permute-start.38 = (f32[4,32,192]{2,1,0:T(8,128)S(1)}, f32[4,32,192]{2,1,0:T(8,128)S(1)}, u32[]{:S(2)}, u32[]{:S(2)}) collective-permute-start(f32[4,32,192]{2,1,0:T(8,128)S(1)} %get-tuple-element.57), channel_id=1, source_target_pairs={{64,96},{72,104},{80,112},{88,120},{65,97},{73,105},{81,113},{89,1... | collective-permute-start | bytes 294920 | tf_op jit(solution)/shard_map/ppermute | solution.py:373
  (31 other events, 312.6 us)
Sparse Core Ops, SparseCore 0:
  10.2 31.9 all-gather.4
  46.6 27.5 all-gather.6

commit v4 on v3

--- a/solution.py
+++ b/solution.py
@@ -14,7 +14,7 @@
 BLOCK = 768
 PIECE = 96
 CELLS = 24
-VMEM = 40 * 1024 * 1024
+VMEM = 16 * 1024 * 1024
 
 SDS = jax.ShapeDtypeStruct
 f32 = jnp.float32
@@ -38,30 +38,39 @@
     return jnp.concatenate([real, imag], axis=0)
 
 
-def slot_of(plane, block):
-    return jnp.minimum(jnp.where(plane < block, block - 1, block), GROUP - 2)
-
-
-def block_weight(ref, slot):
-    return ref[:, slot].reshape(BLOCK, 2 * SLAB)
-
-
-def slabs_dot(slabs, weight_ref, slot, q, keep=None):
+def own_block(block):
+    return lambda i, place: (
+        0,
+        jnp.minimum(jnp.where(place[0] < block, block - 1, block), GROUP - 2),
+        0,
+        0,
+    )
+
+
+def second_factor(block):
+    return lambda i, place: (0, block, 0, 0)
+
+
+def block_weight(ref):
+    return ref[:, 0].reshape(BLOCK, 2 * SLAB)
+
+
+def slabs_dot(slabs, weight_ref, q, keep=None):
     total = None
     for d, slab in enumerate(slabs):
         source = lax.rem(q - d + GROUP, GROUP)
         if keep is not None:
             keep[source] = slab
-        weight = weight_ref[pl.ds(2 * source, 2), slot].reshape(SLAB, 2 * SLAB)
+        weight = weight_ref[pl.ds(2 * source, 2), 0].reshape(SLAB, 2 * SLAB)
         part = complex_dot(slab, weight)
         total = part if total is None else total + part
     return total
 
 
-def sent_dot(sent_ref, weight_ref, slot):
+def sent_dot(sent_ref, weight_ref):
     total = None
     for s in range(GROUP):
-        weight = weight_ref[2 * s : 2 * s + 2, slot].reshape(SLAB, 2 * SLAB)
+        weight = weight_ref[2 * s : 2 * s + 2, 0].reshape(SLAB, 2 * SLAB)
         part = complex_dot(sent_ref[s], weight)
         total = part if total is None else total + part
     return total
@@ -74,25 +83,29 @@
     return total
 
 
-def call(body, out_shape, inputs, scratch=()):
-    specs = []
-    for value in inputs:
-        if value.dtype == jnp.int32:
-            specs.append(pl.BlockSpec(memory_space=pltpu.SMEM))
-        else:
-            specs.append(pl.BlockSpec(value.shape, lambda i, n=value.ndim: (0,) * n))
-    outs = tuple(
-        pl.BlockSpec(shape.shape, lambda i, n=len(shape.shape): (0,) * n) for shape in out_shape
-    )
+def call(body, out_shape, scalars, inputs, blocks=(), scratch=()):
+    def whole(shape):
+        return pl.BlockSpec(
+            shape, lambda i, place, n=len(shape): (0,) * n, pipeline_mode=pl.Buffered(1)
+        )
+
+    specs = [whole(value.shape) for value in inputs]
+    for _, at in blocks:
+        specs.append(
+            pl.BlockSpec((8, 1, PIECE, 2 * SLAB), at, pipeline_mode=pl.Buffered(1))
+        )
     return pl.pallas_call(
         body,
-        grid=(1,),
-        in_specs=specs,
-        out_specs=outs,
+        grid_spec=pltpu.PrefetchScalarGridSpec(
+            num_scalar_prefetch=1,
+            grid=(1,),
+            in_specs=specs,
+            out_specs=tuple(whole(shape.shape) for shape in out_shape),
+            scratch_shapes=scratch,
+        ),
         out_shape=tuple(out_shape),
-        scratch_shapes=scratch,
         compiler_params=pltpu.CompilerParams(vmem_limit_bytes=VMEM),
-    )(*inputs)
+    )(scalars, *inputs, *[array for array, _ in blocks])
 
 
 def turn_first_kernel(place_ref, factor_ref, out_ref, turned_ref):
@@ -104,7 +117,7 @@
         out_ref[PIECE * slot : PIECE * slot + PIECE, :] = turned_ref[pl.ds(block * PIECE, PIECE), :]
 
 
-def pack_kernel(first_ref, second_ref, link_ref, out_ref):
+def pack_kernel(place_ref, first_ref, second_ref, link_ref, out_ref):
     lane = lax.broadcasted_iota(jnp.int32, (6, 128), 1)
     for y in range(2):
         parts = []
@@ -128,7 +141,7 @@
             at = step * 16 + u
             source = where_ref[at]
             rows_ref[pl.ds(at, 1), :] = cells_ref[pl.ds(source, 1), :]
-            links_ref[pl.ds(at, 1), :] = cells_ref[pl.ds(source | 15, 1), :]
+            links_ref[pl.ds(at, 1), :] = cells_ref[pl.ds(where_ref[1024 + at], 1), :]
         return carry
 
     lax.fori_loop(0, 64, some, 0)
@@ -147,51 +160,59 @@
 
 
 def start_kernel(place_ref, rhs_ref, weight_ref, acc_ref):
-    slot = slot_of(place_ref[0], 0)
-    product = complex_dot(rhs_ref[0:ROWS, 0:BLOCK], block_weight(weight_ref, slot))
+    product = complex_dot(rhs_ref[0:ROWS, 0:BLOCK], block_weight(weight_ref))
     slab = rhs_ref[0:ROWS, BLOCK : BLOCK + SLAB]
     acc_ref[...] = jnp.where(place_ref[0] > 0, slab - product, slab)
 
 
 def forward_one_kernel(place_ref, acc_ref, y0, y1, y2, y3, weight_ref, out_ref, keep_ref):
     slabs = [y0[...], y1[...], y2[...], y3[...]]
-    slot = slot_of(place_ref[0], 1)
-    out_ref[...] = acc_ref[...] - slabs_dot(slabs, weight_ref, slot, place_ref[1], keep_ref)
+    out_ref[...] = acc_ref[...] - slabs_dot(slabs, weight_ref, place_ref[1], keep_ref)
 
 
 def forward_two_kernel(
-    place_ref, acc_ref, sent_ref, y0, y1, y2, y3, weight_ref, inverse_ref, out_ref, part_ref
-):
-    plane, q = place_ref[0], place_ref[1]
+    place_ref, acc_ref, inverse_ref, sent_ref, y0, y1, y2, y3, weight1_ref, weight2_ref, out_ref, part_ref
+):
     slabs = [y0[...], y1[...], y2[...], y3[...]]
     solved = (
         acc_ref[...]
-        - sent_dot(sent_ref, weight_ref, slot_of(plane, 1))
-        - slabs_dot(slabs, weight_ref, slot_of(plane, 2), q)
+        - sent_dot(sent_ref, weight1_ref)
+        - slabs_dot(slabs, weight2_ref, place_ref[1])
     )
     out_ref[...] = solved
     part_ref[...] = complex_dot(solved, inverse_ref[...])
 
 
 def back_three_kernel(
-    place_ref, acc_ref, p0, p1, p2, p3, weight_ref, inverse_ref, x_ref, acc_out_ref, part_ref
+    place_ref, acc_ref, inverse_ref, p0, p1, p2, p3, weight_ref, x_ref, acc_out_ref, part_ref
 ):
     x = add_refs([p0, p1, p2, p3])
-    acc = acc_ref[...] - complex_dot(x, block_weight(weight_ref, slot_of(place_ref[0], 3)))
+    acc = acc_ref[...] - complex_dot(x, block_weight(weight_ref))
     x_ref[...] = x
     acc_out_ref[...] = acc
     part_ref[...] = complex_dot(acc, inverse_ref[...])
 
 
 def back_two_kernel(
-    place_ref, acc_ref, p0, p1, p2, p3, x3_ref, weight_ref, inverse_ref, x_ref, acc_out_ref, part_ref
-):
-    plane = place_ref[0]
+    place_ref,
+    acc_ref,
+    inverse_ref,
+    p0,
+    p1,
+    p2,
+    p3,
+    x3_ref,
+    weight2_ref,
+    weight3_ref,
+    x_ref,
+    acc_out_ref,
+    part_ref,
+):
     x = add_refs([p0, p1, p2, p3])
     acc = (
         acc_ref[...]
-        - complex_dot(x3_ref[...], block_weight(weight_ref, slot_of(plane, 3)))
-        - complex_dot(x, block_weight(weight_ref, slot_of(plane, 2)))
+        - complex_dot(x3_ref[...], block_weight(weight3_ref))
+        - complex_dot(x, block_weight(weight2_ref))
     )
     x_ref[...] = x
     acc_out_ref[...] = acc
@@ -201,25 +222,26 @@
 def back_one_kernel(
     place_ref,
     acc_ref,
+    inverse_ref,
     p0,
     p1,
     p2,
     p3,
     x2_ref,
     x3_ref,
-    weight_ref,
-    inverse_ref,
+    weight1_ref,
+    weight2_ref,
+    weight3_ref,
     x_ref,
     both_ref,
     part_ref,
 ):
-    plane = place_ref[0]
     x = add_refs([p0, p1, p2, p3])
     acc = (
         acc_ref[...]
-        - complex_dot(x3_ref[...], block_weight(weight_ref, slot_of(plane, 3)))
-        - complex_dot(x2_ref[...], block_weight(weight_ref, slot_of(plane, 2)))
-        - complex_dot(x, block_weight(weight_ref, slot_of(plane, 1)))
+        - complex_dot(x3_ref[...], block_weight(weight3_ref))
+        - complex_dot(x2_ref[...], block_weight(weight2_ref))
+        - complex_dot(x, block_weight(weight1_ref))
     )
     part_ref[...] = complex_dot(acc, inverse_ref[...])
     x_ref[...] = x
@@ -250,29 +272,13 @@
 
 
 def couple_kernel(
-    place_ref,
-    rhs_ref,
-    link_ref,
-    p0,
-    p1,
-    p2,
-    p3,
-    x1_ref,
-    x2_ref,
-    x3_ref,
-    weight_ref,
-    x0_ref,
-    slab_ref,
-    out_ref,
-):
-    plane, q = place_ref[0], place_ref[1]
+    place_ref, rhs_ref, link_ref, p0, p1, p2, p3, x1_ref, weight_ref, x0_ref, out_ref
+):
     x0 = add_refs([p0, p1, p2, p3])
-    own = jnp.where(plane == 1, x1_ref[...], jnp.where(plane == 2, x2_ref[...], x3_ref[...]))
-    slab = second_slab(rhs_ref, link_ref, own, q)
     x0_ref[...] = x0
-    slab_ref[...] = slab
+    slab = second_slab(rhs_ref, link_ref, x1_ref[...], place_ref[1])
     out_ref[...] = slab - complex_dot(
-        second_block(rhs_ref, link_ref, x0), block_weight(weight_ref, 0)
+        second_block(rhs_ref, link_ref, x0), block_weight(weight_ref)
     )
 
 
@@ -280,33 +286,45 @@
     place_ref,
     rhs_ref,
     link_ref,
-    slab_ref,
+    acc_ref,
+    x0_ref,
+    x2_ref,
+    f0,
+    f1,
+    f2,
+    f3,
+    weight0_ref,
+    weight1_ref,
+    out_ref,
+    keep_ref,
+):
+    q = place_ref[1]
+    slab = second_slab(rhs_ref, link_ref, x2_ref[...], q)
+    product = complex_dot(second_block(rhs_ref, link_ref, x0_ref[...]), block_weight(weight0_ref))
+    slabs = [f0[...], f1[...], f2[...], f3[...]]
+    solved = slab - product - slabs_dot(slabs, weight1_ref, q, keep_ref)
+    out_ref[...] = jnp.where(place_ref[0] == 1, acc_ref[...], solved)
+
+
+def second_base_kernel(
+    place_ref, rhs_ref, link_ref, acc_ref, x0_zero, x0_three, x3_ref, weight_ref, out_ref
+):
+    plane, q = place_ref[0], place_ref[1]
+    x0 = x0_zero[...] + x0_three[...]
+    own = jnp.where(plane == 0, x0, x3_ref[...])
+    slab = second_slab(rhs_ref, link_ref, own, q)
+    product = complex_dot(second_block(rhs_ref, link_ref, x0), block_weight(weight_ref))
+    out_ref[...] = jnp.where(
+        plane == 0, slab, jnp.where(plane == 3, slab - product, acc_ref[...])
+    )
+
+
+def cells_kernel(
+    where_ref,
     x0_one,
     x0_two,
     x0_zero,
     x0_three,
-    f0,
-    f1,
-    f2,
-    f3,
-    weight_ref,
-    out_ref,
-    keep_ref,
-    x0_ref,
-):
-    plane, q = place_ref[0], place_ref[1]
-    x0 = add_refs([x0_one, x0_two, x0_zero, x0_three])
-    x0_ref[...] = x0
-    first = second_slab(rhs_ref, link_ref, x0, q)
-    slabs = [f0[...], f1[...], f2[...], f3[...]]
-    product = complex_dot(second_block(rhs_ref, link_ref, x0), block_weight(weight_ref, 0))
-    later = slab_ref[...] - product - slabs_dot(slabs, weight_ref, 1, q, keep_ref)
-    out_ref[...] = jnp.where(plane == 0, first, later)
-
-
-def cells_kernel(
-    where_ref,
-    x0_ref,
     both_zero,
     x1_one,
     x1_two,
@@ -322,7 +340,7 @@
     rows_ref,
 ):
     blocks = (
-        x0_ref[...],
+        x0_one[...] + x0_two[...] + x0_zero[...] + x0_three[...],
         both_zero[0] + x1_one[...] + x1_two[...] + both_three[0],
         both_zero[1] + x2_one[...] + x2_two[...] + both_three[1],
         x3_zero[...] + x3_one[...] + x3_two[...] + x3_three[...],
@@ -341,13 +359,13 @@
 
 
 def second_two_kernel(
-    place_ref, acc_ref, sent_ref, f0, f1, f2, f3, cells_ref, weight_ref, out_ref
+    place_ref, acc_ref, cells_ref, sent_ref, f0, f1, f2, f3, weight1_ref, weight2_ref, out_ref
 ):
     slabs = [f0[...], f1[...], f2[...], f3[...]]
     solved = (
         acc_ref[...]
-        - sent_dot(sent_ref, weight_ref, 1)
-        - slabs_dot(slabs, weight_ref, 2, place_ref[1])
+        - sent_dot(sent_ref, weight1_ref)
+        - slabs_dot(slabs, weight2_ref, place_ref[1])
     )
     lane = lax.broadcasted_iota(jnp.int32, (ROWS, 128), 1)
     tail = jnp.concatenate([solved[:, 128:], jnp.zeros((ROWS, 64), f32)], axis=1)
@@ -356,7 +374,7 @@
         out_ref[c, :, 128:256] = jnp.where(lane < 64, tail, cells_ref[c])
 
 
-def out_kernel(got_ref, solution_ref, forward_ref):
+def out_kernel(place_ref, got_ref, solution_ref, forward_ref):
     for part in range(2):
         wide = got_ref[:, CHUNK * part : CHUNK * part + CHUNK, :].reshape(128, 256)
         forward_ref[part, 0:128, :] = wide[:, 0:128].T
@@ -392,30 +410,35 @@
     (turned1,) = call(
         turn_first_kernel,
         [SDS((3 * PIECE, 2 * SLAB), f32)],
-        [place, factor1],
+        place,
+        [factor1],
         scratch=[pltpu.VMEM((4 * PIECE, 2 * SLAB), f32)],
     )
     matrix1 = gather_blocks(turned1)
 
     links = jnp.pad(coupling.reshape(2, CELLS), ((0, 0), (0, 32 - CELLS))).reshape(1, 64)
     links = jnp.pad(links, ((0, 0), (0, 64)))
-    (packed,) = call(pack_kernel, [SDS((8, 16, 128), f32)], [source1, source2, links])
+    (packed,) = call(
+        pack_kernel, [SDS((8, 16, 128), f32)], place, [source1, source2, links]
+    )
     packed = lax.all_to_all(packed, "col", 0, 0)
-    packed = jnp.broadcast_to(packed[None], (16, 8, 16, 128))
-    cells = lax.all_to_all(packed, "row", 0, 0).reshape(128 * 16, 128)
+    packed = jnp.broadcast_to(packed[:, :13].reshape(1, 104, 128), (16, 104, 128))
+    cells = lax.all_to_all(packed, "row", 0, 0).reshape(16 * 104, 128)
 
     cell_y = front_order // 48
     cell_x = front_order % 48
-    place_of = ((cell_y // 4) * 8 + cell_x // 6) * 16 + (cell_y % 2) * 6 + cell_x % 6
+    group_of = (cell_y // 4) * 104 + (cell_x // 6) * 13
+    place_of = group_of + (cell_y % 2) * 6 + cell_x % 6
     upper = (cell_y % 4) // 2
     inner = (cell_y % 4) * 6 + cell_x % 6
-    every = jnp.stack([place_of, upper, inner])
+    every = jnp.stack([place_of, group_of + 12, upper, inner])
     own = lax.dynamic_slice_in_dim(every, row_id * SLAB, SLAB, 1)
-    every = jnp.concatenate([every[:, :BLOCK], own, jnp.zeros((3, 64), jnp.int32)], axis=1)
+    every = jnp.concatenate([every[:, :BLOCK], own, jnp.zeros((4, 64), jnp.int32)], axis=1)
     rhs, link = call(
         front_kernel,
         [SDS((64, 1024), f32), SDS((16, 1024), f32)],
-        [every[0], cells, every[1:].astype(f32)],
+        every[:2].reshape(2048),
+        [cells, every[2:].astype(f32)],
         scratch=[pltpu.VMEM((1024, 128), f32), pltpu.VMEM((1024, 128), f32)],
     )
     factor2, diag_inv, cells = lax.optimization_barrier((factor2, diag_inv, cells))
@@ -428,62 +451,88 @@
     pair_shape = SDS((2, ROWS, BLOCK), f32)
     sent_shape = SDS((GROUP, ROWS, SLAB), f32)
 
-    (acc,) = call(start_kernel, [slab_shape], [place, rhs, matrix1])
+    def first_blocks(*blocks):
+        return [(matrix1, own_block(block)) for block in blocks]
+
+    (acc,) = call(start_kernel, [slab_shape], place, [rhs], first_blocks(0))
     got = plane_spread(acc, 1, 2)
     acc, kept = call(
-        forward_one_kernel, [slab_shape, sent_shape], [place, acc, *got, matrix1]
+        forward_one_kernel, [slab_shape, sent_shape], place, [acc, *got], first_blocks(1)
     )
     got = plane_spread(acc, 2, 3)
     sent = plane_send(kept, 2, 3)
     acc, part = call(
         forward_two_kernel,
         [slab_shape, block_shape],
-        [place, acc, sent, *got, matrix1, inverse],
+        place,
+        [acc, inverse, sent, *got],
+        first_blocks(1, 2),
     )
     got = plane_spread(part, 3, 2)
     x3_two, acc, part = call(
         back_three_kernel,
         [block_shape, slab_shape, block_shape],
-        [place, acc, *got, matrix1, inverse],
+        place,
+        [acc, inverse, *got],
+        first_blocks(3),
     )
     got = plane_spread(part, 2, 1)
     x3_one = plane_send(x3_two, 2, 1)
     x3_three = plane_send(after(x3_two, got[1]), 2, 3)
+    x3_zero = plane_send(after(x3_two, got[1]), 2, 0)
     x2_one, acc, part = call(
         back_two_kernel,
         [block_shape, slab_shape, block_shape],
-        [place, acc, *got, x3_one, matrix1, inverse],
+        place,
+        [acc, inverse, *got, x3_one],
+        first_blocks(2, 3),
     )
     matrix2, part = lax.optimization_barrier((matrix2, part))
+
+    def second_blocks(*blocks):
+        return [(matrix2, second_factor(block)) for block in blocks]
+
     got = plane_spread(part, 1, 0)
     x2_zero = plane_send(x2_one, 1, 0)
-    x3_zero = plane_send(x3_three, 3, 0)
     x2_two = plane_send(after(x2_one, got[1]), 1, 2)
     x1_zero, both_zero, part = call(
         back_one_kernel,
         [block_shape, pair_shape, block_shape],
-        [place, acc, *got, x2_zero, x3_zero, matrix1, inverse],
+        place,
+        [acc, inverse, *got, x2_zero, x3_zero],
+        first_blocks(1, 2, 3),
     )
     got = plane_spread(part, 0, 1)
     x1_one = plane_send(x1_zero, 0, 1)
-    both_three = plane_send(after(both_zero, got[1]), 0, 3)
-    x0_one, slab, acc = call(
+    x0_one, acc = call(
         couple_kernel,
-        [block_shape, slab_shape, slab_shape],
-        [place, rhs, link, *got, x1_one, x2_two, x3_three, matrix2],
+        [block_shape, slab_shape],
+        place,
+        [rhs, link, *got, x1_one],
+        second_blocks(0),
     )
     got = plane_spread(acc, 1, 2)
     x0_two = plane_send(x0_one, 1, 2)
     x0_zero = plane_send(after(x0_one, got[1]), 1, 0)
     x0_three = plane_send(after(x0_one, got[1]), 1, 3)
-    x1_two = plane_send(after(x1_one, got[2]), 1, 2)
-    acc, kept, x0_all = call(
+    both_three = plane_send(after(both_zero, got[1]), 0, 3)
+    acc, kept = call(
         second_one_kernel,
-        [slab_shape, sent_shape, block_shape],
-        [place, rhs, link, slab, x0_one, x0_two, x0_zero, x0_three, *got, matrix2],
+        [slab_shape, sent_shape],
+        place,
+        [rhs, link, acc, x0_two, x2_two, *got],
+        second_blocks(0, 1),
     )
     got = plane_spread(acc, 2, 3)
     sent = plane_send(kept, 2, 3)
+    x1_two = plane_send(after(x1_one, got[1]), 1, 2)
+    (acc,) = call(
+        second_base_kernel,
+        [slab_shape],
+        place,
+        [rhs, link, acc, x0_zero, x0_three, x3_three],
+        second_blocks(0),
+    )
 
     at = jnp.arange(SLAB, dtype=jnp.int32)
     own_c, own_y, own_x = at // CELLS, at % CELLS // 6, at % 6
@@ -493,9 +542,12 @@
     (mine,) = call(
         cells_kernel,
         [SDS((8, ROWS, 128), f32)],
+        slots,
         [
-            slots,
-            x0_all,
+            x0_one,
+            x0_two,
+            x0_zero,
+            x0_three,
             both_zero,
             x1_one,
             x1_two,
@@ -512,11 +564,16 @@
     (last,) = call(
         second_two_kernel,
         [SDS((8, ROWS, 256), f32)],
-        [place, acc, sent, *got, mine, matrix2],
+        place,
+        [acc, mine, sent, *got],
+        second_blocks(1, 2),
     )
     arrived = lax.all_to_all(last, "col", 0, 0)
     return call(
-        out_kernel, [SDS((2, 4, 6, 128), f32), SDS((2, SLAB, 128), f32)], [arrived]
+        out_kernel,
+        [SDS((2, 4, 6, 128), f32), SDS((2, SLAB, 128), f32)],
+        place,
+        [arrived],
     )
 
 

time: 200 us -> 195 us (0.975)
  Pallas kernels: 21.9 us -> 26.2 us
  starting transfers between devices: 59.3 us -> 56.3 us
  local copies, waits for them, and re-layouts: 17.7 us -> 15.4 us
  blocking collectives: 42.6 us -> 40.5 us
    pallas_call x14 -> x15, Pallas kernels: 21.9 us -> 26.2 us  [call(): pl.pallas_call(body, grid_spec=pltpu.PrefetchScalarGridSpec(num_scalar_pr...]
    ppermute x45, starting transfers between devices: 59.2 us -> 56.2 us  [plane_send(): return lax.ppermute(value, 'row', pairs)]
    unnamed x66 -> x69, local copies, waits for them, and re-layouts: 14.9 us -> 12.6 us
    all_to_all x1, blocking collectives: 21.9 us -> 19.8 us  [on_device(): cells = lax.all_to_all(packed, 'row', 0, 0).reshape(16 * 104, 128)]
  transfers between devices with their start and end apart: 47 -> 47, of which waited for: 16 -> 17; matrix products, arithmetic and copies ran while one was open for 2% -> 2% of each run, Pallas kernels for 8% -> 8%
where the time goes in v4:
time: 195 us; the launch traced here: 193 us
  starting transfers between devices  56.3 us (29%)
  blocking collectives  40.5 us (21%)
  waiting for transfers between devices  39.4 us (20%)
  Pallas kernels  26.2 us (13%)
  local copies, waits for them, and re-layouts  15.4 us (8%)
  between operations  14.9 us (8%)
    ppermute x45, starting transfers between devices, plane_send(): return lax.ppermute(value, 'row', pairs)  56.2 us
    ppermute x45, waiting for transfers between devices, plane_send(): return lax.ppermute(value, 'row', pairs)  39.4 us
    pallas_call x15, Pallas kernels, call(): pl.pallas_call(body, grid_spec=pltpu.PrefetchScalarGridSpec(num_scalar_pr...  26.2 us
    all_to_all x1, blocking collectives, on_device(): cells = lax.all_to_all(packed, 'row', 0, 0).reshape(16 * 104, 128)  19.8 us
    unnamed x69, local copies, waits for them, and re-layouts  12.6 us
    all_to_all x1, blocking collectives, on_device(): packed = lax.all_to_all(packed, 'col', 0, 0)  10.7 us
    all_to_all x1, blocking collectives, on_device(): arrived = lax.all_to_all(last, 'col', 0, 0)  9.95 us
  transfers between devices with their start and end apart: 47, of which 17 were waited for; matrix products, arithmetic and copies ran while one was open for 2% of the time, Pallas kernels for 8%

profile of v4, /device:TPU:4, one launch (start us, length us, event | category | flops | bytes accessed | tf_op | source)
XLA Modules:
  0.0 193.4 jit_solution(5485275036144025487)
XLA Ops:
  8.4 1.7 shard_map.88
  13.2 10.7 %all_to_all.15 = f32[8,16,128]{2,1,0:T(8,128)S(1)} all-to-all(f32[8,16,128]{2,1,0:T(8,128)S(1)} %shard_map.86), channel_id=1, replica_groups=mesh['row'=16,'col'=8] {'col'}, dimensions={0} | all-to-all | bytes 131072 | tf_op jit(solution)/shard_map/all_to_all | solution.py:424
  24.0 19.8 %all_to_all.16 = f32[16,104,128]{2,1,0:T(8,128)S(1)} all-to-all(f32[16,104,128]{2,1,0:T(8,128)S(1)} %broadcast_in_dim.27), channel_id=1, replica_groups=mesh['row'=16,'col'=8] {'row'}, dimensions={0} | all-to-all | bytes 1703936 | tf_op jit(solution)/shard_map/all_to_all | solution.py:426
  45.2 2.9 %shard_map.87 = (f32[64,1024]{1,0:T(8,128)S(1)}, f32[16,1024]{1,0:T(8,128)S(1)}) custom-call(s32[2048]{0:T(1024)S(1)} %bitcast.43, f32[1664,128]{1,0:T(8,128)S(1)} %bitcast.42, f32[2,1024]{1,0:T(2,128)S(1)} %get-tuple-element.66.mark_ref), custom_call_target="tpu_custom_call" | custom-call | tf_op jit(solution)/shard_map/pallas_call | solution.py:97
  49.4 2.0 %copy-done = f32[2304,384]{1,0:T(8,128)S(1)} copy-done((f32[2304,384]{1,0:T(8,128)S(1)}, f32[2304,384]{1,0:T(8,128)}, u32[]{:S(2)}) %copy-start) | copy-done | bytes 3538968
  53.4 1.6 collective-permute-start
  54.9 1.3 collective-permute-start.1
  56.2 1.3 collective-permute-start.2
  57.5 1.3 collective-permute-start.3
  59.4 3.5 %collective-permute-done.1.y1 = f32[32,192]{1,0:T(8,128)S(1)} collective-permute-done((f32[32,192]{1,0:T(8,128)S(1)}, f32[32,192]{1,0:T(8,128)S(1)}, u32[]{:S(2)}, u32[]{:S(2)}) %collective-permute-start.1) | collective-permute-done | bytes 24608 | tf_op jit(solution)/shard_map/ppermute | solution.py:391
  62.9 1.5 collective-permute-done.2.y2
  72.4 1.3 collective-permute-done.8.y3
  73.7 1.7 shard_map.91
  75.4 1.3 collective-permute-start.9
  76.7 1.3 collective-permute-start.10
  78.0 1.3 collective-permute-start.11
  79.3 1.3 collective-permute-start.12
  80.6 2.7 %collective-permute-done.9.p0 = f32[32,768]{1,0:T(8,128)S(1)} collective-permute-done((f32[32,768]{1,0:T(8,128)S(1)}, f32[32,768]{1,0:T(8,128)S(1)}, u32[]{:S(2)}, u32[]{:S(2)}) %collective-permute-start.9) | collective-permute-done | bytes 98336 | tf_op jit(solution)/shard_map/ppermute | solution.py:391
  83.3 3.1 %collective-permute-done.10.p1 = f32[32,768]{1,0:T(8,128)S(1)} collective-permute-done((f32[32,768]{1,0:T(8,128)S(1)}, f32[32,768]{1,0:T(8,128)S(1)}, u32[]{:S(2)}, u32[]{:S(2)}) %collective-permute-start.10) | collective-permute-done | bytes 98336 | tf_op jit(solution)/shard_map/ppermute | solution.py:391
  88.0 1.9 shard_map.92
  91.2 1.3 collective-permute-start.14
  92.5 1.3 collective-permute-start.15
  93.8 1.3 collective-permute-start.16
  95.1 1.3 collective-permute-start.17
  96.4 1.6 collective-permute-done.15.p2
  100.2 1.6 shard_map.93
  103.1 1.3 collective-permute-start.22
  104.4 1.9 collective-permute-start.23
  111.1 3.1 %shard_map.94 = (f32[32,768]{1,0:T(8,128)S(1)}, f32[2,32,768]{2,1,0:T(8,128)S(1)}, f32[32,768]{1,0:T(8,128)S(1)}) custom-call(s32[2]{0:T(128)S(1)} %pad_add_fusion.1.place_ref, f32[32,192]{1,0:T(8,128)S(1)} %copy-done.27, f32[192,1536]{1,0:T(8,128)S(1)} %bitcast.41, f32[32,768]{1,0:T(8,128)S(1)} %collective-permute-done.18.p0, ...), custom_call_target="tpu_custom_call" | custom-call | tf_op jit(solution)/shard_map/pallas_call | solution.py:97
  117.6 1.3 collective-permute-start.30
  121.3 1.6 collective-permute-start.31
  122.9 1.3 collective-permute-start.32
  124.2 1.3 collective-permute-start.33
  125.5 9.2 %collective-permute-done.30.x2_ref.x2_two = f32[32,768]{1,0:T(8,128)S(1)} collective-permute-done((f32[32,768]{1,0:T(8,128)}, f32[32,768]{1,0:T(8,128)S(1)}, u32[]{:S(2)}, u32[]{:S(2)}) %collective-permute-start.30) | collective-permute-done | bytes 98336 | tf_op jit(solution)/shard_map/ppermute | solution.py:391
  136.0 7.1 %collective-permute-done.31.f0 = f32[32,192]{1,0:T(8,128)S(1)} collective-permute-done((f32[32,192]{1,0:T(8,128)S(1)}, f32[32,192]{1,0:T(8,128)S(1)}, u32[]{:S(2)}, u32[]{:S(2)}) %collective-permute-start.31) | collective-permute-done | bytes 24608 | tf_op jit(solution)/shard_map/ppermute | solution.py:391
  143.0 2.8 %collective-permute-done.32.f1 = f32[32,192]{1,0:T(8,128)S(1)} collective-permute-done((f32[32,192]{1,0:T(8,128)S(1)}, f32[32,192]{1,0:T(8,128)S(1)}, u32[]{:S(2)}, u32[]{:S(2)}) %collective-permute-start.32) | collective-permute-done | bytes 24608 | tf_op jit(solution)/shard_map/ppermute | solution.py:391
  145.9 1.3 collective-permute-done.33.f2
  147.8 2.0 %shard_map.96 = (f32[32,192]{1,0:T(8,128)}, f32[4,32,192]{2,1,0:T(8,128)S(1)}) custom-call(s32[2]{0:T(128)S(1)} %pad_add_fusion.1.place_ref, f32[64,1024]{1,0:T(8,128)S(1)} %copy-done.8, f32[16,1024]{1,0:T(8,128)S(1)} %copy-done.11, f32[32,192]{1,0:T(8,128)S(1)} %get-tuple-element.49.acc_ref, f32[32,768]{1,0:T(8,128)S(1)} %collective-permute-done.29.x0_ref.x0_two, ...), custom_call_target="tpu_custom_call" | custom-call | tf_op jit(solution)/shard_map/pallas_call | solution.py:97
  150.5 1.9 collective-permute-start.38
  155.7 1.3 collective-permute-start.39
  157.1 3.3 %collective-permute-start.42 = (f32[32,192]{1,0:T(8,128)}, f32[32,192]{1,0:T(8,128)S(1)}, u32[]{:S(2)}, u32[]{:S(2)}) collective-permute-start(f32[32,192]{1,0:T(8,128)} %get-tuple-element.52.acc_ref), channel_id=1, source_target_pairs={{64,96},{72,104},{80,112},{88,120},{65,97},{73,105},{81,113},{89,1... | collective-permute-start | bytes 73736 | tf_op jit(solution)/shard_map/ppermute | solution.py:391
  160.4 3.1 %collective-permute-start.43 = (f32[32,192]{1,0:T(8,128)}, f32[32,192]{1,0:T(8,128)S(1)}, u32[]{:S(2)}, u32[]{:S(2)}) collective-permute-start(f32[32,192]{1,0:T(8,128)} %get-tuple-element.52.acc_ref), channel_id=1, source_target_pairs={{64,112},{72,120},{80,96},{88,104},{65,113},{73,121},{81,97},{89,1... | collective-permute-start | bytes 73736 | tf_op jit(solution)/shard_map/ppermute | solution.py:391
  164.8 1.3 collective-permute-start.41
  168.4 1.8 shard_map.97.acc_ref
  170.2 2.3 %shard_map.98.cells_ref = f32[8,32,128]{2,1,0:T(8,128)S(1)} custom-call(s32[192]{0:T(256)S(1)} %select_reduce_fusion.where_ref, f32[32,768]{1,0:T(8,128)S(1)} %copy-done.25, f32[32,768]{1,0:T(8,128)S(1)} %copy-done.19, f32[32,768]{1,0:T(8,128)S(1)} %collective-permute-done.35.x0_zero, f32[32,768]{1,0:T(8,128)S(1)} %collective-permute-done.36.x0_three, ...), custom_call_target="tpu_custom_call" | custom-call | tf_op jit(solution)/shard_map/pallas_call | solution.py:97
  172.5 2.1 %shard_map.99 = f32[8,32,256]{2,1,0:T(8,128)S(1)} custom-call(s32[2]{0:T(128)S(1)} %pad_add_fusion.1.place_ref, f32[32,192]{1,0:T(8,128)S(1)} %shard_map.97.acc_ref, f32[8,32,128]{2,1,0:T(8,128)S(1)} %shard_map.98.cells_ref, f32[4,32,192]{2,1,0:T(8,128)S(1)} %collective-permute-done.41.sent_ref, f32[32,192]{1,0:T(8,128)S(1)} %collective-permute-done.42.f0, ...), custom_call_target="tpu_custom_call" | custom-call | tf_op jit(solution)/shard_map/pallas_call | solution.py:97
  174.6 9.9 %all_to_all.17.got_ref = f32[8,32,256]{2,1,0:T(8,128)S(1)} all-to-all(f32[8,32,256]{2,1,0:T(8,128)S(1)} %shard_map.99), channel_id=1, replica_groups=mesh['row'=16,'col'=8] {'col'}, dimensions={0} | all-to-all | bytes 524288 | tf_op jit(solution)/shard_map/all_to_all | solution.py:571
  184.6 1.3 shard_map.100
  (156 shorter events, 44.3 us)
Async XLA Ops:
  7.2 42.2 %all-gather.5.cloned.1.call-start = ((), (), s32[]{:S(2)}) async-start(), calls=%async_computation.3 | async-start | bytes 3981312 | tf_op jit(solution)/shard_map/all_gather | solution.py:408
  10.1 96.3 %all-gather.7.cloned.1.call-start = ((), (), s32[]{:S(2)}) async-start(), calls=%async_computation.4 | async-start | bytes 3981312 | tf_op jit(solution)/shard_map/all_gather | solution.py:408
  53.4 6.1 %collective-permute-start = (f32[32,192]{1,0:T(8,128)S(1)}, f32[32,192]{1,0:T(8,128)S(1)}, u32[]{:S(2)}, u32[]{:S(2)}) collective-permute-start(f32[32,192]{1,0:T(8,128)S(1)} %shard_map.89.acc_ref), channel_id=1, source_target_pairs={{32,64},{40,72},{48,80},{56,88},{33,65},{41,73},{49,81},{57,89},{3... | collective-permute-start | bytes 73736 | tf_op jit(solution)/shard_map/ppermute | solution.py:391
  54.9 8.0 %collective-permute-start.1 = (f32[32,192]{1,0:T(8,128)S(1)}, f32[32,192]{1,0:T(8,128)S(1)}, u32[]{:S(2)}, u32[]{:S(2)}) collective-permute-start(f32[32,192]{1,0:T(8,128)S(1)} %shard_map.89.acc_ref), channel_id=1, source_target_pairs={{32,72},{40,80},{48,88},{56,64},{33,73},{41,81},{49,89},{57,65},{3... | collective-permute-start | bytes 73736 | tf_op jit(solution)/shard_map/ppermute | solution.py:391
  56.2 8.2 %collective-permute-start.2 = (f32[32,192]{1,0:T(8,128)S(1)}, f32[32,192]{1,0:T(8,128)S(1)}, u32[]{:S(2)}, u32[]{:S(2)}) collective-permute-start(f32[32,192]{1,0:T(8,128)S(1)} %shard_map.89.acc_ref), channel_id=1, source_target_pairs={{32,80},{40,88},{48,64},{56,72},{33,81},{41,89},{49,65},{57,73},{3... | collective-permute-start | bytes 73736 | tf_op jit(solution)/shard_map/ppermute | solution.py:391
  57.5 6.9 %collective-permute-start.3 = (f32[32,192]{1,0:T(8,128)S(1)}, f32[32,192]{1,0:T(8,128)S(1)}, u32[]{:S(2)}, u32[]{:S(2)}) collective-permute-start(f32[32,192]{1,0:T(8,128)S(1)} %shard_map.89.acc_ref), channel_id=1, source_target_pairs={{32,88},{40,64},{48,72},{56,80},{33,89},{41,65},{49,73},{57,81},{3... | collective-permute-start | bytes 73736 | tf_op jit(solution)/shard_map/ppermute | solution.py:391
  65.6 8.1 %collective-permute-start.4 = (f32[4,32,192]{2,1,0:T(8,128)S(1)}, f32[4,32,192]{2,1,0:T(8,128)S(1)}, u32[]{:S(2)}, u32[]{:S(2)}) collective-permute-start(f32[4,32,192]{2,1,0:T(8,128)S(1)} %get-tuple-element.34), channel_id=1, source_target_pairs={{64,96},{72,104},{80,112},{88,120},{65,97},{73,105},{81,113},{89,1... | collective-permute-start | bytes 294920 | tf_op jit(solution)/shard_map/ppermute | solution.py:391
  66.9 5.4 %collective-permute-start.5 = (f32[32,192]{1,0:T(8,128)S(1)}, f32[32,192]{1,0:T(8,128)S(1)}, u32[]{:S(2)}, u32[]{:S(2)}) collective-permute-start(f32[32,192]{1,0:T(8,128)S(1)} %get-tuple-element.32.acc_ref), channel_id=1, source_target_pairs={{64,96},{72,104},{80,112},{88,120},{65,97},{73,105},{81,113},{89,1... | collective-permute-start | bytes 73736 | tf_op jit(solution)/shard_map/ppermute | solution.py:391
  68.2 4.1 %collective-permute-start.6 = (f32[32,192]{1,0:T(8,128)S(1)}, f32[32,192]{1,0:T(8,128)S(1)}, u32[]{:S(2)}, u32[]{:S(2)}) collective-permute-start(f32[32,192]{1,0:T(8,128)S(1)} %get-tuple-element.32.acc_ref), channel_id=1, source_target_pairs={{64,104},{72,112},{80,120},{88,96},{65,105},{73,113},{81,121},{89,... | collective-permute-start | bytes 73736 | tf_op jit(solution)/shard_map/ppermute | solution.py:391
  69.5 2.9 %collective-permute-start.7 = (f32[32,192]{1,0:T(8,128)S(1)}, f32[32,192]{1,0:T(8,128)S(1)}, u32[]{:S(2)}, u32[]{:S(2)}) collective-permute-start(f32[32,192]{1,0:T(8,128)S(1)} %get-tuple-element.32.acc_ref), channel_id=1, source_target_pairs={{64,112},{72,120},{80,96},{88,104},{65,113},{73,121},{81,97},{89,1... | collective-permute-start | bytes 73736 | tf_op jit(solution)/shard_map/ppermute | solution.py:391
  70.8 2.9 %collective-permute-start.8 = (f32[32,192]{1,0:T(8,128)S(1)}, f32[32,192]{1,0:T(8,128)S(1)}, u32[]{:S(2)}, u32[]{:S(2)}) collective-permute-start(f32[32,192]{1,0:T(8,128)S(1)} %get-tuple-element.32.acc_ref), channel_id=1, source_target_pairs={{64,120},{72,96},{80,104},{88,112},{65,121},{73,97},{81,105},{89,1... | collective-permute-start | bytes 73736 | tf_op jit(solution)/shard_map/ppermute | solution.py:391
  75.4 7.9 %collective-permute-start.9 = (f32[32,768]{1,0:T(8,128)S(1)}, f32[32,768]{1,0:T(8,128)S(1)}, u32[]{:S(2)}, u32[]{:S(2)}) collective-permute-start(f32[32,768]{1,0:T(8,128)S(1)} %get-tuple-element.36), channel_id=1, source_target_pairs={{96,64},{104,72},{112,80},{120,88},{97,65},{105,73},{113,81},{121,... | collective-permute-start | bytes 294920 | tf_op jit(solution)/shard_map/ppermute | solution.py:391
  76.7 9.7 %collective-permute-start.10 = (f32[32,768]{1,0:T(8,128)S(1)}, f32[32,768]{1,0:T(8,128)S(1)}, u32[]{:S(2)}, u32[]{:S(2)}) collective-permute-start(f32[32,768]{1,0:T(8,128)S(1)} %get-tuple-element.36), channel_id=1, source_target_pairs={{96,72},{104,80},{112,88},{120,64},{97,73},{105,81},{113,89},{121,... | collective-permute-start | bytes 294920 | tf_op jit(solution)/shard_map/ppermute | solution.py:391
  78.0 9.5 %collective-permute-start.11 = (f32[32,768]{1,0:T(8,128)S(1)}, f32[32,768]{1,0:T(8,128)S(1)}, u32[]{:S(2)}, u32[]{:S(2)}) collective-permute-start(f32[32,768]{1,0:T(8,128)S(1)} %get-tuple-element.36), channel_id=1, source_target_pairs={{96,80},{104,88},{112,64},{120,72},{97,81},{105,89},{113,65},{121,... | collective-permute-start | bytes 294920 | tf_op jit(solution)/shard_map/ppermute | solution.py:391
  79.3 8.7 %collective-permute-start.12 = (f32[32,768]{1,0:T(8,128)S(1)}, f32[32,768]{1,0:T(8,128)S(1)}, u32[]{:S(2)}, u32[]{:S(2)}) collective-permute-start(f32[32,768]{1,0:T(8,128)S(1)} %get-tuple-element.36), channel_id=1, source_target_pairs={{96,88},{104,64},{112,72},{120,80},{97,89},{105,65},{113,73},{121,... | collective-permute-start | bytes 294920 | tf_op jit(solution)/shard_map/ppermute | solution.py:391
  89.9 6.5 %collective-permute-start.13 = (f32[32,768]{1,0:T(8,128)S(1)}, f32[32,768]{1,0:T(8,128)S(1)}, u32[]{:S(2)}, u32[]{:S(2)}) collective-permute-start(f32[32,768]{1,0:T(8,128)S(1)} %get-tuple-element.38), channel_id=1, source_target_pairs={{64,32},{72,40},{80,48},{88,56},{65,33},{73,41},{81,49},{89,57},{6... | collective-permute-start | bytes 294920 | tf_op jit(solution)/shard_map/ppermute | solution.py:391
  91.2 5.2 %collective-permute-start.14 = (f32[32,768]{1,0:T(8,128)S(1)}, f32[32,768]{1,0:T(8,128)S(1)}, u32[]{:S(2)}, u32[]{:S(2)}) collective-permute-start(f32[32,768]{1,0:T(8,128)S(1)} %get-tuple-element.38), channel_id=1, source_target_pairs={{64,40},{72,48},{80,56},{88,32},{65,41},{73,49},{81,57},{89,33},{6... | collective-permute-start | bytes 294920 | tf_op jit(solution)/shard_map/ppermute | solution.py:391
  92.5 5.5 %collective-permute-start.15 = (f32[32,768]{1,0:T(8,128)S(1)}, f32[32,768]{1,0:T(8,128)S(1)}, u32[]{:S(2)}, u32[]{:S(2)}) collective-permute-start(f32[32,768]{1,0:T(8,128)S(1)} %get-tuple-element.38), channel_id=1, source_target_pairs={{64,48},{72,56},{80,32},{88,40},{65,49},{73,57},{81,33},{89,41},{6... | collective-permute-start | bytes 294920 | tf_op jit(solution)/shard_map/ppermute | solution.py:391
  93.8 5.3 %collective-permute-start.16 = (f32[32,768]{1,0:T(8,128)S(1)}, f32[32,768]{1,0:T(8,128)S(1)}, u32[]{:S(2)}, u32[]{:S(2)}) collective-permute-start(f32[32,768]{1,0:T(8,128)S(1)} %get-tuple-element.38), channel_id=1, source_target_pairs={{64,56},{72,32},{80,40},{88,48},{65,57},{73,33},{81,41},{89,49},{6... | collective-permute-start | bytes 294920 | tf_op jit(solution)/shard_map/ppermute | solution.py:391
  95.1 5.2 %collective-permute-start.17 = (f32[32,768]{1,0:T(8,128)}, f32[32,768]{1,0:T(8,128)S(1)}, u32[]{:S(2)}, u32[]{:S(2)}) collective-permute-start(f32[32,768]{1,0:T(8,128)} %get-tuple-element.45.x3_two), channel_id=1, source_target_pairs={{64,32},{72,40},{80,48},{88,56},{65,33},{73,41},{81,49},{89,57},{6... | collective-permute-start | bytes 294920 | tf_op jit(solution)/shard_map/ppermute | solution.py:391
  103.1 5.2 %collective-permute-start.22 = (f32[32,768]{1,0:T(8,128)}, f32[32,768]{1,0:T(8,128)}, u32[]{:S(2)}, u32[]{:S(2)}) collective-permute-start(f32[32,768]{1,0:T(8,128)} %get-tuple-element.51.x2_one), channel_id=1, source_target_pairs={{32,0},{40,8},{48,16},{56,24},{33,1},{41,9},{49,17},{57,25},{34,2}... | collective-permute-start | bytes 294920 | tf_op jit(solution)/shard_map/ppermute | solution.py:391
  104.4 4.6 %collective-permute-start.23 = (f32[32,768]{1,0:T(8,128)}, f32[32,768]{1,0:T(8,128)}, u32[]{:S(2)}, u32[]{:S(2)}) collective-permute-start(f32[32,768]{1,0:T(8,128)} %get-tuple-element.45.x3_two), channel_id=1, source_target_pairs={{64,0},{72,8},{80,16},{88,24},{65,1},{73,9},{81,17},{89,25},{66,2}... | collective-permute-start | bytes 294920 | tf_op jit(solution)/shard_map/ppermute | solution.py:391
  106.3 2.7 %collective-permute-start.18 = (f32[32,768]{1,0:T(8,128)}, f32[32,768]{1,0:T(8,128)S(1)}, u32[]{:S(2)}, u32[]{:S(2)}) collective-permute-start(f32[32,768]{1,0:T(8,128)} %copy-done.29), channel_id=1, source_target_pairs={{32,0},{40,8},{48,16},{56,24},{33,1},{41,9},{49,17},{57,25},{34,2}... | collective-permute-start | bytes 294920 | tf_op jit(solution)/shard_map/ppermute | solution.py:391
  107.0 2.1 %collective-permute-start.19 = (f32[32,768]{1,0:T(8,128)}, f32[32,768]{1,0:T(8,128)S(1)}, u32[]{:S(2)}, u32[]{:S(2)}) collective-permute-start(f32[32,768]{1,0:T(8,128)} %copy-done.29), channel_id=1, source_target_pairs={{32,8},{40,16},{48,24},{56,0},{33,9},{41,17},{49,25},{57,1},{34,10... | collective-permute-start | bytes 294920 | tf_op jit(solution)/shard_map/ppermute | solution.py:391
  107.7 1.4 collective-permute-start.20
  108.4 0.7 collective-permute-start.21
  114.2 3.4 %collective-permute-start.24 = (f32[32,768]{1,0:T(8,128)S(1)}, f32[32,768]{1,0:T(8,128)S(1)}, u32[]{:S(2)}, u32[]{:S(2)}) collective-permute-start(f32[32,768]{1,0:T(8,128)S(1)} %get-tuple-element.46), channel_id=1, source_target_pairs={{0,32},{8,40},{16,48},{24,56},{1,33},{9,41},{17,49},{25,57},{2,34}... | collective-permute-start | bytes 294920 | tf_op jit(solution)/shard_map/ppermute | solution.py:391
  114.9 4.0 %collective-permute-start.25 = (f32[32,768]{1,0:T(8,128)S(1)}, f32[32,768]{1,0:T(8,128)S(1)}, u32[]{:S(2)}, u32[]{:S(2)}) collective-permute-start(f32[32,768]{1,0:T(8,128)S(1)} %get-tuple-element.46), channel_id=1, source_target_pairs={{0,40},{8,48},{16,56},{24,32},{1,41},{9,49},{17,57},{25,33},{2,42}... | collective-permute-start | bytes 294920 | tf_op jit(solution)/shard_map/ppermute | solution.py:391
  115.6 3.3 %collective-permute-start.26 = (f32[32,768]{1,0:T(8,128)S(1)}, f32[32,768]{1,0:T(8,128)S(1)}, u32[]{:S(2)}, u32[]{:S(2)}) collective-permute-start(f32[32,768]{1,0:T(8,128)S(1)} %get-tuple-element.46), channel_id=1, source_target_pairs={{0,48},{8,56},{16,32},{24,40},{1,49},{9,57},{17,33},{25,41},{2,50}... | collective-permute-start | bytes 294920 | tf_op jit(solution)/shard_map/ppermute | solution.py:391
  116.2 2.7 %collective-permute-start.27 = (f32[32,768]{1,0:T(8,128)S(1)}, f32[32,768]{1,0:T(8,128)S(1)}, u32[]{:S(2)}, u32[]{:S(2)}) collective-permute-start(f32[32,768]{1,0:T(8,128)S(1)} %get-tuple-element.46), channel_id=1, source_target_pairs={{0,56},{8,32},{16,40},{24,48},{1,57},{9,33},{17,41},{25,49},{2,58}... | collective-permute-start | bytes 294920 | tf_op jit(solution)/shard_map/ppermute | solution.py:391
  116.9 2.0 %collective-permute-start.28 = (f32[32,768]{1,0:T(8,128)S(1)}, f32[32,768]{1,0:T(8,128)S(1)}, u32[]{:S(2)}, u32[]{:S(2)}) collective-permute-start(f32[32,768]{1,0:T(8,128)S(1)} %get-tuple-element.47), channel_id=1, source_target_pairs={{0,32},{8,40},{16,48},{24,56},{1,33},{9,41},{17,49},{25,57},{2,34}... | collective-permute-start | bytes 294920 | tf_op jit(solution)/shard_map/ppermute | solution.py:391
  117.6 17.1 %collective-permute-start.30 = (f32[32,768]{1,0:T(8,128)}, f32[32,768]{1,0:T(8,128)S(1)}, u32[]{:S(2)}, u32[]{:S(2)}) collective-permute-start(f32[32,768]{1,0:T(8,128)} %get-tuple-element.51.x2_one), channel_id=1, source_target_pairs={{32,64},{40,72},{48,80},{56,88},{33,65},{41,73},{49,81},{57,89},{3... | collective-permute-start | bytes 294920 | tf_op jit(solution)/shard_map/ppermute | solution.py:391
  120.0 27.8 %collective-permute-start.29 = (f32[32,768]{1,0:T(8,128)S(1)}, f32[32,768]{1,0:T(8,128)S(1)}, u32[]{:S(2)}, u32[]{:S(2)}) collective-permute-start(f32[32,768]{1,0:T(8,128)S(1)} %get-tuple-element.53.x0_one), channel_id=1, source_target_pairs={{32,64},{40,72},{48,80},{56,88},{33,65},{41,73},{49,81},{57,89},{3... | collective-permute-start | bytes 294920 | tf_op jit(solution)/shard_map/ppermute | solution.py:391
  121.3 45.2 %copy-start.3 = (f32[2304,384]{1,0:T(8,128)S(1)}, f32[2304,384]{1,0:T(8,128)}, u32[]{:S(2)}) copy-start(f32[2304,384]{1,0:T(8,128)} %all-gather.7.cloned.1.call-done) | copy-start | bytes 10616836
  121.3 21.7 %collective-permute-start.31 = (f32[32,192]{1,0:T(8,128)S(1)}, f32[32,192]{1,0:T(8,128)S(1)}, u32[]{:S(2)}, u32[]{:S(2)}) collective-permute-start(f32[32,192]{1,0:T(8,128)S(1)} %get-tuple-element.49.acc_ref), channel_id=1, source_target_pairs={{32,64},{40,72},{48,80},{56,88},{33,65},{41,73},{49,81},{57,89},{3... | collective-permute-start | bytes 73736 | tf_op jit(solution)/shard_map/ppermute | solution.py:391
  122.9 23.0 %collective-permute-start.32 = (f32[32,192]{1,0:T(8,128)S(1)}, f32[32,192]{1,0:T(8,128)S(1)}, u32[]{:S(2)}, u32[]{:S(2)}) collective-permute-start(f32[32,192]{1,0:T(8,128)S(1)} %get-tuple-element.49.acc_ref), channel_id=1, source_target_pairs={{32,72},{40,80},{48,88},{56,64},{33,73},{41,81},{49,89},{57,65},{3... | collective-permute-start | bytes 73736 | tf_op jit(solution)/shard_map/ppermute | solution.py:391
  124.2 23.0 %collective-permute-start.33 = (f32[32,192]{1,0:T(8,128)S(1)}, f32[32,192]{1,0:T(8,128)S(1)}, u32[]{:S(2)}, u32[]{:S(2)}) collective-permute-start(f32[32,192]{1,0:T(8,128)S(1)} %get-tuple-element.49.acc_ref), channel_id=1, source_target_pairs={{32,80},{40,88},{48,64},{56,72},{33,81},{41,89},{49,65},{57,73},{3... | collective-permute-start | bytes 73736 | tf_op jit(solution)/shard_map/ppermute | solution.py:391
  134.7 13.1 %collective-permute-start.34 = (f32[32,192]{1,0:T(8,128)S(1)}, f32[32,192]{1,0:T(8,128)S(1)}, u32[]{:S(2)}, u32[]{:S(2)}) collective-permute-start(f32[32,192]{1,0:T(8,128)S(1)} %get-tuple-element.49.acc_ref), channel_id=1, source_target_pairs={{32,88},{40,64},{48,72},{56,80},{33,89},{41,65},{49,73},{57,81},{3... | collective-permute-start | bytes 73736 | tf_op jit(solution)/shard_map/ppermute | solution.py:391
  150.5 5.2 %collective-permute-start.38 = (f32[32,192]{1,0:T(8,128)}, f32[32,192]{1,0:T(8,128)}, u32[]{:S(2)}, u32[]{:S(2)}) collective-permute-start(f32[32,192]{1,0:T(8,128)} %get-tuple-element.52.acc_ref), channel_id=1, source_target_pairs={{64,104},{72,112},{80,120},{88,96},{65,105},{73,113},{81,121},{89,... | collective-permute-start | bytes 73736 | tf_op jit(solution)/shard_map/ppermute | solution.py:391
  152.4 4.7 %collective-permute-start.37 = (f32[32,768]{1,0:T(8,128)}, f32[32,768]{1,0:T(8,128)S(1)}, u32[]{:S(2)}, u32[]{:S(2)}) collective-permute-start(f32[32,768]{1,0:T(8,128)} %get-tuple-element.45.x3_two), channel_id=1, source_target_pairs={{64,96},{72,104},{80,112},{88,120},{65,97},{73,105},{81,113},{89,1... | collective-permute-start | bytes 294920 | tf_op jit(solution)/shard_map/ppermute | solution.py:391
  153.7 6.7 %collective-permute-start.35 = (f32[32,768]{1,0:T(8,128)}, f32[32,768]{1,0:T(8,128)S(1)}, u32[]{:S(2)}, u32[]{:S(2)}) collective-permute-start(f32[32,768]{1,0:T(8,128)} %copy-done.24), channel_id=1, source_target_pairs={{32,0},{40,8},{48,16},{56,24},{33,1},{41,9},{49,17},{57,25},{34,2}... | collective-permute-start | bytes 294920 | tf_op jit(solution)/shard_map/ppermute | solution.py:391
  154.4 9.1 %collective-permute-start.36 = (f32[32,768]{1,0:T(8,128)}, f32[32,768]{1,0:T(8,128)S(1)}, u32[]{:S(2)}, u32[]{:S(2)}) collective-permute-start(f32[32,768]{1,0:T(8,128)} %copy-done.24), channel_id=1, source_target_pairs={{32,96},{40,104},{48,112},{56,120},{33,97},{41,105},{49,113},{57,1... | collective-permute-start | bytes 294920 | tf_op jit(solution)/shard_map/ppermute | solution.py:391
  155.0 15.1 %collective-permute-start.40 = (f32[2,32,768]{2,1,0:T(8,128)}, f32[2,32,768]{2,1,0:T(8,128)S(1)}, u32[]{:S(2)}, u32[]{:S(2)}) collective-permute-start(f32[2,32,768]{2,1,0:T(8,128)} %copy-done.22), channel_id=1, source_target_pairs={{0,96},{8,104},{16,112},{24,120},{1,97},{9,105},{17,113},{25,121},... | collective-permute-start | bytes 589832 | tf_op jit(solution)/shard_map/ppermute | solution.py:391
  155.7 9.1 %collective-permute-start.39 = (f32[32,768]{1,0:T(8,128)}, f32[32,768]{1,0:T(8,128)S(1)}, u32[]{:S(2)}, u32[]{:S(2)}) collective-permute-start(f32[32,768]{1,0:T(8,128)} %copy-done.20), channel_id=1, source_target_pairs={{32,64},{40,72},{48,80},{56,88},{33,65},{41,73},{49,81},{57,89},{3... | collective-permute-start | bytes 294920 | tf_op jit(solution)/shard_map/ppermute | solution.py:391
  157.1 15.4 %collective-permute-start.42 = (f32[32,192]{1,0:T(8,128)}, f32[32,192]{1,0:T(8,128)S(1)}, u32[]{:S(2)}, u32[]{:S(2)}) collective-permute-start(f32[32,192]{1,0:T(8,128)} %get-tuple-element.52.acc_ref), channel_id=1, source_target_pairs={{64,96},{72,104},{80,112},{88,120},{65,97},{73,105},{81,113},{89,1... | collective-permute-start | bytes 73736 | tf_op jit(solution)/shard_map/ppermute | solution.py:391
  160.4 12.1 %collective-permute-start.43 = (f32[32,192]{1,0:T(8,128)}, f32[32,192]{1,0:T(8,128)S(1)}, u32[]{:S(2)}, u32[]{:S(2)}) collective-permute-start(f32[32,192]{1,0:T(8,128)} %get-tuple-element.52.acc_ref), channel_id=1, source_target_pairs={{64,112},{72,120},{80,96},{88,104},{65,113},{73,121},{81,97},{89,1... | collective-permute-start | bytes 73736 | tf_op jit(solution)/shard_map/ppermute | solution.py:391
  163.5 9.0 %collective-permute-start.44 = (f32[32,192]{1,0:T(8,128)}, f32[32,192]{1,0:T(8,128)S(1)}, u32[]{:S(2)}, u32[]{:S(2)}) collective-permute-start(f32[32,192]{1,0:T(8,128)} %get-tuple-element.52.acc_ref), channel_id=1, source_target_pairs={{64,120},{72,96},{80,104},{88,112},{65,121},{73,97},{81,105},{89,1... | collective-permute-start | bytes 73736 | tf_op jit(solution)/shard_map/ppermute | solution.py:391
  164.8 7.7 %collective-permute-start.41 = (f32[4,32,192]{2,1,0:T(8,128)}, f32[4,32,192]{2,1,0:T(8,128)S(1)}, u32[]{:S(2)}, u32[]{:S(2)}) collective-permute-start(f32[4,32,192]{2,1,0:T(8,128)} %copy-done.28), channel_id=1, source_target_pairs={{64,96},{72,104},{80,112},{88,120},{65,97},{73,105},{81,113},{89,1... | collective-permute-start | bytes 294920 | tf_op jit(solution)/shard_map/ppermute | solution.py:391
  (32 other events, 287.0 us)
Sparse Core Ops, SparseCore 0:
  10.2 31.9 all-gather.4
  44.9 28.2 all-gather.6

commit v5 on v4

--- a/solution.py
+++ b/solution.py
@@ -84,28 +84,26 @@
 
 
 def call(body, out_shape, scalars, inputs, blocks=(), scratch=()):
-    def whole(shape):
-        return pl.BlockSpec(
-            shape, lambda i, place, n=len(shape): (0,) * n, pipeline_mode=pl.Buffered(1)
-        )
-
-    specs = [whole(value.shape) for value in inputs]
+    vmem = pl.BlockSpec(memory_space=pltpu.VMEM)
+    specs = [vmem] * len(inputs)
     for _, at in blocks:
         specs.append(
             pl.BlockSpec((8, 1, PIECE, 2 * SLAB), at, pipeline_mode=pl.Buffered(1))
         )
+    near = [pltpu.with_memory_space_constraint(value, pltpu.VMEM) for value in inputs]
+    far = [pltpu.with_memory_space_constraint(array, pltpu.HBM) for array, _ in blocks]
     return pl.pallas_call(
         body,
         grid_spec=pltpu.PrefetchScalarGridSpec(
             num_scalar_prefetch=1,
             grid=(1,),
             in_specs=specs,
-            out_specs=tuple(whole(shape.shape) for shape in out_shape),
+            out_specs=(vmem,) * len(out_shape),
             scratch_shapes=scratch,
         ),
-        out_shape=tuple(out_shape),
+        out_shape=tuple(pltpu.VMEM(shape.shape, shape.dtype) for shape in out_shape),
         compiler_params=pltpu.CompilerParams(vmem_limit_bytes=VMEM),
-    )(scalars, *inputs, *[array for array, _ in blocks])
+    )(scalars, *near, *far)
 
 
 def turn_first_kernel(place_ref, factor_ref, out_ref, turned_ref):
@@ -204,7 +202,7 @@
     x3_ref,
     weight2_ref,
     weight3_ref,
-    x_ref,
+    both_ref,
     acc_out_ref,
     part_ref,
 ):
@@ -214,7 +212,8 @@
         - complex_dot(x3_ref[...], block_weight(weight3_ref))
         - complex_dot(x, block_weight(weight2_ref))
     )
-    x_ref[...] = x
+    both_ref[0] = x
+    both_ref[1] = x3_ref[...]
     acc_out_ref[...] = acc
     part_ref[...] = complex_dot(acc, inverse_ref[...])
 
@@ -227,26 +226,27 @@
     p1,
     p2,
     p3,
+    later_ref,
     x2_ref,
     x3_ref,
     weight1_ref,
     weight2_ref,
     weight3_ref,
-    x_ref,
+    newest_ref,
     both_ref,
     part_ref,
 ):
     x = add_refs([p0, p1, p2, p3])
     acc = (
         acc_ref[...]
-        - complex_dot(x3_ref[...], block_weight(weight3_ref))
-        - complex_dot(x2_ref[...], block_weight(weight2_ref))
+        - complex_dot(later_ref[1], block_weight(weight3_ref))
+        - complex_dot(later_ref[0], block_weight(weight2_ref))
         - complex_dot(x, block_weight(weight1_ref))
     )
     part_ref[...] = complex_dot(acc, inverse_ref[...])
-    x_ref[...] = x
+    newest_ref[...] = x + x2_ref[0] + x3_ref[...]
     both_ref[0] = x
-    both_ref[1] = x2_ref[...]
+    both_ref[1] = later_ref[0]
 
 
 def coupled(rhs, link_real, link_imag, x):
@@ -272,14 +272,16 @@
 
 
 def couple_kernel(
-    place_ref, rhs_ref, link_ref, p0, p1, p2, p3, x1_ref, weight_ref, x0_ref, out_ref
+    place_ref, rhs_ref, link_ref, p0, p1, p2, p3, own_ref, zero_ref, weight_ref, pass_ref, out_ref
 ):
     x0 = add_refs([p0, p1, p2, p3])
-    x0_ref[...] = x0
-    slab = second_slab(rhs_ref, link_ref, x1_ref[...], place_ref[1])
+    slab = second_slab(rhs_ref, link_ref, own_ref[...], place_ref[1])
     out_ref[...] = slab - complex_dot(
         second_block(rhs_ref, link_ref, x0), block_weight(weight_ref)
     )
+    zero = place_ref[0] == 0
+    pass_ref[0] = jnp.where(zero, zero_ref[0], x0)
+    pass_ref[1] = jnp.where(zero, zero_ref[1], own_ref[...])
 
 
 def second_one_kernel(
@@ -287,8 +289,9 @@
     rhs_ref,
     link_ref,
     acc_ref,
-    x0_ref,
-    x2_ref,
+    own_ref,
+    sent_ref,
+    got_ref,
     f0,
     f1,
     f2,
@@ -298,20 +301,27 @@
     out_ref,
     keep_ref,
 ):
-    q = place_ref[1]
-    slab = second_slab(rhs_ref, link_ref, x2_ref[...], q)
-    product = complex_dot(second_block(rhs_ref, link_ref, x0_ref[...]), block_weight(weight0_ref))
+    plane, q = place_ref[0], place_ref[1]
+    x0 = jnp.where(plane == 1, sent_ref[0], got_ref[0])
+    for s in range(GROUP):
+        keep_ref[GROUP + s] = x0[:, SLAB * s : SLAB * s + SLAB]
+    slab = second_slab(rhs_ref, link_ref, own_ref[...], q)
+    product = complex_dot(second_block(rhs_ref, link_ref, x0), block_weight(weight0_ref))
     slabs = [f0[...], f1[...], f2[...], f3[...]]
     solved = slab - product - slabs_dot(slabs, weight1_ref, q, keep_ref)
-    out_ref[...] = jnp.where(place_ref[0] == 1, acc_ref[...], solved)
+    out_ref[...] = jnp.where(plane == 1, acc_ref[...], solved)
+
+
+def joined(ref, first):
+    return jnp.concatenate([ref[first + s] for s in range(GROUP)], axis=1)
 
 
 def second_base_kernel(
-    place_ref, rhs_ref, link_ref, acc_ref, x0_zero, x0_three, x3_ref, weight_ref, out_ref
+    place_ref, rhs_ref, link_ref, acc_ref, got_ref, own_ref, weight_ref, out_ref
 ):
     plane, q = place_ref[0], place_ref[1]
-    x0 = x0_zero[...] + x0_three[...]
-    own = jnp.where(plane == 0, x0, x3_ref[...])
+    x0 = joined(got_ref, GROUP)
+    own = jnp.where(plane == 0, x0, own_ref[...])
     slab = second_slab(rhs_ref, link_ref, own, q)
     product = complex_dot(second_block(rhs_ref, link_ref, x0), block_weight(weight_ref))
     out_ref[...] = jnp.where(
@@ -320,30 +330,22 @@
 
 
 def cells_kernel(
-    where_ref,
-    x0_one,
-    x0_two,
-    x0_zero,
-    x0_three,
-    both_zero,
-    x1_one,
-    x1_two,
-    both_three,
-    x2_one,
-    x2_two,
-    x3_zero,
-    x3_one,
-    x3_two,
-    x3_three,
-    out_ref,
-    front_ref,
-    rows_ref,
-):
+    where_ref, got_ref, pass_ref, passed_ref, newest_ref, own_ref, both_zero, later_ref, x3_one, out_ref, front_ref, rows_ref
+):
+    plane = where_ref[SLAB]
+
+    def pick(*by_plane):
+        value = by_plane[0]
+        for at in range(1, GROUP):
+            value = jnp.where(plane == at, by_plane[at], value)
+        return value
+
+    last = joined(got_ref, GROUP)
     blocks = (
-        x0_one[...] + x0_two[...] + x0_zero[...] + x0_three[...],
-        both_zero[0] + x1_one[...] + x1_two[...] + both_three[0],
-        both_zero[1] + x2_one[...] + x2_two[...] + both_three[1],
-        x3_zero[...] + x3_one[...] + x3_two[...] + x3_three[...],
+        pick(last, pass_ref[0], passed_ref[0], last),
+        pick(newest_ref[...], own_ref[...], passed_ref[1], passed_ref[0]),
+        pick(both_zero[1], newest_ref[...], own_ref[...], passed_ref[1]),
+        pick(later_ref[1], x3_one[...], newest_ref[...], own_ref[...]),
     )
     for k, x in enumerate(blocks):
         for part in range(6):
@@ -384,19 +386,17 @@
             solution_ref[part, y] = turned[64 + 6 * y : 70 + 6 * y]
 
 
-def plane_send(value, source, target, turn=0):
+def plane_send(value, *moves, turn=0):
     pairs = [
-        (GROUP * source + q, GROUP * target + (q + turn) % GROUP) for q in range(GROUP)
+        (GROUP * source + q, GROUP * target + (q + turn) % GROUP)
+        for source, target in moves
+        for q in range(GROUP)
     ]
     return lax.ppermute(value, "row", pairs)
 
 
 def plane_spread(value, source, target):
-    return [plane_send(value, source, target, d) for d in range(GROUP)]
-
-
-def after(value, arrived):
-    return lax.optimization_barrier((value, arrived))[0]
+    return [plane_send(value, (source, target), turn=d) for d in range(GROUP)]
 
 
 def on_device(source1, source2, coupling, factor1, factor2, diag_inv, front_order):
@@ -459,8 +459,8 @@
     acc, kept = call(
         forward_one_kernel, [slab_shape, sent_shape], place, [acc, *got], first_blocks(1)
     )
+    sent = plane_send(kept, (2, 3))
     got = plane_spread(acc, 2, 3)
-    sent = plane_send(kept, 2, 3)
     acc, part = call(
         forward_two_kernel,
         [slab_shape, block_shape],
@@ -476,13 +476,11 @@
         [acc, inverse, *got],
         first_blocks(3),
     )
+    x3_one = plane_send(x3_two, (2, 1))
     got = plane_spread(part, 2, 1)
-    x3_one = plane_send(x3_two, 2, 1)
-    x3_three = plane_send(after(x3_two, got[1]), 2, 3)
-    x3_zero = plane_send(after(x3_two, got[1]), 2, 0)
-    x2_one, acc, part = call(
+    both_one, acc, part = call(
         back_two_kernel,
-        [block_shape, slab_shape, block_shape],
+        [pair_shape, slab_shape, block_shape],
         place,
         [acc, inverse, *got, x3_one],
         first_blocks(2, 3),
@@ -492,45 +490,40 @@
     def second_blocks(*blocks):
         return [(matrix2, second_factor(block)) for block in blocks]
 
+    later = plane_send(both_one, (1, 0))
     got = plane_spread(part, 1, 0)
-    x2_zero = plane_send(x2_one, 1, 0)
-    x2_two = plane_send(after(x2_one, got[1]), 1, 2)
-    x1_zero, both_zero, part = call(
+    newest, both_zero, part = call(
         back_one_kernel,
         [block_shape, pair_shape, block_shape],
         place,
-        [acc, inverse, *got, x2_zero, x3_zero],
+        [acc, inverse, *got, later, both_one, x3_two],
         first_blocks(1, 2, 3),
     )
+    own = plane_send(newest, (0, 1), (1, 2), (2, 3))
     got = plane_spread(part, 0, 1)
-    x1_one = plane_send(x1_zero, 0, 1)
-    x0_one, acc = call(
+    passing, acc = call(
         couple_kernel,
-        [block_shape, slab_shape],
-        place,
-        [rhs, link, *got, x1_one],
+        [pair_shape, slab_shape],
+        place,
+        [rhs, link, *got, own, both_zero],
         second_blocks(0),
     )
+    passed = plane_send(passing, (1, 2), (0, 3))
     got = plane_spread(acc, 1, 2)
-    x0_two = plane_send(x0_one, 1, 2)
-    x0_zero = plane_send(after(x0_one, got[1]), 1, 0)
-    x0_three = plane_send(after(x0_one, got[1]), 1, 3)
-    both_three = plane_send(after(both_zero, got[1]), 0, 3)
     acc, kept = call(
         second_one_kernel,
-        [slab_shape, sent_shape],
-        place,
-        [rhs, link, acc, x0_two, x2_two, *got],
+        [slab_shape, SDS((2 * GROUP, ROWS, SLAB), f32)],
+        place,
+        [rhs, link, acc, own, passing, passed, *got],
         second_blocks(0, 1),
     )
+    sent = plane_send(kept, (2, 3), (1, 0))
     got = plane_spread(acc, 2, 3)
-    sent = plane_send(kept, 2, 3)
-    x1_two = plane_send(after(x1_one, got[1]), 1, 2)
     (acc,) = call(
         second_base_kernel,
         [slab_shape],
         place,
-        [rhs, link, acc, x0_zero, x0_three, x3_three],
+        [rhs, link, acc, sent, own],
         second_blocks(0),
     )
 
@@ -542,23 +535,8 @@
     (mine,) = call(
         cells_kernel,
         [SDS((8, ROWS, 128), f32)],
-        slots,
-        [
-            x0_one,
-            x0_two,
-            x0_zero,
-            x0_three,
-            both_zero,
-            x1_one,
-            x1_two,
-            both_three,
-            x2_one,
-            x2_two,
-            x3_zero,
-            x3_one,
-            x3_two,
-            x3_three,
-        ],
+        jnp.concatenate([slots, place]),
+        [sent, passing, passed, newest, own, both_zero, later, x3_one],
         scratch=[pltpu.VMEM((4 * BLOCK, 128), f32), pltpu.VMEM((128, 128), f32)],
     )
     (last,) = call(

time: 195 us -> 183 us (0.938)
  starting transfers between devices: 56.3 us -> 44.3 us
  local copies, waits for them, and re-layouts: 15.4 us -> 6.1 us
  Pallas kernels: 26.2 us -> 35.2 us
    ppermute x45 -> x38, starting transfers between devices: 56.2 us -> 44.3 us  [plane_send(): return lax.ppermute(value, 'row', pairs)]
    unnamed x69 -> x12, local copies, waits for them, and re-layouts: 12.6 us -> 3.24 us
    pallas_call x15, Pallas kernels: 26.2 us -> 35.2 us  [call(): pl.pallas_call(body, grid_spec=pltpu.PrefetchScalarGridSpec(num_scalar_pr...]
    ppermute x45 -> x38, waiting for transfers between devices: 39.4 us -> 40.3 us  [plane_send(): return lax.ppermute(value, 'row', pairs)]
  transfers between devices with their start and end apart: 47 -> 40, of which waited for: 17 -> 16; matrix products, arithmetic and copies ran while one was open for 2% -> 2% of each run, Pallas kernels for 8% -> 11%
where the time goes in v5:
time: 183 us; the launch traced here: 182 us
  starting transfers between devices  44.3 us (24%)
  blocking collectives  40.5 us (22%)
  waiting for transfers between devices  40.4 us (22%)
  Pallas kernels  35.2 us (19%)
  between operations  14.6 us (8%)
  local copies, waits for them, and re-layouts  6.1 us (3%)
    ppermute x38, starting transfers between devices, plane_send(): return lax.ppermute(value, 'row', pairs)  44.3 us
    ppermute x38, waiting for transfers between devices, plane_send(): return lax.ppermute(value, 'row', pairs)  40.3 us
    pallas_call x15, Pallas kernels, call(): pl.pallas_call(body, grid_spec=pltpu.PrefetchScalarGridSpec(num_scalar_pr...  35.2 us
    all_to_all x1, blocking collectives, on_device(): cells = lax.all_to_all(packed, 'row', 0, 0).reshape(16 * 104, 128)  19.8 us
    all_to_all x1, blocking collectives, on_device(): packed = lax.all_to_all(packed, 'col', 0, 0)  10.7 us
    all_to_all x1, blocking collectives, on_device(): arrived = lax.all_to_all(last, 'col', 0, 0)  9.95 us
  transfers between devices with their start and end apart: 40, of which 16 were waited for; matrix products, arithmetic and copies ran while one was open for 2% of the time, Pallas kernels for 11%

profile of v5, /device:TPU:4, one launch (start us, length us, event | category | flops | bytes accessed | tf_op | source)
XLA Modules:
  0.0 181.8 jit_solution(8925157489282964486)
XLA Ops:
  8.4 1.7 shard_map.88
  13.2 10.7 %all_to_all.15 = f32[8,16,128]{2,1,0:T(8,128)S(1)} all-to-all(f32[8,16,128]{2,1,0:T(8,128)S(1)} %shard_map.86), channel_id=1, replica_groups=mesh['row'=16,'col'=8] {'col'}, dimensions={0} | all-to-all | bytes 131072 | tf_op jit(solution)/shard_map/all_to_all | solution.py:424
  24.0 19.8 %all_to_all.16 = f32[16,104,128]{2,1,0:T(8,128)S(1)} all-to-all(f32[16,104,128]{2,1,0:T(8,128)S(1)} %broadcast_in_dim.27), channel_id=1, replica_groups=mesh['row'=16,'col'=8] {'row'}, dimensions={0} | all-to-all | bytes 1703936 | tf_op jit(solution)/shard_map/all_to_all | solution.py:426
  45.2 2.9 %shard_map.87 = (f32[64,1024]{1,0:T(8,128)S(1)}, f32[16,1024]{1,0:T(8,128)S(1)}) custom-call(s32[2048]{0:T(1024)S(1)} %bitcast.27, f32[1664,128]{1,0:T(8,128)S(1)} %bitcast.26, f32[2,1024]{1,0:T(2,128)S(1)} %get-tuple-element.56.mark_ref), custom_call_target="tpu_custom_call" | custom-call | tf_op jit(solution)/shard_map/pallas_call | solution.py:95
  48.1 2.3 %shard_map.89.acc_ref = f32[32,192]{1,0:T(8,128)S(1)} custom-call(s32[2]{0:T(128)S(1)} %pad_add_fusion.2.place_ref, f32[64,1024]{1,0:T(8,128)S(1)} %get-tuple-element.25.rhs_ref, f32[8,3,96,384]{3,2,1,0:T(8,128)} %bitcast.28), custom_call_target="tpu_custom_call" | custom-call | tf_op jit(solution)/shard_map/pallas_call | solution.py:95
  50.4 1.4 collective-permute-start.3
  51.8 1.3 collective-permute-start.2
  53.1 1.3 collective-permute-start.1
  54.4 1.3 collective-permute-start
  55.7 1.8 collective-permute-done.3.y3
  57.5 2.8 %collective-permute-done.2.y2 = f32[32,192]{1,0:T(8,128)S(1)} collective-permute-done((f32[32,192]{1,0:T(8,128)S(1)}, f32[32,192]{1,0:T(8,128)S(1)}, u32[]{:S(2)}, u32[]{:S(2)}) %collective-permute-start.2) | collective-permute-done | bytes 24608 | tf_op jit(solution)/shard_map/ppermute | solution.py:395
  61.3 2.3 %shard_map.90 = (f32[32,192]{1,0:T(8,128)S(1)}, f32[4,32,192]{2,1,0:T(8,128)S(1)}) custom-call(s32[2]{0:T(128)S(1)} %pad_add_fusion.2.place_ref, f32[32,192]{1,0:T(8,128)S(1)} %shard_map.89.acc_ref, f32[32,192]{1,0:T(8,128)S(1)} %collective-permute-done.y0, f32[32,192]{1,0:T(8,128)S(1)} %collective-permute-done.1.y1, ...), custom_call_target="tpu_custom_call" | custom-call | tf_op jit(solution)/shard_map/pallas_call | solution.py:95
  64.9 1.3 collective-permute-start.8
  66.2 1.3 collective-permute-start.7
  67.5 1.3 collective-permute-start.6
  68.8 1.3 collective-permute-start.5
  70.4 1.3 collective-permute-done.5.y0
  71.7 3.2 %shard_map.91 = (f32[32,192]{1,0:T(8,128)S(1)}, f32[32,768]{1,0:T(8,128)S(1)}) custom-call(s32[2]{0:T(128)S(1)} %pad_add_fusion.2.place_ref, f32[32,192]{1,0:T(8,128)S(1)} %get-tuple-element.27.acc_ref, f32[192,1536]{1,0:T(8,128)S(1)} %bitcast.22, f32[4,32,192]{2,1,0:T(8,128)S(1)} %collective-permute-done.4.sent_ref, ...), custom_call_target="tpu_custom_call" | custom-call | tf_op jit(solution)/shard_map/pallas_call | solution.py:95
  74.9 1.3 collective-permute-start.12
  76.2 1.3 collective-permute-start.11
  77.5 1.3 collective-permute-start.10
  78.8 1.3 collective-permute-start.9
  80.1 3.2 %collective-permute-done.12.p3 = f32[32,768]{1,0:T(8,128)S(1)} collective-permute-done((f32[32,768]{1,0:T(8,128)S(1)}, f32[32,768]{1,0:T(8,128)S(1)}, u32[]{:S(2)}, u32[]{:S(2)}) %collective-permute-start.12) | collective-permute-done | bytes 98336 | tf_op jit(solution)/shard_map/ppermute | solution.py:395
  83.4 2.7 %collective-permute-done.11.p2 = f32[32,768]{1,0:T(8,128)S(1)} collective-permute-done((f32[32,768]{1,0:T(8,128)S(1)}, f32[32,768]{1,0:T(8,128)S(1)}, u32[]{:S(2)}, u32[]{:S(2)}) %collective-permute-start.11) | collective-permute-done | bytes 98336 | tf_op jit(solution)/shard_map/ppermute | solution.py:395
  87.0 2.6 %shard_map.92 = (f32[32,768]{1,0:T(8,128)S(1)}, f32[32,192]{1,0:T(8,128)S(1)}, f32[32,768]{1,0:T(8,128)S(1)}) custom-call(s32[2]{0:T(128)S(1)} %pad_add_fusion.2.place_ref, f32[32,192]{1,0:T(8,128)S(1)} %get-tuple-element.30.acc_ref, f32[192,1536]{1,0:T(8,128)S(1)} %bitcast.23, f32[32,768]{1,0:T(8,128)S(1)} %collective-permute-done.9.p0, ...), custom_call_target="tpu_custom_call" | custom-call | tf_op jit(solution)/shard_map/pallas_call | solution.py:95
  89.6 1.3 collective-permute-start.17
  90.9 1.3 collective-permute-start.16
  92.2 1.3 collective-permute-start.15
  93.5 1.3 collective-permute-start.14
  94.8 1.3 collective-permute-start.13
  99.3 3.2 %shard_map.93 = (f32[2,32,768]{2,1,0:T(8,128)S(1)}, f32[32,192]{1,0:T(8,128)S(1)}, f32[32,768]{1,0:T(8,128)S(1)}) custom-call(s32[2]{0:T(128)S(1)} %pad_add_fusion.2.place_ref, f32[32,192]{1,0:T(8,128)S(1)} %get-tuple-element.32.acc_ref, f32[192,1536]{1,0:T(8,128)S(1)} %bitcast.24, f32[32,768]{1,0:T(8,128)S(1)} %collective-permute-done.13.p0, ...), custom_call_target="tpu_custom_call" | custom-call | tf_op jit(solution)/shard_map/pallas_call | solution.py:95
  105.9 3.9 %shard_map.94 = (f32[32,768]{1,0:T(8,128)S(1)}, f32[2,32,768]{2,1,0:T(8,128)S(1)}, f32[32,768]{1,0:T(8,128)S(1)}) custom-call(s32[2]{0:T(128)S(1)} %pad_add_fusion.2.place_ref, f32[32,192]{1,0:T(8,128)S(1)} %get-tuple-element.35.acc_ref, f32[192,1536]{1,0:T(8,128)S(1)} %bitcast.25, f32[32,768]{1,0:T(8,128)S(1)} %collective-permute-done.18.p0, ...), custom_call_target="tpu_custom_call" | custom-call | tf_op jit(solution)/shard_map/pallas_call | solution.py:95
  109.8 1.9 %collective-permute-start.27 = (f32[32,768]{1,0:T(8,128)S(1)}, f32[32,768]{1,0:T(8,128)S(1)}, u32[]{:S(2)}, u32[]{:S(2)}) collective-permute-start(f32[32,768]{1,0:T(8,128)S(1)} %get-tuple-element.41.newest_ref), channel_id=1, source_target_pairs={{0,32},{8,40},{16,48},{24,56},{32,64},{40,72},{48,80},{56,88},{64,... | collective-permute-start | bytes 294920 | tf_op jit(solution)/shard_map/ppermute | solution.py:395
  114.5 10.5 %collective-permute-done.27.own_ref = f32[32,768]{1,0:T(8,128)S(1)} collective-permute-done((f32[32,768]{1,0:T(8,128)S(1)}, f32[32,768]{1,0:T(8,128)S(1)}, u32[]{:S(2)}, u32[]{:S(2)}) %collective-permute-start.27) | collective-permute-done | bytes 98336 | tf_op jit(solution)/shard_map/ppermute | solution.py:395
  125.0 2.3 %shard_map.95 = (f32[2,32,768]{2,1,0:T(8,128)S(1)}, f32[32,192]{1,0:T(8,128)S(1)}) custom-call(s32[2]{0:T(128)S(1)} %pad_add_fusion.2.place_ref, f32[64,1024]{1,0:T(8,128)S(1)} %get-tuple-element.25.rhs_ref, f32[16,1024]{1,0:T(8,128)S(1)} %get-tuple-element.26.link_ref, f32[32,768]{1,0:T(8,128)S(1)} %collective-permute-done.23.p0, ...), custom_call_target="tpu_custom_call" | custom-call | tf_op jit(solution)/shard_map/pallas_call | solution.py:95
  128.6 1.3 collective-permute-start.32
  129.9 1.3 collective-permute-start.31
  131.2 1.3 collective-permute-start.30
  132.5 1.3 collective-permute-start.29
  133.8 10.1 %collective-permute-done.32.f3 = f32[32,192]{1,0:T(8,128)S(1)} collective-permute-done((f32[32,192]{1,0:T(8,128)S(1)}, f32[32,192]{1,0:T(8,128)S(1)}, u32[]{:S(2)}, u32[]{:S(2)}) %collective-permute-start.32) | collective-permute-done | bytes 24608 | tf_op jit(solution)/shard_map/ppermute | solution.py:395
  143.8 1.6 collective-permute-done.31.f2
  146.6 2.9 %shard_map.96 = (f32[32,192]{1,0:T(8,128)S(1)}, f32[8,32,192]{2,1,0:T(8,128)S(1)}) custom-call(s32[2]{0:T(128)S(1)} %pad_add_fusion.2.place_ref, f32[64,1024]{1,0:T(8,128)S(1)} %get-tuple-element.25.rhs_ref, f32[16,1024]{1,0:T(8,128)S(1)} %get-tuple-element.26.link_ref, f32[32,192]{1,0:T(8,128)S(1)} %get-tuple-element.44.acc_ref, ...), custom_call_target="tpu_custom_call" | custom-call | tf_op jit(solution)/shard_map/pallas_call | solution.py:95
  149.4 1.3 collective-permute-start.33
  152.4 1.3 collective-permute-start.36
  156.4 2.3 %shard_map.97.acc_ref = f32[32,192]{1,0:T(8,128)S(1)} custom-call(s32[2]{0:T(128)S(1)} %pad_add_fusion.2.place_ref, f32[64,1024]{1,0:T(8,128)S(1)} %get-tuple-element.25.rhs_ref, f32[16,1024]{1,0:T(8,128)S(1)} %get-tuple-element.26.link_ref, f32[32,192]{1,0:T(8,128)S(1)} %get-tuple-element.46.acc_ref, ...), custom_call_target="tpu_custom_call" | custom-call | tf_op jit(solution)/shard_map/pallas_call | solution.py:95
  158.7 1.3 shard_map.98.cells_ref
  160.1 3.0 %shard_map.99 = f32[8,32,256]{2,1,0:T(8,128)S(1)} custom-call(s32[2]{0:T(128)S(1)} %pad_add_fusion.2.place_ref, f32[32,192]{1,0:T(8,128)S(1)} %shard_map.97.acc_ref, f32[8,32,128]{2,1,0:T(8,128)S(1)} %shard_map.98.cells_ref, f32[8,32,192]{2,1,0:T(8,128)S(1)} %collective-permute-done.33.got_ref.sent_ref, f32[32,192]{1,0:T(8,128)S(1)} %collective-permute-done.34.f0, ...), custom_call_target="tpu_custom_call" | custom-call | tf_op jit(solution)/shard_map/pallas_call | solution.py:95
  163.1 9.9 %all_to_all.17.got_ref = f32[8,32,256]{2,1,0:T(8,128)S(1)} all-to-all(f32[8,32,256]{2,1,0:T(8,128)S(1)} %shard_map.99), channel_id=1, replica_groups=mesh['row'=16,'col'=8] {'col'}, dimensions={0} | all-to-all | bytes 524288 | tf_op jit(solution)/shard_map/all_to_all | solution.py:549
  (86 shorter events, 27.3 us)
Async XLA Ops:
  7.2 40.9 %all-gather.5.cloned.1.call-start = ((), (), s32[]{:S(2)}) async-start(), calls=%async_computation.3 | async-start | bytes 3981312 | tf_op jit(solution)/shard_map/all_gather | solution.py:408
  7.3 1.1 copy-start
  8.4 35.4 %copy-start.2 = (f32[2,192,384]{2,1,0:T(8,128)S(1)}, f32[2,192,384]{2,1,0:T(8,128)}, u32[]{:S(2)}) copy-start(f32[2,192,384]{2,1,0:T(8,128)} %param.11) | copy-start | bytes 1769476
  10.1 34.9 %copy-start.3 = (s32[3072]{0:T(1024)S(1)}, s32[3072]{0:T(1024)}, u32[]{:S(2)}) copy-start(s32[3072]{0:T(1024)} %param.13) | copy-start | bytes 36868
  10.1 93.1 %all-gather.7.cloned.1.call-start = ((), (), s32[]{:S(2)}) async-start(), calls=%async_computation.4 | async-start | bytes 3981312 | tf_op jit(solution)/shard_map/all_gather | solution.py:408
  50.4 19.7 %copy-start.1 = (f32[2,768,192]{1,2,0:T(8,128)S(1)}, f32[2,768,192]{1,2,0:T(8,128)}, u32[]{:S(2)}) copy-start(f32[2,768,192]{1,2,0:T(8,128)} %param.12) | copy-start | bytes 3538948
  50.4 7.1 %collective-permute-start.3 = (f32[32,192]{1,0:T(8,128)S(1)}, f32[32,192]{1,0:T(8,128)S(1)}, u32[]{:S(2)}, u32[]{:S(2)}) collective-permute-start(f32[32,192]{1,0:T(8,128)S(1)} %shard_map.89.acc_ref), channel_id=1, source_target_pairs={{32,88},{40,64},{48,72},{56,80},{33,89},{41,65},{49,73},{57,81},{3... | collective-permute-start | bytes 73736 | tf_op jit(solution)/shard_map/ppermute | solution.py:395
  51.8 8.4 %collective-permute-start.2 = (f32[32,192]{1,0:T(8,128)S(1)}, f32[32,192]{1,0:T(8,128)S(1)}, u32[]{:S(2)}, u32[]{:S(2)}) collective-permute-start(f32[32,192]{1,0:T(8,128)S(1)} %shard_map.89.acc_ref), channel_id=1, source_target_pairs={{32,80},{40,88},{48,64},{56,72},{33,81},{41,89},{49,65},{57,73},{3... | collective-permute-start | bytes 73736 | tf_op jit(solution)/shard_map/ppermute | solution.py:395
  53.1 7.9 %collective-permute-start.1 = (f32[32,192]{1,0:T(8,128)S(1)}, f32[32,192]{1,0:T(8,128)S(1)}, u32[]{:S(2)}, u32[]{:S(2)}) collective-permute-start(f32[32,192]{1,0:T(8,128)S(1)} %shard_map.89.acc_ref), channel_id=1, source_target_pairs={{32,72},{40,80},{48,88},{56,64},{33,73},{41,81},{49,89},{57,65},{3... | collective-permute-start | bytes 73736 | tf_op jit(solution)/shard_map/ppermute | solution.py:395
  54.4 6.8 %collective-permute-start = (f32[32,192]{1,0:T(8,128)S(1)}, f32[32,192]{1,0:T(8,128)S(1)}, u32[]{:S(2)}, u32[]{:S(2)}) collective-permute-start(f32[32,192]{1,0:T(8,128)S(1)} %shard_map.89.acc_ref), channel_id=1, source_target_pairs={{32,64},{40,72},{48,80},{56,88},{33,65},{41,73},{49,81},{57,89},{3... | collective-permute-start | bytes 73736 | tf_op jit(solution)/shard_map/ppermute | solution.py:395
  63.6 8.1 %collective-permute-start.4 = (f32[4,32,192]{2,1,0:T(8,128)S(1)}, f32[4,32,192]{2,1,0:T(8,128)S(1)}, u32[]{:S(2)}, u32[]{:S(2)}) collective-permute-start(f32[4,32,192]{2,1,0:T(8,128)S(1)} %get-tuple-element.29), channel_id=1, source_target_pairs={{64,96},{72,104},{80,112},{88,120},{65,97},{73,105},{81,113},{89,1... | collective-permute-start | bytes 294920 | tf_op jit(solution)/shard_map/ppermute | solution.py:395
  64.9 5.3 %collective-permute-start.8 = (f32[32,192]{1,0:T(8,128)S(1)}, f32[32,192]{1,0:T(8,128)S(1)}, u32[]{:S(2)}, u32[]{:S(2)}) collective-permute-start(f32[32,192]{1,0:T(8,128)S(1)} %get-tuple-element.27.acc_ref), channel_id=1, source_target_pairs={{64,120},{72,96},{80,104},{88,112},{65,121},{73,97},{81,105},{89,1... | collective-permute-start | bytes 73736 | tf_op jit(solution)/shard_map/ppermute | solution.py:395
  66.2 4.0 %collective-permute-start.7 = (f32[32,192]{1,0:T(8,128)S(1)}, f32[32,192]{1,0:T(8,128)S(1)}, u32[]{:S(2)}, u32[]{:S(2)}) collective-permute-start(f32[32,192]{1,0:T(8,128)S(1)} %get-tuple-element.27.acc_ref), channel_id=1, source_target_pairs={{64,112},{72,120},{80,96},{88,104},{65,113},{73,121},{81,97},{89,1... | collective-permute-start | bytes 73736 | tf_op jit(solution)/shard_map/ppermute | solution.py:395
  67.5 2.9 %collective-permute-start.6 = (f32[32,192]{1,0:T(8,128)S(1)}, f32[32,192]{1,0:T(8,128)S(1)}, u32[]{:S(2)}, u32[]{:S(2)}) collective-permute-start(f32[32,192]{1,0:T(8,128)S(1)} %get-tuple-element.27.acc_ref), channel_id=1, source_target_pairs={{64,104},{72,112},{80,120},{88,96},{65,105},{73,113},{81,121},{89,... | collective-permute-start | bytes 73736 | tf_op jit(solution)/shard_map/ppermute | solution.py:395
  68.8 2.9 %collective-permute-start.5 = (f32[32,192]{1,0:T(8,128)S(1)}, f32[32,192]{1,0:T(8,128)S(1)}, u32[]{:S(2)}, u32[]{:S(2)}) collective-permute-start(f32[32,192]{1,0:T(8,128)S(1)} %get-tuple-element.27.acc_ref), channel_id=1, source_target_pairs={{64,96},{72,104},{80,112},{88,120},{65,97},{73,105},{81,113},{89,1... | collective-permute-start | bytes 73736 | tf_op jit(solution)/shard_map/ppermute | solution.py:395
  74.9 8.4 %collective-permute-start.12 = (f32[32,768]{1,0:T(8,128)S(1)}, f32[32,768]{1,0:T(8,128)S(1)}, u32[]{:S(2)}, u32[]{:S(2)}) collective-permute-start(f32[32,768]{1,0:T(8,128)S(1)} %get-tuple-element.31), channel_id=1, source_target_pairs={{96,88},{104,64},{112,72},{120,80},{97,89},{105,65},{113,73},{121,... | collective-permute-start | bytes 294920 | tf_op jit(solution)/shard_map/ppermute | solution.py:395
  76.2 9.8 %collective-permute-start.11 = (f32[32,768]{1,0:T(8,128)S(1)}, f32[32,768]{1,0:T(8,128)S(1)}, u32[]{:S(2)}, u32[]{:S(2)}) collective-permute-start(f32[32,768]{1,0:T(8,128)S(1)} %get-tuple-element.31), channel_id=1, source_target_pairs={{96,80},{104,88},{112,64},{120,72},{97,81},{105,89},{113,65},{121,... | collective-permute-start | bytes 294920 | tf_op jit(solution)/shard_map/ppermute | solution.py:395
  77.5 9.5 %collective-permute-start.10 = (f32[32,768]{1,0:T(8,128)S(1)}, f32[32,768]{1,0:T(8,128)S(1)}, u32[]{:S(2)}, u32[]{:S(2)}) collective-permute-start(f32[32,768]{1,0:T(8,128)S(1)} %get-tuple-element.31), channel_id=1, source_target_pairs={{96,72},{104,80},{112,88},{120,64},{97,73},{105,81},{113,89},{121,... | collective-permute-start | bytes 294920 | tf_op jit(solution)/shard_map/ppermute | solution.py:395
  78.8 8.2 %collective-permute-start.9 = (f32[32,768]{1,0:T(8,128)S(1)}, f32[32,768]{1,0:T(8,128)S(1)}, u32[]{:S(2)}, u32[]{:S(2)}) collective-permute-start(f32[32,768]{1,0:T(8,128)S(1)} %get-tuple-element.31), channel_id=1, source_target_pairs={{96,64},{104,72},{112,80},{120,88},{97,65},{105,73},{113,81},{121,... | collective-permute-start | bytes 294920 | tf_op jit(solution)/shard_map/ppermute | solution.py:395
  89.6 6.5 %collective-permute-start.17 = (f32[32,768]{1,0:T(8,128)S(1)}, f32[32,768]{1,0:T(8,128)S(1)}, u32[]{:S(2)}, u32[]{:S(2)}) collective-permute-start(f32[32,768]{1,0:T(8,128)S(1)} %get-tuple-element.34.x3_ref), channel_id=1, source_target_pairs={{64,32},{72,40},{80,48},{88,56},{65,33},{73,41},{81,49},{89,57},{6... | collective-permute-start | bytes 294920 | tf_op jit(solution)/shard_map/ppermute | solution.py:395
  90.9 5.2 %collective-permute-start.16 = (f32[32,768]{1,0:T(8,128)S(1)}, f32[32,768]{1,0:T(8,128)S(1)}, u32[]{:S(2)}, u32[]{:S(2)}) collective-permute-start(f32[32,768]{1,0:T(8,128)S(1)} %get-tuple-element.33), channel_id=1, source_target_pairs={{64,56},{72,32},{80,40},{88,48},{65,57},{73,33},{81,41},{89,49},{6... | collective-permute-start | bytes 294920 | tf_op jit(solution)/shard_map/ppermute | solution.py:395
  92.2 5.0 %collective-permute-start.15 = (f32[32,768]{1,0:T(8,128)S(1)}, f32[32,768]{1,0:T(8,128)S(1)}, u32[]{:S(2)}, u32[]{:S(2)}) collective-permute-start(f32[32,768]{1,0:T(8,128)S(1)} %get-tuple-element.33), channel_id=1, source_target_pairs={{64,48},{72,56},{80,32},{88,40},{65,49},{73,57},{81,33},{89,41},{6... | collective-permute-start | bytes 294920 | tf_op jit(solution)/shard_map/ppermute | solution.py:395
  93.5 4.7 %collective-permute-start.14 = (f32[32,768]{1,0:T(8,128)S(1)}, f32[32,768]{1,0:T(8,128)S(1)}, u32[]{:S(2)}, u32[]{:S(2)}) collective-permute-start(f32[32,768]{1,0:T(8,128)S(1)} %get-tuple-element.33), channel_id=1, source_target_pairs={{64,40},{72,48},{80,56},{88,32},{65,41},{73,49},{81,57},{89,33},{6... | collective-permute-start | bytes 294920 | tf_op jit(solution)/shard_map/ppermute | solution.py:395
  94.8 4.5 %collective-permute-start.13 = (f32[32,768]{1,0:T(8,128)S(1)}, f32[32,768]{1,0:T(8,128)S(1)}, u32[]{:S(2)}, u32[]{:S(2)}) collective-permute-start(f32[32,768]{1,0:T(8,128)S(1)} %get-tuple-element.33), channel_id=1, source_target_pairs={{64,32},{72,40},{80,48},{88,56},{65,33},{73,41},{81,49},{89,57},{6... | collective-permute-start | bytes 294920 | tf_op jit(solution)/shard_map/ppermute | solution.py:395
  102.5 3.4 %collective-permute-start.22 = (f32[2,32,768]{2,1,0:T(8,128)S(1)}, f32[2,32,768]{2,1,0:T(8,128)S(1)}, u32[]{:S(2)}, u32[]{:S(2)}) collective-permute-start(f32[2,32,768]{2,1,0:T(8,128)S(1)} %get-tuple-element.39.x2_ref), channel_id=1, source_target_pairs={{32,0},{40,8},{48,16},{56,24},{33,1},{41,9},{49,17},{57,25},{34,2}... | collective-permute-start | bytes 589832 | tf_op jit(solution)/shard_map/ppermute | solution.py:395
  103.2 2.7 %collective-permute-start.21 = (f32[32,768]{1,0:T(8,128)S(1)}, f32[32,768]{1,0:T(8,128)S(1)}, u32[]{:S(2)}, u32[]{:S(2)}) collective-permute-start(f32[32,768]{1,0:T(8,128)S(1)} %get-tuple-element.38), channel_id=1, source_target_pairs={{32,24},{40,0},{48,8},{56,16},{33,25},{41,1},{49,9},{57,17},{34,26... | collective-permute-start | bytes 294920 | tf_op jit(solution)/shard_map/ppermute | solution.py:395
  103.9 2.0 %collective-permute-start.20 = (f32[32,768]{1,0:T(8,128)S(1)}, f32[32,768]{1,0:T(8,128)S(1)}, u32[]{:S(2)}, u32[]{:S(2)}) collective-permute-start(f32[32,768]{1,0:T(8,128)S(1)} %get-tuple-element.38), channel_id=1, source_target_pairs={{32,16},{40,24},{48,0},{56,8},{33,17},{41,25},{49,1},{57,9},{34,18... | collective-permute-start | bytes 294920 | tf_op jit(solution)/shard_map/ppermute | solution.py:395
  104.5 1.4 collective-permute-start.19
  105.2 0.7 collective-permute-start.18
  109.8 15.1 %collective-permute-start.27 = (f32[32,768]{1,0:T(8,128)S(1)}, f32[32,768]{1,0:T(8,128)S(1)}, u32[]{:S(2)}, u32[]{:S(2)}) collective-permute-start(f32[32,768]{1,0:T(8,128)S(1)} %get-tuple-element.41.newest_ref), channel_id=1, source_target_pairs={{0,32},{8,40},{16,48},{24,56},{32,64},{40,72},{48,80},{56,88},{64,... | collective-permute-start | bytes 294920 | tf_op jit(solution)/shard_map/ppermute | solution.py:395
  111.8 13.2 %collective-permute-start.26 = (f32[32,768]{1,0:T(8,128)S(1)}, f32[32,768]{1,0:T(8,128)S(1)}, u32[]{:S(2)}, u32[]{:S(2)}) collective-permute-start(f32[32,768]{1,0:T(8,128)S(1)} %get-tuple-element.40), channel_id=1, source_target_pairs={{0,56},{8,32},{16,40},{24,48},{1,57},{9,33},{17,41},{25,49},{2,58}... | collective-permute-start | bytes 294920 | tf_op jit(solution)/shard_map/ppermute | solution.py:395
  112.5 12.5 %collective-permute-start.25 = (f32[32,768]{1,0:T(8,128)S(1)}, f32[32,768]{1,0:T(8,128)S(1)}, u32[]{:S(2)}, u32[]{:S(2)}) collective-permute-start(f32[32,768]{1,0:T(8,128)S(1)} %get-tuple-element.40), channel_id=1, source_target_pairs={{0,48},{8,56},{16,32},{24,40},{1,49},{9,57},{17,33},{25,41},{2,50}... | collective-permute-start | bytes 294920 | tf_op jit(solution)/shard_map/ppermute | solution.py:395
  113.1 11.8 %collective-permute-start.24 = (f32[32,768]{1,0:T(8,128)S(1)}, f32[32,768]{1,0:T(8,128)S(1)}, u32[]{:S(2)}, u32[]{:S(2)}) collective-permute-start(f32[32,768]{1,0:T(8,128)S(1)} %get-tuple-element.40), channel_id=1, source_target_pairs={{0,40},{8,48},{16,56},{24,32},{1,41},{9,49},{17,57},{25,33},{2,42}... | collective-permute-start | bytes 294920 | tf_op jit(solution)/shard_map/ppermute | solution.py:395
  113.8 11.1 %collective-permute-start.23 = (f32[32,768]{1,0:T(8,128)S(1)}, f32[32,768]{1,0:T(8,128)S(1)}, u32[]{:S(2)}, u32[]{:S(2)}) collective-permute-start(f32[32,768]{1,0:T(8,128)S(1)} %get-tuple-element.40), channel_id=1, source_target_pairs={{0,32},{8,40},{16,48},{24,56},{1,33},{9,41},{17,49},{25,57},{2,34}... | collective-permute-start | bytes 294920 | tf_op jit(solution)/shard_map/ppermute | solution.py:395
  127.3 19.3 %collective-permute-start.28 = (f32[2,32,768]{2,1,0:T(8,128)S(1)}, f32[2,32,768]{2,1,0:T(8,128)S(1)}, u32[]{:S(2)}, u32[]{:S(2)}) collective-permute-start(f32[2,32,768]{2,1,0:T(8,128)S(1)} %get-tuple-element.45.sent_ref.pass_ref), channel_id=1, source_target_pairs={{32,64},{40,72},{48,80},{56,88},{0,96},{8,104},{16,112},{24,120},{... | collective-permute-start | bytes 589832 | tf_op jit(solution)/shard_map/ppermute | solution.py:395
  128.6 15.3 %collective-permute-start.32 = (f32[32,192]{1,0:T(8,128)S(1)}, f32[32,192]{1,0:T(8,128)S(1)}, u32[]{:S(2)}, u32[]{:S(2)}) collective-permute-start(f32[32,192]{1,0:T(8,128)S(1)} %get-tuple-element.44.acc_ref), channel_id=1, source_target_pairs={{32,88},{40,64},{48,72},{56,80},{33,89},{41,65},{49,73},{57,81},{3... | collective-permute-start | bytes 73736 | tf_op jit(solution)/shard_map/ppermute | solution.py:395
  129.9 15.5 %collective-permute-start.31 = (f32[32,192]{1,0:T(8,128)S(1)}, f32[32,192]{1,0:T(8,128)S(1)}, u32[]{:S(2)}, u32[]{:S(2)}) collective-permute-start(f32[32,192]{1,0:T(8,128)S(1)} %get-tuple-element.44.acc_ref), channel_id=1, source_target_pairs={{32,80},{40,88},{48,64},{56,72},{33,81},{41,89},{49,65},{57,73},{3... | collective-permute-start | bytes 73736 | tf_op jit(solution)/shard_map/ppermute | solution.py:395
  131.2 14.2 %collective-permute-start.30 = (f32[32,192]{1,0:T(8,128)S(1)}, f32[32,192]{1,0:T(8,128)S(1)}, u32[]{:S(2)}, u32[]{:S(2)}) collective-permute-start(f32[32,192]{1,0:T(8,128)S(1)} %get-tuple-element.44.acc_ref), channel_id=1, source_target_pairs={{32,72},{40,80},{48,88},{56,64},{33,73},{41,81},{49,89},{57,65},{3... | collective-permute-start | bytes 73736 | tf_op jit(solution)/shard_map/ppermute | solution.py:395
  132.5 14.1 %collective-permute-start.29 = (f32[32,192]{1,0:T(8,128)S(1)}, f32[32,192]{1,0:T(8,128)S(1)}, u32[]{:S(2)}, u32[]{:S(2)}) collective-permute-start(f32[32,192]{1,0:T(8,128)S(1)} %get-tuple-element.44.acc_ref), channel_id=1, source_target_pairs={{32,64},{40,72},{48,80},{56,88},{33,65},{41,73},{49,81},{57,89},{3... | collective-permute-start | bytes 73736 | tf_op jit(solution)/shard_map/ppermute | solution.py:395
  149.4 7.0 %collective-permute-start.33 = (f32[8,32,192]{2,1,0:T(8,128)S(1)}, f32[8,32,192]{2,1,0:T(8,128)S(1)}, u32[]{:S(2)}, u32[]{:S(2)}) collective-permute-start(f32[8,32,192]{2,1,0:T(8,128)S(1)} %get-tuple-element.47), channel_id=1, source_target_pairs={{64,96},{72,104},{80,112},{88,120},{32,0},{40,8},{48,16},{56,24},{... | collective-permute-start | bytes 589832 | tf_op jit(solution)/shard_map/ppermute | solution.py:395
  151.2 8.9 %collective-permute-start.37 = (f32[32,192]{1,0:T(8,128)S(1)}, f32[32,192]{1,0:T(8,128)S(1)}, u32[]{:S(2)}, u32[]{:S(2)}) collective-permute-start(f32[32,192]{1,0:T(8,128)S(1)} %get-tuple-element.46.acc_ref), channel_id=1, source_target_pairs={{64,120},{72,96},{80,104},{88,112},{65,121},{73,97},{81,105},{89,1... | collective-permute-start | bytes 73736 | tf_op jit(solution)/shard_map/ppermute | solution.py:395
  152.4 7.6 %collective-permute-start.36 = (f32[32,192]{1,0:T(8,128)S(1)}, f32[32,192]{1,0:T(8,128)S(1)}, u32[]{:S(2)}, u32[]{:S(2)}) collective-permute-start(f32[32,192]{1,0:T(8,128)S(1)} %get-tuple-element.46.acc_ref), channel_id=1, source_target_pairs={{64,112},{72,120},{80,96},{88,104},{65,113},{73,121},{81,97},{89,1... | collective-permute-start | bytes 73736 | tf_op jit(solution)/shard_map/ppermute | solution.py:395
  153.7 6.3 %collective-permute-start.35 = (f32[32,192]{1,0:T(8,128)S(1)}, f32[32,192]{1,0:T(8,128)S(1)}, u32[]{:S(2)}, u32[]{:S(2)}) collective-permute-start(f32[32,192]{1,0:T(8,128)S(1)} %get-tuple-element.46.acc_ref), channel_id=1, source_target_pairs={{64,104},{72,112},{80,120},{88,96},{65,105},{73,113},{81,121},{89,... | collective-permute-start | bytes 73736 | tf_op jit(solution)/shard_map/ppermute | solution.py:395
  155.0 5.0 %collective-permute-start.34 = (f32[32,192]{1,0:T(8,128)S(1)}, f32[32,192]{1,0:T(8,128)S(1)}, u32[]{:S(2)}, u32[]{:S(2)}) collective-permute-start(f32[32,192]{1,0:T(8,128)S(1)} %get-tuple-element.46.acc_ref), channel_id=1, source_target_pairs={{64,96},{72,104},{80,112},{88,120},{65,97},{73,105},{81,113},{89,1... | collective-permute-start | bytes 73736 | tf_op jit(solution)/shard_map/ppermute | solution.py:395
Sparse Core Ops, SparseCore 0:
  10.2 31.9 all-gather.4
  45.0 28.2 all-gather.6

commit v6 on v5

v6 whole, which is shorter than its diff:
```python
import functools

import jax
import jax.numpy as jnp
from jax import lax
from jax.experimental import pallas as pl
from jax.experimental.pallas import tpu as pltpu
from jax.sharding import PartitionSpec as P

GROUP = 4
CHUNK = 16
ROWS = 2 * CHUNK
SLAB = 192
BLOCK = 768
PIECE = 96
CELLS = 24
VMEM = 16 * 1024 * 1024

SDS = jax.ShapeDtypeStruct
f32 = jnp.float32


def split(value):
    high = value.astype(jnp.bfloat16)
    return high, (value - high.astype(f32)).astype(jnp.bfloat16)


def complex_dot(vector, weight):
    weight_high, weight_low = weight
    half = weight_high.shape[1] // 2
    high, low = split(vector)
    both = jnp.dot(
        jnp.concatenate([high, low], axis=0), weight_high, preferred_element_type=f32
    )
    total = both[:ROWS] + both[ROWS:] + jnp.dot(high, weight_low, preferred_element_type=f32)
    real = total[:CHUNK, :half] - total[CHUNK:, half:]
    imag = total[:CHUNK, half:] + total[CHUNK:, :half]
    return jnp.concatenate([real, imag], axis=0)


def slot_of(plane, block):
    return jnp.minimum(jnp.where(plane < block, block - 1, block), GROUP - 2)


def block_weight(parts, slot):
    return tuple(ref[slot] for ref in parts)


def slab_weight(parts, slot, source):
    at = pl.multiple_of(SLAB * source, SLAB)
    return tuple(ref[slot, pl.ds(at, SLAB), :] for ref in parts)


def slabs_dot(slabs, parts, slot, q, keep=None):
    total = None
    for d, slab in enumerate(slabs):
        source = lax.rem(q - d + GROUP, GROUP)
        if keep is not None:
            keep[source] = slab
        part = complex_dot(slab, slab_weight(parts, slot, source))
        total = part if total is None else total + part
    return total


def sent_dot(sent_ref, parts, slot):
    total = None
    for s in range(GROUP):
        part = complex_dot(sent_ref[s], slab_weight(parts, slot, s))
        total = part if total is None else total + part
    return total


def add_refs(refs):
    total = refs[0][...]
    for ref in refs[1:]:
        total = total + ref[...]
    return total


def call(body, out_shape, scalars, inputs, blocks=(), scratch=(), steps=1):
    vmem = pl.BlockSpec(memory_space=pltpu.VMEM)
    specs = [vmem] * len(inputs)
    for _, at in blocks:
        specs.append(pl.BlockSpec((8, 1, PIECE, 2 * SLAB), at))
    near = [pltpu.with_memory_space_constraint(value, pltpu.VMEM) for value in inputs]
    far = [pltpu.with_memory_space_constraint(array, pltpu.HBM) for array, _ in blocks]
    return pl.pallas_call(
        body,
        grid_spec=pltpu.PrefetchScalarGridSpec(
            num_scalar_prefetch=1,
            grid=(steps,),
            in_specs=specs,
            out_specs=(vmem,) * len(out_shape),
            scratch_shapes=scratch,
        ),
        out_shape=tuple(pltpu.VMEM(shape.shape, shape.dtype) for shape in out_shape),
        compiler_params=pltpu.CompilerParams(vmem_limit_bytes=VMEM),
    )(scalars, *near, *far)


def turn_first_kernel(place_ref, factor_ref, out_ref, turned_ref):
    rows = factor_ref[...].reshape(2 * SLAB, 4 * PIECE)
    for part in range(3):
        turned_ref[128 * part : 128 * part + 128, :] = rows[:, 128 * part : 128 * part + 128].T
    for slot in range(GROUP - 1):
        block = slot + jnp.where(place_ref[0] > slot, 0, 1)
        out_ref[PIECE * slot : PIECE * slot + PIECE, :] = turned_ref[pl.ds(block * PIECE, PIECE), :]


def pack_kernel(place_ref, first_ref, second_ref, link_ref, out_ref):
    lane = lax.broadcasted_iota(jnp.int32, (6, 128), 1)
    for at_row, ref in ((0, first_ref), (8, second_ref)):
        parts = [ref[part, y] for y in range(4) for part in range(2)]
        for c in range(8):
            row = jnp.zeros((6, 128), f32)
            for at, part in enumerate(parts):
                shift = (16 * at - 16 * c) % 128
                moved = pltpu.roll(part, shift, 1) if shift else part
                row = jnp.where((lane >= 16 * at) & (lane < 16 * at + 16), moved, row)
            out_ref[c, at_row : at_row + 6, :] = row
            out_ref[c, at_row + 6 : at_row + 8, :] = jnp.broadcast_to(link_ref[...], (2, 128))


def gather_rows(where_ref, first, cells_ref, rows_ref):
    def some(step, carry):
        for u in range(16):
            at = step * 16 + u
            rows_ref[pl.ds(at, 1), :] = cells_ref[pl.ds(where_ref[first + at], 1), :]
        return carry

    lax.fori_loop(0, 64, some, 0)


def turn_rows(rows_ref, mark_ref, rhs_ref):
    for part in range(8):
        at = slice(128 * part, 128 * part + 128)
        turned = rows_ref[at, :].T
        quarter = mark_ref[0:1, at]
        value = turned[0:32]
        for y in range(1, 4):
            value = jnp.where(quarter == y, turned[32 * y : 32 * y + 32], value)
        rhs_ref[:, at] = value


def first_front_kernel(where_ref, cells_ref, mark_ref, rhs_ref, rows_ref):
    gather_rows(where_ref, 0, cells_ref, rows_ref)
    turn_rows(rows_ref, mark_ref, rhs_ref)


def second_front_kernel(where_ref, cells_ref, mark_ref, rhs_ref, link_ref, rows_ref):
    gather_rows(where_ref, 0, cells_ref, rows_ref)
    turn_rows(rows_ref, mark_ref, rhs_ref)
    gather_rows(where_ref, 1024, cells_ref, rows_ref)
    lane = lax.broadcasted_iota(jnp.int32, (32, 128), 0).astype(f32)
    for part in range(8):
        at = slice(128 * part, 128 * part + 128)
        turned = rows_ref[at, :].T
        own = mark_ref[1:2, at] == lane
        real = jnp.sum(jnp.where(own, turned[0:32], 0.0), axis=0, keepdims=True)
        imag = jnp.sum(jnp.where(own, turned[32:64], 0.0), axis=0, keepdims=True)
        link_ref[0:8, at] = jnp.broadcast_to(real, (8, 128))
        link_ref[8:16, at] = jnp.broadcast_to(imag, (8, 128))


def split_kernel(place_ref, weight_ref, high_ref, low_ref):
    slot = pl.program_id(0)
    high, low = split(weight_ref[:, 0].reshape(BLOCK, 2 * SLAB))
    high_ref[slot] = high
    low_ref[slot] = low


def split_inverse_kernel(place_ref, weight_ref, high_ref, low_ref):
    high_ref[...], low_ref[...] = split(weight_ref[...])


def start_kernel(place_ref, rhs_ref, weight_ref, acc_ref):
    weight = split(weight_ref[:, 0].reshape(BLOCK, 2 * SLAB))
    product = complex_dot(rhs_ref[:, 0:BLOCK], weight)
    slab = rhs_ref[:, BLOCK : BLOCK + SLAB]
    acc_ref[...] = jnp.where(place_ref[0] > 0, slab - product, slab)


def forward_one_kernel(place_ref, acc_ref, y0, y1, y2, y3, high, low, out_ref, keep_ref):
    plane, q = place_ref[0], place_ref[1]
    slabs = [y0[...], y1[...], y2[...], y3[...]]
    out_ref[...] = acc_ref[...] - slabs_dot(slabs, (high, low), slot_of(plane, 1), q, keep_ref)


def forward_two_kernel(
    place_ref, acc_ref, inverse_high, inverse_low, sent_ref, y0, y1, y2, y3, high, low, out_ref, part_ref
):
    plane, q = place_ref[0], place_ref[1]
    slabs = [y0[...], y1[...], y2[...], y3[...]]
    solved = (
        acc_ref[...]
        - sent_dot(sent_ref, (high, low), slot_of(plane, 1))
        - slabs_dot(slabs, (high, low), slot_of(plane, 2), q)
    )
    out_ref[...] = solved
    part_ref[...] = complex_dot(solved, (inverse_high[...], inverse_low[...]))


def back_three_kernel(
    place_ref,
    acc_ref,
    inverse_high,
    inverse_low,
    p0,
    p1,
    p2,
    p3,
    high,
    low,
    x_ref,
    acc_out_ref,
    part_ref,
):
    x = add_refs([p0, p1, p2, p3])
    weight = block_weight((high, low), slot_of(place_ref[0], 3))
    acc = acc_ref[...] - complex_dot(x, weight)
    x_ref[...] = x
    acc_out_ref[...] = acc
    part_ref[...] = complex_dot(acc, (inverse_high[...], inverse_low[...]))


def back_two_kernel(
    place_ref,
    acc_ref,
    inverse_high,
    inverse_low,
    p0,
    p1,
    p2,
    p3,
    x3_ref,
    high,
    low,
    both_ref,
    acc_out_ref,
    part_ref,
):
    plane = place_ref[0]
    x = add_refs([p0, p1, p2, p3])
    acc = (
        acc_ref[...]
        - complex_dot(x3_ref[...], block_weight((high, low), slot_of(plane, 3)))
        - complex_dot(x, block_weight((high, low), slot_of(plane, 2)))
    )
    both_ref[0] = x
    both_ref[1] = x3_ref[...]
    acc_out_ref[...] = acc
    part_ref[...] = complex_dot(acc, (inverse_high[...], inverse_low[...]))


def back_one_kernel(
    place_ref,
    acc_ref,
    inverse_high,
    inverse_low,
    p0,
    p1,
    p2,
    p3,
    later_ref,
    x2_ref,
    x3_ref,
    high,
    low,
    newest_ref,
    both_ref,
    part_ref,
):
    plane = place_ref[0]
    x = add_refs([p0, p1, p2, p3])
    acc = (
        acc_ref[...]
        - complex_dot(later_ref[1], block_weight((high, low), slot_of(plane, 3)))
        - complex_dot(later_ref[0], block_weight((high, low), slot_of(plane, 2)))
        - complex_dot(x, block_weight((high, low), slot_of(plane, 1)))
    )
    part_ref[...] = complex_dot(acc, (inverse_high[...], inverse_low[...]))
    newest_ref[...] = x + x2_ref[0] + x3_ref[...]
    both_ref[0] = x
    both_ref[1] = later_ref[0]


def coupled(rhs, link_real, link_imag, x):
    real = rhs[:CHUNK] - (link_real * x[:CHUNK] - link_imag * x[CHUNK:])
    imag = rhs[CHUNK:] - (link_real * x[CHUNK:] + link_imag * x[:CHUNK])
    return jnp.concatenate([real, imag], axis=0)


def second_block(rhs_ref, link_ref, x):
    return coupled(
        rhs_ref[:, 0:BLOCK], link_ref[0:1, 0:BLOCK], link_ref[8:9, 0:BLOCK], x
    )


def second_slab(rhs_ref, link_ref, x, q):
    own = x[:, 0:SLAB]
    for s in range(1, GROUP):
        own = jnp.where(q == s, x[:, SLAB * s : SLAB * s + SLAB], own)
    end = BLOCK + SLAB
    return coupled(
        rhs_ref[:, BLOCK:end], link_ref[0:1, BLOCK:end], link_ref[8:9, BLOCK:end], own
    )


def couple_kernel(
    place_ref, rhs_ref, link_ref, p0, p1, p2, p3, own_ref, zero_ref, high, low, pass_ref, out_ref
):
    x0 = add_refs([p0, p1, p2, p3])
    slab = second_slab(rhs_ref, link_ref, own_ref[...], place_ref[1])
    out_ref[...] = slab - complex_dot(
        second_block(rhs_ref, link_ref, x0), block_weight((high, low), 0)
    )
    zero = place_ref[0] == 0
    pass_ref[0] = jnp.where(zero, zero_ref[0], x0)
    pass_ref[1] = jnp.where(zero, zero_ref[1], own_ref[...])


def second_one_kernel(
    place_ref,
    rhs_ref,
    link_ref,
    acc_ref,
    own_ref,
    sent_ref,
    got_ref,
    f0,
    f1,
    f2,
    f3,
    high,
    low,
    out_ref,
    keep_ref,
):
    plane, q = place_ref[0], place_ref[1]
    x0 = jnp.where(plane == 1, sent_ref[0], got_ref[0])
    for s in range(GROUP):
        keep_ref[GROUP + s] = x0[:, SLAB * s : SLAB * s + SLAB]
    slab = second_slab(rhs_ref, link_ref, own_ref[...], q)
    product = complex_dot(second_block(rhs_ref, link_ref, x0), block_weight((high, low), 0))
    slabs = [f0[...], f1[...], f2[...], f3[...]]
    solved = slab - product - slabs_dot(slabs, (high, low), 1, q, keep_ref)
    out_ref[...] = jnp.where(plane == 1, acc_ref[...], solved)


def joined(ref, first):
    return jnp.concatenate([ref[first + s] for s in range(GROUP)], axis=1)


def second_base_kernel(
    place_ref, rhs_ref, link_ref, acc_ref, got_ref, own_ref, high, low, out_ref
):
    plane, q = place_ref[0], place_ref[1]
    x0 = joined(got_ref, GROUP)
    own = jnp.where(plane == 0, x0, own_ref[...])
    slab = second_slab(rhs_ref, link_ref, own, q)
    product = complex_dot(second_block(rhs_ref, link_ref, x0), block_weight((high, low), 0))
    out_ref[...] = jnp.where(
        plane == 0, slab, jnp.where(plane == 3, slab - product, acc_ref[...])
    )


def cells_kernel(
    where_ref, got_ref, pass_ref, passed_ref, newest_ref, own_ref, both_zero, later_ref, x3_one, out_ref, front_ref, rows_ref
):
    plane = where_ref[SLAB]

    def pick(*by_plane):
        value = by_plane[0]
        for at in range(1, GROUP):
            value = jnp.where(plane == at, by_plane[at], value)
        return value

    last = joined(got_ref, GROUP)
    blocks = (
        pick(last, pass_ref[0], passed_ref[0], last),
        pick(newest_ref[...], own_ref[...], passed_ref[1], passed_ref[0]),
        pick(both_zero[1], newest_ref[...], own_ref[...], passed_ref[1]),
        pick(later_ref[1], x3_one[...], newest_ref[...], own_ref[...]),
    )
    for k, x in enumerate(blocks):
        for part in range(6):
            at = BLOCK * k + 128 * part
            piece = x[:, 128 * part : 128 * part + 128]
            wide = jnp.concatenate([piece, jnp.zeros((128 - ROWS, 128), f32)], axis=0)
            front_ref[at : at + 128, :] = wide.T
    rows_ref[...] = jnp.zeros_like(rows_ref)
    for c in range(8):
        for u in range(CELLS):
            rows_ref[64 + u : 65 + u, :] = front_ref[pl.ds(where_ref[CELLS * c + u], 1), :]
        out_ref[c] = rows_ref[...].T[:ROWS]


def second_two_kernel(
    place_ref, acc_ref, cells_ref, sent_ref, f0, f1, f2, f3, high, low, out_ref
):
    slabs = [f0[...], f1[...], f2[...], f3[...]]
    solved = (
        acc_ref[...]
        - sent_dot(sent_ref, (high, low), 1)
        - slabs_dot(slabs, (high, low), 2, place_ref[1])
    )
    lane = lax.broadcasted_iota(jnp.int32, (ROWS, 128), 1)
    tail = jnp.concatenate([solved[:, 128:], jnp.zeros((ROWS, 64), f32)], axis=1)
    for c in range(8):
        out_ref[c, :, 0:128] = solved[:, 0:128]
        out_ref[c, :, 128:256] = jnp.where(lane < 64, tail, cells_ref[c])


def out_kernel(place_ref, got_ref, solution_ref, forward_ref):
    for part in range(2):
        wide = got_ref[:, CHUNK * part : CHUNK * part + CHUNK, :].reshape(128, 256)
        forward_ref[part, 0:128, :] = wide[:, 0:128].T
        turned = wide[:, 128:256].T
        forward_ref[part, 128:SLAB, :] = turned[0:64]
        for y in range(4):
            solution_ref[part, y] = turned[64 + 6 * y : 70 + 6 * y]


def plane_send(value, *moves, turn=0):
    pairs = [
        (GROUP * source + q, GROUP * target + (q + turn) % GROUP)
        for source, target in moves
        for q in range(GROUP)
    ]
    return lax.ppermute(value, "row", pairs)


def plane_spread(value, source, target):
    return [plane_send(value, (source, target), turn=d) for d in range(GROUP)]


def after(value, arrived):
    return lax.optimization_barrier((value, arrived))[0]


def on_device(source1, source2, coupling, factor1, factor2, diag_inv, front_order):
    row_id = lax.axis_index("row")
    col_id = lax.axis_index("col")
    place = jnp.stack([row_id // GROUP, row_id % GROUP]).astype(jnp.int32)

    def gather_blocks(turned):
        return lax.all_gather(turned, "col").reshape(8, GROUP - 1, PIECE, 2 * SLAB)

    (turned1,) = call(
        turn_first_kernel,
        [SDS((3 * PIECE, 2 * SLAB), f32)],
        place,
        [factor1],
        scratch=[pltpu.VMEM((4 * PIECE, 2 * SLAB), f32)],
    )
    matrix1 = gather_blocks(turned1)

    links = jnp.pad(coupling.reshape(2, CELLS), ((0, 0), (0, 32 - CELLS))).reshape(1, 64)
    links = jnp.pad(links, ((0, 0), (0, 64)))
    (packed,) = call(
        pack_kernel, [SDS((8, 16, 128), f32)], place, [source1, source2, links]
    )
    packed = lax.all_to_all(packed, "col", 0, 0)
    early = jnp.broadcast_to(packed[:, :8].reshape(1, 64, 128), (16, 64, 128))
    early = lax.all_to_all(early, "row", 0, 0).reshape(1024, 128)
    late = packed[:, 8:].reshape(64, 128)

    cell_y = front_order // 48
    cell_x = front_order % 48
    group_of = (cell_y // 4) * 64 + (cell_x // 6) * 8
    quarter = cell_y % 4
    inner = quarter * 6 + cell_x % 6
    every = jnp.stack([group_of + cell_x % 6, group_of + 6, quarter, inner])
    own = lax.dynamic_slice_in_dim(every, row_id * SLAB, SLAB, 1)
    every = jnp.concatenate([every[:, :BLOCK], own, jnp.zeros((4, 64), jnp.int32)], axis=1)
    where, mark = every[:2].reshape(2048), every[2:].astype(f32)
    rows_shape = SDS((ROWS, 1024), f32)
    rows_scratch = [pltpu.VMEM((1024, 128), f32)]
    (rhs,) = call(first_front_kernel, [rows_shape], where, [early, mark], scratch=rows_scratch)

    slab_shape = SDS((ROWS, SLAB), f32)
    block_shape = SDS((ROWS, BLOCK), f32)
    pair_shape = SDS((2, ROWS, BLOCK), f32)
    sent_shape = SDS((GROUP, ROWS, SLAB), f32)

    def split_factor(matrix):
        shape = SDS((GROUP - 1, BLOCK, 2 * SLAB), jnp.bfloat16)
        blocks = [(matrix, lambda i, place: (0, i, 0, 0))]
        return call(split_kernel, [shape, shape], place, [], blocks, steps=GROUP - 1)

    first = [(matrix1, lambda i, place: (0, slot_of(place[0], 0), 0, 0))]
    (acc,) = call(start_kernel, [slab_shape], place, [rhs], first)
    got = plane_spread(acc, 1, 2)
    matrix1, diag_inv = after((matrix1, diag_inv), acc)
    parts1 = split_factor(matrix1)
    inverse = diag_inv.reshape(2 * BLOCK, SLAB).T
    shape = SDS((SLAB, 2 * BLOCK), jnp.bfloat16)
    inverse = call(split_inverse_kernel, [shape, shape], place, [inverse])
    acc, kept = call(
        forward_one_kernel, [slab_shape, sent_shape], place, [acc, *got, *parts1]
    )
    late, factor2 = after((late, factor2), acc)
    late = jnp.broadcast_to(late[None], (16, 64, 128))
    late = lax.all_to_all(late, "row", 0, 0).reshape(1024, 128)
    turned2 = factor2[:, :, : 3 * PIECE].reshape(2 * SLAB, 3 * PIECE).T
    matrix2 = gather_blocks(turned2)

    sent = plane_send(kept, (2, 3))
    got = plane_spread(acc, 2, 3)
    acc, part = call(
        forward_two_kernel,
        [slab_shape, block_shape],
        place,
        [acc, *inverse, sent, *got, *parts1],
    )
    got = plane_spread(part, 3, 2)
    x3_two, acc, part = call(
        back_three_kernel,
        [block_shape, slab_shape, block_shape],
        place,
        [acc, *inverse, *got, *parts1],
    )
    x3_one = plane_send(x3_two, (2, 1))
    got = plane_spread(part, 2, 1)
    both_one, acc, part = call(
        back_two_kernel,
        [pair_shape, slab_shape, block_shape],
        place,
        [acc, *inverse, *got, x3_one, *parts1],
    )
    later = plane_send(both_one, (1, 0))
    got = plane_spread(part, 1, 0)
    late = after(late, part)
    rhs, link = call(
        second_front_kernel,
        [rows_shape, SDS((16, 1024), f32)],
        where,
        [late, mark],
        scratch=rows_scratch,
    )
    newest, both_zero, part = call(
        back_one_kernel,
        [block_shape, pair_shape, block_shape],
        place,
        [acc, *inverse, *got, later, both_one, x3_two, *parts1],
    )
    own = plane_send(newest, (0, 1), (1, 2), (2, 3))
    got = plane_spread(part, 0, 1)
    parts2 = split_factor(after(matrix2, part))
    passing, acc = call(
        couple_kernel,
        [pair_shape, slab_shape],
        place,
        [rhs, link, *got, own, both_zero, *parts2],
    )
    passed = plane_send(passing, (1, 2), (0, 3))
    got = plane_spread(acc, 1, 2)
    acc, kept = call(
        second_one_kernel,
        [slab_shape, SDS((2 * GROUP, ROWS, SLAB), f32)],
        place,
        [rhs, link, acc, own, passing, passed, *got, *parts2],
    )
    sent = plane_send(kept, (2, 3), (1, 0))
    got = plane_spread(acc, 2, 3)
    (acc,) = call(
        second_base_kernel,
        [slab_shape],
        place,
        [rhs, link, acc, sent, own, *parts2],
    )

    at = jnp.arange(SLAB, dtype=jnp.int32)
    own_c, own_y, own_x = at // CELLS, at % CELLS // 6, at % 6
    own_cells = (row_id * 4 + own_y) * 48 + own_c * 6 + own_x
    hits = front_order[None, :] == own_cells[:, None]
    slots = jnp.sum(jnp.where(hits, jnp.arange(4 * BLOCK, dtype=jnp.int32)[None, :], 0), axis=1)
    (mine,) = call(
        cells_kernel,
        [SDS((8, ROWS, 128), f32)],
        jnp.concatenate([slots, place]),
        [sent, passing, passed, newest, own, both_zero, later, x3_one],
        scratch=[pltpu.VMEM((4 * BLOCK, 128), f32), pltpu.VMEM((128, 128), f32)],
    )
    (last,) = call(
        second_two_kernel,
        [SDS((8, ROWS, 256), f32)],
        place,
        [acc, mine, sent, *got, *parts2],
    )
    arrived = lax.all_to_all(last, "col", 0, 0)
    return call(
        out_kernel,
        [SDS((2, 4, 6, 128), f32), SDS((2, SLAB, 128), f32)],
        place,
        [arrived],
    )


def solution(mesh):
    in_specs = (
        P(None, "row", "col", None),
        P(None, "row", "col", None),
        P(None, "row", "col"),
        P(None, "row", "col"),
        P(None, "row", "col"),
        P(None, None, "row"),
        P(),
    )
    out_specs = (P(None, "row", "col", None), P(None, "row", None))
    return jax.shard_map(
        on_device, mesh=mesh, in_specs=in_specs, out_specs=out_specs, check_vma=False
    )
```

time: 183 us -> 201 us (1.098)
  starting transfers between devices: 44.3 us -> 79.1 us
  blocking collectives: 40.5 us -> 10 us
  local copies, waits for them, and re-layouts: 6.1 us -> 21.2 us
  waiting for transfers between devices: 40.4 us -> 32.5 us
  Pallas kernels: 35.2 us -> 40.2 us
    all_to_all x2 -> x0, blocking collectives: 30.5 us -> none  [the longest x1 19.8 us: on_device(): cells = lax.all_to_all(packed, 'row', 0, 0).reshape(16 * 104, 128)]
    all_to_all x0 -> x3, starting transfers between devices: none -> 24.2 us  [the longest x1 11.4 us: on_device(): late = lax.all_to_all(late, 'row', 0, 0).reshape(1024, 128)]
    ppermute x38, waiting for transfers between devices: 40.3 us -> 18.9 us  [plane_send(): return lax.ppermute(value, 'row', pairs)]
    all_to_all x0 -> x3, waiting for transfers between devices: none -> 13.6 us  [the longest x1 8.77 us: on_device(): early = lax.all_to_all(early, 'row', 0, 0).reshape(1024, 128)]
    ppermute x38, starting transfers between devices: 44.3 us -> 54.8 us  [plane_send(): return lax.ppermute(value, 'row', pairs)]
    unnamed x12 -> x62, local copies, waits for them, and re-layouts: 3.24 us -> 13.8 us
    pallas_call x15 -> x19, Pallas kernels: 35.2 us -> 40.2 us  [call(): pl.pallas_call(body, grid_spec=pltpu.PrefetchScalarGridSpec(num_scalar_pr...]
    broadcast_in_dim x2 -> x3, local copies, waits for them, and re-layouts: 0.06 us -> 2.31 us  [the longest x2 1.45 us: on_device(): early = jnp.broadcast_to(packed[:, :8].reshape(1, 64, 128), (16, 64, 128))]
  transfers between devices with their start and end apart: 40 -> 43, of which waited for: 16 -> 12; matrix products, arithmetic and copies ran while one was open for 2% -> 4% of each run, Pallas kernels for 11% -> 14%
where the time goes in v6:
time: 201 us; the launch traced here: 199 us
  starting transfers between devices  79.1 us (39%)
  Pallas kernels  40.2 us (20%)
  waiting for transfers between devices  32.5 us (16%)
  local copies, waits for them, and re-layouts  21.2 us (11%)
  between operations  14.8 us (7%)
  blocking collectives  10 us (5%)
    ppermute x38, starting transfers between devices, plane_send(): return lax.ppermute(value, 'row', pairs)  54.8 us
    pallas_call x19, Pallas kernels, call(): pl.pallas_call(body, grid_spec=pltpu.PrefetchScalarGridSpec(num_scalar_pr...  40.2 us
    ppermute x38, waiting for transfers between devices, plane_send(): return lax.ppermute(value, 'row', pairs)  18.9 us
    unnamed x62, local copies, waits for them, and re-layouts  13.8 us
    all_to_all x1, starting transfers between devices, on_device(): late = lax.all_to_all(late, 'row', 0, 0).reshape(1024, 128)  11.4 us
    all_to_all x1, blocking collectives, on_device(): arrived = lax.all_to_all(last, 'col', 0, 0)  10 us
    all_to_all x1, waiting for transfers between devices, on_device(): early = lax.all_to_all(early, 'row', 0, 0).reshape(1024, 128)  8.77 us
    all_to_all x1, starting transfers between devices, on_device(): early = lax.all_to_all(early, 'row', 0, 0).reshape(1024, 128)  7.45 us
  transfers between devices with their start and end apart: 43, of which 12 were waited for; matrix products, arithmetic and copies ran while one was open for 4% of the time, Pallas kernels for 14%

profile of v6, /device:TPU:4, one launch (start us, length us, event | category | flops | bytes accessed | tf_op | source)
XLA Modules:
  0.0 199.3 jit_solution(18129349900927692041)
XLA Ops:
  8.4 1.7 shard_map.88
  12.4 1.4 shard_map.86
  13.8 5.3 %all-to-all-start = ((f32[8,16,128]{2,1,0:T(8,128)}), f32[8,16,128]{2,1,0:T(8,128)S(1)}, u32[]{:S(2)}, u32[]{:S(2)}) async-start(f32[8,16,128]{2,1,0:T(8,128)} %shard_map.86), calls=%async_computation | async-start | bytes 131072 | tf_op jit(solution)/shard_map/all_to_all | solution.py:463
  19.9 4.8 %all-to-all-done = f32[8,16,128]{2,1,0:T(8,128)S(1)} async-done(((f32[8,16,128]{2,1,0:T(8,128)}), f32[8,16,128]{2,1,0:T(8,128)S(1)}, u32[]{:S(2)}, u32[]{:S(2)}) %all-to-all-start) | async-done | bytes 65568 | tf_op jit(solution)/shard_map/all_to_all | solution.py:463
  26.2 7.5 %all-to-all-start.1 = ((f32[16,64,128]{2,1,0:T(8,128)}), f32[16,64,128]{2,1,0:T(8,128)S(1)}, u32[]{:S(2)}, u32[]{:S(2)}) async-start(f32[16,64,128]{2,1,0:T(8,128)} %broadcast_in_dim.33), calls=%async_computation.1 | async-start | bytes 1048576 | tf_op jit(solution)/shard_map/all_to_all | solution.py:465
  33.9 8.8 %all-to-all-done.1 = f32[16,64,128]{2,1,0:T(8,128)S(1)} async-done(((f32[16,64,128]{2,1,0:T(8,128)}), f32[16,64,128]{2,1,0:T(8,128)S(1)}, u32[]{:S(2)}, u32[]{:S(2)}) %all-to-all-start.1) | async-done | bytes 524320 | tf_op jit(solution)/shard_map/all_to_all | solution.py:465
  42.6 1.9 shard_map.87.rhs_ref
  44.6 2.3 %shard_map.89.acc_ref = f32[32,192]{1,0:T(8,128)S(1)} custom-call(s32[2]{0:T(128)S(1)} %pad_add_fusion.2.place_ref, f32[32,1024]{1,0:T(8,128)S(1)} %shard_map.87.rhs_ref, f32[8,3,96,384]{3,2,1,0:T(8,128)} %bitcast.30), custom_call_target="tpu_custom_call" | custom-call | tf_op jit(solution)/shard_map/pallas_call | solution.py:87
  46.9 1.3 collective-permute-start
  48.2 1.3 collective-permute-start.1
  49.5 1.3 collective-permute-start.2
  50.8 1.3 collective-permute-start.3
  52.1 3.5 %shard_map.90 = (bf16[3,768,384]{2,1,0:T(8,128)(2,1)S(1)}, bf16[3,768,384]{2,1,0:T(8,128)(2,1)S(1)}) custom-call(s32[2]{0:T(128)S(1)} %pad_add_fusion.2.place_ref, f32[8,3,96,384]{3,2,1,0:T(8,128)} %bitcast.31), custom_call_target="tpu_custom_call" | custom-call | tf_op jit(solution)/shard_map/pallas_call | solution.py:87
  56.1 1.6 collective-permute-done.2.y2
  60.0 2.0 %copy.17 = f32[384,288]{0,1:T(8,128)} copy(f32[384,288]{1,0:T(8,128)} %bitcast.35) | data formatting | bytes 884736 | tf_op jit(solution)/shard_map/reshape | solution.py:505
  62.1 1.3 collective-permute-start.4
  68.6 1.4 copy.19
  70.9 2.3 %shard_map.93 = (f32[32,192]{1,0:T(8,128)S(1)}, f32[32,768]{1,0:T(8,128)}) custom-call(s32[2]{0:T(128)S(1)} %pad_add_fusion.2.place_ref, f32[32,192]{1,0:T(8,128)S(1)} %copy-done.25, bf16[192,1536]{1,0:T(8,128)(2,1)S(1)} %get-tuple-element.39.inverse_high, bf16[192,1536]{1,0:T(8,128)(2,1)S(1)} %get-tuple-element.40.inverse_low, ...), custom_call_target="tpu_custom_call" | custom-call | tf_op jit(solution)/shard_map/pallas_call | solution.py:87
  75.0 1.3 collective-permute-start.11
  79.8 11.4 %all-to-all-start.2 = ((f32[16,64,128]{2,1,0:T(8,128)}), f32[16,64,128]{2,1,0:T(8,128)}, u32[]{:S(2)}, u32[]{:S(2)}) async-start(f32[16,64,128]{2,1,0:T(8,128)} %broadcast_in_dim.34), calls=%async_computation.2 | async-start | bytes 1048576 | tf_op jit(solution)/shard_map/all_to_all | solution.py:504
  94.1 2.4 %shard_map.94 = (f32[32,768]{1,0:T(8,128)S(1)}, f32[32,192]{1,0:T(8,128)S(1)}, f32[32,768]{1,0:T(8,128)S(1)}) custom-call(s32[2]{0:T(128)S(1)} %pad_add_fusion.2.place_ref, f32[32,192]{1,0:T(8,128)S(1)} %copy-done.23, bf16[192,1536]{1,0:T(8,128)(2,1)S(1)} %copy-done.1, bf16[192,1536]{1,0:T(8,128)(2,1)S(1)} %copy-done.3, ...), custom_call_target="tpu_custom_call" | custom-call | tf_op jit(solution)/shard_map/pallas_call | solution.py:87
  96.5 2.5 %collective-permute-start.13 = (f32[32,768]{1,0:T(8,128)S(1)}, f32[32,768]{1,0:T(8,128)S(1)}, u32[]{:S(2)}, u32[]{:S(2)}) collective-permute-start(f32[32,768]{1,0:T(8,128)S(1)} %get-tuple-element.45), channel_id=1, source_target_pairs={{64,32},{72,40},{80,48},{88,56},{65,33},{73,41},{81,49},{89,57},{6... | collective-permute-start | bytes 294920 | tf_op jit(solution)/shard_map/ppermute | solution.py:430
  99.0 2.2 %collective-permute-start.14 = (f32[32,768]{1,0:T(8,128)S(1)}, f32[32,768]{1,0:T(8,128)S(1)}, u32[]{:S(2)}, u32[]{:S(2)}) collective-permute-start(f32[32,768]{1,0:T(8,128)S(1)} %get-tuple-element.45), channel_id=1, source_target_pairs={{64,40},{72,48},{80,56},{88,32},{65,41},{73,49},{81,57},{89,33},{6... | collective-permute-start | bytes 294920 | tf_op jit(solution)/shard_map/ppermute | solution.py:430
  101.2 2.8 %collective-permute-start.15 = (f32[32,768]{1,0:T(8,128)S(1)}, f32[32,768]{1,0:T(8,128)S(1)}, u32[]{:S(2)}, u32[]{:S(2)}) collective-permute-start(f32[32,768]{1,0:T(8,128)S(1)} %get-tuple-element.45), channel_id=1, source_target_pairs={{64,48},{72,56},{80,32},{88,40},{65,49},{73,57},{81,33},{89,41},{6... | collective-permute-start | bytes 294920 | tf_op jit(solution)/shard_map/ppermute | solution.py:430
  104.0 1.3 collective-permute-start.16
  105.3 1.3 collective-permute-start.17
  108.9 1.5 shard_map.95
  113.9 2.5 %shard_map.97 = (f32[32,768]{1,0:T(8,128)}, f32[2,32,768]{2,1,0:T(8,128)S(1)}, f32[32,768]{1,0:T(8,128)}) custom-call(s32[2]{0:T(128)S(1)} %pad_add_fusion.2.place_ref, f32[32,192]{1,0:T(8,128)S(1)} %get-tuple-element.51.acc_ref, bf16[192,1536]{1,0:T(8,128)(2,1)S(1)} %copy-done.1, bf16[192,1536]{1,0:T(8,128)(2,1)S(1)} %copy-done.3, ...), custom_call_target="tpu_custom_call" | custom-call | tf_op jit(solution)/shard_map/pallas_call | solution.py:87
  121.0 1.3 collective-permute-start.26
  122.2 1.9 collective-permute-start.27
  124.9 4.2 %shard_map.96 = (f32[32,1024]{1,0:T(8,128)S(1)}, f32[16,1024]{1,0:T(8,128)S(1)}) custom-call(s32[2048]{0:T(1024)S(1)} %bitcast.29, f32[1024,128]{1,0:T(8,128)} %bitcast.10.cells_ref, f32[2,1024]{1,0:T(2,128)S(1)} %copy-done.19), custom_call_target="tpu_custom_call" | custom-call | tf_op jit(solution)/shard_map/pallas_call | solution.py:87
  130.4 3.5 %shard_map.98 = (bf16[3,768,384]{2,1,0:T(8,128)(2,1)S(1)}, bf16[3,768,384]{2,1,0:T(8,128)(2,1)S(1)}) custom-call(s32[2]{0:T(128)S(1)} %pad_add_fusion.2.place_ref, f32[8,3,96,384]{3,2,1,0:T(8,128)} %bitcast.32), custom_call_target="tpu_custom_call" | custom-call | tf_op jit(solution)/shard_map/pallas_call | solution.py:87
  134.0 4.0 %collective-permute-done.27.own_ref = f32[32,768]{1,0:T(8,128)} collective-permute-done((f32[32,768]{1,0:T(8,128)}, f32[32,768]{1,0:T(8,128)}, u32[]{:S(2)}, u32[]{:S(2)}) %collective-permute-start.27) | collective-permute-done | bytes 98336 | tf_op jit(solution)/shard_map/ppermute | solution.py:430
  137.9 2.7 %shard_map.99 = (f32[2,32,768]{2,1,0:T(8,128)}, f32[32,192]{1,0:T(8,128)S(1)}) custom-call(s32[2]{0:T(128)S(1)} %pad_add_fusion.2.place_ref, f32[32,1024]{1,0:T(8,128)S(1)} %copy-done.5, f32[16,1024]{1,0:T(8,128)S(1)} %copy-done.13, f32[32,768]{1,0:T(8,128)} %collective-permute-done.23.p0, f32[32,768]{1,0:T(8,128)} %collective-permute-done.24.p1, ...), custom_call_target="tpu_custom_call" | custom-call | tf_op jit(solution)/shard_map/pallas_call | solution.py:87
  142.6 1.3 collective-permute-start.29
  143.9 1.3 collective-permute-start.30
  145.2 1.3 collective-permute-start.31
  146.5 1.3 collective-permute-start.32
  147.8 6.6 %collective-permute-done.29.f0 = f32[32,192]{1,0:T(8,128)S(1)} collective-permute-done((f32[32,192]{1,0:T(8,128)}, f32[32,192]{1,0:T(8,128)S(1)}, u32[]{:S(2)}, u32[]{:S(2)}) %collective-permute-start.29) | collective-permute-done | bytes 24608 | tf_op jit(solution)/shard_map/ppermute | solution.py:430
  154.4 2.9 %collective-permute-done.30.f1 = f32[32,192]{1,0:T(8,128)S(1)} collective-permute-done((f32[32,192]{1,0:T(8,128)}, f32[32,192]{1,0:T(8,128)S(1)}, u32[]{:S(2)}, u32[]{:S(2)}) %collective-permute-start.30) | collective-permute-done | bytes 24608 | tf_op jit(solution)/shard_map/ppermute | solution.py:430
  160.7 2.3 %shard_map.100 = (f32[32,192]{1,0:T(8,128)S(1)}, f32[8,32,192]{2,1,0:T(8,128)S(1)}) custom-call(s32[2]{0:T(128)S(1)} %pad_add_fusion.2.place_ref, f32[32,1024]{1,0:T(8,128)S(1)} %copy-done.6, f32[16,1024]{1,0:T(8,128)S(1)} %copy-done.14, f32[32,192]{1,0:T(8,128)S(1)} %copy-done.21, f32[32,768]{1,0:T(8,128)} %collective-permute-done.27.own_ref, ...), custom_call_target="tpu_custom_call" | custom-call | tf_op jit(solution)/shard_map/pallas_call | solution.py:87
  163.0 4.0 %collective-permute-start.33 = (f32[8,32,192]{2,1,0:T(8,128)S(1)}, f32[8,32,192]{2,1,0:T(8,128)S(1)}, u32[]{:S(2)}, u32[]{:S(2)}) collective-permute-start(f32[8,32,192]{2,1,0:T(8,128)S(1)} %get-tuple-element.63), channel_id=1, source_target_pairs={{64,96},{72,104},{80,112},{88,120},{32,0},{40,8},{48,16},{56,24},{... | collective-permute-start | bytes 589832 | tf_op jit(solution)/shard_map/ppermute | solution.py:430
  168.8 2.5 %collective-permute-start.35 = (f32[32,192]{1,0:T(8,128)S(1)}, f32[32,192]{1,0:T(8,128)S(1)}, u32[]{:S(2)}, u32[]{:S(2)}) collective-permute-start(f32[32,192]{1,0:T(8,128)S(1)} %get-tuple-element.62.acc_ref), channel_id=1, source_target_pairs={{64,104},{72,112},{80,120},{88,96},{65,105},{73,113},{81,121},{89,... | collective-permute-start | bytes 73736 | tf_op jit(solution)/shard_map/ppermute | solution.py:430
  171.3 2.0 %collective-permute-start.36 = (f32[32,192]{1,0:T(8,128)S(1)}, f32[32,192]{1,0:T(8,128)S(1)}, u32[]{:S(2)}, u32[]{:S(2)}) collective-permute-start(f32[32,192]{1,0:T(8,128)S(1)} %get-tuple-element.62.acc_ref), channel_id=1, source_target_pairs={{64,112},{72,120},{80,96},{88,104},{65,113},{73,121},{81,97},{89,1... | collective-permute-start | bytes 73736 | tf_op jit(solution)/shard_map/ppermute | solution.py:430
  174.7 1.9 shard_map.101.acc_ref
  176.7 2.5 %shard_map.102.cells_ref = f32[8,32,128]{2,1,0:T(8,128)S(1)} custom-call(s32[194]{0:T(256)S(1)} %pad_add_fusion.1.where_ref, f32[8,32,192]{2,1,0:T(8,128)S(1)} %collective-permute-done.33.got_ref.sent_ref, f32[2,32,768]{2,1,0:T(8,128)} %get-tuple-element.61.sent_ref.pass_ref, f32[2,32,768]{2,1,0:T(8,128)} %collective-permute-done.28.got_ref.passed_ref, ...), custom_call_target="tpu_custom_call" | custom-call | tf_op jit(solution)/shard_map/pallas_call | solution.py:87
  179.1 1.3 shard_map.103
  180.5 10.0 %all_to_all.20.got_ref = f32[8,32,256]{2,1,0:T(8,128)S(1)} all-to-all(f32[8,32,256]{2,1,0:T(8,128)S(1)} %shard_map.103), channel_id=1, replica_groups=mesh['row'=16,'col'=8] {'col'}, dimensions={0} | all-to-all | bytes 524288 | tf_op jit(solution)/shard_map/all_to_all | solution.py:591
  (145 shorter events, 45.7 us)
Async XLA Ops:
  7.2 37.4 %all-gather.5.cloned.1.call-start = ((), (), s32[]{:S(2)}) async-start(), calls=%async_computation.4 | async-start | bytes 3981312 | tf_op jit(solution)/shard_map/all_gather | solution.py:447
  13.8 10.9 %all-to-all-start = ((f32[8,16,128]{2,1,0:T(8,128)}), f32[8,16,128]{2,1,0:T(8,128)S(1)}, u32[]{:S(2)}, u32[]{:S(2)}) async-start(f32[8,16,128]{2,1,0:T(8,128)} %shard_map.86), calls=%async_computation | async-start | bytes 131072 | tf_op jit(solution)/shard_map/all_to_all | solution.py:463
  26.2 16.5 %all-to-all-start.1 = ((f32[16,64,128]{2,1,0:T(8,128)}), f32[16,64,128]{2,1,0:T(8,128)S(1)}, u32[]{:S(2)}, u32[]{:S(2)}) async-start(f32[16,64,128]{2,1,0:T(8,128)} %broadcast_in_dim.33), calls=%async_computation.1 | async-start | bytes 1048576 | tf_op jit(solution)/shard_map/all_to_all | solution.py:465
  33.6 96.8 %all-gather.7.cloned.1.call-start = ((), (), s32[]{:S(2)}) async-start(), calls=%async_computation.5 | async-start | bytes 3981312 | tf_op jit(solution)/shard_map/all_gather | solution.py:447
  33.8 16.9 %copy-start.18 = (f32[2,1024]{1,0:T(2,128)}, f32[2,1024]{1,0:T(2,128)S(1)}, u32[]{:S(2)}) copy-start(f32[2,1024]{1,0:T(2,128)S(1)} %get-tuple-element.72.mark_ref) | copy-start | bytes 24580
  46.9 8.7 %collective-permute-start = (f32[32,192]{1,0:T(8,128)S(1)}, f32[32,192]{1,0:T(8,128)S(1)}, u32[]{:S(2)}, u32[]{:S(2)}) collective-permute-start(f32[32,192]{1,0:T(8,128)S(1)} %shard_map.89.acc_ref), channel_id=1, source_target_pairs={{32,64},{40,72},{48,80},{56,88},{33,65},{41,73},{49,81},{57,89},{3... | collective-permute-start | bytes 73736 | tf_op jit(solution)/shard_map/ppermute | solution.py:430
  48.2 7.9 %collective-permute-start.1 = (f32[32,192]{1,0:T(8,128)S(1)}, f32[32,192]{1,0:T(8,128)S(1)}, u32[]{:S(2)}, u32[]{:S(2)}) collective-permute-start(f32[32,192]{1,0:T(8,128)S(1)} %shard_map.89.acc_ref), channel_id=1, source_target_pairs={{32,72},{40,80},{48,88},{56,64},{33,73},{41,81},{49,89},{57,65},{3... | collective-permute-start | bytes 73736 | tf_op jit(solution)/shard_map/ppermute | solution.py:430
  49.5 8.2 %collective-permute-start.2 = (f32[32,192]{1,0:T(8,128)S(1)}, f32[32,192]{1,0:T(8,128)S(1)}, u32[]{:S(2)}, u32[]{:S(2)}) collective-permute-start(f32[32,192]{1,0:T(8,128)S(1)} %shard_map.89.acc_ref), channel_id=1, source_target_pairs={{32,80},{40,88},{48,64},{56,72},{33,81},{41,89},{49,65},{57,73},{3... | collective-permute-start | bytes 73736 | tf_op jit(solution)/shard_map/ppermute | solution.py:430
  50.8 6.9 %collective-permute-start.3 = (f32[32,192]{1,0:T(8,128)S(1)}, f32[32,192]{1,0:T(8,128)S(1)}, u32[]{:S(2)}, u32[]{:S(2)}) collective-permute-start(f32[32,192]{1,0:T(8,128)S(1)} %shard_map.89.acc_ref), channel_id=1, source_target_pairs={{32,88},{40,64},{48,72},{56,80},{33,89},{41,65},{49,73},{57,81},{3... | collective-permute-start | bytes 73736 | tf_op jit(solution)/shard_map/ppermute | solution.py:430
  62.1 8.7 %collective-permute-start.4 = (f32[4,32,192]{2,1,0:T(8,128)}, f32[4,32,192]{2,1,0:T(8,128)S(1)}, u32[]{:S(2)}, u32[]{:S(2)}) collective-permute-start(f32[4,32,192]{2,1,0:T(8,128)} %copy-done.26), channel_id=1, source_target_pairs={{64,96},{72,104},{80,112},{88,120},{65,97},{73,105},{81,113},{89,1... | collective-permute-start | bytes 294920 | tf_op jit(solution)/shard_map/ppermute | solution.py:430
  63.4 7.4 %collective-permute-start.5 = (f32[32,192]{1,0:T(8,128)}, f32[32,192]{1,0:T(8,128)S(1)}, u32[]{:S(2)}, u32[]{:S(2)}) collective-permute-start(f32[32,192]{1,0:T(8,128)} %copy-done.24), channel_id=1, source_target_pairs={{64,96},{72,104},{80,112},{88,120},{65,97},{73,105},{81,113},{89,1... | collective-permute-start | bytes 73736 | tf_op jit(solution)/shard_map/ppermute | solution.py:430
  64.7 6.1 %collective-permute-start.6 = (f32[32,192]{1,0:T(8,128)}, f32[32,192]{1,0:T(8,128)S(1)}, u32[]{:S(2)}, u32[]{:S(2)}) collective-permute-start(f32[32,192]{1,0:T(8,128)} %copy-done.24), channel_id=1, source_target_pairs={{64,104},{72,112},{80,120},{88,96},{65,105},{73,113},{81,121},{89,... | collective-permute-start | bytes 73736 | tf_op jit(solution)/shard_map/ppermute | solution.py:430
  66.0 4.8 %collective-permute-start.7 = (f32[32,192]{1,0:T(8,128)}, f32[32,192]{1,0:T(8,128)S(1)}, u32[]{:S(2)}, u32[]{:S(2)}) collective-permute-start(f32[32,192]{1,0:T(8,128)} %copy-done.24), channel_id=1, source_target_pairs={{64,112},{72,120},{80,96},{88,104},{65,113},{73,121},{81,97},{89,1... | collective-permute-start | bytes 73736 | tf_op jit(solution)/shard_map/ppermute | solution.py:430
  67.3 3.5 %collective-permute-start.8 = (f32[32,192]{1,0:T(8,128)}, f32[32,192]{1,0:T(8,128)S(1)}, u32[]{:S(2)}, u32[]{:S(2)}) collective-permute-start(f32[32,192]{1,0:T(8,128)} %copy-done.24), channel_id=1, source_target_pairs={{64,120},{72,96},{80,104},{88,112},{65,121},{73,97},{81,105},{89,1... | collective-permute-start | bytes 73736 | tf_op jit(solution)/shard_map/ppermute | solution.py:430
  73.7 17.5 %collective-permute-start.10 = (f32[32,768]{1,0:T(8,128)}, f32[32,768]{1,0:T(8,128)}, u32[]{:S(2)}, u32[]{:S(2)}) collective-permute-start(f32[32,768]{1,0:T(8,128)} %get-tuple-element.43), channel_id=1, source_target_pairs={{96,72},{104,80},{112,88},{120,64},{97,73},{105,81},{113,89},{121,... | collective-permute-start | bytes 294920 | tf_op jit(solution)/shard_map/ppermute | solution.py:430
  75.0 16.2 %collective-permute-start.11 = (f32[32,768]{1,0:T(8,128)}, f32[32,768]{1,0:T(8,128)}, u32[]{:S(2)}, u32[]{:S(2)}) collective-permute-start(f32[32,768]{1,0:T(8,128)} %get-tuple-element.43), channel_id=1, source_target_pairs={{96,80},{104,88},{112,64},{120,72},{97,81},{105,89},{113,65},{121,... | collective-permute-start | bytes 294920 | tf_op jit(solution)/shard_map/ppermute | solution.py:430
  76.3 14.9 %collective-permute-start.12 = (f32[32,768]{1,0:T(8,128)}, f32[32,768]{1,0:T(8,128)}, u32[]{:S(2)}, u32[]{:S(2)}) collective-permute-start(f32[32,768]{1,0:T(8,128)} %get-tuple-element.43), channel_id=1, source_target_pairs={{96,88},{104,64},{112,72},{120,80},{97,89},{105,65},{113,73},{121,... | collective-permute-start | bytes 294920 | tf_op jit(solution)/shard_map/ppermute | solution.py:430
  77.6 13.6 %collective-permute-start.9 = (f32[32,768]{1,0:T(8,128)}, f32[32,768]{1,0:T(8,128)}, u32[]{:S(2)}, u32[]{:S(2)}) collective-permute-start(f32[32,768]{1,0:T(8,128)} %get-tuple-element.43), channel_id=1, source_target_pairs={{96,64},{104,72},{112,80},{120,88},{97,65},{105,73},{113,81},{121,... | collective-permute-start | bytes 294920 | tf_op jit(solution)/shard_map/ppermute | solution.py:430
  79.8 44.4 %all-to-all-start.2 = ((f32[16,64,128]{2,1,0:T(8,128)}), f32[16,64,128]{2,1,0:T(8,128)}, u32[]{:S(2)}, u32[]{:S(2)}) async-start(f32[16,64,128]{2,1,0:T(8,128)} %broadcast_in_dim.34), calls=%async_computation.2 | async-start | bytes 1048576 | tf_op jit(solution)/shard_map/all_to_all | solution.py:504
  96.5 10.1 %collective-permute-start.13 = (f32[32,768]{1,0:T(8,128)S(1)}, f32[32,768]{1,0:T(8,128)S(1)}, u32[]{:S(2)}, u32[]{:S(2)}) collective-permute-start(f32[32,768]{1,0:T(8,128)S(1)} %get-tuple-element.45), channel_id=1, source_target_pairs={{64,32},{72,40},{80,48},{88,56},{65,33},{73,41},{81,49},{89,57},{6... | collective-permute-start | bytes 294920 | tf_op jit(solution)/shard_map/ppermute | solution.py:430
  99.0 7.6 %collective-permute-start.14 = (f32[32,768]{1,0:T(8,128)S(1)}, f32[32,768]{1,0:T(8,128)S(1)}, u32[]{:S(2)}, u32[]{:S(2)}) collective-permute-start(f32[32,768]{1,0:T(8,128)S(1)} %get-tuple-element.45), channel_id=1, source_target_pairs={{64,40},{72,48},{80,56},{88,32},{65,41},{73,49},{81,57},{89,33},{6... | collective-permute-start | bytes 294920 | tf_op jit(solution)/shard_map/ppermute | solution.py:430
  101.2 5.7 %collective-permute-start.15 = (f32[32,768]{1,0:T(8,128)S(1)}, f32[32,768]{1,0:T(8,128)S(1)}, u32[]{:S(2)}, u32[]{:S(2)}) collective-permute-start(f32[32,768]{1,0:T(8,128)S(1)} %get-tuple-element.45), channel_id=1, source_target_pairs={{64,48},{72,56},{80,32},{88,40},{65,49},{73,57},{81,33},{89,41},{6... | collective-permute-start | bytes 294920 | tf_op jit(solution)/shard_map/ppermute | solution.py:430
  104.0 3.9 %collective-permute-start.16 = (f32[32,768]{1,0:T(8,128)S(1)}, f32[32,768]{1,0:T(8,128)S(1)}, u32[]{:S(2)}, u32[]{:S(2)}) collective-permute-start(f32[32,768]{1,0:T(8,128)S(1)} %get-tuple-element.45), channel_id=1, source_target_pairs={{64,56},{72,32},{80,40},{88,48},{65,57},{73,33},{81,41},{89,49},{6... | collective-permute-start | bytes 294920 | tf_op jit(solution)/shard_map/ppermute | solution.py:430
  105.3 3.7 %collective-permute-start.17 = (f32[32,768]{1,0:T(8,128)S(1)}, f32[32,768]{1,0:T(8,128)S(1)}, u32[]{:S(2)}, u32[]{:S(2)}) collective-permute-start(f32[32,768]{1,0:T(8,128)S(1)} %get-tuple-element.46.x3_ref), channel_id=1, source_target_pairs={{64,32},{72,40},{80,48},{88,56},{65,33},{73,41},{81,49},{89,57},{6... | collective-permute-start | bytes 294920 | tf_op jit(solution)/shard_map/ppermute | solution.py:430
  110.4 3.4 %collective-permute-start.22 = (f32[2,32,768]{2,1,0:T(8,128)S(1)}, f32[2,32,768]{2,1,0:T(8,128)S(1)}, u32[]{:S(2)}, u32[]{:S(2)}) collective-permute-start(f32[2,32,768]{2,1,0:T(8,128)S(1)} %get-tuple-element.52.x2_ref), channel_id=1, source_target_pairs={{32,0},{40,8},{48,16},{56,24},{33,1},{41,9},{49,17},{57,25},{34,2}... | collective-permute-start | bytes 589832 | tf_op jit(solution)/shard_map/ppermute | solution.py:430
  111.1 2.7 %collective-permute-start.18 = (f32[32,768]{1,0:T(8,128)S(1)}, f32[32,768]{1,0:T(8,128)S(1)}, u32[]{:S(2)}, u32[]{:S(2)}) collective-permute-start(f32[32,768]{1,0:T(8,128)S(1)} %get-tuple-element.47), channel_id=1, source_target_pairs={{32,0},{40,8},{48,16},{56,24},{33,1},{41,9},{49,17},{57,25},{34,2}... | collective-permute-start | bytes 294920 | tf_op jit(solution)/shard_map/ppermute | solution.py:430
  111.8 2.0 %collective-permute-start.19 = (f32[32,768]{1,0:T(8,128)S(1)}, f32[32,768]{1,0:T(8,128)S(1)}, u32[]{:S(2)}, u32[]{:S(2)}) collective-permute-start(f32[32,768]{1,0:T(8,128)S(1)} %get-tuple-element.47), channel_id=1, source_target_pairs={{32,8},{40,16},{48,24},{56,0},{33,9},{41,17},{49,25},{57,1},{34,10... | collective-permute-start | bytes 294920 | tf_op jit(solution)/shard_map/ppermute | solution.py:430
  112.5 1.4 collective-permute-start.20
  113.1 0.7 collective-permute-start.21
  117.1 16.8 %collective-permute-start.23 = (f32[32,768]{1,0:T(8,128)}, f32[32,768]{1,0:T(8,128)}, u32[]{:S(2)}, u32[]{:S(2)}) collective-permute-start(f32[32,768]{1,0:T(8,128)} %get-tuple-element.53), channel_id=1, source_target_pairs={{0,32},{8,40},{16,48},{24,56},{1,33},{9,41},{17,49},{25,57},{2,34}... | collective-permute-start | bytes 294920 | tf_op jit(solution)/shard_map/ppermute | solution.py:430
  118.4 15.6 %collective-permute-start.24 = (f32[32,768]{1,0:T(8,128)}, f32[32,768]{1,0:T(8,128)}, u32[]{:S(2)}, u32[]{:S(2)}) collective-permute-start(f32[32,768]{1,0:T(8,128)} %get-tuple-element.53), channel_id=1, source_target_pairs={{0,40},{8,48},{16,56},{24,32},{1,41},{9,49},{17,57},{25,33},{2,42}... | collective-permute-start | bytes 294920 | tf_op jit(solution)/shard_map/ppermute | solution.py:430
  119.7 14.3 %collective-permute-start.25 = (f32[32,768]{1,0:T(8,128)}, f32[32,768]{1,0:T(8,128)}, u32[]{:S(2)}, u32[]{:S(2)}) collective-permute-start(f32[32,768]{1,0:T(8,128)} %get-tuple-element.53), channel_id=1, source_target_pairs={{0,48},{8,56},{16,32},{24,40},{1,49},{9,57},{17,33},{25,41},{2,50}... | collective-permute-start | bytes 294920 | tf_op jit(solution)/shard_map/ppermute | solution.py:430
  121.0 13.0 %collective-permute-start.26 = (f32[32,768]{1,0:T(8,128)}, f32[32,768]{1,0:T(8,128)}, u32[]{:S(2)}, u32[]{:S(2)}) collective-permute-start(f32[32,768]{1,0:T(8,128)} %get-tuple-element.53), channel_id=1, source_target_pairs={{0,56},{8,32},{16,40},{24,48},{1,57},{9,33},{17,41},{25,49},{2,58}... | collective-permute-start | bytes 294920 | tf_op jit(solution)/shard_map/ppermute | solution.py:430
  122.2 15.7 %collective-permute-start.27 = (f32[32,768]{1,0:T(8,128)}, f32[32,768]{1,0:T(8,128)}, u32[]{:S(2)}, u32[]{:S(2)}) collective-permute-start(f32[32,768]{1,0:T(8,128)} %get-tuple-element.54.newest_ref), channel_id=1, source_target_pairs={{0,32},{8,40},{16,48},{24,56},{32,64},{40,72},{48,80},{56,88},{64,... | collective-permute-start | bytes 294920 | tf_op jit(solution)/shard_map/ppermute | solution.py:430
  137.9 29.1 %copy-start.28 = (s32[3072]{0:T(1024)S(1)}, s32[3072]{0:T(1024)}, u32[]{:S(2)}) copy-start(s32[3072]{0:T(1024)} %param.13) | copy-start | bytes 36868
  141.3 16.9 %collective-permute-start.28 = (f32[2,32,768]{2,1,0:T(8,128)}, f32[2,32,768]{2,1,0:T(8,128)}, u32[]{:S(2)}, u32[]{:S(2)}) collective-permute-start(f32[2,32,768]{2,1,0:T(8,128)} %get-tuple-element.61.sent_ref.pass_ref), channel_id=1, source_target_pairs={{32,64},{40,72},{48,80},{56,88},{0,96},{8,104},{16,112},{24,120},{... | collective-permute-start | bytes 589832 | tf_op jit(solution)/shard_map/ppermute | solution.py:430
  142.6 11.8 %collective-permute-start.29 = (f32[32,192]{1,0:T(8,128)}, f32[32,192]{1,0:T(8,128)S(1)}, u32[]{:S(2)}, u32[]{:S(2)}) collective-permute-start(f32[32,192]{1,0:T(8,128)} %copy-done.20), channel_id=1, source_target_pairs={{32,64},{40,72},{48,80},{56,88},{33,65},{41,73},{49,81},{57,89},{3... | collective-permute-start | bytes 73736 | tf_op jit(solution)/shard_map/ppermute | solution.py:430
  143.9 13.4 %collective-permute-start.30 = (f32[32,192]{1,0:T(8,128)}, f32[32,192]{1,0:T(8,128)S(1)}, u32[]{:S(2)}, u32[]{:S(2)}) collective-permute-start(f32[32,192]{1,0:T(8,128)} %copy-done.20), channel_id=1, source_target_pairs={{32,72},{40,80},{48,88},{56,64},{33,73},{41,81},{49,89},{57,65},{3... | collective-permute-start | bytes 73736 | tf_op jit(solution)/shard_map/ppermute | solution.py:430
  145.2 12.9 %collective-permute-start.31 = (f32[32,192]{1,0:T(8,128)}, f32[32,192]{1,0:T(8,128)S(1)}, u32[]{:S(2)}, u32[]{:S(2)}) collective-permute-start(f32[32,192]{1,0:T(8,128)} %copy-done.20), channel_id=1, source_target_pairs={{32,80},{40,88},{48,64},{56,72},{33,81},{41,89},{49,65},{57,73},{3... | collective-permute-start | bytes 73736 | tf_op jit(solution)/shard_map/ppermute | solution.py:430
  146.5 11.7 %collective-permute-start.32 = (f32[32,192]{1,0:T(8,128)}, f32[32,192]{1,0:T(8,128)S(1)}, u32[]{:S(2)}, u32[]{:S(2)}) collective-permute-start(f32[32,192]{1,0:T(8,128)} %copy-done.20), channel_id=1, source_target_pairs={{32,88},{40,64},{48,72},{56,80},{33,89},{41,65},{49,73},{57,81},{3... | collective-permute-start | bytes 73736 | tf_op jit(solution)/shard_map/ppermute | solution.py:430
  163.0 13.6 %copy-start.8 = (f32[2,32,768]{2,1,0:T(8,128)S(1)}, f32[2,32,768]{2,1,0:T(8,128)}, u32[]{:S(2)}) copy-start(f32[2,32,768]{2,1,0:T(8,128)} %copy-done.7) | copy-start | bytes 589828
  163.0 13.6 %copy-start.11 = (f32[2,32,768]{2,1,0:T(8,128)S(1)}, f32[2,32,768]{2,1,0:T(8,128)}, u32[]{:S(2)}) copy-start(f32[2,32,768]{2,1,0:T(8,128)} %copy-done.9) | copy-start | bytes 589828
  163.0 13.6 %copy-start.17 = (f32[32,768]{1,0:T(8,128)S(1)}, f32[32,768]{1,0:T(8,128)}, u32[]{:S(2)}) copy-start(f32[32,768]{1,0:T(8,128)} %copy-done.16) | copy-start | bytes 294916
  163.0 11.7 %collective-permute-start.33 = (f32[8,32,192]{2,1,0:T(8,128)S(1)}, f32[8,32,192]{2,1,0:T(8,128)S(1)}, u32[]{:S(2)}, u32[]{:S(2)}) collective-permute-start(f32[8,32,192]{2,1,0:T(8,128)S(1)} %get-tuple-element.63), channel_id=1, source_target_pairs={{64,96},{72,104},{80,112},{88,120},{32,0},{40,8},{48,16},{56,24},{... | collective-permute-start | bytes 589832 | tf_op jit(solution)/shard_map/ppermute | solution.py:430
  167.5 11.6 %collective-permute-start.34 = (f32[32,192]{1,0:T(8,128)S(1)}, f32[32,192]{1,0:T(8,128)S(1)}, u32[]{:S(2)}, u32[]{:S(2)}) collective-permute-start(f32[32,192]{1,0:T(8,128)S(1)} %get-tuple-element.62.acc_ref), channel_id=1, source_target_pairs={{64,96},{72,104},{80,112},{88,120},{65,97},{73,105},{81,113},{89,1... | collective-permute-start | bytes 73736 | tf_op jit(solution)/shard_map/ppermute | solution.py:430
  168.8 10.4 %collective-permute-start.35 = (f32[32,192]{1,0:T(8,128)S(1)}, f32[32,192]{1,0:T(8,128)S(1)}, u32[]{:S(2)}, u32[]{:S(2)}) collective-permute-start(f32[32,192]{1,0:T(8,128)S(1)} %get-tuple-element.62.acc_ref), channel_id=1, source_target_pairs={{64,104},{72,112},{80,120},{88,96},{65,105},{73,113},{81,121},{89,... | collective-permute-start | bytes 73736 | tf_op jit(solution)/shard_map/ppermute | solution.py:430
  171.3 7.8 %collective-permute-start.36 = (f32[32,192]{1,0:T(8,128)S(1)}, f32[32,192]{1,0:T(8,128)S(1)}, u32[]{:S(2)}, u32[]{:S(2)}) collective-permute-start(f32[32,192]{1,0:T(8,128)S(1)} %get-tuple-element.62.acc_ref), channel_id=1, source_target_pairs={{64,112},{72,120},{80,96},{88,104},{65,113},{73,121},{81,97},{89,1... | collective-permute-start | bytes 73736 | tf_op jit(solution)/shard_map/ppermute | solution.py:430
  173.3 5.8 %collective-permute-start.37 = (f32[32,192]{1,0:T(8,128)S(1)}, f32[32,192]{1,0:T(8,128)S(1)}, u32[]{:S(2)}, u32[]{:S(2)}) collective-permute-start(f32[32,192]{1,0:T(8,128)S(1)} %get-tuple-element.62.acc_ref), channel_id=1, source_target_pairs={{64,120},{72,96},{80,104},{88,112},{65,121},{73,97},{81,105},{89,1... | collective-permute-start | bytes 73736 | tf_op jit(solution)/shard_map/ppermute | solution.py:430
  (24 other events, 59.7 us)
Sparse Core Ops, SparseCore 0:
  10.2 31.9 all-gather.4
  62.2 28.4 all-gather.6

commit v7 on v6

--- a/solution.py
+++ b/solution.py
@@ -14,6 +14,7 @@
 BLOCK = 768
 PIECE = 96
 CELLS = 24
+LATE = 5
 VMEM = 16 * 1024 * 1024
 
 SDS = jax.ShapeDtypeStruct
@@ -26,8 +27,8 @@
 
 
 def complex_dot(vector, weight):
-    weight_high, weight_low = weight
-    half = weight_high.shape[1] // 2
+    weight_high, weight_low = split(weight)
+    half = weight.shape[1] // 2
     high, low = split(vector)
     both = jnp.dot(
         jnp.concatenate([high, low], axis=0), weight_high, preferred_element_type=f32
@@ -42,30 +43,26 @@
     return jnp.minimum(jnp.where(plane < block, block - 1, block), GROUP - 2)
 
 
-def block_weight(parts, slot):
-    return tuple(ref[slot] for ref in parts)
-
-
-def slab_weight(parts, slot, source):
+def slab_weight(ref, source):
     at = pl.multiple_of(SLAB * source, SLAB)
-    return tuple(ref[slot, pl.ds(at, SLAB), :] for ref in parts)
-
-
-def slabs_dot(slabs, parts, slot, q, keep=None):
+    return ref[pl.ds(at, SLAB), :]
+
+
+def slabs_dot(slabs, ref, q, keep=None):
     total = None
     for d, slab in enumerate(slabs):
         source = lax.rem(q - d + GROUP, GROUP)
         if keep is not None:
             keep[source] = slab
-        part = complex_dot(slab, slab_weight(parts, slot, source))
+        part = complex_dot(slab, slab_weight(ref, source))
         total = part if total is None else total + part
     return total
 
 
-def sent_dot(sent_ref, parts, slot):
+def sent_dot(sent_ref, ref):
     total = None
     for s in range(GROUP):
-        part = complex_dot(sent_ref[s], slab_weight(parts, slot, s))
+        part = complex_dot(sent_ref[s], slab_weight(ref, s))
         total = part if total is None else total + part
     return total
 
@@ -77,18 +74,18 @@
     return total
 
 
-def call(body, out_shape, scalars, inputs, blocks=(), scratch=(), steps=1):
+def call(body, out_shape, scalars, inputs, blocks=(), scratch=()):
     vmem = pl.BlockSpec(memory_space=pltpu.VMEM)
     specs = [vmem] * len(inputs)
-    for _, at in blocks:
-        specs.append(pl.BlockSpec((8, 1, PIECE, 2 * SLAB), at))
+    for _, shape, at in blocks:
+        specs.append(pl.BlockSpec(shape, at, pipeline_mode=pl.Buffered(1)))
     near = [pltpu.with_memory_space_constraint(value, pltpu.VMEM) for value in inputs]
-    far = [pltpu.with_memory_space_constraint(array, pltpu.HBM) for array, _ in blocks]
+    far = [pltpu.with_memory_space_constraint(array, pltpu.HBM) for array, _, _ in blocks]
     return pl.pallas_call(
         body,
         grid_spec=pltpu.PrefetchScalarGridSpec(
             num_scalar_prefetch=1,
-            grid=(steps,),
+            grid=(1,),
             in_specs=specs,
             out_specs=(vmem,) * len(out_shape),
             scratch_shapes=scratch,
@@ -147,7 +144,8 @@
     turn_rows(rows_ref, mark_ref, rhs_ref)
 
 
-def second_front_kernel(where_ref, cells_ref, mark_ref, rhs_ref, link_ref, rows_ref):
+def second_front_kernel(where_ref, mark_ref, late_ref, rhs_ref, link_ref, cells_ref, rows_ref):
+    cells_ref[...] = late_ref[...].reshape(1024, 128)
     gather_rows(where_ref, 0, cells_ref, rows_ref)
     turn_rows(rows_ref, mark_ref, rhs_ref)
     gather_rows(where_ref, 1024, cells_ref, rows_ref)
@@ -162,101 +160,87 @@
         link_ref[8:16, at] = jnp.broadcast_to(imag, (8, 128))
 
 
-def split_kernel(place_ref, weight_ref, high_ref, low_ref):
-    slot = pl.program_id(0)
-    high, low = split(weight_ref[:, 0].reshape(BLOCK, 2 * SLAB))
-    high_ref[slot] = high
-    low_ref[slot] = low
-
-
-def split_inverse_kernel(place_ref, weight_ref, high_ref, low_ref):
-    high_ref[...], low_ref[...] = split(weight_ref[...])
+def load_kernel(place_ref, *refs):
+    count = len(refs) // 2
+    for block_ref, out_ref in zip(refs[:count], refs[count:]):
+        out_ref[...] = block_ref[:, 0].reshape(BLOCK, 2 * SLAB)
 
 
 def start_kernel(place_ref, rhs_ref, weight_ref, acc_ref):
-    weight = split(weight_ref[:, 0].reshape(BLOCK, 2 * SLAB))
-    product = complex_dot(rhs_ref[:, 0:BLOCK], weight)
+    product = complex_dot(rhs_ref[:, 0:BLOCK], weight_ref[:, 0].reshape(BLOCK, 2 * SLAB))
     slab = rhs_ref[:, BLOCK : BLOCK + SLAB]
     acc_ref[...] = jnp.where(place_ref[0] > 0, slab - product, slab)
 
 
-def forward_one_kernel(place_ref, acc_ref, y0, y1, y2, y3, high, low, out_ref, keep_ref):
-    plane, q = place_ref[0], place_ref[1]
+def forward_one_kernel(place_ref, acc_ref, y0, y1, y2, y3, weight_ref, out_ref, keep_ref):
     slabs = [y0[...], y1[...], y2[...], y3[...]]
-    out_ref[...] = acc_ref[...] - slabs_dot(slabs, (high, low), slot_of(plane, 1), q, keep_ref)
+    out_ref[...] = acc_ref[...] - slabs_dot(slabs, weight_ref, place_ref[1], keep_ref)
 
 
 def forward_two_kernel(
-    place_ref, acc_ref, inverse_high, inverse_low, sent_ref, y0, y1, y2, y3, high, low, out_ref, part_ref
-):
-    plane, q = place_ref[0], place_ref[1]
+    place_ref, acc_ref, inverse_ref, sent_ref, y0, y1, y2, y3, weight1_ref, weight2_ref, out_ref, part_ref
+):
     slabs = [y0[...], y1[...], y2[...], y3[...]]
     solved = (
         acc_ref[...]
-        - sent_dot(sent_ref, (high, low), slot_of(plane, 1))
-        - slabs_dot(slabs, (high, low), slot_of(plane, 2), q)
+        - sent_dot(sent_ref, weight1_ref)
+        - slabs_dot(slabs, weight2_ref, place_ref[1])
     )
     out_ref[...] = solved
-    part_ref[...] = complex_dot(solved, (inverse_high[...], inverse_low[...]))
+    part_ref[...] = complex_dot(solved, inverse_ref[...])
 
 
 def back_three_kernel(
     place_ref,
     acc_ref,
-    inverse_high,
-    inverse_low,
+    inverse_ref,
     p0,
     p1,
     p2,
     p3,
-    high,
-    low,
+    weight_ref,
     x_ref,
     acc_out_ref,
     part_ref,
 ):
     x = add_refs([p0, p1, p2, p3])
-    weight = block_weight((high, low), slot_of(place_ref[0], 3))
-    acc = acc_ref[...] - complex_dot(x, weight)
+    acc = acc_ref[...] - complex_dot(x, weight_ref[...])
     x_ref[...] = x
     acc_out_ref[...] = acc
-    part_ref[...] = complex_dot(acc, (inverse_high[...], inverse_low[...]))
+    part_ref[...] = complex_dot(acc, inverse_ref[...])
 
 
 def back_two_kernel(
     place_ref,
     acc_ref,
-    inverse_high,
-    inverse_low,
+    inverse_ref,
     p0,
     p1,
     p2,
     p3,
     x3_ref,
-    high,
-    low,
+    weight2_ref,
+    weight3_ref,
     both_ref,
     acc_out_ref,
     part_ref,
 ):
-    plane = place_ref[0]
     x = add_refs([p0, p1, p2, p3])
     acc = (
         acc_ref[...]
-        - complex_dot(x3_ref[...], block_weight((high, low), slot_of(plane, 3)))
-        - complex_dot(x, block_weight((high, low), slot_of(plane, 2)))
+        - complex_dot(x3_ref[...], weight3_ref[...])
+        - complex_dot(x, weight2_ref[...])
     )
     both_ref[0] = x
     both_ref[1] = x3_ref[...]
     acc_out_ref[...] = acc
-    part_ref[...] = complex_dot(acc, (inverse_high[...], inverse_low[...]))
+    part_ref[...] = complex_dot(acc, inverse_ref[...])
 
 
 def back_one_kernel(
     place_ref,
     acc_ref,
-    inverse_high,
-    inverse_low,
+    inverse_ref,
     p0,
     p1,
     p2,
@@ -264,21 +248,21 @@
     later_ref,
     x2_ref,
     x3_ref,
-    high,
-    low,
+    weight1_ref,
+    weight2_ref,
+    weight3_ref,
     newest_ref,
     both_ref,
     part_ref,
 ):
-    plane = place_ref[0]
     x = add_refs([p0, p1, p2, p3])
     acc = (
         acc_ref[...]
-        - complex_dot(later_ref[1], block_weight((high, low), slot_of(plane, 3)))
-        - complex_dot(later_ref[0], block_weight((high, low), slot_of(plane, 2)))
-        - complex_dot(x, block_weight((high, low), slot_of(plane, 1)))
-    )
-    part_ref[...] = complex_dot(acc, (inverse_high[...], inverse_low[...]))
+        - complex_dot(later_ref[1], weight3_ref[...])
+        - complex_dot(later_ref[0], weight2_ref[...])
+        - complex_dot(x, weight1_ref[...])
+    )
+    part_ref[...] = complex_dot(acc, inverse_ref[...])
     newest_ref[...] = x + x2_ref[0] + x3_ref[...]
     both_ref[0] = x
     both_ref[1] = later_ref[0]
@@ -307,12 +291,12 @@
 
 
 def couple_kernel(
-    place_ref, rhs_ref, link_ref, p0, p1, p2, p3, own_ref, zero_ref, high, low, pass_ref, out_ref
+    place_ref, rhs_ref, link_ref, p0, p1, p2, p3, own_ref, zero_ref, weight_ref, pass_ref, out_ref
 ):
     x0 = add_refs([p0, p1, p2, p3])
     slab = second_slab(rhs_ref, link_ref, own_ref[...], place_ref[1])
     out_ref[...] = slab - complex_dot(
-        second_block(rhs_ref, link_ref, x0), block_weight((high, low), 0)
+        second_block(rhs_ref, link_ref, x0), weight_ref[...]
     )
     zero = place_ref[0] == 0
     pass_ref[0] = jnp.where(zero, zero_ref[0], x0)
@@ -331,8 +315,8 @@
     f1,
     f2,
     f3,
-    high,
-    low,
+    weight0_ref,
+    weight1_ref,
     out_ref,
     keep_ref,
 ):
@@ -341,9 +325,9 @@
     for s in range(GROUP):
         keep_ref[GROUP + s] = x0[:, SLAB * s : SLAB * s + SLAB]
     slab = second_slab(rhs_ref, link_ref, own_ref[...], q)
-    product = complex_dot(second_block(rhs_ref, link_ref, x0), block_weight((high, low), 0))
+    product = complex_dot(second_block(rhs_ref, link_ref, x0), weight0_ref[...])
     slabs = [f0[...], f1[...], f2[...], f3[...]]
-    solved = slab - product - slabs_dot(slabs, (high, low), 1, q, keep_ref)
+    solved = slab - product - slabs_dot(slabs, weight1_ref, q, keep_ref)
     out_ref[...] = jnp.where(plane == 1, acc_ref[...], solved)
 
 
@@ -352,13 +336,13 @@
 
 
 def second_base_kernel(
-    place_ref, rhs_ref, link_ref, acc_ref, got_ref, own_ref, high, low, out_ref
+    place_ref, rhs_ref, link_ref, acc_ref, got_ref, own_ref, weight_ref, out_ref
 ):
     plane, q = place_ref[0], place_ref[1]
     x0 = joined(got_ref, GROUP)
     own = jnp.where(plane == 0, x0, own_ref[...])
     slab = second_slab(rhs_ref, link_ref, own, q)
-    product = complex_dot(second_block(rhs_ref, link_ref, x0), block_weight((high, low), 0))
+    product = complex_dot(second_block(rhs_ref, link_ref, x0), weight_ref[...])
     out_ref[...] = jnp.where(
         plane == 0, slab, jnp.where(plane == 3, slab - product, acc_ref[...])
     )
@@ -396,13 +380,13 @@
 
 
 def second_two_kernel(
-    place_ref, acc_ref, cells_ref, sent_ref, f0, f1, f2, f3, high, low, out_ref
+    place_ref, acc_ref, cells_ref, sent_ref, f0, f1, f2, f3, weight1_ref, weight2_ref, out_ref
 ):
     slabs = [f0[...], f1[...], f2[...], f3[...]]
     solved = (
         acc_ref[...]
-        - sent_dot(sent_ref, (high, low), 1)
-        - slabs_dot(slabs, (high, low), 2, place_ref[1])
+        - sent_dot(sent_ref, weight1_ref)
+        - slabs_dot(slabs, weight2_ref, place_ref[1])
     )
     lane = lax.broadcasted_iota(jnp.int32, (ROWS, 128), 1)
     tail = jnp.concatenate([solved[:, 128:], jnp.zeros((ROWS, 64), f32)], axis=1)
@@ -460,10 +444,13 @@
     (packed,) = call(
         pack_kernel, [SDS((8, 16, 128), f32)], place, [source1, source2, links]
     )
+    factor2 = after(factor2, packed)
+    turned2 = factor2[:, :, : 3 * PIECE].reshape(2 * SLAB, 3 * PIECE).T
     packed = lax.all_to_all(packed, "col", 0, 0)
     early = jnp.broadcast_to(packed[:, :8].reshape(1, 64, 128), (16, 64, 128))
     early = lax.all_to_all(early, "row", 0, 0).reshape(1024, 128)
     late = packed[:, 8:].reshape(64, 128)
+    late = jnp.broadcast_to(late[:, None], (64, LATE, 128)).reshape(64, LATE * 128)
 
     cell_y = front_order // 48
     cell_x = front_order % 48
@@ -483,91 +470,104 @@
     pair_shape = SDS((2, ROWS, BLOCK), f32)
     sent_shape = SDS((GROUP, ROWS, SLAB), f32)
 
-    def split_factor(matrix):
-        shape = SDS((GROUP - 1, BLOCK, 2 * SLAB), jnp.bfloat16)
-        blocks = [(matrix, lambda i, place: (0, i, 0, 0))]
-        return call(split_kernel, [shape, shape], place, [], blocks, steps=GROUP - 1)
-
-    first = [(matrix1, lambda i, place: (0, slot_of(place[0], 0), 0, 0))]
+    def load(matrix, numbers, arrived, second=False):
+        matrix = after(matrix, arrived)
+        blocks = [
+            (
+                matrix,
+                (8, 1, PIECE, 2 * SLAB),
+                (lambda i, place, n=number: (0, n, 0, 0))
+                if second
+                else (lambda i, place, n=number: (0, slot_of(place[0], n), 0, 0)),
+            )
+            for number in numbers
+        ]
+        shapes = [SDS((BLOCK, 2 * SLAB), f32)] * len(numbers)
+        return call(load_kernel, shapes, place, [], blocks)
+
+    first = [
+        (matrix1, (8, 1, PIECE, 2 * SLAB), lambda i, place: (0, slot_of(place[0], 0), 0, 0))
+    ]
     (acc,) = call(start_kernel, [slab_shape], place, [rhs], first)
     got = plane_spread(acc, 1, 2)
-    matrix1, diag_inv = after((matrix1, diag_inv), acc)
-    parts1 = split_factor(matrix1)
+    late, turned2, diag_inv = after((late, turned2, diag_inv), acc)
+    late = lax.all_gather(late, "row")
+    matrix2 = gather_blocks(turned2)
+    weights = load(matrix1, [1], acc)
     inverse = diag_inv.reshape(2 * BLOCK, SLAB).T
-    shape = SDS((SLAB, 2 * BLOCK), jnp.bfloat16)
-    inverse = call(split_inverse_kernel, [shape, shape], place, [inverse])
     acc, kept = call(
-        forward_one_kernel, [slab_shape, sent_shape], place, [acc, *got, *parts1]
-    )
-    late, factor2 = after((late, factor2), acc)
-    late = jnp.broadcast_to(late[None], (16, 64, 128))
-    late = lax.all_to_all(late, "row", 0, 0).reshape(1024, 128)
-    turned2 = factor2[:, :, : 3 * PIECE].reshape(2 * SLAB, 3 * PIECE).T
-    matrix2 = gather_blocks(turned2)
-
+        forward_one_kernel, [slab_shape, sent_shape], place, [acc, *got, *weights]
+    )
     sent = plane_send(kept, (2, 3))
     got = plane_spread(acc, 2, 3)
+    weights = load(matrix1, [1, 2], acc)
     acc, part = call(
         forward_two_kernel,
         [slab_shape, block_shape],
         place,
-        [acc, *inverse, sent, *got, *parts1],
+        [acc, inverse, sent, *got, *weights],
     )
     got = plane_spread(part, 3, 2)
+    weights = load(matrix1, [3], part)
     x3_two, acc, part = call(
         back_three_kernel,
         [block_shape, slab_shape, block_shape],
         place,
-        [acc, *inverse, *got, *parts1],
+        [acc, inverse, *got, *weights],
     )
     x3_one = plane_send(x3_two, (2, 1))
     got = plane_spread(part, 2, 1)
+    weights = load(matrix1, [2, 3], part)
     both_one, acc, part = call(
         back_two_kernel,
         [pair_shape, slab_shape, block_shape],
         place,
-        [acc, *inverse, *got, x3_one, *parts1],
+        [acc, inverse, *got, x3_one, *weights],
     )
     later = plane_send(both_one, (1, 0))
     got = plane_spread(part, 1, 0)
+    weights = load(matrix1, [1, 2, 3], part)
+    newest, both_zero, part = call(
+        back_one_kernel,
+        [block_shape, pair_shape, block_shape],
+        place,
+        [acc, inverse, *got, later, both_one, x3_two, *weights],
+    )
+    own = plane_send(newest, (0, 1), (1, 2), (2, 3))
+    got = plane_spread(part, 0, 1)
     late = after(late, part)
     rhs, link = call(
         second_front_kernel,
         [rows_shape, SDS((16, 1024), f32)],
         where,
-        [late, mark],
-        scratch=rows_scratch,
-    )
-    newest, both_zero, part = call(
-        back_one_kernel,
-        [block_shape, pair_shape, block_shape],
-        place,
-        [acc, *inverse, *got, later, both_one, x3_two, *parts1],
-    )
-    own = plane_send(newest, (0, 1), (1, 2), (2, 3))
-    got = plane_spread(part, 0, 1)
-    parts2 = split_factor(after(matrix2, part))
+        [mark],
+        [(late, (16, 64, 128), lambda i, place: (0, 0, 0))],
+        scratch=rows_scratch * 2,
+    )
+    weights = load(matrix2, [0], part, True)
     passing, acc = call(
         couple_kernel,
         [pair_shape, slab_shape],
         place,
-        [rhs, link, *got, own, both_zero, *parts2],
+        [rhs, link, *got, own, both_zero, *weights],
     )
     passed = plane_send(passing, (1, 2), (0, 3))
     got = plane_spread(acc, 1, 2)
+    weights = load(matrix2, [0, 1], acc, True)
     acc, kept = call(
         second_one_kernel,
         [slab_shape, SDS((2 * GROUP, ROWS, SLAB), f32)],
         place,
-        [rhs, link, acc, own, passing, passed, *got, *parts2],
+        [rhs, link, acc, own, passing, passed, *got, *weights],
     )
     sent = plane_send(kept, (2, 3), (1, 0))
     got = plane_spread(acc, 2, 3)
+    weights = load(matrix2, [0, 1, 2], acc, True)
     (acc,) = call(
         second_base_kernel,
         [slab_shape],
         place,
-        [rhs, link, acc, sent, own, *parts2],
+        [rhs, link, acc, sent, own, weights[0]],
     )
 
     at = jnp.arange(SLAB, dtype=jnp.int32)
@@ -586,7 +586,7 @@
         second_two_kernel,
         [SDS((8, ROWS, 256), f32)],
         place,
-        [acc, mine, sent, *got, *parts2],
+        [acc, mine, sent, *got, *weights[1:]],
     )
     arrived = lax.all_to_all(last, "col", 0, 0)
     return call(

time: 201 us -> 182 us (0.905)
  starting transfers between devices: 79.1 us -> 58.5 us
  local copies, waits for them, and re-layouts: 21.2 us -> 5.44 us
  waiting for transfers between devices: 32.5 us -> 47.9 us
  Pallas kernels: 40.2 us -> 44 us
    all_to_all x1 -> x0, starting transfers between devices: 11.4 us -> none  [on_device(): late = lax.all_to_all(late, 'row', 0, 0).reshape(1024, 128)]
    unnamed x62 -> x19, local copies, waits for them, and re-layouts: 13.8 us -> 2.48 us
    ppermute x38, waiting for transfers between devices: 18.9 us -> 30.1 us  [plane_send(): return lax.ppermute(value, 'row', pairs)]
    ppermute x38, starting transfers between devices: 54.8 us -> 45.7 us  [plane_send(): return lax.ppermute(value, 'row', pairs)]
    all_gather x2, waiting for transfers between devices: 0.02 us -> 4.52 us  [gather_blocks(): return lax.all_gather(turned, 'col').reshape(8, GROUP - 1, PIECE, 2 * SLAB)]
    pallas_call x19 -> x24, Pallas kernels: 40.2 us -> 44 us  [call(): pl.pallas_call(body, grid_spec=pltpu.PrefetchScalarGridSpec(num_scalar_pr...]
  transfers between devices with their start and end apart: 43 -> 43, of which waited for: 12 -> 18; matrix products, arithmetic and copies ran while one was open for 4% -> 2% of each run, Pallas kernels for 14% -> 20%
where the time goes in v7:
time: 182 us; the launch traced here: 181 us
  starting transfers between devices  58.5 us (32%)
  waiting for transfers between devices  47.9 us (26%)
  Pallas kernels  44 us (24%)
  between operations  14.5 us (8%)
  blocking collectives  9.95 us (5%)
  local copies, waits for them, and re-layouts  5.44 us (3%)
    ppermute x38, starting transfers between devices, plane_send(): return lax.ppermute(value, 'row', pairs)  45.7 us
    pallas_call x24, Pallas kernels, call(): pl.pallas_call(body, grid_spec=pltpu.PrefetchScalarGridSpec(num_scalar_pr...  44 us
    ppermute x38, waiting for transfers between devices, plane_send(): return lax.ppermute(value, 'row', pairs)  30.1 us
    all_to_all x1, blocking collectives, on_device(): arrived = lax.all_to_all(last, 'col', 0, 0)  9.95 us
    all_to_all x1, starting transfers between devices, on_device(): early = lax.all_to_all(early, 'row', 0, 0).reshape(1024, 128)  7.45 us
    all_to_all x1, waiting for transfers between devices, on_device(): early = lax.all_to_all(early, 'row', 0, 0).reshape(1024, 128)  7.08 us
    all_to_all x1, waiting for transfers between devices, on_device(): packed = lax.all_to_all(packed, 'col', 0, 0)  5.5 us
    all_to_all x1, starting transfers between devices, on_device(): packed = lax.all_to_all(packed, 'col', 0, 0)  5.31 us
  transfers between devices with their start and end apart: 43, of which 18 were waited for; matrix products, arithmetic and copies ran while one was open for 2% of the time, Pallas kernels for 20%

profile of v7, /device:TPU:4, one launch (start us, length us, event | category | flops | bytes accessed | tf_op | source)
XLA Modules:
  0.0 181.0 jit_solution(1381466482728496283)
XLA Ops:
  8.4 1.6 shard_map.88
  10.3 1.4 shard_map.86
  11.7 5.3 %all-to-all-start = ((f32[8,16,128]{2,1,0:T(8,128)}), f32[8,16,128]{2,1,0:T(8,128)S(1)}, u32[]{:S(2)}, u32[]{:S(2)}) async-start(f32[8,16,128]{2,1,0:T(8,128)} %shard_map.86), calls=%async_computation | async-start | bytes 131072 | tf_op jit(solution)/shard_map/all_to_all | solution.py:449
  17.1 5.5 %all-to-all-done = f32[8,16,128]{2,1,0:T(8,128)S(1)} async-done(((f32[8,16,128]{2,1,0:T(8,128)}), f32[8,16,128]{2,1,0:T(8,128)S(1)}, u32[]{:S(2)}, u32[]{:S(2)}) %all-to-all-start) | async-done | bytes 65568 | tf_op jit(solution)/shard_map/all_to_all | solution.py:449
  23.5 7.5 %all-to-all-start.1 = ((f32[16,64,128]{2,1,0:T(8,128)}), f32[16,64,128]{2,1,0:T(8,128)S(1)}, u32[]{:S(2)}, u32[]{:S(2)}) async-start(f32[16,64,128]{2,1,0:T(8,128)} %broadcast_in_dim.36), calls=%async_computation.1 | async-start | bytes 1048576 | tf_op jit(solution)/shard_map/all_to_all | solution.py:451
  32.9 7.1 %all-to-all-done.1 = f32[16,64,128]{2,1,0:T(8,128)S(1)} async-done(((f32[16,64,128]{2,1,0:T(8,128)}), f32[16,64,128]{2,1,0:T(8,128)S(1)}, u32[]{:S(2)}, u32[]{:S(2)}) %all-to-all-start.1) | async-done | bytes 524320 | tf_op jit(solution)/shard_map/all_to_all | solution.py:451
  39.9 1.9 %shard_map.87.rhs_ref = f32[32,1024]{1,0:T(8,128)S(1)} custom-call(s32[2048]{0:T(1024)S(1)} %bitcast.35, f32[1024,128]{1,0:T(8,128)S(1)} %bitcast.34, f32[2,1024]{1,0:T(2,128)S(1)} %get-tuple-element.100.mark_ref), custom_call_target="tpu_custom_call" | custom-call | tf_op jit(solution)/shard_map/pallas_call | solution.py:84
  42.2 2.3 %shard_map.89.acc_ref = f32[32,192]{1,0:T(8,128)S(1)} custom-call(s32[2]{0:T(128)S(1)} %pad_add_fusion.2.place_ref, f32[32,1024]{1,0:T(8,128)S(1)} %shard_map.87.rhs_ref, f32[8,3,96,384]{3,2,1,0:T(8,128)} %bitcast.37), custom_call_target="tpu_custom_call" | custom-call | tf_op jit(solution)/shard_map/pallas_call | solution.py:84
  45.2 1.3 collective-permute-start
  46.5 1.3 collective-permute-start.1
  47.8 1.3 collective-permute-start.2
  50.4 1.9 %shard_map.90.weight_ref = f32[768,384]{1,0:T(8,128)S(1)} custom-call(s32[2]{0:T(128)S(1)} %pad_add_fusion.2.place_ref, f32[8,3,96,384]{3,2,1,0:T(8,128)} %bitcast.38), custom_call_target="tpu_custom_call" | custom-call | tf_op jit(solution)/shard_map/pallas_call | solution.py:84
  52.3 2.2 %collective-permute-done.1.y1 = f32[32,192]{1,0:T(8,128)S(1)} collective-permute-done((f32[32,192]{1,0:T(8,128)S(1)}, f32[32,192]{1,0:T(8,128)S(1)}, u32[]{:S(2)}, u32[]{:S(2)}) %collective-permute-start.1) | collective-permute-done | bytes 24608 | tf_op jit(solution)/shard_map/ppermute | solution.py:414
  54.5 2.2 %collective-permute-done.2.y2 = f32[32,192]{1,0:T(8,128)S(1)} collective-permute-done((f32[32,192]{1,0:T(8,128)S(1)}, f32[32,192]{1,0:T(8,128)S(1)}, u32[]{:S(2)}, u32[]{:S(2)}) %collective-permute-start.2) | collective-permute-done | bytes 24608 | tf_op jit(solution)/shard_map/ppermute | solution.py:414
  65.2 2.3 %shard_map.92 = (f32[768,384]{1,0:T(8,128)S(1)}, f32[768,384]{1,0:T(8,128)S(1)}) custom-call(s32[2]{0:T(128)S(1)} %pad_add_fusion.2.place_ref, f32[8,3,96,384]{3,2,1,0:T(8,128)} %bitcast.39, f32[8,3,96,384]{3,2,1,0:T(8,128)} %bitcast.40), custom_call_target="tpu_custom_call" | custom-call | tf_op jit(solution)/shard_map/pallas_call | solution.py:84
  67.6 1.6 shard_map.93
  69.2 1.3 collective-permute-start.10
  74.4 1.9 %shard_map.94.weight_ref = f32[768,384]{1,0:T(8,128)S(1)} custom-call(s32[2]{0:T(128)S(1)} %pad_add_fusion.2.place_ref, f32[8,3,96,384]{3,2,1,0:T(8,128)} %bitcast.41), custom_call_target="tpu_custom_call" | custom-call | tf_op jit(solution)/shard_map/pallas_call | solution.py:84
  76.3 2.6 %collective-permute-done.10.p1 = f32[32,768]{1,0:T(8,128)S(1)} collective-permute-done((f32[32,768]{1,0:T(8,128)S(1)}, f32[32,768]{1,0:T(8,128)S(1)}, u32[]{:S(2)}, u32[]{:S(2)}) %collective-permute-start.10) | collective-permute-done | bytes 98336 | tf_op jit(solution)/shard_map/ppermute | solution.py:414
  78.9 6.4 %collective-permute-done.11.p2 = f32[32,768]{1,0:T(8,128)S(1)} collective-permute-done((f32[32,768]{1,0:T(8,128)S(1)}, f32[32,768]{1,0:T(8,128)S(1)}, u32[]{:S(2)}, u32[]{:S(2)}) %collective-permute-start.11) | collective-permute-done | bytes 98336 | tf_op jit(solution)/shard_map/ppermute | solution.py:414
  85.3 1.5 collective-permute-done.12.p3
  86.8 1.9 %collective-permute-done.9.p0 = f32[32,768]{1,0:T(8,128)S(1)} collective-permute-done((f32[32,768]{1,0:T(8,128)S(1)}, f32[32,768]{1,0:T(8,128)S(1)}, u32[]{:S(2)}, u32[]{:S(2)}) %collective-permute-start.9) | collective-permute-done | bytes 98336 | tf_op jit(solution)/shard_map/ppermute | solution.py:414
  88.7 1.4 shard_map.95
  90.1 1.3 collective-permute-start.13
  91.4 1.3 collective-permute-start.14
  92.7 1.3 collective-permute-start.15
  94.0 1.3 collective-permute-start.16
  95.3 1.3 collective-permute-start.17
  96.6 2.3 %shard_map.96 = (f32[768,384]{1,0:T(8,128)S(1)}, f32[768,384]{1,0:T(8,128)S(1)}) custom-call(s32[2]{0:T(128)S(1)} %pad_add_fusion.2.place_ref, f32[8,3,96,384]{3,2,1,0:T(8,128)} %bitcast.42, f32[8,3,96,384]{3,2,1,0:T(8,128)} %bitcast.43), custom_call_target="tpu_custom_call" | custom-call | tf_op jit(solution)/shard_map/pallas_call | solution.py:84
  99.0 1.5 collective-permute-done.16.p3
  101.5 1.6 shard_map.97
  106.4 2.8 %shard_map.98 = (f32[768,384]{1,0:T(8,128)S(1)}, f32[768,384]{1,0:T(8,128)S(1)}, f32[768,384]{1,0:T(8,128)S(1)}) custom-call(s32[2]{0:T(128)S(1)} %pad_add_fusion.2.place_ref, f32[8,3,96,384]{3,2,1,0:T(8,128)} %bitcast.44, f32[8,3,96,384]{3,2,1,0:T(8,128)} %bitcast.45, f32[8,3,96,384]{3,2,1,0:T(8,128)} %bitcast.46), custom_call_target="tpu_custom_call" | custom-call | tf_op jit(solution)/shard_map/pallas_call | solution.py:84
  109.3 2.0 %shard_map.99 = (f32[32,768]{1,0:T(8,128)S(1)}, f32[2,32,768]{2,1,0:T(8,128)S(1)}, f32[32,768]{1,0:T(8,128)S(1)}) custom-call(s32[2]{0:T(128)S(1)} %pad_add_fusion.2.place_ref, f32[32,192]{1,0:T(8,128)S(1)} %get-tuple-element.64.acc_ref, f32[192,1536]{1,0:T(8,128)S(1)} %bitcast.33, f32[32,768]{1,0:T(8,128)S(1)} %collective-permute-done.18.p0, ...), custom_call_target="tpu_custom_call" | custom-call | tf_op jit(solution)/shard_map/pallas_call | solution.py:84
  113.9 1.9 %collective-permute-start.27 = (f32[32,768]{1,0:T(8,128)S(1)}, f32[32,768]{1,0:T(8,128)S(1)}, u32[]{:S(2)}, u32[]{:S(2)}) collective-permute-start(f32[32,768]{1,0:T(8,128)S(1)} %get-tuple-element.75.newest_ref), channel_id=1, source_target_pairs={{0,32},{8,40},{16,48},{24,56},{32,64},{40,72},{48,80},{56,88},{64,... | collective-permute-start | bytes 294920 | tf_op jit(solution)/shard_map/ppermute | solution.py:414
  115.9 4.3 %shard_map.100 = (f32[32,1024]{1,0:T(8,128)S(1)}, f32[16,1024]{1,0:T(8,128)S(1)}) custom-call(s32[2048]{0:T(1024)S(1)} %bitcast.36, f32[2,1024]{1,0:T(2,128)S(1)} %get-tuple-element.100.mark_ref, f32[16,64,640]{2,1,0:T(8,128)} %bitcast.53), custom_call_target="tpu_custom_call" | custom-call | tf_op jit(solution)/shard_map/pallas_call | solution.py:84
  120.2 4.3 %all-gather.11.cloned.1.call-done = f32[2304,384]{1,0:T(8,128)} async-done(((f32[288,384]{1,0:T(8,128)}), f32[2304,384]{1,0:T(8,128)}) %all-gather.11.cloned.1.call-update) | async-done | bytes 3538960 | tf_op jit(solution)/shard_map/all_gather | solution.py:431
  124.5 1.9 %shard_map.101.weight_ref = f32[768,384]{1,0:T(8,128)S(1)} custom-call(s32[2]{0:T(128)S(1)} %pad_add_fusion.2.place_ref, f32[8,3,96,384]{3,2,1,0:T(8,128)} %bitcast.47), custom_call_target="tpu_custom_call" | custom-call | tf_op jit(solution)/shard_map/pallas_call | solution.py:84
  126.4 3.9 %collective-permute-done.27.own_ref = f32[32,768]{1,0:T(8,128)S(1)} collective-permute-done((f32[32,768]{1,0:T(8,128)S(1)}, f32[32,768]{1,0:T(8,128)S(1)}, u32[]{:S(2)}, u32[]{:S(2)}) %collective-permute-start.27) | collective-permute-done | bytes 98336 | tf_op jit(solution)/shard_map/ppermute | solution.py:414
  137.9 2.3 %shard_map.103 = (f32[768,384]{1,0:T(8,128)S(1)}, f32[768,384]{1,0:T(8,128)S(1)}) custom-call(s32[2]{0:T(128)S(1)} %pad_add_fusion.2.place_ref, f32[8,3,96,384]{3,2,1,0:T(8,128)} %bitcast.48, f32[8,3,96,384]{3,2,1,0:T(8,128)} %bitcast.49), custom_call_target="tpu_custom_call" | custom-call | tf_op jit(solution)/shard_map/pallas_call | solution.py:84
  140.2 3.9 %collective-permute-done.29.f0 = f32[32,192]{1,0:T(8,128)S(1)} collective-permute-done((f32[32,192]{1,0:T(8,128)S(1)}, f32[32,192]{1,0:T(8,128)S(1)}, u32[]{:S(2)}, u32[]{:S(2)}) %collective-permute-start.29) | collective-permute-done | bytes 24608 | tf_op jit(solution)/shard_map/ppermute | solution.py:414
  144.2 1.8 %collective-permute-done.30.f1 = f32[32,192]{1,0:T(8,128)S(1)} collective-permute-done((f32[32,192]{1,0:T(8,128)S(1)}, f32[32,192]{1,0:T(8,128)S(1)}, u32[]{:S(2)}, u32[]{:S(2)}) %collective-permute-start.30) | collective-permute-done | bytes 24608 | tf_op jit(solution)/shard_map/ppermute | solution.py:414
  147.5 1.3 collective-permute-start.33
  151.8 2.2 %collective-permute-start.36 = (f32[32,192]{1,0:T(8,128)S(1)}, f32[32,192]{1,0:T(8,128)S(1)}, u32[]{:S(2)}, u32[]{:S(2)}) collective-permute-start(f32[32,192]{1,0:T(8,128)S(1)} %get-tuple-element.84.acc_ref), channel_id=1, source_target_pairs={{64,112},{72,120},{80,96},{88,104},{65,113},{73,121},{81,97},{89,1... | collective-permute-start | bytes 73736 | tf_op jit(solution)/shard_map/ppermute | solution.py:414
  154.1 1.9 %collective-permute-start.37 = (f32[32,192]{1,0:T(8,128)S(1)}, f32[32,192]{1,0:T(8,128)S(1)}, u32[]{:S(2)}, u32[]{:S(2)}) collective-permute-start(f32[32,192]{1,0:T(8,128)S(1)} %get-tuple-element.84.acc_ref), channel_id=1, source_target_pairs={{64,120},{72,96},{80,104},{88,112},{65,121},{73,97},{81,105},{89,1... | collective-permute-start | bytes 73736 | tf_op jit(solution)/shard_map/ppermute | solution.py:414
  156.0 2.8 %shard_map.105 = (f32[768,384]{1,0:T(8,128)S(1)}, f32[768,384]{1,0:T(8,128)S(1)}, f32[768,384]{1,0:T(8,128)S(1)}) custom-call(s32[2]{0:T(128)S(1)} %pad_add_fusion.2.place_ref, f32[8,3,96,384]{3,2,1,0:T(8,128)} %bitcast.50, f32[8,3,96,384]{3,2,1,0:T(8,128)} %bitcast.51, f32[8,3,96,384]{3,2,1,0:T(8,128)} %bitcast.52), custom_call_target="tpu_custom_call" | custom-call | tf_op jit(solution)/shard_map/pallas_call | solution.py:84
  158.8 1.3 shard_map.107.cells_ref
  161.2 1.3 shard_map.108
  162.6 9.9 %all_to_all.15.got_ref = f32[8,32,256]{2,1,0:T(8,128)S(1)} all-to-all(f32[8,32,256]{2,1,0:T(8,128)S(1)} %shard_map.108), channel_id=1, replica_groups=mesh['row'=16,'col'=8] {'col'}, dimensions={0} | all-to-all | bytes 524288 | tf_op jit(solution)/shard_map/all_to_all | solution.py:591
  (108 shorter events, 41.2 us)
Async XLA Ops:
  7.2 2.9 %copy-start.4 = (f32[2,4,6,128]{3,1,2,0:T(4,128)S(1)}, f32[2,4,6,128]{3,1,2,0:T(4,128)}, u32[]{:S(2)}) copy-start(f32[2,4,6,128]{3,1,2,0:T(4,128)} %param.7) | copy-start | bytes 73732
  7.2 2.9 %copy-start.6 = (f32[2,4,6]{2,1,0:T(4,128)S(1)}, f32[2,4,6]{2,1,0:T(4,128)}, u32[]{:S(2)}) copy-start(f32[2,4,6]{2,1,0:T(4,128)} %param.9) | copy-start | bytes 580
  7.2 9.8 %copy-start.3 = (s32[3072]{0:T(1024)S(1)}, s32[3072]{0:T(1024)}, u32[]{:S(2)}) copy-start(s32[3072]{0:T(1024)} %param.13) | copy-start | bytes 36868
  7.2 35.0 %all-gather.7.cloned.1.call-start = ((), (), s32[]{:S(2)}) async-start(), calls=%async_computation.3 | async-start | bytes 3981312 | tf_op jit(solution)/shard_map/all_gather | solution.py:431
  10.1 21.1 %copy-start.2 = (f32[2,192,384]{2,1,0:T(8,128)S(1)}, f32[2,192,384]{2,1,0:T(8,128)}, u32[]{:S(2)}) copy-start(f32[2,192,384]{2,1,0:T(8,128)} %param.11) | copy-start | bytes 1769476
  11.7 10.9 %all-to-all-start = ((f32[8,16,128]{2,1,0:T(8,128)}), f32[8,16,128]{2,1,0:T(8,128)S(1)}, u32[]{:S(2)}, u32[]{:S(2)}) async-start(f32[8,16,128]{2,1,0:T(8,128)} %shard_map.86), calls=%async_computation | async-start | bytes 131072 | tf_op jit(solution)/shard_map/all_to_all | solution.py:449
  23.5 16.5 %all-to-all-start.1 = ((f32[16,64,128]{2,1,0:T(8,128)}), f32[16,64,128]{2,1,0:T(8,128)S(1)}, u32[]{:S(2)}, u32[]{:S(2)}) async-start(f32[16,64,128]{2,1,0:T(8,128)} %broadcast_in_dim.36), calls=%async_computation.1 | async-start | bytes 1048576 | tf_op jit(solution)/shard_map/all_to_all | solution.py:451
  30.9 85.0 %all-gather.9.cloned.1.call-start = ((), (), s32[]{:S(2)}) async-start(), calls=%async_computation.4 | async-start | bytes 2785280 | tf_op jit(solution)/shard_map/all_gather | solution.py:494
  44.5 80.0 %all-gather.11.cloned.1.call-start = ((), (), s32[]{:S(2)}) async-start(), calls=%async_computation.5 | async-start | bytes 3981312 | tf_op jit(solution)/shard_map/all_gather | solution.py:431
  45.2 7.1 %collective-permute-start = (f32[32,192]{1,0:T(8,128)S(1)}, f32[32,192]{1,0:T(8,128)S(1)}, u32[]{:S(2)}, u32[]{:S(2)}) collective-permute-start(f32[32,192]{1,0:T(8,128)S(1)} %shard_map.89.acc_ref), channel_id=1, source_target_pairs={{32,64},{40,72},{48,80},{56,88},{33,65},{41,73},{49,81},{57,89},{3... | collective-permute-start | bytes 73736 | tf_op jit(solution)/shard_map/ppermute | solution.py:414
  46.5 8.0 %collective-permute-start.1 = (f32[32,192]{1,0:T(8,128)S(1)}, f32[32,192]{1,0:T(8,128)S(1)}, u32[]{:S(2)}, u32[]{:S(2)}) collective-permute-start(f32[32,192]{1,0:T(8,128)S(1)} %shard_map.89.acc_ref), channel_id=1, source_target_pairs={{32,72},{40,80},{48,88},{56,64},{33,73},{41,81},{49,89},{57,65},{3... | collective-permute-start | bytes 73736 | tf_op jit(solution)/shard_map/ppermute | solution.py:414
  47.8 8.9 %collective-permute-start.2 = (f32[32,192]{1,0:T(8,128)S(1)}, f32[32,192]{1,0:T(8,128)S(1)}, u32[]{:S(2)}, u32[]{:S(2)}) collective-permute-start(f32[32,192]{1,0:T(8,128)S(1)} %shard_map.89.acc_ref), channel_id=1, source_target_pairs={{32,80},{40,88},{48,64},{56,72},{33,81},{41,89},{49,65},{57,73},{3... | collective-permute-start | bytes 73736 | tf_op jit(solution)/shard_map/ppermute | solution.py:414
  49.1 8.4 %collective-permute-start.3 = (f32[32,192]{1,0:T(8,128)S(1)}, f32[32,192]{1,0:T(8,128)S(1)}, u32[]{:S(2)}, u32[]{:S(2)}) collective-permute-start(f32[32,192]{1,0:T(8,128)S(1)} %shard_map.89.acc_ref), channel_id=1, source_target_pairs={{32,88},{40,64},{48,72},{56,80},{33,89},{41,65},{49,73},{57,81},{3... | collective-permute-start | bytes 73736 | tf_op jit(solution)/shard_map/ppermute | solution.py:414
  52.3 12.8 %copy-start.1 = (f32[2,768,192]{1,2,0:T(8,128)S(1)}, f32[2,768,192]{1,2,0:T(8,128)}, u32[]{:S(2)}) copy-start(f32[2,768,192]{1,2,0:T(8,128)} %param.12) | copy-start | bytes 3538948
  58.6 9.0 %collective-permute-start.4 = (f32[4,32,192]{2,1,0:T(8,128)S(1)}, f32[4,32,192]{2,1,0:T(8,128)S(1)}, u32[]{:S(2)}, u32[]{:S(2)}) collective-permute-start(f32[4,32,192]{2,1,0:T(8,128)S(1)} %get-tuple-element.51), channel_id=1, source_target_pairs={{64,96},{72,104},{80,112},{88,120},{65,97},{73,105},{81,113},{89,1... | collective-permute-start | bytes 294920 | tf_op jit(solution)/shard_map/ppermute | solution.py:414
  59.9 7.7 %collective-permute-start.5 = (f32[32,192]{1,0:T(8,128)S(1)}, f32[32,192]{1,0:T(8,128)S(1)}, u32[]{:S(2)}, u32[]{:S(2)}) collective-permute-start(f32[32,192]{1,0:T(8,128)S(1)} %get-tuple-element.49.acc_ref), channel_id=1, source_target_pairs={{64,96},{72,104},{80,112},{88,120},{65,97},{73,105},{81,113},{89,1... | collective-permute-start | bytes 73736 | tf_op jit(solution)/shard_map/ppermute | solution.py:414
  61.1 6.4 %collective-permute-start.6 = (f32[32,192]{1,0:T(8,128)S(1)}, f32[32,192]{1,0:T(8,128)S(1)}, u32[]{:S(2)}, u32[]{:S(2)}) collective-permute-start(f32[32,192]{1,0:T(8,128)S(1)} %get-tuple-element.49.acc_ref), channel_id=1, source_target_pairs={{64,104},{72,112},{80,120},{88,96},{65,105},{73,113},{81,121},{89,... | collective-permute-start | bytes 73736 | tf_op jit(solution)/shard_map/ppermute | solution.py:414
  62.4 5.1 %collective-permute-start.7 = (f32[32,192]{1,0:T(8,128)S(1)}, f32[32,192]{1,0:T(8,128)S(1)}, u32[]{:S(2)}, u32[]{:S(2)}) collective-permute-start(f32[32,192]{1,0:T(8,128)S(1)} %get-tuple-element.49.acc_ref), channel_id=1, source_target_pairs={{64,112},{72,120},{80,96},{88,104},{65,113},{73,121},{81,97},{89,1... | collective-permute-start | bytes 73736 | tf_op jit(solution)/shard_map/ppermute | solution.py:414
  63.7 3.8 %collective-permute-start.8 = (f32[32,192]{1,0:T(8,128)S(1)}, f32[32,192]{1,0:T(8,128)S(1)}, u32[]{:S(2)}, u32[]{:S(2)}) collective-permute-start(f32[32,192]{1,0:T(8,128)S(1)} %get-tuple-element.49.acc_ref), channel_id=1, source_target_pairs={{64,120},{72,96},{80,104},{88,112},{65,121},{73,97},{81,105},{89,1... | collective-permute-start | bytes 73736 | tf_op jit(solution)/shard_map/ppermute | solution.py:414
  69.2 9.7 %collective-permute-start.10 = (f32[32,768]{1,0:T(8,128)S(1)}, f32[32,768]{1,0:T(8,128)S(1)}, u32[]{:S(2)}, u32[]{:S(2)}) collective-permute-start(f32[32,768]{1,0:T(8,128)S(1)} %get-tuple-element.56), channel_id=1, source_target_pairs={{96,72},{104,80},{112,88},{120,64},{97,73},{105,81},{113,89},{121,... | collective-permute-start | bytes 294920 | tf_op jit(solution)/shard_map/ppermute | solution.py:414
  70.5 14.8 %collective-permute-start.11 = (f32[32,768]{1,0:T(8,128)S(1)}, f32[32,768]{1,0:T(8,128)S(1)}, u32[]{:S(2)}, u32[]{:S(2)}) collective-permute-start(f32[32,768]{1,0:T(8,128)S(1)} %get-tuple-element.56), channel_id=1, source_target_pairs={{96,80},{104,88},{112,64},{120,72},{97,81},{105,89},{113,65},{121,... | collective-permute-start | bytes 294920 | tf_op jit(solution)/shard_map/ppermute | solution.py:414
  71.8 15.0 %collective-permute-start.12 = (f32[32,768]{1,0:T(8,128)S(1)}, f32[32,768]{1,0:T(8,128)S(1)}, u32[]{:S(2)}, u32[]{:S(2)}) collective-permute-start(f32[32,768]{1,0:T(8,128)S(1)} %get-tuple-element.56), channel_id=1, source_target_pairs={{96,88},{104,64},{112,72},{120,80},{97,89},{105,65},{113,73},{121,... | collective-permute-start | bytes 294920 | tf_op jit(solution)/shard_map/ppermute | solution.py:414
  73.1 15.6 %collective-permute-start.9 = (f32[32,768]{1,0:T(8,128)S(1)}, f32[32,768]{1,0:T(8,128)S(1)}, u32[]{:S(2)}, u32[]{:S(2)}) collective-permute-start(f32[32,768]{1,0:T(8,128)S(1)} %get-tuple-element.56), channel_id=1, source_target_pairs={{96,64},{104,72},{112,80},{120,88},{97,65},{105,73},{113,81},{121,... | collective-permute-start | bytes 294920 | tf_op jit(solution)/shard_map/ppermute | solution.py:414
  90.1 8.8 %collective-permute-start.13 = (f32[32,768]{1,0:T(8,128)S(1)}, f32[32,768]{1,0:T(8,128)S(1)}, u32[]{:S(2)}, u32[]{:S(2)}) collective-permute-start(f32[32,768]{1,0:T(8,128)S(1)} %get-tuple-element.59), channel_id=1, source_target_pairs={{64,32},{72,40},{80,48},{88,56},{65,33},{73,41},{81,49},{89,57},{6... | collective-permute-start | bytes 294920 | tf_op jit(solution)/shard_map/ppermute | solution.py:414
  91.4 7.6 %collective-permute-start.14 = (f32[32,768]{1,0:T(8,128)S(1)}, f32[32,768]{1,0:T(8,128)S(1)}, u32[]{:S(2)}, u32[]{:S(2)}) collective-permute-start(f32[32,768]{1,0:T(8,128)S(1)} %get-tuple-element.59), channel_id=1, source_target_pairs={{64,40},{72,48},{80,56},{88,32},{65,41},{73,49},{81,57},{89,33},{6... | collective-permute-start | bytes 294920 | tf_op jit(solution)/shard_map/ppermute | solution.py:414
  92.7 6.3 %collective-permute-start.15 = (f32[32,768]{1,0:T(8,128)S(1)}, f32[32,768]{1,0:T(8,128)S(1)}, u32[]{:S(2)}, u32[]{:S(2)}) collective-permute-start(f32[32,768]{1,0:T(8,128)S(1)} %get-tuple-element.59), channel_id=1, source_target_pairs={{64,48},{72,56},{80,32},{88,40},{65,49},{73,57},{81,33},{89,41},{6... | collective-permute-start | bytes 294920 | tf_op jit(solution)/shard_map/ppermute | solution.py:414
  94.0 6.4 %collective-permute-start.16 = (f32[32,768]{1,0:T(8,128)S(1)}, f32[32,768]{1,0:T(8,128)S(1)}, u32[]{:S(2)}, u32[]{:S(2)}) collective-permute-start(f32[32,768]{1,0:T(8,128)S(1)} %get-tuple-element.59), channel_id=1, source_target_pairs={{64,56},{72,32},{80,40},{88,48},{65,57},{73,33},{81,41},{89,49},{6... | collective-permute-start | bytes 294920 | tf_op jit(solution)/shard_map/ppermute | solution.py:414
  95.3 6.2 %collective-permute-start.17 = (f32[32,768]{1,0:T(8,128)S(1)}, f32[32,768]{1,0:T(8,128)S(1)}, u32[]{:S(2)}, u32[]{:S(2)}) collective-permute-start(f32[32,768]{1,0:T(8,128)S(1)} %get-tuple-element.60.x3_ref), channel_id=1, source_target_pairs={{64,32},{72,40},{80,48},{88,56},{65,33},{73,41},{81,49},{89,57},{6... | collective-permute-start | bytes 294920 | tf_op jit(solution)/shard_map/ppermute | solution.py:414
  103.1 6.2 %collective-permute-start.22 = (f32[2,32,768]{2,1,0:T(8,128)S(1)}, f32[2,32,768]{2,1,0:T(8,128)S(1)}, u32[]{:S(2)}, u32[]{:S(2)}) collective-permute-start(f32[2,32,768]{2,1,0:T(8,128)S(1)} %get-tuple-element.66.x2_ref), channel_id=1, source_target_pairs={{32,0},{40,8},{48,16},{56,24},{33,1},{41,9},{49,17},{57,25},{34,2}... | collective-permute-start | bytes 589832 | tf_op jit(solution)/shard_map/ppermute | solution.py:414
  103.7 5.5 %collective-permute-start.18 = (f32[32,768]{1,0:T(8,128)S(1)}, f32[32,768]{1,0:T(8,128)S(1)}, u32[]{:S(2)}, u32[]{:S(2)}) collective-permute-start(f32[32,768]{1,0:T(8,128)S(1)} %get-tuple-element.65), channel_id=1, source_target_pairs={{32,0},{40,8},{48,16},{56,24},{33,1},{41,9},{49,17},{57,25},{34,2}... | collective-permute-start | bytes 294920 | tf_op jit(solution)/shard_map/ppermute | solution.py:414
  104.4 4.8 %collective-permute-start.19 = (f32[32,768]{1,0:T(8,128)S(1)}, f32[32,768]{1,0:T(8,128)S(1)}, u32[]{:S(2)}, u32[]{:S(2)}) collective-permute-start(f32[32,768]{1,0:T(8,128)S(1)} %get-tuple-element.65), channel_id=1, source_target_pairs={{32,8},{40,16},{48,24},{56,0},{33,9},{41,17},{49,25},{57,1},{34,10... | collective-permute-start | bytes 294920 | tf_op jit(solution)/shard_map/ppermute | solution.py:414
  105.1 4.1 %collective-permute-start.20 = (f32[32,768]{1,0:T(8,128)S(1)}, f32[32,768]{1,0:T(8,128)S(1)}, u32[]{:S(2)}, u32[]{:S(2)}) collective-permute-start(f32[32,768]{1,0:T(8,128)S(1)} %get-tuple-element.65), channel_id=1, source_target_pairs={{32,16},{40,24},{48,0},{56,8},{33,17},{41,25},{49,1},{57,9},{34,18... | collective-permute-start | bytes 294920 | tf_op jit(solution)/shard_map/ppermute | solution.py:414
  105.8 3.5 %collective-permute-start.21 = (f32[32,768]{1,0:T(8,128)S(1)}, f32[32,768]{1,0:T(8,128)S(1)}, u32[]{:S(2)}, u32[]{:S(2)}) collective-permute-start(f32[32,768]{1,0:T(8,128)S(1)} %get-tuple-element.65), channel_id=1, source_target_pairs={{32,24},{40,0},{48,8},{56,16},{33,25},{41,1},{49,9},{57,17},{34,26... | collective-permute-start | bytes 294920 | tf_op jit(solution)/shard_map/ppermute | solution.py:414
  111.2 15.1 %collective-permute-start.23 = (f32[32,768]{1,0:T(8,128)S(1)}, f32[32,768]{1,0:T(8,128)S(1)}, u32[]{:S(2)}, u32[]{:S(2)}) collective-permute-start(f32[32,768]{1,0:T(8,128)S(1)} %get-tuple-element.71), channel_id=1, source_target_pairs={{0,32},{8,40},{16,48},{24,56},{1,33},{9,41},{17,49},{25,57},{2,34}... | collective-permute-start | bytes 294920 | tf_op jit(solution)/shard_map/ppermute | solution.py:414
  111.9 14.5 %collective-permute-start.24 = (f32[32,768]{1,0:T(8,128)S(1)}, f32[32,768]{1,0:T(8,128)S(1)}, u32[]{:S(2)}, u32[]{:S(2)}) collective-permute-start(f32[32,768]{1,0:T(8,128)S(1)} %get-tuple-element.71), channel_id=1, source_target_pairs={{0,40},{8,48},{16,56},{24,32},{1,41},{9,49},{17,57},{25,33},{2,42}... | collective-permute-start | bytes 294920 | tf_op jit(solution)/shard_map/ppermute | solution.py:414
  112.6 13.8 %collective-permute-start.25 = (f32[32,768]{1,0:T(8,128)S(1)}, f32[32,768]{1,0:T(8,128)S(1)}, u32[]{:S(2)}, u32[]{:S(2)}) collective-permute-start(f32[32,768]{1,0:T(8,128)S(1)} %get-tuple-element.71), channel_id=1, source_target_pairs={{0,48},{8,56},{16,32},{24,40},{1,49},{9,57},{17,33},{25,41},{2,50}... | collective-permute-start | bytes 294920 | tf_op jit(solution)/shard_map/ppermute | solution.py:414
  113.3 13.1 %collective-permute-start.26 = (f32[32,768]{1,0:T(8,128)S(1)}, f32[32,768]{1,0:T(8,128)S(1)}, u32[]{:S(2)}, u32[]{:S(2)}) collective-permute-start(f32[32,768]{1,0:T(8,128)S(1)} %get-tuple-element.71), channel_id=1, source_target_pairs={{0,56},{8,32},{16,40},{24,48},{1,57},{9,33},{17,41},{25,49},{2,58}... | collective-permute-start | bytes 294920 | tf_op jit(solution)/shard_map/ppermute | solution.py:414
  113.9 16.4 %collective-permute-start.27 = (f32[32,768]{1,0:T(8,128)S(1)}, f32[32,768]{1,0:T(8,128)S(1)}, u32[]{:S(2)}, u32[]{:S(2)}) collective-permute-start(f32[32,768]{1,0:T(8,128)S(1)} %get-tuple-element.75.newest_ref), channel_id=1, source_target_pairs={{0,32},{8,40},{16,48},{24,56},{32,64},{40,72},{48,80},{56,88},{64,... | collective-permute-start | bytes 294920 | tf_op jit(solution)/shard_map/ppermute | solution.py:414
  131.4 14.9 %collective-permute-start.28 = (f32[2,32,768]{2,1,0:T(8,128)S(1)}, f32[2,32,768]{2,1,0:T(8,128)S(1)}, u32[]{:S(2)}, u32[]{:S(2)}) collective-permute-start(f32[2,32,768]{2,1,0:T(8,128)S(1)} %get-tuple-element.80.sent_ref.pass_ref), channel_id=1, source_target_pairs={{32,64},{40,72},{48,80},{56,88},{0,96},{8,104},{16,112},{24,120},{... | collective-permute-start | bytes 589832 | tf_op jit(solution)/shard_map/ppermute | solution.py:414
  132.7 11.5 %collective-permute-start.29 = (f32[32,192]{1,0:T(8,128)S(1)}, f32[32,192]{1,0:T(8,128)S(1)}, u32[]{:S(2)}, u32[]{:S(2)}) collective-permute-start(f32[32,192]{1,0:T(8,128)S(1)} %get-tuple-element.79.acc_ref), channel_id=1, source_target_pairs={{32,64},{40,72},{48,80},{56,88},{33,65},{41,73},{49,81},{57,89},{3... | collective-permute-start | bytes 73736 | tf_op jit(solution)/shard_map/ppermute | solution.py:414
  134.0 12.0 %collective-permute-start.30 = (f32[32,192]{1,0:T(8,128)S(1)}, f32[32,192]{1,0:T(8,128)S(1)}, u32[]{:S(2)}, u32[]{:S(2)}) collective-permute-start(f32[32,192]{1,0:T(8,128)S(1)} %get-tuple-element.79.acc_ref), channel_id=1, source_target_pairs={{32,72},{40,80},{48,88},{56,64},{33,73},{41,81},{49,89},{57,65},{3... | collective-permute-start | bytes 73736 | tf_op jit(solution)/shard_map/ppermute | solution.py:414
  135.3 10.8 %collective-permute-start.31 = (f32[32,192]{1,0:T(8,128)S(1)}, f32[32,192]{1,0:T(8,128)S(1)}, u32[]{:S(2)}, u32[]{:S(2)}) collective-permute-start(f32[32,192]{1,0:T(8,128)S(1)} %get-tuple-element.79.acc_ref), channel_id=1, source_target_pairs={{32,80},{40,88},{48,64},{56,72},{33,81},{41,89},{49,65},{57,73},{3... | collective-permute-start | bytes 73736 | tf_op jit(solution)/shard_map/ppermute | solution.py:414
  136.6 9.7 %collective-permute-start.32 = (f32[32,192]{1,0:T(8,128)S(1)}, f32[32,192]{1,0:T(8,128)S(1)}, u32[]{:S(2)}, u32[]{:S(2)}) collective-permute-start(f32[32,192]{1,0:T(8,128)S(1)} %get-tuple-element.79.acc_ref), channel_id=1, source_target_pairs={{32,88},{40,64},{48,72},{56,80},{33,89},{41,65},{49,73},{57,81},{3... | collective-permute-start | bytes 73736 | tf_op jit(solution)/shard_map/ppermute | solution.py:414
  147.5 11.3 %collective-permute-start.33 = (f32[8,32,192]{2,1,0:T(8,128)S(1)}, f32[8,32,192]{2,1,0:T(8,128)S(1)}, u32[]{:S(2)}, u32[]{:S(2)}) collective-permute-start(f32[8,32,192]{2,1,0:T(8,128)S(1)} %get-tuple-element.85), channel_id=1, source_target_pairs={{64,96},{72,104},{80,112},{88,120},{32,0},{40,8},{48,16},{56,24},{... | collective-permute-start | bytes 589832 | tf_op jit(solution)/shard_map/ppermute | solution.py:414
  149.3 11.9 %collective-permute-start.34 = (f32[32,192]{1,0:T(8,128)S(1)}, f32[32,192]{1,0:T(8,128)S(1)}, u32[]{:S(2)}, u32[]{:S(2)}) collective-permute-start(f32[32,192]{1,0:T(8,128)S(1)} %get-tuple-element.84.acc_ref), channel_id=1, source_target_pairs={{64,96},{72,104},{80,112},{88,120},{65,97},{73,105},{81,113},{89,1... | collective-permute-start | bytes 73736 | tf_op jit(solution)/shard_map/ppermute | solution.py:414
  150.5 10.6 %collective-permute-start.35 = (f32[32,192]{1,0:T(8,128)S(1)}, f32[32,192]{1,0:T(8,128)S(1)}, u32[]{:S(2)}, u32[]{:S(2)}) collective-permute-start(f32[32,192]{1,0:T(8,128)S(1)} %get-tuple-element.84.acc_ref), channel_id=1, source_target_pairs={{64,104},{72,112},{80,120},{88,96},{65,105},{73,113},{81,121},{89,... | collective-permute-start | bytes 73736 | tf_op jit(solution)/shard_map/ppermute | solution.py:414
  151.8 9.4 %collective-permute-start.36 = (f32[32,192]{1,0:T(8,128)S(1)}, f32[32,192]{1,0:T(8,128)S(1)}, u32[]{:S(2)}, u32[]{:S(2)}) collective-permute-start(f32[32,192]{1,0:T(8,128)S(1)} %get-tuple-element.84.acc_ref), channel_id=1, source_target_pairs={{64,112},{72,120},{80,96},{88,104},{65,113},{73,121},{81,97},{89,1... | collective-permute-start | bytes 73736 | tf_op jit(solution)/shard_map/ppermute | solution.py:414
  154.1 7.2 %collective-permute-start.37 = (f32[32,192]{1,0:T(8,128)S(1)}, f32[32,192]{1,0:T(8,128)S(1)}, u32[]{:S(2)}, u32[]{:S(2)}) collective-permute-start(f32[32,192]{1,0:T(8,128)S(1)} %get-tuple-element.84.acc_ref), channel_id=1, source_target_pairs={{64,120},{72,96},{80,104},{88,112},{65,121},{73,97},{81,105},{89,1... | collective-permute-start | bytes 73736 | tf_op jit(solution)/shard_map/ppermute | solution.py:414
  (2 other events, 2.7 us)
Sparse Core Ops, SparseCore 0:
  10.2 31.9 all-gather.6
  44.9 48.2 all-gather.8
  94.9 29.4 all-gather.10

commit v8 on v7

--- a/solution.py
+++ b/solution.py
@@ -14,7 +14,7 @@
 BLOCK = 768
 PIECE = 96
 CELLS = 24
-LATE = 5
+LATE = 2
 VMEM = 16 * 1024 * 1024
 
 SDS = jax.ShapeDtypeStruct
@@ -291,13 +291,14 @@
 
 
 def couple_kernel(
-    place_ref, rhs_ref, link_ref, p0, p1, p2, p3, own_ref, zero_ref, weight_ref, pass_ref, out_ref
+    place_ref, rhs_ref, link_ref, p0, p1, p2, p3, own_ref, zero_ref, weight_ref, x0_ref, pass_ref, out_ref
 ):
     x0 = add_refs([p0, p1, p2, p3])
     slab = second_slab(rhs_ref, link_ref, own_ref[...], place_ref[1])
     out_ref[...] = slab - complex_dot(
         second_block(rhs_ref, link_ref, x0), weight_ref[...]
     )
+    x0_ref[...] = x0
     zero = place_ref[0] == 0
     pass_ref[0] = jnp.where(zero, zero_ref[0], x0)
     pass_ref[1] = jnp.where(zero, zero_ref[1], own_ref[...])
@@ -322,24 +323,24 @@
 ):
     plane, q = place_ref[0], place_ref[1]
     x0 = jnp.where(plane == 1, sent_ref[0], got_ref[0])
-    for s in range(GROUP):
-        keep_ref[GROUP + s] = x0[:, SLAB * s : SLAB * s + SLAB]
     slab = second_slab(rhs_ref, link_ref, own_ref[...], q)
     product = complex_dot(second_block(rhs_ref, link_ref, x0), weight0_ref[...])
     slabs = [f0[...], f1[...], f2[...], f3[...]]
     solved = slab - product - slabs_dot(slabs, weight1_ref, q, keep_ref)
     out_ref[...] = jnp.where(plane == 1, acc_ref[...], solved)
-
-
-def joined(ref, first):
-    return jnp.concatenate([ref[first + s] for s in range(GROUP)], axis=1)
+    for s in range(GROUP):
+        keep_ref[s] = jnp.where(plane == 1, x0[:, SLAB * s : SLAB * s + SLAB], keep_ref[s])
+
+
+def joined(ref):
+    return jnp.concatenate([ref[s] for s in range(GROUP)], axis=1)
 
 
 def second_base_kernel(
-    place_ref, rhs_ref, link_ref, acc_ref, got_ref, own_ref, weight_ref, out_ref
+    place_ref, rhs_ref, link_ref, acc_ref, got_ref, x0_three, own_ref, weight_ref, out_ref
 ):
     plane, q = place_ref[0], place_ref[1]
-    x0 = joined(got_ref, GROUP)
+    x0 = jnp.where(plane == 0, joined(got_ref), x0_three[...])
     own = jnp.where(plane == 0, x0, own_ref[...])
     slab = second_slab(rhs_ref, link_ref, own, q)
     product = complex_dot(second_block(rhs_ref, link_ref, x0), weight_ref[...])
@@ -349,7 +350,7 @@
 
 
 def cells_kernel(
-    where_ref, got_ref, pass_ref, passed_ref, newest_ref, own_ref, both_zero, later_ref, x3_one, out_ref, front_ref, rows_ref
+    where_ref, got_ref, x0_three, pass_ref, passed_ref, newest_ref, own_ref, both_zero, later_ref, x3_one, out_ref, front_ref, rows_ref
 ):
     plane = where_ref[SLAB]
 
@@ -359,9 +360,8 @@
             value = jnp.where(plane == at, by_plane[at], value)
         return value
 
-    last = joined(got_ref, GROUP)
     blocks = (
-        pick(last, pass_ref[0], passed_ref[0], last),
+        pick(joined(got_ref), pass_ref[0], passed_ref[0], x0_three[...]),
         pick(newest_ref[...], own_ref[...], passed_ref[1], passed_ref[0]),
         pick(both_zero[1], newest_ref[...], own_ref[...], passed_ref[1]),
         pick(later_ref[1], x3_one[...], newest_ref[...], own_ref[...]),
@@ -388,6 +388,7 @@
         - sent_dot(sent_ref, weight1_ref)
         - slabs_dot(slabs, weight2_ref, place_ref[1])
     )
+    solved = jnp.where(place_ref[0] == 0, acc_ref[...], solved)
     lane = lax.broadcasted_iota(jnp.int32, (ROWS, 128), 1)
     tail = jnp.concatenate([solved[:, 128:], jnp.zeros((ROWS, 64), f32)], axis=1)
     for c in range(8):
@@ -434,8 +435,9 @@
         turn_first_kernel,
         [SDS((3 * PIECE, 2 * SLAB), f32)],
         place,
-        [factor1],
-        scratch=[pltpu.VMEM((4 * PIECE, 2 * SLAB), f32)],
+        [],
+        [(factor1, factor1.shape, lambda i, place: (0, 0, 0))],
+        [pltpu.VMEM((4 * PIECE, 2 * SLAB), f32)],
     )
     matrix1 = gather_blocks(turned1)
 
@@ -545,21 +547,23 @@
         scratch=rows_scratch * 2,
     )
     weights = load(matrix2, [0], part, True)
-    passing, acc = call(
+    x0_one, passing, acc = call(
         couple_kernel,
-        [pair_shape, slab_shape],
+        [block_shape, pair_shape, slab_shape],
         place,
         [rhs, link, *got, own, both_zero, *weights],
     )
     passed = plane_send(passing, (1, 2), (0, 3))
     got = plane_spread(acc, 1, 2)
+    x0_three = plane_send(after(x0_one, got[1]), (1, 3))
     weights = load(matrix2, [0, 1], acc, True)
     acc, kept = call(
         second_one_kernel,
-        [slab_shape, SDS((2 * GROUP, ROWS, SLAB), f32)],
+        [slab_shape, sent_shape],
         place,
         [rhs, link, acc, own, passing, passed, *got, *weights],
     )
+    acc, kept, x0_three = lax.optimization_barrier((acc, kept, x0_three))
     sent = plane_send(kept, (2, 3), (1, 0))
     got = plane_spread(acc, 2, 3)
     weights = load(matrix2, [0, 1, 2], acc, True)
@@ -567,7 +571,7 @@
         second_base_kernel,
         [slab_shape],
         place,
-        [rhs, link, acc, sent, own, weights[0]],
+        [rhs, link, acc, sent, x0_three, own, weights[0]],
     )
 
     at = jnp.arange(SLAB, dtype=jnp.int32)
@@ -579,7 +583,7 @@
         cells_kernel,
         [SDS((8, ROWS, 128), f32)],
         jnp.concatenate([slots, place]),
-        [sent, passing, passed, newest, own, both_zero, later, x3_one],
+        [sent, x0_three, passing, passed, newest, own, both_zero, later, x3_one],
         scratch=[pltpu.VMEM((4 * BLOCK, 128), f32), pltpu.VMEM((128, 128), f32)],
     )
     (last,) = call(

time: 182 us -> 183 us (level)
  waiting for transfers between devices: 47.9 us -> 43.8 us
  starting transfers between devices: 58.5 us -> 62.2 us
    ppermute x38 -> x39, starting transfers between devices: 45.7 us -> 49.3 us  [plane_send(): return lax.ppermute(value, 'row', pairs)]
    all_gather x2, waiting for transfers between devices: 4.52 us -> 1.75 us  [gather_blocks(): return lax.all_gather(turned, 'col').reshape(8, GROUP - 1, PIECE, 2 * SLAB)]
    ppermute x38 -> x39, waiting for transfers between devices: 30.1 us -> 28.7 us  [plane_send(): return lax.ppermute(value, 'row', pairs)]
  transfers between devices with their start and end apart: 43 -> 44, of which waited for: 18 -> 17; matrix products, arithmetic and copies ran while one was open for 2% -> 2% of each run, Pallas kernels for 20% -> 21%
where the time goes in v8:
time: 183 us; the launch traced here: 181 us
  starting transfers between devices  62.2 us (34%)
  Pallas kernels  45.1 us (25%)
  waiting for transfers between devices  43.8 us (24%)
  between operations  14.5 us (8%)
  blocking collectives  9.95 us (5%)
  local copies, waits for them, and re-layouts  4.33 us (2%)
    ppermute x39, starting transfers between devices, plane_send(): return lax.ppermute(value, 'row', pairs)  49.3 us
    pallas_call x24, Pallas kernels, call(): pl.pallas_call(body, grid_spec=pltpu.PrefetchScalarGridSpec(num_scalar_pr...  45.1 us
    ppermute x39, waiting for transfers between devices, plane_send(): return lax.ppermute(value, 'row', pairs)  28.7 us
    all_to_all x1, blocking collectives, on_device(): arrived = lax.all_to_all(last, 'col', 0, 0)  9.95 us
    all_to_all x1, starting transfers between devices, on_device(): early = lax.all_to_all(early, 'row', 0, 0).reshape(1024, 128)  7.45 us
    all_to_all x1, waiting for transfers between devices, on_device(): early = lax.all_to_all(early, 'row', 0, 0).reshape(1024, 128)  7.12 us
    all_to_all x1, waiting for transfers between devices, on_device(): packed = lax.all_to_all(packed, 'col', 0, 0)  5.5 us
    all_to_all x1, starting transfers between devices, on_device(): packed = lax.all_to_all(packed, 'col', 0, 0)  5.31 us
  transfers between devices with their start and end apart: 44, of which 17 were waited for; matrix products, arithmetic and copies ran while one was open for 2% of the time, Pallas kernels for 21%

profile of v8, /device:TPU:4, one launch (start us, length us, event | category | flops | bytes accessed | tf_op | source)
XLA Modules:
  0.0 180.6 jit_solution(1679813023005467277)
XLA Ops:
  7.3 2.7 %shard_map.88 = f32[288,384]{1,0:T(8,128)} custom-call(s32[2]{0:T(128)S(1)} %pad_add_fusion.2.place_ref, f32[2,192,384]{2,1,0:T(8,128)} %factor_ref.1), custom_call_target="tpu_custom_call" | custom-call | tf_op jit(solution)/shard_map/pallas_call | solution.py:84
  10.3 1.4 shard_map.86
  11.7 5.3 %all-to-all-start = ((f32[8,16,128]{2,1,0:T(8,128)}), f32[8,16,128]{2,1,0:T(8,128)S(1)}, u32[]{:S(2)}, u32[]{:S(2)}) async-start(f32[8,16,128]{2,1,0:T(8,128)} %shard_map.86), calls=%async_computation | async-start | bytes 131072 | tf_op jit(solution)/shard_map/all_to_all | solution.py:451
  17.1 5.5 %all-to-all-done = f32[8,16,128]{2,1,0:T(8,128)S(1)} async-done(((f32[8,16,128]{2,1,0:T(8,128)}), f32[8,16,128]{2,1,0:T(8,128)S(1)}, u32[]{:S(2)}, u32[]{:S(2)}) %all-to-all-start) | async-done | bytes 65568 | tf_op jit(solution)/shard_map/all_to_all | solution.py:451
  23.5 7.5 %all-to-all-start.1 = ((f32[16,64,128]{2,1,0:T(8,128)}), f32[16,64,128]{2,1,0:T(8,128)S(1)}, u32[]{:S(2)}, u32[]{:S(2)}) async-start(f32[16,64,128]{2,1,0:T(8,128)} %broadcast_in_dim.36), calls=%async_computation.1 | async-start | bytes 1048576 | tf_op jit(solution)/shard_map/all_to_all | solution.py:453
  32.8 7.1 %all-to-all-done.1 = f32[16,64,128]{2,1,0:T(8,128)S(1)} async-done(((f32[16,64,128]{2,1,0:T(8,128)}), f32[16,64,128]{2,1,0:T(8,128)S(1)}, u32[]{:S(2)}, u32[]{:S(2)}) %all-to-all-start.1) | async-done | bytes 524320 | tf_op jit(solution)/shard_map/all_to_all | solution.py:453
  40.0 1.9 %shard_map.87.rhs_ref = f32[32,1024]{1,0:T(8,128)S(1)} custom-call(s32[2048]{0:T(1024)S(1)} %bitcast.35, f32[1024,128]{1,0:T(8,128)S(1)} %bitcast.34, f32[2,1024]{1,0:T(2,128)S(1)} %get-tuple-element.108.mark_ref), custom_call_target="tpu_custom_call" | custom-call | tf_op jit(solution)/shard_map/pallas_call | solution.py:84
  42.2 2.3 %shard_map.89.acc_ref = f32[32,192]{1,0:T(8,128)S(1)} custom-call(s32[2]{0:T(128)S(1)} %pad_add_fusion.2.place_ref, f32[32,1024]{1,0:T(8,128)S(1)} %shard_map.87.rhs_ref, f32[8,3,96,384]{3,2,1,0:T(8,128)} %bitcast.37), custom_call_target="tpu_custom_call" | custom-call | tf_op jit(solution)/shard_map/pallas_call | solution.py:84
  45.2 1.3 collective-permute-start
  46.5 1.3 collective-permute-start.1
  47.8 1.3 collective-permute-start.2
  49.1 1.3 collective-permute-start.3
  50.4 1.9 %shard_map.90.weight_ref = f32[768,384]{1,0:T(8,128)S(1)} custom-call(s32[2]{0:T(128)S(1)} %pad_add_fusion.2.place_ref, f32[8,3,96,384]{3,2,1,0:T(8,128)} %bitcast.38), custom_call_target="tpu_custom_call" | custom-call | tf_op jit(solution)/shard_map/pallas_call | solution.py:84
  52.3 2.2 %collective-permute-done.1.y1 = f32[32,192]{1,0:T(8,128)S(1)} collective-permute-done((f32[32,192]{1,0:T(8,128)S(1)}, f32[32,192]{1,0:T(8,128)S(1)}, u32[]{:S(2)}, u32[]{:S(2)}) %collective-permute-start.1) | collective-permute-done | bytes 24608 | tf_op jit(solution)/shard_map/ppermute | solution.py:415
  54.5 2.2 %collective-permute-done.2.y2 = f32[32,192]{1,0:T(8,128)S(1)} collective-permute-done((f32[32,192]{1,0:T(8,128)S(1)}, f32[32,192]{1,0:T(8,128)S(1)}, u32[]{:S(2)}, u32[]{:S(2)}) %collective-permute-start.2) | collective-permute-done | bytes 24608 | tf_op jit(solution)/shard_map/ppermute | solution.py:415
  65.3 2.3 %shard_map.92 = (f32[768,384]{1,0:T(8,128)S(1)}, f32[768,384]{1,0:T(8,128)S(1)}) custom-call(s32[2]{0:T(128)S(1)} %pad_add_fusion.2.place_ref, f32[8,3,96,384]{3,2,1,0:T(8,128)} %bitcast.39, f32[8,3,96,384]{3,2,1,0:T(8,128)} %bitcast.40), custom_call_target="tpu_custom_call" | custom-call | tf_op jit(solution)/shard_map/pallas_call | solution.py:84
  67.7 1.6 shard_map.93
  69.3 1.3 collective-permute-start.10
  70.6 1.3 collective-permute-start.11
  74.5 1.9 %shard_map.94.weight_ref = f32[768,384]{1,0:T(8,128)S(1)} custom-call(s32[2]{0:T(128)S(1)} %pad_add_fusion.2.place_ref, f32[8,3,96,384]{3,2,1,0:T(8,128)} %bitcast.41), custom_call_target="tpu_custom_call" | custom-call | tf_op jit(solution)/shard_map/pallas_call | solution.py:84
  76.4 3.2 %collective-permute-done.10.p1 = f32[32,768]{1,0:T(8,128)S(1)} collective-permute-done((f32[32,768]{1,0:T(8,128)S(1)}, f32[32,768]{1,0:T(8,128)S(1)}, u32[]{:S(2)}, u32[]{:S(2)}) %collective-permute-start.10) | collective-permute-done | bytes 98336 | tf_op jit(solution)/shard_map/ppermute | solution.py:415
  79.6 5.1 %collective-permute-done.11.p2 = f32[32,768]{1,0:T(8,128)S(1)} collective-permute-done((f32[32,768]{1,0:T(8,128)S(1)}, f32[32,768]{1,0:T(8,128)S(1)}, u32[]{:S(2)}, u32[]{:S(2)}) %collective-permute-start.11) | collective-permute-done | bytes 98336 | tf_op jit(solution)/shard_map/ppermute | solution.py:415
  85.2 1.4 shard_map.95
  87.9 1.3 collective-permute-start.14
  89.2 1.3 collective-permute-start.15
  90.5 1.3 collective-permute-start.16
  91.8 1.3 collective-permute-start.17
  93.1 2.3 %shard_map.96 = (f32[768,384]{1,0:T(8,128)S(1)}, f32[768,384]{1,0:T(8,128)S(1)}) custom-call(s32[2]{0:T(128)S(1)} %pad_add_fusion.2.place_ref, f32[8,3,96,384]{3,2,1,0:T(8,128)} %bitcast.42, f32[8,3,96,384]{3,2,1,0:T(8,128)} %bitcast.43), custom_call_target="tpu_custom_call" | custom-call | tf_op jit(solution)/shard_map/pallas_call | solution.py:84
  95.5 1.8 %collective-permute-done.16.p3 = f32[32,768]{1,0:T(8,128)S(1)} collective-permute-done((f32[32,768]{1,0:T(8,128)S(1)}, f32[32,768]{1,0:T(8,128)S(1)}, u32[]{:S(2)}, u32[]{:S(2)}) %collective-permute-start.16) | collective-permute-done | bytes 98336 | tf_op jit(solution)/shard_map/ppermute | solution.py:415
  98.3 1.6 shard_map.97
  103.3 2.8 %shard_map.98 = (f32[768,384]{1,0:T(8,128)S(1)}, f32[768,384]{1,0:T(8,128)S(1)}, f32[768,384]{1,0:T(8,128)S(1)}) custom-call(s32[2]{0:T(128)S(1)} %pad_add_fusion.2.place_ref, f32[8,3,96,384]{3,2,1,0:T(8,128)} %bitcast.44, f32[8,3,96,384]{3,2,1,0:T(8,128)} %bitcast.45, f32[8,3,96,384]{3,2,1,0:T(8,128)} %bitcast.46), custom_call_target="tpu_custom_call" | custom-call | tf_op jit(solution)/shard_map/pallas_call | solution.py:84
  106.2 2.0 %shard_map.99 = (f32[32,768]{1,0:T(8,128)S(1)}, f32[2,32,768]{2,1,0:T(8,128)S(1)}, f32[32,768]{1,0:T(8,128)S(1)}) custom-call(s32[2]{0:T(128)S(1)} %pad_add_fusion.2.place_ref, f32[32,192]{1,0:T(8,128)S(1)} %get-tuple-element.69.acc_ref, f32[192,1536]{1,0:T(8,128)S(1)} %bitcast.33, f32[32,768]{1,0:T(8,128)S(1)} %collective-permute-done.18.p0, ...), custom_call_target="tpu_custom_call" | custom-call | tf_op jit(solution)/shard_map/pallas_call | solution.py:84
  110.9 1.9 %collective-permute-start.27 = (f32[32,768]{1,0:T(8,128)S(1)}, f32[32,768]{1,0:T(8,128)S(1)}, u32[]{:S(2)}, u32[]{:S(2)}) collective-permute-start(f32[32,768]{1,0:T(8,128)S(1)} %get-tuple-element.80.newest_ref), channel_id=1, source_target_pairs={{0,32},{8,40},{16,48},{24,56},{32,64},{40,72},{48,80},{56,88},{64,... | collective-permute-start | bytes 294920 | tf_op jit(solution)/shard_map/ppermute | solution.py:415
  112.8 4.3 %shard_map.100 = (f32[32,1024]{1,0:T(8,128)S(1)}, f32[16,1024]{1,0:T(8,128)S(1)}) custom-call(s32[2048]{0:T(1024)S(1)} %bitcast.36, f32[2,1024]{1,0:T(2,128)S(1)} %get-tuple-element.108.mark_ref, f32[16,64,256]{2,1,0:T(8,128)} %bitcast.55), custom_call_target="tpu_custom_call" | custom-call | tf_op jit(solution)/shard_map/pallas_call | solution.py:84
  117.1 1.5 all-gather.11.cloned.1.call-done
  118.6 1.9 %shard_map.101.weight_ref = f32[768,384]{1,0:T(8,128)S(1)} custom-call(s32[2]{0:T(128)S(1)} %pad_add_fusion.2.place_ref, f32[8,3,96,384]{3,2,1,0:T(8,128)} %bitcast.47), custom_call_target="tpu_custom_call" | custom-call | tf_op jit(solution)/shard_map/pallas_call | solution.py:84
  120.5 7.0 %collective-permute-done.27.own_ref = f32[32,768]{1,0:T(8,128)S(1)} collective-permute-done((f32[32,768]{1,0:T(8,128)S(1)}, f32[32,768]{1,0:T(8,128)S(1)}, u32[]{:S(2)}, u32[]{:S(2)}) %collective-permute-start.27) | collective-permute-done | bytes 98336 | tf_op jit(solution)/shard_map/ppermute | solution.py:415
  135.1 4.4 %collective-permute-done.30.f1 = f32[32,192]{1,0:T(8,128)S(1)} collective-permute-done((f32[32,192]{1,0:T(8,128)S(1)}, f32[32,192]{1,0:T(8,128)S(1)}, u32[]{:S(2)}, u32[]{:S(2)}) %collective-permute-start.30) | collective-permute-done | bytes 24608 | tf_op jit(solution)/shard_map/ppermute | solution.py:415
  140.6 2.3 %shard_map.103 = (f32[768,384]{1,0:T(8,128)S(1)}, f32[768,384]{1,0:T(8,128)S(1)}) custom-call(s32[2]{0:T(128)S(1)} %pad_add_fusion.2.place_ref, f32[8,3,96,384]{3,2,1,0:T(8,128)} %bitcast.48, f32[8,3,96,384]{3,2,1,0:T(8,128)} %bitcast.49), custom_call_target="tpu_custom_call" | custom-call | tf_op jit(solution)/shard_map/pallas_call | solution.py:84
  143.2 1.3 shard_map.104
  144.6 4.7 %collective-permute-start.35 = (f32[32,192]{1,0:T(8,128)S(1)}, f32[32,192]{1,0:T(8,128)S(1)}, u32[]{:S(2)}, u32[]{:S(2)}) collective-permute-start(f32[32,192]{1,0:T(8,128)S(1)} %get-tuple-element.93.acc_ref), channel_id=1, source_target_pairs={{64,96},{72,104},{80,112},{88,120},{65,97},{73,105},{81,113},{89,1... | collective-permute-start | bytes 73736 | tf_op jit(solution)/shard_map/ppermute | solution.py:415
  150.5 2.3 %collective-permute-start.37 = (f32[32,192]{1,0:T(8,128)S(1)}, f32[32,192]{1,0:T(8,128)S(1)}, u32[]{:S(2)}, u32[]{:S(2)}) collective-permute-start(f32[32,192]{1,0:T(8,128)S(1)} %get-tuple-element.93.acc_ref), channel_id=1, source_target_pairs={{64,112},{72,120},{80,96},{88,104},{65,113},{73,121},{81,97},{89,1... | collective-permute-start | bytes 73736 | tf_op jit(solution)/shard_map/ppermute | solution.py:415
  152.8 1.4 collective-permute-start.38
  154.3 1.3 collective-permute-start.34
  155.7 2.8 %shard_map.105 = (f32[768,384]{1,0:T(8,128)S(1)}, f32[768,384]{1,0:T(8,128)S(1)}, f32[768,384]{1,0:T(8,128)S(1)}) custom-call(s32[2]{0:T(128)S(1)} %pad_add_fusion.2.place_ref, f32[8,3,96,384]{3,2,1,0:T(8,128)} %bitcast.50, f32[8,3,96,384]{3,2,1,0:T(8,128)} %bitcast.51, f32[8,3,96,384]{3,2,1,0:T(8,128)} %bitcast.52), custom_call_target="tpu_custom_call" | custom-call | tf_op jit(solution)/shard_map/pallas_call | solution.py:84
  158.4 1.3 shard_map.107.cells_ref
  160.8 1.3 shard_map.108
  162.2 9.9 %all_to_all.15.got_ref = f32[8,32,256]{2,1,0:T(8,128)S(1)} all-to-all(f32[8,32,256]{2,1,0:T(8,128)S(1)} %shard_map.108), channel_id=1, replica_groups=mesh['row'=16,'col'=8] {'col'}, dimensions={0} | all-to-all | bytes 524288 | tf_op jit(solution)/shard_map/all_to_all | solution.py:595
  (108 shorter events, 37.6 us)
Async XLA Ops:
  7.2 2.9 %copy-start.5 = (f32[2,4,6]{2,1,0:T(4,128)S(1)}, f32[2,4,6]{2,1,0:T(4,128)}, u32[]{:S(2)}) copy-start(f32[2,4,6]{2,1,0:T(4,128)} %param.9) | copy-start | bytes 580
  7.2 9.8 %copy-start.2 = (s32[3072]{0:T(1024)S(1)}, s32[3072]{0:T(1024)}, u32[]{:S(2)}) copy-start(s32[3072]{0:T(1024)} %param.13) | copy-start | bytes 36868
  7.2 35.0 %all-gather.7.cloned.1.call-start = ((), (), s32[]{:S(2)}) async-start(), calls=%async_computation.3 | async-start | bytes 3981312 | tf_op jit(solution)/shard_map/all_gather | solution.py:432
  10.1 21.1 %copy-start.1 = (f32[2,192,384]{2,1,0:T(8,128)S(1)}, f32[2,192,384]{2,1,0:T(8,128)}, u32[]{:S(2)}) copy-start(f32[2,192,384]{2,1,0:T(8,128)} %param.11) | copy-start | bytes 1769476
  11.7 10.9 %all-to-all-start = ((f32[8,16,128]{2,1,0:T(8,128)}), f32[8,16,128]{2,1,0:T(8,128)S(1)}, u32[]{:S(2)}, u32[]{:S(2)}) async-start(f32[8,16,128]{2,1,0:T(8,128)} %shard_map.86), calls=%async_computation | async-start | bytes 131072 | tf_op jit(solution)/shard_map/all_to_all | solution.py:451
  23.5 16.5 %all-to-all-start.1 = ((f32[16,64,128]{2,1,0:T(8,128)}), f32[16,64,128]{2,1,0:T(8,128)S(1)}, u32[]{:S(2)}, u32[]{:S(2)}) async-start(f32[16,64,128]{2,1,0:T(8,128)} %broadcast_in_dim.36), calls=%async_computation.1 | async-start | bytes 1048576 | tf_op jit(solution)/shard_map/all_to_all | solution.py:453
  30.9 81.9 %all-gather.9.cloned.1.call-start = ((), (), s32[]{:S(2)}) async-start(), calls=%async_computation.4 | async-start | bytes 1114112 | tf_op jit(solution)/shard_map/all_gather | solution.py:496
  44.5 74.1 %all-gather.11.cloned.1.call-start = ((), (), s32[]{:S(2)}) async-start(), calls=%async_computation.5 | async-start | bytes 3981312 | tf_op jit(solution)/shard_map/all_gather | solution.py:432
  45.2 7.1 %collective-permute-start = (f32[32,192]{1,0:T(8,128)S(1)}, f32[32,192]{1,0:T(8,128)S(1)}, u32[]{:S(2)}, u32[]{:S(2)}) collective-permute-start(f32[32,192]{1,0:T(8,128)S(1)} %shard_map.89.acc_ref), channel_id=1, source_target_pairs={{32,64},{40,72},{48,80},{56,88},{33,65},{41,73},{49,81},{57,89},{3... | collective-permute-start | bytes 73736 | tf_op jit(solution)/shard_map/ppermute | solution.py:415
  46.5 8.0 %collective-permute-start.1 = (f32[32,192]{1,0:T(8,128)S(1)}, f32[32,192]{1,0:T(8,128)S(1)}, u32[]{:S(2)}, u32[]{:S(2)}) collective-permute-start(f32[32,192]{1,0:T(8,128)S(1)} %shard_map.89.acc_ref), channel_id=1, source_target_pairs={{32,72},{40,80},{48,88},{56,64},{33,73},{41,81},{49,89},{57,65},{3... | collective-permute-start | bytes 73736 | tf_op jit(solution)/shard_map/ppermute | solution.py:415
  47.8 8.9 %collective-permute-start.2 = (f32[32,192]{1,0:T(8,128)S(1)}, f32[32,192]{1,0:T(8,128)S(1)}, u32[]{:S(2)}, u32[]{:S(2)}) collective-permute-start(f32[32,192]{1,0:T(8,128)S(1)} %shard_map.89.acc_ref), channel_id=1, source_target_pairs={{32,80},{40,88},{48,64},{56,72},{33,81},{41,89},{49,65},{57,73},{3... | collective-permute-start | bytes 73736 | tf_op jit(solution)/shard_map/ppermute | solution.py:415
  49.1 8.5 %collective-permute-start.3 = (f32[32,192]{1,0:T(8,128)S(1)}, f32[32,192]{1,0:T(8,128)S(1)}, u32[]{:S(2)}, u32[]{:S(2)}) collective-permute-start(f32[32,192]{1,0:T(8,128)S(1)} %shard_map.89.acc_ref), channel_id=1, source_target_pairs={{32,88},{40,64},{48,72},{56,80},{33,89},{41,65},{49,73},{57,81},{3... | collective-permute-start | bytes 73736 | tf_op jit(solution)/shard_map/ppermute | solution.py:415
  52.3 12.9 %copy-start = (f32[2,768,192]{1,2,0:T(8,128)S(1)}, f32[2,768,192]{1,2,0:T(8,128)}, u32[]{:S(2)}) copy-start(f32[2,768,192]{1,2,0:T(8,128)} %param.12) | copy-start | bytes 3538948
  58.7 9.0 %collective-permute-start.4 = (f32[4,32,192]{2,1,0:T(8,128)S(1)}, f32[4,32,192]{2,1,0:T(8,128)S(1)}, u32[]{:S(2)}, u32[]{:S(2)}) collective-permute-start(f32[4,32,192]{2,1,0:T(8,128)S(1)} %get-tuple-element.56), channel_id=1, source_target_pairs={{64,96},{72,104},{80,112},{88,120},{65,97},{73,105},{81,113},{89,1... | collective-permute-start | bytes 294920 | tf_op jit(solution)/shard_map/ppermute | solution.py:415
  60.0 7.7 %collective-permute-start.5 = (f32[32,192]{1,0:T(8,128)S(1)}, f32[32,192]{1,0:T(8,128)S(1)}, u32[]{:S(2)}, u32[]{:S(2)}) collective-permute-start(f32[32,192]{1,0:T(8,128)S(1)} %get-tuple-element.54.acc_ref), channel_id=1, source_target_pairs={{64,96},{72,104},{80,112},{88,120},{65,97},{73,105},{81,113},{89,1... | collective-permute-start | bytes 73736 | tf_op jit(solution)/shard_map/ppermute | solution.py:415
  61.3 6.4 %collective-permute-start.6 = (f32[32,192]{1,0:T(8,128)S(1)}, f32[32,192]{1,0:T(8,128)S(1)}, u32[]{:S(2)}, u32[]{:S(2)}) collective-permute-start(f32[32,192]{1,0:T(8,128)S(1)} %get-tuple-element.54.acc_ref), channel_id=1, source_target_pairs={{64,104},{72,112},{80,120},{88,96},{65,105},{73,113},{81,121},{89,... | collective-permute-start | bytes 73736 | tf_op jit(solution)/shard_map/ppermute | solution.py:415
  62.6 5.1 %collective-permute-start.7 = (f32[32,192]{1,0:T(8,128)S(1)}, f32[32,192]{1,0:T(8,128)S(1)}, u32[]{:S(2)}, u32[]{:S(2)}) collective-permute-start(f32[32,192]{1,0:T(8,128)S(1)} %get-tuple-element.54.acc_ref), channel_id=1, source_target_pairs={{64,112},{72,120},{80,96},{88,104},{65,113},{73,121},{81,97},{89,1... | collective-permute-start | bytes 73736 | tf_op jit(solution)/shard_map/ppermute | solution.py:415
  63.9 3.8 %collective-permute-start.8 = (f32[32,192]{1,0:T(8,128)S(1)}, f32[32,192]{1,0:T(8,128)S(1)}, u32[]{:S(2)}, u32[]{:S(2)}) collective-permute-start(f32[32,192]{1,0:T(8,128)S(1)} %get-tuple-element.54.acc_ref), channel_id=1, source_target_pairs={{64,120},{72,96},{80,104},{88,112},{65,121},{73,97},{81,105},{89,1... | collective-permute-start | bytes 73736 | tf_op jit(solution)/shard_map/ppermute | solution.py:415
  69.3 10.3 %collective-permute-start.10 = (f32[32,768]{1,0:T(8,128)S(1)}, f32[32,768]{1,0:T(8,128)S(1)}, u32[]{:S(2)}, u32[]{:S(2)}) collective-permute-start(f32[32,768]{1,0:T(8,128)S(1)} %get-tuple-element.61), channel_id=1, source_target_pairs={{96,72},{104,80},{112,88},{120,64},{97,73},{105,81},{113,89},{121,... | collective-permute-start | bytes 294920 | tf_op jit(solution)/shard_map/ppermute | solution.py:415
  70.6 14.1 %collective-permute-start.11 = (f32[32,768]{1,0:T(8,128)S(1)}, f32[32,768]{1,0:T(8,128)S(1)}, u32[]{:S(2)}, u32[]{:S(2)}) collective-permute-start(f32[32,768]{1,0:T(8,128)S(1)} %get-tuple-element.61), channel_id=1, source_target_pairs={{96,80},{104,88},{112,64},{120,72},{97,81},{105,89},{113,65},{121,... | collective-permute-start | bytes 294920 | tf_op jit(solution)/shard_map/ppermute | solution.py:415
  71.9 13.0 %collective-permute-start.12 = (f32[32,768]{1,0:T(8,128)S(1)}, f32[32,768]{1,0:T(8,128)S(1)}, u32[]{:S(2)}, u32[]{:S(2)}) collective-permute-start(f32[32,768]{1,0:T(8,128)S(1)} %get-tuple-element.61), channel_id=1, source_target_pairs={{96,88},{104,64},{112,72},{120,80},{97,89},{105,65},{113,73},{121,... | collective-permute-start | bytes 294920 | tf_op jit(solution)/shard_map/ppermute | solution.py:415
  73.2 12.0 %collective-permute-start.9 = (f32[32,768]{1,0:T(8,128)S(1)}, f32[32,768]{1,0:T(8,128)S(1)}, u32[]{:S(2)}, u32[]{:S(2)}) collective-permute-start(f32[32,768]{1,0:T(8,128)S(1)} %get-tuple-element.61), channel_id=1, source_target_pairs={{96,64},{104,72},{112,80},{120,88},{97,65},{105,73},{113,81},{121,... | collective-permute-start | bytes 294920 | tf_op jit(solution)/shard_map/ppermute | solution.py:415
  86.6 8.8 %collective-permute-start.13 = (f32[32,768]{1,0:T(8,128)S(1)}, f32[32,768]{1,0:T(8,128)S(1)}, u32[]{:S(2)}, u32[]{:S(2)}) collective-permute-start(f32[32,768]{1,0:T(8,128)S(1)} %get-tuple-element.64), channel_id=1, source_target_pairs={{64,32},{72,40},{80,48},{88,56},{65,33},{73,41},{81,49},{89,57},{6... | collective-permute-start | bytes 294920 | tf_op jit(solution)/shard_map/ppermute | solution.py:415
  87.9 7.6 %collective-permute-start.14 = (f32[32,768]{1,0:T(8,128)S(1)}, f32[32,768]{1,0:T(8,128)S(1)}, u32[]{:S(2)}, u32[]{:S(2)}) collective-permute-start(f32[32,768]{1,0:T(8,128)S(1)} %get-tuple-element.64), channel_id=1, source_target_pairs={{64,40},{72,48},{80,56},{88,32},{65,41},{73,49},{81,57},{89,33},{6... | collective-permute-start | bytes 294920 | tf_op jit(solution)/shard_map/ppermute | solution.py:415
  89.2 6.3 %collective-permute-start.15 = (f32[32,768]{1,0:T(8,128)S(1)}, f32[32,768]{1,0:T(8,128)S(1)}, u32[]{:S(2)}, u32[]{:S(2)}) collective-permute-start(f32[32,768]{1,0:T(8,128)S(1)} %get-tuple-element.64), channel_id=1, source_target_pairs={{64,48},{72,56},{80,32},{88,40},{65,49},{73,57},{81,33},{89,41},{6... | collective-permute-start | bytes 294920 | tf_op jit(solution)/shard_map/ppermute | solution.py:415
  90.5 6.8 %collective-permute-start.16 = (f32[32,768]{1,0:T(8,128)S(1)}, f32[32,768]{1,0:T(8,128)S(1)}, u32[]{:S(2)}, u32[]{:S(2)}) collective-permute-start(f32[32,768]{1,0:T(8,128)S(1)} %get-tuple-element.64), channel_id=1, source_target_pairs={{64,56},{72,32},{80,40},{88,48},{65,57},{73,33},{81,41},{89,49},{6... | collective-permute-start | bytes 294920 | tf_op jit(solution)/shard_map/ppermute | solution.py:415
  91.8 6.5 %collective-permute-start.17 = (f32[32,768]{1,0:T(8,128)S(1)}, f32[32,768]{1,0:T(8,128)S(1)}, u32[]{:S(2)}, u32[]{:S(2)}) collective-permute-start(f32[32,768]{1,0:T(8,128)S(1)} %get-tuple-element.65.x3_ref), channel_id=1, source_target_pairs={{64,32},{72,40},{80,48},{88,56},{65,33},{73,41},{81,49},{89,57},{6... | collective-permute-start | bytes 294920 | tf_op jit(solution)/shard_map/ppermute | solution.py:415
  99.9 6.3 %collective-permute-start.22 = (f32[2,32,768]{2,1,0:T(8,128)S(1)}, f32[2,32,768]{2,1,0:T(8,128)S(1)}, u32[]{:S(2)}, u32[]{:S(2)}) collective-permute-start(f32[2,32,768]{2,1,0:T(8,128)S(1)} %get-tuple-element.71.x2_ref), channel_id=1, source_target_pairs={{32,0},{40,8},{48,16},{56,24},{33,1},{41,9},{49,17},{57,25},{34,2}... | collective-permute-start | bytes 589832 | tf_op jit(solution)/shard_map/ppermute | solution.py:415
  100.6 5.5 %collective-permute-start.18 = (f32[32,768]{1,0:T(8,128)S(1)}, f32[32,768]{1,0:T(8,128)S(1)}, u32[]{:S(2)}, u32[]{:S(2)}) collective-permute-start(f32[32,768]{1,0:T(8,128)S(1)} %get-tuple-element.70), channel_id=1, source_target_pairs={{32,0},{40,8},{48,16},{56,24},{33,1},{41,9},{49,17},{57,25},{34,2}... | collective-permute-start | bytes 294920 | tf_op jit(solution)/shard_map/ppermute | solution.py:415
  101.3 4.9 %collective-permute-start.19 = (f32[32,768]{1,0:T(8,128)S(1)}, f32[32,768]{1,0:T(8,128)S(1)}, u32[]{:S(2)}, u32[]{:S(2)}) collective-permute-start(f32[32,768]{1,0:T(8,128)S(1)} %get-tuple-element.70), channel_id=1, source_target_pairs={{32,8},{40,16},{48,24},{56,0},{33,9},{41,17},{49,25},{57,1},{34,10... | collective-permute-start | bytes 294920 | tf_op jit(solution)/shard_map/ppermute | solution.py:415
  101.9 4.2 %collective-permute-start.20 = (f32[32,768]{1,0:T(8,128)S(1)}, f32[32,768]{1,0:T(8,128)S(1)}, u32[]{:S(2)}, u32[]{:S(2)}) collective-permute-start(f32[32,768]{1,0:T(8,128)S(1)} %get-tuple-element.70), channel_id=1, source_target_pairs={{32,16},{40,24},{48,0},{56,8},{33,17},{41,25},{49,1},{57,9},{34,18... | collective-permute-start | bytes 294920 | tf_op jit(solution)/shard_map/ppermute | solution.py:415
  102.6 3.5 %collective-permute-start.21 = (f32[32,768]{1,0:T(8,128)S(1)}, f32[32,768]{1,0:T(8,128)S(1)}, u32[]{:S(2)}, u32[]{:S(2)}) collective-permute-start(f32[32,768]{1,0:T(8,128)S(1)} %get-tuple-element.70), channel_id=1, source_target_pairs={{32,24},{40,0},{48,8},{56,16},{33,25},{41,1},{49,9},{57,17},{34,26... | collective-permute-start | bytes 294920 | tf_op jit(solution)/shard_map/ppermute | solution.py:415
  108.1 12.3 %collective-permute-start.23 = (f32[32,768]{1,0:T(8,128)S(1)}, f32[32,768]{1,0:T(8,128)S(1)}, u32[]{:S(2)}, u32[]{:S(2)}) collective-permute-start(f32[32,768]{1,0:T(8,128)S(1)} %get-tuple-element.76), channel_id=1, source_target_pairs={{0,32},{8,40},{16,48},{24,56},{1,33},{9,41},{17,49},{25,57},{2,34}... | collective-permute-start | bytes 294920 | tf_op jit(solution)/shard_map/ppermute | solution.py:415
  108.8 11.7 %collective-permute-start.24 = (f32[32,768]{1,0:T(8,128)S(1)}, f32[32,768]{1,0:T(8,128)S(1)}, u32[]{:S(2)}, u32[]{:S(2)}) collective-permute-start(f32[32,768]{1,0:T(8,128)S(1)} %get-tuple-element.76), channel_id=1, source_target_pairs={{0,40},{8,48},{16,56},{24,32},{1,41},{9,49},{17,57},{25,33},{2,42}... | collective-permute-start | bytes 294920 | tf_op jit(solution)/shard_map/ppermute | solution.py:415
  109.5 11.0 %collective-permute-start.25 = (f32[32,768]{1,0:T(8,128)S(1)}, f32[32,768]{1,0:T(8,128)S(1)}, u32[]{:S(2)}, u32[]{:S(2)}) collective-permute-start(f32[32,768]{1,0:T(8,128)S(1)} %get-tuple-element.76), channel_id=1, source_target_pairs={{0,48},{8,56},{16,32},{24,40},{1,49},{9,57},{17,33},{25,41},{2,50}... | collective-permute-start | bytes 294920 | tf_op jit(solution)/shard_map/ppermute | solution.py:415
  110.2 10.3 %collective-permute-start.26 = (f32[32,768]{1,0:T(8,128)S(1)}, f32[32,768]{1,0:T(8,128)S(1)}, u32[]{:S(2)}, u32[]{:S(2)}) collective-permute-start(f32[32,768]{1,0:T(8,128)S(1)} %get-tuple-element.76), channel_id=1, source_target_pairs={{0,56},{8,32},{16,40},{24,48},{1,57},{9,33},{17,41},{25,49},{2,58}... | collective-permute-start | bytes 294920 | tf_op jit(solution)/shard_map/ppermute | solution.py:415
  110.9 16.6 %collective-permute-start.27 = (f32[32,768]{1,0:T(8,128)S(1)}, f32[32,768]{1,0:T(8,128)S(1)}, u32[]{:S(2)}, u32[]{:S(2)}) collective-permute-start(f32[32,768]{1,0:T(8,128)S(1)} %get-tuple-element.80.newest_ref), channel_id=1, source_target_pairs={{0,32},{8,40},{16,48},{24,56},{32,64},{40,72},{48,80},{56,88},{64,... | collective-permute-start | bytes 294920 | tf_op jit(solution)/shard_map/ppermute | solution.py:415
  128.5 10.9 %collective-permute-start.30 = (f32[32,192]{1,0:T(8,128)S(1)}, f32[32,192]{1,0:T(8,128)S(1)}, u32[]{:S(2)}, u32[]{:S(2)}) collective-permute-start(f32[32,192]{1,0:T(8,128)S(1)} %get-tuple-element.84.acc_ref), channel_id=1, source_target_pairs={{32,72},{40,80},{48,88},{56,64},{33,73},{41,81},{49,89},{57,65},{3... | collective-permute-start | bytes 73736 | tf_op jit(solution)/shard_map/ppermute | solution.py:415
  129.8 13.4 %collective-permute-start.28 = (f32[2,32,768]{2,1,0:T(8,128)S(1)}, f32[2,32,768]{2,1,0:T(8,128)S(1)}, u32[]{:S(2)}, u32[]{:S(2)}) collective-permute-start(f32[2,32,768]{2,1,0:T(8,128)S(1)} %get-tuple-element.85.sent_ref.pass_ref), channel_id=1, source_target_pairs={{32,64},{40,72},{48,80},{56,88},{0,96},{8,104},{16,112},{24,120},{... | collective-permute-start | bytes 589832 | tf_op jit(solution)/shard_map/ppermute | solution.py:415
  131.2 11.7 %collective-permute-start.29 = (f32[32,192]{1,0:T(8,128)S(1)}, f32[32,192]{1,0:T(8,128)S(1)}, u32[]{:S(2)}, u32[]{:S(2)}) collective-permute-start(f32[32,192]{1,0:T(8,128)S(1)} %get-tuple-element.84.acc_ref), channel_id=1, source_target_pairs={{32,64},{40,72},{48,80},{56,88},{33,65},{41,73},{49,81},{57,89},{3... | collective-permute-start | bytes 73736 | tf_op jit(solution)/shard_map/ppermute | solution.py:415
  132.5 10.7 %collective-permute-start.31 = (f32[32,192]{1,0:T(8,128)S(1)}, f32[32,192]{1,0:T(8,128)S(1)}, u32[]{:S(2)}, u32[]{:S(2)}) collective-permute-start(f32[32,192]{1,0:T(8,128)S(1)} %get-tuple-element.84.acc_ref), channel_id=1, source_target_pairs={{32,80},{40,88},{48,64},{56,72},{33,81},{41,89},{49,65},{57,73},{3... | collective-permute-start | bytes 73736 | tf_op jit(solution)/shard_map/ppermute | solution.py:415
  133.8 9.5 %collective-permute-start.32 = (f32[32,192]{1,0:T(8,128)S(1)}, f32[32,192]{1,0:T(8,128)S(1)}, u32[]{:S(2)}, u32[]{:S(2)}) collective-permute-start(f32[32,192]{1,0:T(8,128)S(1)} %get-tuple-element.84.acc_ref), channel_id=1, source_target_pairs={{32,88},{40,64},{48,72},{56,80},{33,89},{41,65},{49,73},{57,81},{3... | collective-permute-start | bytes 73736 | tf_op jit(solution)/shard_map/ppermute | solution.py:415
  139.5 5.1 %collective-permute-start.33 = (f32[32,768]{1,0:T(8,128)S(1)}, f32[32,768]{1,0:T(8,128)S(1)}, u32[]{:S(2)}, u32[]{:S(2)}) collective-permute-start(f32[32,768]{1,0:T(8,128)S(1)} %get-tuple-element.92), channel_id=1, source_target_pairs={{32,96},{40,104},{48,112},{56,120},{33,97},{41,105},{49,113},{57,1... | collective-permute-start | bytes 294920 | tf_op jit(solution)/shard_map/ppermute | solution.py:415
  144.6 16.2 %collective-permute-start.35 = (f32[32,192]{1,0:T(8,128)S(1)}, f32[32,192]{1,0:T(8,128)S(1)}, u32[]{:S(2)}, u32[]{:S(2)}) collective-permute-start(f32[32,192]{1,0:T(8,128)S(1)} %get-tuple-element.93.acc_ref), channel_id=1, source_target_pairs={{64,96},{72,104},{80,112},{88,120},{65,97},{73,105},{81,113},{89,1... | collective-permute-start | bytes 73736 | tf_op jit(solution)/shard_map/ppermute | solution.py:415
  149.2 11.6 %collective-permute-start.36 = (f32[32,192]{1,0:T(8,128)S(1)}, f32[32,192]{1,0:T(8,128)S(1)}, u32[]{:S(2)}, u32[]{:S(2)}) collective-permute-start(f32[32,192]{1,0:T(8,128)S(1)} %get-tuple-element.93.acc_ref), channel_id=1, source_target_pairs={{64,104},{72,112},{80,120},{88,96},{65,105},{73,113},{81,121},{89,... | collective-permute-start | bytes 73736 | tf_op jit(solution)/shard_map/ppermute | solution.py:415
  150.5 10.3 %collective-permute-start.37 = (f32[32,192]{1,0:T(8,128)S(1)}, f32[32,192]{1,0:T(8,128)S(1)}, u32[]{:S(2)}, u32[]{:S(2)}) collective-permute-start(f32[32,192]{1,0:T(8,128)S(1)} %get-tuple-element.93.acc_ref), channel_id=1, source_target_pairs={{64,112},{72,120},{80,96},{88,104},{65,113},{73,121},{81,97},{89,1... | collective-permute-start | bytes 73736 | tf_op jit(solution)/shard_map/ppermute | solution.py:415
  152.8 8.0 %collective-permute-start.38 = (f32[32,192]{1,0:T(8,128)S(1)}, f32[32,192]{1,0:T(8,128)S(1)}, u32[]{:S(2)}, u32[]{:S(2)}) collective-permute-start(f32[32,192]{1,0:T(8,128)S(1)} %get-tuple-element.93.acc_ref), channel_id=1, source_target_pairs={{64,120},{72,96},{80,104},{88,112},{65,121},{73,97},{81,105},{89,1... | collective-permute-start | bytes 73736 | tf_op jit(solution)/shard_map/ppermute | solution.py:415
  154.3 4.1 %collective-permute-start.34 = (f32[4,32,192]{2,1,0:T(8,128)S(1)}, f32[4,32,192]{2,1,0:T(8,128)S(1)}, u32[]{:S(2)}, u32[]{:S(2)}) collective-permute-start(f32[4,32,192]{2,1,0:T(8,128)S(1)} %get-tuple-element.94), channel_id=1, source_target_pairs={{64,96},{72,104},{80,112},{88,120},{32,0},{40,8},{48,16},{56,24},{... | collective-permute-start | bytes 294920 | tf_op jit(solution)/shard_map/ppermute | solution.py:415
  (2 other events, 5.8 us)
Sparse Core Ops, SparseCore 0:
  10.2 31.9 all-gather.6
  44.9 43.3 all-gather.8
  90.0 28.5 all-gather.10

commit v9 on v8

--- a/solution.py
+++ b/solution.py
@@ -328,19 +328,13 @@
     slabs = [f0[...], f1[...], f2[...], f3[...]]
     solved = slab - product - slabs_dot(slabs, weight1_ref, q, keep_ref)
     out_ref[...] = jnp.where(plane == 1, acc_ref[...], solved)
-    for s in range(GROUP):
-        keep_ref[s] = jnp.where(plane == 1, x0[:, SLAB * s : SLAB * s + SLAB], keep_ref[s])
-
-
-def joined(ref):
-    return jnp.concatenate([ref[s] for s in range(GROUP)], axis=1)
 
 
 def second_base_kernel(
-    place_ref, rhs_ref, link_ref, acc_ref, got_ref, x0_three, own_ref, weight_ref, out_ref
+    place_ref, rhs_ref, link_ref, acc_ref, x0_zero, x0_three, own_ref, weight_ref, out_ref
 ):
     plane, q = place_ref[0], place_ref[1]
-    x0 = jnp.where(plane == 0, joined(got_ref), x0_three[...])
+    x0 = x0_zero[...] + x0_three[...]
     own = jnp.where(plane == 0, x0, own_ref[...])
     slab = second_slab(rhs_ref, link_ref, own, q)
     product = complex_dot(second_block(rhs_ref, link_ref, x0), weight_ref[...])
@@ -350,7 +344,7 @@
 
 
 def cells_kernel(
-    where_ref, got_ref, x0_three, pass_ref, passed_ref, newest_ref, own_ref, both_zero, later_ref, x3_one, out_ref, front_ref, rows_ref
+    where_ref, x0_zero, x0_three, pass_ref, passed_ref, newest_ref, own_ref, both_zero, later_ref, x3_one, out_ref, front_ref, rows_ref
 ):
     plane = where_ref[SLAB]
 
@@ -361,7 +355,7 @@
         return value
 
     blocks = (
-        pick(joined(got_ref), pass_ref[0], passed_ref[0], x0_three[...]),
+        pick(x0_zero[...], pass_ref[0], passed_ref[0], x0_three[...]),
         pick(newest_ref[...], own_ref[...], passed_ref[1], passed_ref[0]),
         pick(both_zero[1], newest_ref[...], own_ref[...], passed_ref[1]),
         pick(later_ref[1], x3_one[...], newest_ref[...], own_ref[...]),
@@ -388,7 +382,6 @@
         - sent_dot(sent_ref, weight1_ref)
         - slabs_dot(slabs, weight2_ref, place_ref[1])
     )
-    solved = jnp.where(place_ref[0] == 0, acc_ref[...], solved)
     lane = lax.broadcasted_iota(jnp.int32, (ROWS, 128), 1)
     tail = jnp.concatenate([solved[:, 128:], jnp.zeros((ROWS, 64), f32)], axis=1)
     for c in range(8):
@@ -466,6 +459,7 @@
     rows_shape = SDS((ROWS, 1024), f32)
     rows_scratch = [pltpu.VMEM((1024, 128), f32)]
     (rhs,) = call(first_front_kernel, [rows_shape], where, [early, mark], scratch=rows_scratch)
+    late = lax.all_gather(after(late, rhs), "row")
 
     slab_shape = SDS((ROWS, SLAB), f32)
     block_shape = SDS((ROWS, BLOCK), f32)
@@ -492,8 +486,7 @@
     ]
     (acc,) = call(start_kernel, [slab_shape], place, [rhs], first)
     got = plane_spread(acc, 1, 2)
-    late, turned2, diag_inv = after((late, turned2, diag_inv), acc)
-    late = lax.all_gather(late, "row")
+    turned2, diag_inv = after((turned2, diag_inv), acc)
     matrix2 = gather_blocks(turned2)
     weights = load(matrix1, [1], acc)
     inverse = diag_inv.reshape(2 * BLOCK, SLAB).T
@@ -529,14 +522,6 @@
     later = plane_send(both_one, (1, 0))
     got = plane_spread(part, 1, 0)
     weights = load(matrix1, [1, 2, 3], part)
-    newest, both_zero, part = call(
-        back_one_kernel,
-        [block_shape, pair_shape, block_shape],
-        place,
-        [acc, inverse, *got, later, both_one, x3_two, *weights],
-    )
-    own = plane_send(newest, (0, 1), (1, 2), (2, 3))
-    got = plane_spread(part, 0, 1)
     late = after(late, part)
     rhs, link = call(
         second_front_kernel,
@@ -546,6 +531,15 @@
         [(late, (16, 64, 128), lambda i, place: (0, 0, 0))],
         scratch=rows_scratch * 2,
     )
+    acc, rhs, link = lax.optimization_barrier((acc, rhs, link))
+    newest, both_zero, part = call(
+        back_one_kernel,
+        [block_shape, pair_shape, block_shape],
+        place,
+        [acc, inverse, *got, later, both_one, x3_two, *weights],
+    )
+    own = plane_send(newest, (0, 1), (1, 2), (2, 3))
+    got = plane_spread(part, 0, 1)
     weights = load(matrix2, [0], part, True)
     x0_one, passing, acc = call(
         couple_kernel,
@@ -556,6 +550,7 @@
     passed = plane_send(passing, (1, 2), (0, 3))
     got = plane_spread(acc, 1, 2)
     x0_three = plane_send(after(x0_one, got[1]), (1, 3))
+    x0_zero = plane_send(after(x0_one, got[1]), (1, 0))
     weights = load(matrix2, [0, 1], acc, True)
     acc, kept = call(
         second_one_kernel,
@@ -563,15 +558,15 @@
         place,
         [rhs, link, acc, own, passing, passed, *got, *weights],
     )
-    acc, kept, x0_three = lax.optimization_barrier((acc, kept, x0_three))
-    sent = plane_send(kept, (2, 3), (1, 0))
+    acc, kept, x0_three, x0_zero = lax.optimization_barrier((acc, kept, x0_three, x0_zero))
+    sent = plane_send(kept, (2, 3))
     got = plane_spread(acc, 2, 3)
     weights = load(matrix2, [0, 1, 2], acc, True)
     (acc,) = call(
         second_base_kernel,
         [slab_shape],
         place,
-        [rhs, link, acc, sent, x0_three, own, weights[0]],
+        [rhs, link, acc, x0_zero, x0_three, own, weights[0]],
     )
 
     at = jnp.arange(SLAB, dtype=jnp.int32)
@@ -583,7 +578,7 @@
         cells_kernel,
         [SDS((8, ROWS, 128), f32)],
         jnp.concatenate([slots, place]),
-        [sent, x0_three, passing, passed, newest, own, both_zero, later, x3_one],
+        [x0_zero, x0_three, passing, passed, newest, own, both_zero, later, x3_one],
         scratch=[pltpu.VMEM((4 * BLOCK, 128), f32), pltpu.VMEM((128, 128), f32)],
     )
     (last,) = call(

time: 183 us -> 196 us (1.071)
  local copies, waits for them, and re-layouts: 4.33 us -> 11.5 us
  Pallas kernels: 45.1 us -> 48.5 us
  starting transfers between devices: 62.2 us -> 65.2 us
    unnamed x17 -> x51, local copies, waits for them, and re-layouts: 1.36 us -> 8.56 us
    pallas_call x24, Pallas kernels: 45.1 us -> 48.5 us  [call(): pl.pallas_call(body, grid_spec=pltpu.PrefetchScalarGridSpec(num_scalar_pr...]
    ppermute x39 -> x40, starting transfers between devices: 49.3 us -> 52.2 us  [plane_send(): return lax.ppermute(value, 'row', pairs)]
    ppermute x39 -> x40, waiting for transfers between devices: 28.7 us -> 30.1 us  [plane_send(): return lax.ppermute(value, 'row', pairs)]
  transfers between devices with their start and end apart: 44 -> 45, of which waited for: 17 -> 14; matrix products, arithmetic and copies ran while one was open for 2% -> 2% of each run, Pallas kernels for 21% -> 22%
where the time goes in v9:
time: 196 us; the launch traced here: 194 us
  starting transfers between devices  65.2 us (33%)
  Pallas kernels  48.5 us (25%)
  waiting for transfers between devices  43.8 us (22%)
  between operations  14.6 us (7%)
  local copies, waits for them, and re-layouts  11.5 us (6%)
  blocking collectives  9.95 us (5%)
    ppermute x40, starting transfers between devices, plane_send(): return lax.ppermute(value, 'row', pairs)  52.2 us
    pallas_call x24, Pallas kernels, call(): pl.pallas_call(body, grid_spec=pltpu.PrefetchScalarGridSpec(num_scalar_pr...  48.5 us
    ppermute x40, waiting for transfers between devices, plane_send(): return lax.ppermute(value, 'row', pairs)  30.1 us
    all_to_all x1, blocking collectives, on_device(): arrived = lax.all_to_all(last, 'col', 0, 0)  9.95 us
    unnamed x51, local copies, waits for them, and re-layouts  8.56 us
    all_to_all x1, waiting for transfers between devices, on_device(): early = lax.all_to_all(early, 'row', 0, 0).reshape(1024, 128)  8.12 us
    all_to_all x1, starting transfers between devices, on_device(): early = lax.all_to_all(early, 'row', 0, 0).reshape(1024, 128)  7.58 us
    all_to_all x1, waiting for transfers between devices, on_device(): packed = lax.all_to_all(packed, 'col', 0, 0)  5.5 us
  transfers between devices with their start and end apart: 45, of which 14 were waited for; matrix products, arithmetic and copies ran while one was open for 2% of the time, Pallas kernels for 22%

profile of v9, /device:TPU:4, one launch (start us, length us, event | category | flops | bytes accessed | tf_op | source)
XLA Modules:
  0.0 194.2 jit_solution(4272140132735070405)
XLA Ops:
  7.3 2.7 %shard_map.88 = f32[288,384]{1,0:T(8,128)} custom-call(s32[2]{0:T(128)S(1)} %pad_add_fusion.2.place_ref, f32[2,192,384]{2,1,0:T(8,128)} %factor_ref.1), custom_call_target="tpu_custom_call" | custom-call | tf_op jit(solution)/shard_map/pallas_call | solution.py:84
  10.3 1.4 shard_map.86
  11.7 5.3 %all-to-all-start = ((f32[8,16,128]{2,1,0:T(8,128)}), f32[8,16,128]{2,1,0:T(8,128)S(1)}, u32[]{:S(2)}, u32[]{:S(2)}) async-start(f32[8,16,128]{2,1,0:T(8,128)} %shard_map.86), calls=%async_computation | async-start | bytes 131072 | tf_op jit(solution)/shard_map/all_to_all | solution.py:444
  17.1 5.5 %all-to-all-done = f32[8,16,128]{2,1,0:T(8,128)S(1)} async-done(((f32[8,16,128]{2,1,0:T(8,128)}), f32[8,16,128]{2,1,0:T(8,128)S(1)}, u32[]{:S(2)}, u32[]{:S(2)}) %all-to-all-start) | async-done | bytes 65568 | tf_op jit(solution)/shard_map/all_to_all | solution.py:444
  23.5 7.6 %all-to-all-start.1 = ((f32[16,64,128]{2,1,0:T(8,128)}), f32[16,64,128]{2,1,0:T(8,128)S(1)}, u32[]{:S(2)}, u32[]{:S(2)}) async-start(f32[16,64,128]{2,1,0:T(8,128)} %broadcast_in_dim.34), calls=%async_computation.1 | async-start | bytes 1048576 | tf_op jit(solution)/shard_map/all_to_all | solution.py:446
  32.0 8.1 %all-to-all-done.1 = f32[16,64,128]{2,1,0:T(8,128)S(1)} async-done(((f32[16,64,128]{2,1,0:T(8,128)}), f32[16,64,128]{2,1,0:T(8,128)S(1)}, u32[]{:S(2)}, u32[]{:S(2)}) %all-to-all-start.1) | async-done | bytes 524320 | tf_op jit(solution)/shard_map/all_to_all | solution.py:446
  40.1 1.9 shard_map.87.rhs_ref
  43.1 2.3 %shard_map.89.acc_ref = f32[32,192]{1,0:T(8,128)S(1)} custom-call(s32[2]{0:T(128)S(1)} %pad_add_fusion.2.place_ref, f32[32,1024]{1,0:T(8,128)S(1)} %shard_map.87.rhs_ref, f32[8,3,96,384]{3,2,1,0:T(8,128)} %bitcast.37), custom_call_target="tpu_custom_call" | custom-call | tf_op jit(solution)/shard_map/pallas_call | solution.py:84
  45.4 1.3 collective-permute-start
  46.7 1.3 collective-permute-start.1
  48.0 1.3 collective-permute-start.2
  49.3 1.3 collective-permute-start.3
  50.6 1.9 shard_map.90.weight_ref
  52.5 2.1 %collective-permute-done.1.y1 = f32[32,192]{1,0:T(8,128)S(1)} collective-permute-done((f32[32,192]{1,0:T(8,128)S(1)}, f32[32,192]{1,0:T(8,128)S(1)}, u32[]{:S(2)}, u32[]{:S(2)}) %collective-permute-start.1) | collective-permute-done | bytes 24608 | tf_op jit(solution)/shard_map/ppermute | solution.py:408
  54.6 1.6 collective-permute-done.2.y2
  64.4 2.3 %shard_map.92 = (f32[768,384]{1,0:T(8,128)S(1)}, f32[768,384]{1,0:T(8,128)S(1)}) custom-call(s32[2]{0:T(128)S(1)} %pad_add_fusion.2.place_ref, f32[8,3,96,384]{3,2,1,0:T(8,128)} %bitcast.39, f32[8,3,96,384]{3,2,1,0:T(8,128)} %bitcast.40), custom_call_target="tpu_custom_call" | custom-call | tf_op jit(solution)/shard_map/pallas_call | solution.py:84
  66.8 1.6 shard_map.93
  68.5 1.3 collective-permute-start.10
  73.7 1.9 shard_map.94.weight_ref
  75.6 2.8 %collective-permute-done.10.p1 = f32[32,768]{1,0:T(8,128)S(1)} collective-permute-done((f32[32,768]{1,0:T(8,128)S(1)}, f32[32,768]{1,0:T(8,128)S(1)}, u32[]{:S(2)}, u32[]{:S(2)}) %collective-permute-start.10) | collective-permute-done | bytes 98336 | tf_op jit(solution)/shard_map/ppermute | solution.py:408
  78.4 5.4 %collective-permute-done.11.p2 = f32[32,768]{1,0:T(8,128)S(1)} collective-permute-done((f32[32,768]{1,0:T(8,128)S(1)}, f32[32,768]{1,0:T(8,128)S(1)}, u32[]{:S(2)}, u32[]{:S(2)}) %collective-permute-start.11) | collective-permute-done | bytes 98336 | tf_op jit(solution)/shard_map/ppermute | solution.py:408
  84.9 1.4 shard_map.95
  87.6 1.3 collective-permute-start.14
  88.9 1.3 collective-permute-start.15
  90.2 1.3 collective-permute-start.16
  91.5 1.3 collective-permute-start.17
  92.8 2.3 %shard_map.96 = (f32[768,384]{1,0:T(8,128)S(1)}, f32[768,384]{1,0:T(8,128)S(1)}) custom-call(s32[2]{0:T(128)S(1)} %pad_add_fusion.2.place_ref, f32[8,3,96,384]{3,2,1,0:T(8,128)} %bitcast.42, f32[8,3,96,384]{3,2,1,0:T(8,128)} %bitcast.43), custom_call_target="tpu_custom_call" | custom-call | tf_op jit(solution)/shard_map/pallas_call | solution.py:84
  95.2 1.5 collective-permute-done.16.p3
  97.7 2.2 %shard_map.97 = (f32[2,32,768]{2,1,0:T(8,128)}, f32[32,192]{1,0:T(8,128)S(1)}, f32[32,768]{1,0:T(8,128)}) custom-call(s32[2]{0:T(128)S(1)} %pad_add_fusion.2.place_ref, f32[32,192]{1,0:T(8,128)S(1)} %get-tuple-element.66.acc_ref, f32[192,1536]{1,0:T(8,128)S(1)} %bitcast.32, f32[32,768]{1,0:T(8,128)S(1)} %collective-permute-done.13.p0, ...), custom_call_target="tpu_custom_call" | custom-call | tf_op jit(solution)/shard_map/pallas_call | solution.py:84
  100.5 1.3 collective-permute-start.22
  101.9 1.3 collective-permute-start.18
  107.0 2.8 %shard_map.99 = (f32[768,384]{1,0:T(8,128)S(1)}, f32[768,384]{1,0:T(8,128)S(1)}, f32[768,384]{1,0:T(8,128)S(1)}) custom-call(s32[2]{0:T(128)S(1)} %pad_add_fusion.2.place_ref, f32[8,3,96,384]{3,2,1,0:T(8,128)} %bitcast.44, f32[8,3,96,384]{3,2,1,0:T(8,128)} %bitcast.45, f32[8,3,96,384]{3,2,1,0:T(8,128)} %bitcast.46), custom_call_target="tpu_custom_call" | custom-call | tf_op jit(solution)/shard_map/pallas_call | solution.py:84
  111.6 4.3 %shard_map.98 = (f32[32,1024]{1,0:T(8,128)S(1)}, f32[16,1024]{1,0:T(8,128)S(1)}) custom-call(s32[2048]{0:T(1024)S(1)} %bitcast.36, f32[2,1024]{1,0:T(2,128)S(1)} %copy-done.13, f32[16,64,256]{2,1,0:T(8,128)} %bitcast.55), custom_call_target="tpu_custom_call" | custom-call | tf_op jit(solution)/shard_map/pallas_call | solution.py:84
  120.2 3.8 %shard_map.100 = (f32[32,768]{1,0:T(8,128)}, f32[2,32,768]{2,1,0:T(8,128)S(1)}, f32[32,768]{1,0:T(8,128)}) custom-call(s32[2]{0:T(128)S(1)} %pad_add_fusion.2.place_ref, f32[32,192]{1,0:T(8,128)S(1)} %copy-done.15, f32[192,1536]{1,0:T(8,128)S(1)} %bitcast.33, f32[32,768]{1,0:T(8,128)} %collective-permute-done.18.p0, f32[32,768]{1,0:T(8,128)} %collective-permute-done.19.p1, ...), custom_call_target="tpu_custom_call" | custom-call | tf_op jit(solution)/shard_map/pallas_call | solution.py:84
  127.3 1.9 collective-permute-start.27
  129.3 1.9 shard_map.101.weight_ref
  131.2 9.4 %collective-permute-done.27.own_ref = f32[32,768]{1,0:T(8,128)S(1)} collective-permute-done((f32[32,768]{1,0:T(8,128)}, f32[32,768]{1,0:T(8,128)S(1)}, u32[]{:S(2)}, u32[]{:S(2)}) %collective-permute-start.27) | collective-permute-done | bytes 98336 | tf_op jit(solution)/shard_map/ppermute | solution.py:408
  148.2 3.2 %collective-permute-done.30.f1 = f32[32,192]{1,0:T(8,128)S(1)} collective-permute-done((f32[32,192]{1,0:T(8,128)S(1)}, f32[32,192]{1,0:T(8,128)S(1)}, u32[]{:S(2)}, u32[]{:S(2)}) %collective-permute-start.30) | collective-permute-done | bytes 24608 | tf_op jit(solution)/shard_map/ppermute | solution.py:408
  153.2 2.3 %shard_map.103 = (f32[768,384]{1,0:T(8,128)S(1)}, f32[768,384]{1,0:T(8,128)S(1)}) custom-call(s32[2]{0:T(128)S(1)} %pad_add_fusion.2.place_ref, f32[8,3,96,384]{3,2,1,0:T(8,128)} %bitcast.48, f32[8,3,96,384]{3,2,1,0:T(8,128)} %bitcast.49), custom_call_target="tpu_custom_call" | custom-call | tf_op jit(solution)/shard_map/pallas_call | solution.py:84
  155.5 1.3 collective-permute-done.31.f2
  158.1 3.5 %collective-permute-start.36 = (f32[32,192]{1,0:T(8,128)S(1)}, f32[32,192]{1,0:T(8,128)S(1)}, u32[]{:S(2)}, u32[]{:S(2)}) collective-permute-start(f32[32,192]{1,0:T(8,128)S(1)} %get-tuple-element.100.acc_ref), channel_id=1, source_target_pairs={{64,96},{72,104},{80,112},{88,120},{65,97},{73,105},{81,113},{89,1... | collective-permute-start | bytes 73736 | tf_op jit(solution)/shard_map/ppermute | solution.py:408
  163.0 2.1 %collective-permute-start.38 = (f32[32,192]{1,0:T(8,128)S(1)}, f32[32,192]{1,0:T(8,128)S(1)}, u32[]{:S(2)}, u32[]{:S(2)}) collective-permute-start(f32[32,192]{1,0:T(8,128)S(1)} %get-tuple-element.100.acc_ref), channel_id=1, source_target_pairs={{64,112},{72,120},{80,96},{88,104},{65,113},{73,121},{81,97},{89,1... | collective-permute-start | bytes 73736 | tf_op jit(solution)/shard_map/ppermute | solution.py:408
  165.1 1.9 collective-permute-start.39
  167.0 1.3 collective-permute-start.35
  168.3 2.8 %shard_map.105 = (f32[768,384]{1,0:T(8,128)S(1)}, f32[768,384]{1,0:T(8,128)S(1)}, f32[768,384]{1,0:T(8,128)S(1)}) custom-call(s32[2]{0:T(128)S(1)} %pad_add_fusion.2.place_ref, f32[8,3,96,384]{3,2,1,0:T(8,128)} %bitcast.50, f32[8,3,96,384]{3,2,1,0:T(8,128)} %bitcast.51, f32[8,3,96,384]{3,2,1,0:T(8,128)} %bitcast.52), custom_call_target="tpu_custom_call" | custom-call | tf_op jit(solution)/shard_map/pallas_call | solution.py:84
  171.1 2.2 %shard_map.107.cells_ref = f32[8,32,128]{2,1,0:T(8,128)S(1)} custom-call(s32[194]{0:T(256)S(1)} %pad_add_fusion.1.where_ref, f32[32,768]{1,0:T(8,128)S(1)} %collective-permute-done.34.x0_zero, f32[32,768]{1,0:T(8,128)S(1)} %collective-permute-done.33.x0_three, f32[2,32,768]{2,1,0:T(8,128)S(1)} %get-tuple-element.92.sent_ref.pass_ref, ...), custom_call_target="tpu_custom_call" | custom-call | tf_op jit(solution)/shard_map/pallas_call | solution.py:84
  174.5 1.3 shard_map.108
  175.8 9.9 %all_to_all.15.got_ref = f32[8,32,256]{2,1,0:T(8,128)S(1)} all-to-all(f32[8,32,256]{2,1,0:T(8,128)S(1)} %shard_map.108), channel_id=1, replica_groups=mesh['row'=16,'col'=8] {'col'}, dimensions={0} | all-to-all | bytes 524288 | tf_op jit(solution)/shard_map/all_to_all | solution.py:590
  (144 shorter events, 47.5 us)
Async XLA Ops:
  7.2 35.9 %all-gather.7.cloned.1.call-start = ((), (), s32[]{:S(2)}) async-start(), calls=%async_computation.3 | async-start | bytes 3981312 | tf_op jit(solution)/shard_map/all_gather | solution.py:425
  11.7 10.9 %all-to-all-start = ((f32[8,16,128]{2,1,0:T(8,128)}), f32[8,16,128]{2,1,0:T(8,128)S(1)}, u32[]{:S(2)}, u32[]{:S(2)}) async-start(f32[8,16,128]{2,1,0:T(8,128)} %shard_map.86), calls=%async_computation | async-start | bytes 131072 | tf_op jit(solution)/shard_map/all_to_all | solution.py:444
  23.5 18.6 %copy-start.17 = (f32[2,192,384]{2,1,0:T(8,128)S(1)}, f32[2,192,384]{2,1,0:T(8,128)}, u32[]{:S(2)}) copy-start(f32[2,192,384]{2,1,0:T(8,128)} %param.11) | copy-start | bytes 1769476
  23.5 16.6 %all-to-all-start.1 = ((f32[16,64,128]{2,1,0:T(8,128)}), f32[16,64,128]{2,1,0:T(8,128)S(1)}, u32[]{:S(2)}, u32[]{:S(2)}) async-start(f32[16,64,128]{2,1,0:T(8,128)} %broadcast_in_dim.34), calls=%async_computation.1 | async-start | bytes 1048576 | tf_op jit(solution)/shard_map/all_to_all | solution.py:446
  31.1 79.8 %all-gather.9.cloned.1.call-start = ((), (), s32[]{:S(2)}) async-start(), calls=%async_computation.4 | async-start | bytes 1114112 | tf_op jit(solution)/shard_map/all_gather | solution.py:462
  31.3 14.1 %copy-start.12 = (f32[2,1024]{1,0:T(2,128)}, f32[2,1024]{1,0:T(2,128)S(1)}, u32[]{:S(2)}) copy-start(f32[2,1024]{1,0:T(2,128)S(1)} %get-tuple-element.116.mark_ref) | copy-start | bytes 24580
  42.1 87.2 %all-gather.11.cloned.1.call-start = ((), (), s32[]{:S(2)}) async-start(), calls=%async_computation.5 | async-start | bytes 3981312 | tf_op jit(solution)/shard_map/all_gather | solution.py:425
  45.4 7.1 %collective-permute-start = (f32[32,192]{1,0:T(8,128)S(1)}, f32[32,192]{1,0:T(8,128)S(1)}, u32[]{:S(2)}, u32[]{:S(2)}) collective-permute-start(f32[32,192]{1,0:T(8,128)S(1)} %shard_map.89.acc_ref), channel_id=1, source_target_pairs={{32,64},{40,72},{48,80},{56,88},{33,65},{41,73},{49,81},{57,89},{3... | collective-permute-start | bytes 73736 | tf_op jit(solution)/shard_map/ppermute | solution.py:408
  46.7 7.9 %collective-permute-start.1 = (f32[32,192]{1,0:T(8,128)S(1)}, f32[32,192]{1,0:T(8,128)S(1)}, u32[]{:S(2)}, u32[]{:S(2)}) collective-permute-start(f32[32,192]{1,0:T(8,128)S(1)} %shard_map.89.acc_ref), channel_id=1, source_target_pairs={{32,72},{40,80},{48,88},{56,64},{33,73},{41,81},{49,89},{57,65},{3... | collective-permute-start | bytes 73736 | tf_op jit(solution)/shard_map/ppermute | solution.py:408
  48.0 8.2 %collective-permute-start.2 = (f32[32,192]{1,0:T(8,128)S(1)}, f32[32,192]{1,0:T(8,128)S(1)}, u32[]{:S(2)}, u32[]{:S(2)}) collective-permute-start(f32[32,192]{1,0:T(8,128)S(1)} %shard_map.89.acc_ref), channel_id=1, source_target_pairs={{32,80},{40,88},{48,64},{56,72},{33,81},{41,89},{49,65},{57,73},{3... | collective-permute-start | bytes 73736 | tf_op jit(solution)/shard_map/ppermute | solution.py:408
  49.3 7.4 %collective-permute-start.3 = (f32[32,192]{1,0:T(8,128)S(1)}, f32[32,192]{1,0:T(8,128)S(1)}, u32[]{:S(2)}, u32[]{:S(2)}) collective-permute-start(f32[32,192]{1,0:T(8,128)S(1)} %shard_map.89.acc_ref), channel_id=1, source_target_pairs={{32,88},{40,64},{48,72},{56,80},{33,89},{41,65},{49,73},{57,81},{3... | collective-permute-start | bytes 73736 | tf_op jit(solution)/shard_map/ppermute | solution.py:408
  57.8 9.0 %collective-permute-start.4 = (f32[4,32,192]{2,1,0:T(8,128)S(1)}, f32[4,32,192]{2,1,0:T(8,128)S(1)}, u32[]{:S(2)}, u32[]{:S(2)}) collective-permute-start(f32[4,32,192]{2,1,0:T(8,128)S(1)} %get-tuple-element.59), channel_id=1, source_target_pairs={{64,96},{72,104},{80,112},{88,120},{65,97},{73,105},{81,113},{89,1... | collective-permute-start | bytes 294920 | tf_op jit(solution)/shard_map/ppermute | solution.py:408
  59.1 7.7 %collective-permute-start.5 = (f32[32,192]{1,0:T(8,128)S(1)}, f32[32,192]{1,0:T(8,128)S(1)}, u32[]{:S(2)}, u32[]{:S(2)}) collective-permute-start(f32[32,192]{1,0:T(8,128)S(1)} %get-tuple-element.56.acc_ref), channel_id=1, source_target_pairs={{64,96},{72,104},{80,112},{88,120},{65,97},{73,105},{81,113},{89,1... | collective-permute-start | bytes 73736 | tf_op jit(solution)/shard_map/ppermute | solution.py:408
  60.4 6.4 %collective-permute-start.6 = (f32[32,192]{1,0:T(8,128)S(1)}, f32[32,192]{1,0:T(8,128)S(1)}, u32[]{:S(2)}, u32[]{:S(2)}) collective-permute-start(f32[32,192]{1,0:T(8,128)S(1)} %get-tuple-element.56.acc_ref), channel_id=1, source_target_pairs={{64,104},{72,112},{80,120},{88,96},{65,105},{73,113},{81,121},{89,... | collective-permute-start | bytes 73736 | tf_op jit(solution)/shard_map/ppermute | solution.py:408
  61.7 5.1 %collective-permute-start.7 = (f32[32,192]{1,0:T(8,128)S(1)}, f32[32,192]{1,0:T(8,128)S(1)}, u32[]{:S(2)}, u32[]{:S(2)}) collective-permute-start(f32[32,192]{1,0:T(8,128)S(1)} %get-tuple-element.56.acc_ref), channel_id=1, source_target_pairs={{64,112},{72,120},{80,96},{88,104},{65,113},{73,121},{81,97},{89,1... | collective-permute-start | bytes 73736 | tf_op jit(solution)/shard_map/ppermute | solution.py:408
  63.0 3.8 %collective-permute-start.8 = (f32[32,192]{1,0:T(8,128)S(1)}, f32[32,192]{1,0:T(8,128)S(1)}, u32[]{:S(2)}, u32[]{:S(2)}) collective-permute-start(f32[32,192]{1,0:T(8,128)S(1)} %get-tuple-element.56.acc_ref), channel_id=1, source_target_pairs={{64,120},{72,96},{80,104},{88,112},{65,121},{73,97},{81,105},{89,1... | collective-permute-start | bytes 73736 | tf_op jit(solution)/shard_map/ppermute | solution.py:408
  68.5 9.9 %collective-permute-start.10 = (f32[32,768]{1,0:T(8,128)S(1)}, f32[32,768]{1,0:T(8,128)S(1)}, u32[]{:S(2)}, u32[]{:S(2)}) collective-permute-start(f32[32,768]{1,0:T(8,128)S(1)} %get-tuple-element.64), channel_id=1, source_target_pairs={{96,72},{104,80},{112,88},{120,64},{97,73},{105,81},{113,89},{121,... | collective-permute-start | bytes 294920 | tf_op jit(solution)/shard_map/ppermute | solution.py:408
  69.8 14.1 %collective-permute-start.11 = (f32[32,768]{1,0:T(8,128)S(1)}, f32[32,768]{1,0:T(8,128)S(1)}, u32[]{:S(2)}, u32[]{:S(2)}) collective-permute-start(f32[32,768]{1,0:T(8,128)S(1)} %get-tuple-element.64), channel_id=1, source_target_pairs={{96,80},{104,88},{112,64},{120,72},{97,81},{105,89},{113,65},{121,... | collective-permute-start | bytes 294920 | tf_op jit(solution)/shard_map/ppermute | solution.py:408
  71.1 13.1 %collective-permute-start.12 = (f32[32,768]{1,0:T(8,128)S(1)}, f32[32,768]{1,0:T(8,128)S(1)}, u32[]{:S(2)}, u32[]{:S(2)}) collective-permute-start(f32[32,768]{1,0:T(8,128)S(1)} %get-tuple-element.64), channel_id=1, source_target_pairs={{96,88},{104,64},{112,72},{120,80},{97,89},{105,65},{113,73},{121,... | collective-permute-start | bytes 294920 | tf_op jit(solution)/shard_map/ppermute | solution.py:408
  72.4 12.6 %collective-permute-start.9 = (f32[32,768]{1,0:T(8,128)S(1)}, f32[32,768]{1,0:T(8,128)S(1)}, u32[]{:S(2)}, u32[]{:S(2)}) collective-permute-start(f32[32,768]{1,0:T(8,128)S(1)} %get-tuple-element.64), channel_id=1, source_target_pairs={{96,64},{104,72},{112,80},{120,88},{97,65},{105,73},{113,81},{121,... | collective-permute-start | bytes 294920 | tf_op jit(solution)/shard_map/ppermute | solution.py:408
  86.3 8.9 %collective-permute-start.13 = (f32[32,768]{1,0:T(8,128)S(1)}, f32[32,768]{1,0:T(8,128)S(1)}, u32[]{:S(2)}, u32[]{:S(2)}) collective-permute-start(f32[32,768]{1,0:T(8,128)S(1)} %get-tuple-element.67), channel_id=1, source_target_pairs={{64,32},{72,40},{80,48},{88,56},{65,33},{73,41},{81,49},{89,57},{6... | collective-permute-start | bytes 294920 | tf_op jit(solution)/shard_map/ppermute | solution.py:408
  87.6 7.6 %collective-permute-start.14 = (f32[32,768]{1,0:T(8,128)S(1)}, f32[32,768]{1,0:T(8,128)S(1)}, u32[]{:S(2)}, u32[]{:S(2)}) collective-permute-start(f32[32,768]{1,0:T(8,128)S(1)} %get-tuple-element.67), channel_id=1, source_target_pairs={{64,40},{72,48},{80,56},{88,32},{65,41},{73,49},{81,57},{89,33},{6... | collective-permute-start | bytes 294920 | tf_op jit(solution)/shard_map/ppermute | solution.py:408
  88.9 6.3 %collective-permute-start.15 = (f32[32,768]{1,0:T(8,128)S(1)}, f32[32,768]{1,0:T(8,128)S(1)}, u32[]{:S(2)}, u32[]{:S(2)}) collective-permute-start(f32[32,768]{1,0:T(8,128)S(1)} %get-tuple-element.67), channel_id=1, source_target_pairs={{64,48},{72,56},{80,32},{88,40},{65,49},{73,57},{81,33},{89,41},{6... | collective-permute-start | bytes 294920 | tf_op jit(solution)/shard_map/ppermute | solution.py:408
  90.2 6.5 %collective-permute-start.16 = (f32[32,768]{1,0:T(8,128)S(1)}, f32[32,768]{1,0:T(8,128)S(1)}, u32[]{:S(2)}, u32[]{:S(2)}) collective-permute-start(f32[32,768]{1,0:T(8,128)S(1)} %get-tuple-element.67), channel_id=1, source_target_pairs={{64,56},{72,32},{80,40},{88,48},{65,57},{73,33},{81,41},{89,49},{6... | collective-permute-start | bytes 294920 | tf_op jit(solution)/shard_map/ppermute | solution.py:408
  91.5 6.2 %collective-permute-start.17 = (f32[32,768]{1,0:T(8,128)S(1)}, f32[32,768]{1,0:T(8,128)S(1)}, u32[]{:S(2)}, u32[]{:S(2)}) collective-permute-start(f32[32,768]{1,0:T(8,128)S(1)} %get-tuple-element.68.x3_ref), channel_id=1, source_target_pairs={{64,32},{72,40},{80,48},{88,56},{65,33},{73,41},{81,49},{89,57},{6... | collective-permute-start | bytes 294920 | tf_op jit(solution)/shard_map/ppermute | solution.py:408
  100.5 16.7 %collective-permute-start.22 = (f32[2,32,768]{2,1,0:T(8,128)}, f32[2,32,768]{2,1,0:T(8,128)}, u32[]{:S(2)}, u32[]{:S(2)}) collective-permute-start(f32[2,32,768]{2,1,0:T(8,128)} %get-tuple-element.81.x2_ref), channel_id=1, source_target_pairs={{32,0},{40,8},{48,16},{56,24},{33,1},{41,9},{49,17},{57,25},{34,2}... | collective-permute-start | bytes 589832 | tf_op jit(solution)/shard_map/ppermute | solution.py:408
  101.9 15.3 %collective-permute-start.18 = (f32[32,768]{1,0:T(8,128)}, f32[32,768]{1,0:T(8,128)}, u32[]{:S(2)}, u32[]{:S(2)}) collective-permute-start(f32[32,768]{1,0:T(8,128)} %get-tuple-element.74), channel_id=1, source_target_pairs={{32,0},{40,8},{48,16},{56,24},{33,1},{41,9},{49,17},{57,25},{34,2}... | collective-permute-start | bytes 294920 | tf_op jit(solution)/shard_map/ppermute | solution.py:408
  103.2 14.1 %collective-permute-start.19 = (f32[32,768]{1,0:T(8,128)}, f32[32,768]{1,0:T(8,128)}, u32[]{:S(2)}, u32[]{:S(2)}) collective-permute-start(f32[32,768]{1,0:T(8,128)} %get-tuple-element.74), channel_id=1, source_target_pairs={{32,8},{40,16},{48,24},{56,0},{33,9},{41,17},{49,25},{57,1},{34,10... | collective-permute-start | bytes 294920 | tf_op jit(solution)/shard_map/ppermute | solution.py:408
  104.4 12.8 %collective-permute-start.20 = (f32[32,768]{1,0:T(8,128)}, f32[32,768]{1,0:T(8,128)}, u32[]{:S(2)}, u32[]{:S(2)}) collective-permute-start(f32[32,768]{1,0:T(8,128)} %get-tuple-element.74), channel_id=1, source_target_pairs={{32,16},{40,24},{48,0},{56,8},{33,17},{41,25},{49,1},{57,9},{34,18... | collective-permute-start | bytes 294920 | tf_op jit(solution)/shard_map/ppermute | solution.py:408
  105.7 11.5 %collective-permute-start.21 = (f32[32,768]{1,0:T(8,128)}, f32[32,768]{1,0:T(8,128)}, u32[]{:S(2)}, u32[]{:S(2)}) collective-permute-start(f32[32,768]{1,0:T(8,128)} %get-tuple-element.74), channel_id=1, source_target_pairs={{32,24},{40,0},{48,8},{56,16},{33,25},{41,1},{49,9},{57,17},{34,26... | collective-permute-start | bytes 294920 | tf_op jit(solution)/shard_map/ppermute | solution.py:408
  124.6 6.6 %collective-permute-start.23 = (f32[32,768]{1,0:T(8,128)}, f32[32,768]{1,0:T(8,128)S(1)}, u32[]{:S(2)}, u32[]{:S(2)}) collective-permute-start(f32[32,768]{1,0:T(8,128)} %get-tuple-element.86), channel_id=1, source_target_pairs={{0,32},{8,40},{16,48},{24,56},{1,33},{9,41},{17,49},{25,57},{2,34}... | collective-permute-start | bytes 294920 | tf_op jit(solution)/shard_map/ppermute | solution.py:408
  125.3 5.9 %collective-permute-start.24 = (f32[32,768]{1,0:T(8,128)}, f32[32,768]{1,0:T(8,128)S(1)}, u32[]{:S(2)}, u32[]{:S(2)}) collective-permute-start(f32[32,768]{1,0:T(8,128)} %get-tuple-element.86), channel_id=1, source_target_pairs={{0,40},{8,48},{16,56},{24,32},{1,41},{9,49},{17,57},{25,33},{2,42}... | collective-permute-start | bytes 294920 | tf_op jit(solution)/shard_map/ppermute | solution.py:408
  126.0 5.3 %collective-permute-start.25 = (f32[32,768]{1,0:T(8,128)}, f32[32,768]{1,0:T(8,128)S(1)}, u32[]{:S(2)}, u32[]{:S(2)}) collective-permute-start(f32[32,768]{1,0:T(8,128)} %get-tuple-element.86), channel_id=1, source_target_pairs={{0,48},{8,56},{16,32},{24,40},{1,49},{9,57},{17,33},{25,41},{2,50}... | collective-permute-start | bytes 294920 | tf_op jit(solution)/shard_map/ppermute | solution.py:408
  126.6 4.6 %collective-permute-start.26 = (f32[32,768]{1,0:T(8,128)}, f32[32,768]{1,0:T(8,128)S(1)}, u32[]{:S(2)}, u32[]{:S(2)}) collective-permute-start(f32[32,768]{1,0:T(8,128)} %get-tuple-element.86), channel_id=1, source_target_pairs={{0,56},{8,32},{16,40},{24,48},{1,57},{9,33},{17,41},{25,49},{2,58}... | collective-permute-start | bytes 294920 | tf_op jit(solution)/shard_map/ppermute | solution.py:408
  127.3 13.3 %collective-permute-start.27 = (f32[32,768]{1,0:T(8,128)}, f32[32,768]{1,0:T(8,128)S(1)}, u32[]{:S(2)}, u32[]{:S(2)}) collective-permute-start(f32[32,768]{1,0:T(8,128)} %get-tuple-element.87.newest_ref), channel_id=1, source_target_pairs={{0,32},{8,40},{16,48},{24,56},{32,64},{40,72},{48,80},{56,88},{64,... | collective-permute-start | bytes 294920 | tf_op jit(solution)/shard_map/ppermute | solution.py:408
  131.2 21.6 %copy-start.19 = (s32[3072]{0:T(1024)S(1)}, s32[3072]{0:T(1024)}, u32[]{:S(2)}) copy-start(s32[3072]{0:T(1024)} %param.13) | copy-start | bytes 36868
  141.7 9.7 %collective-permute-start.30 = (f32[32,192]{1,0:T(8,128)S(1)}, f32[32,192]{1,0:T(8,128)S(1)}, u32[]{:S(2)}, u32[]{:S(2)}) collective-permute-start(f32[32,192]{1,0:T(8,128)S(1)} %get-tuple-element.91.acc_ref), channel_id=1, source_target_pairs={{32,72},{40,80},{48,88},{56,64},{33,73},{41,81},{49,89},{57,65},{3... | collective-permute-start | bytes 73736 | tf_op jit(solution)/shard_map/ppermute | solution.py:408
  143.0 9.1 %collective-permute-start.29 = (f32[32,192]{1,0:T(8,128)S(1)}, f32[32,192]{1,0:T(8,128)S(1)}, u32[]{:S(2)}, u32[]{:S(2)}) collective-permute-start(f32[32,192]{1,0:T(8,128)S(1)} %get-tuple-element.91.acc_ref), channel_id=1, source_target_pairs={{32,64},{40,72},{48,80},{56,88},{33,65},{41,73},{49,81},{57,89},{3... | collective-permute-start | bytes 73736 | tf_op jit(solution)/shard_map/ppermute | solution.py:408
  144.3 12.5 %collective-permute-start.28 = (f32[2,32,768]{2,1,0:T(8,128)S(1)}, f32[2,32,768]{2,1,0:T(8,128)S(1)}, u32[]{:S(2)}, u32[]{:S(2)}) collective-permute-start(f32[2,32,768]{2,1,0:T(8,128)S(1)} %get-tuple-element.92.sent_ref.pass_ref), channel_id=1, source_target_pairs={{32,64},{40,72},{48,80},{56,88},{0,96},{8,104},{16,112},{24,120},{... | collective-permute-start | bytes 589832 | tf_op jit(solution)/shard_map/ppermute | solution.py:408
  145.6 11.2 %collective-permute-start.31 = (f32[32,192]{1,0:T(8,128)S(1)}, f32[32,192]{1,0:T(8,128)S(1)}, u32[]{:S(2)}, u32[]{:S(2)}) collective-permute-start(f32[32,192]{1,0:T(8,128)S(1)} %get-tuple-element.91.acc_ref), channel_id=1, source_target_pairs={{32,80},{40,88},{48,64},{56,72},{33,81},{41,89},{49,65},{57,73},{3... | collective-permute-start | bytes 73736 | tf_op jit(solution)/shard_map/ppermute | solution.py:408
  146.9 9.9 %collective-permute-start.32 = (f32[32,192]{1,0:T(8,128)S(1)}, f32[32,192]{1,0:T(8,128)S(1)}, u32[]{:S(2)}, u32[]{:S(2)}) collective-permute-start(f32[32,192]{1,0:T(8,128)S(1)} %get-tuple-element.91.acc_ref), channel_id=1, source_target_pairs={{32,88},{40,64},{48,72},{56,80},{33,89},{41,65},{49,73},{57,81},{3... | collective-permute-start | bytes 73736 | tf_op jit(solution)/shard_map/ppermute | solution.py:408
  151.4 6.7 %collective-permute-start.33 = (f32[32,768]{1,0:T(8,128)S(1)}, f32[32,768]{1,0:T(8,128)S(1)}, u32[]{:S(2)}, u32[]{:S(2)}) collective-permute-start(f32[32,768]{1,0:T(8,128)S(1)} %get-tuple-element.99), channel_id=1, source_target_pairs={{32,96},{40,104},{48,112},{56,120},{33,97},{41,105},{49,113},{57,1... | collective-permute-start | bytes 294920 | tf_op jit(solution)/shard_map/ppermute | solution.py:408
  152.1 6.0 %collective-permute-start.34 = (f32[32,768]{1,0:T(8,128)S(1)}, f32[32,768]{1,0:T(8,128)S(1)}, u32[]{:S(2)}, u32[]{:S(2)}) collective-permute-start(f32[32,768]{1,0:T(8,128)S(1)} %get-tuple-element.99), channel_id=1, source_target_pairs={{32,0},{40,8},{48,16},{56,24},{33,1},{41,9},{49,17},{57,25},{34,2}... | collective-permute-start | bytes 294920 | tf_op jit(solution)/shard_map/ppermute | solution.py:408
  158.1 16.3 %collective-permute-start.36 = (f32[32,192]{1,0:T(8,128)S(1)}, f32[32,192]{1,0:T(8,128)S(1)}, u32[]{:S(2)}, u32[]{:S(2)}) collective-permute-start(f32[32,192]{1,0:T(8,128)S(1)} %get-tuple-element.100.acc_ref), channel_id=1, source_target_pairs={{64,96},{72,104},{80,112},{88,120},{65,97},{73,105},{81,113},{89,1... | collective-permute-start | bytes 73736 | tf_op jit(solution)/shard_map/ppermute | solution.py:408
  161.7 12.8 %collective-permute-start.37 = (f32[32,192]{1,0:T(8,128)S(1)}, f32[32,192]{1,0:T(8,128)S(1)}, u32[]{:S(2)}, u32[]{:S(2)}) collective-permute-start(f32[32,192]{1,0:T(8,128)S(1)} %get-tuple-element.100.acc_ref), channel_id=1, source_target_pairs={{64,104},{72,112},{80,120},{88,96},{65,105},{73,113},{81,121},{89,... | collective-permute-start | bytes 73736 | tf_op jit(solution)/shard_map/ppermute | solution.py:408
  163.0 11.5 %collective-permute-start.38 = (f32[32,192]{1,0:T(8,128)S(1)}, f32[32,192]{1,0:T(8,128)S(1)}, u32[]{:S(2)}, u32[]{:S(2)}) collective-permute-start(f32[32,192]{1,0:T(8,128)S(1)} %get-tuple-element.100.acc_ref), channel_id=1, source_target_pairs={{64,112},{72,120},{80,96},{88,104},{65,113},{73,121},{81,97},{89,1... | collective-permute-start | bytes 73736 | tf_op jit(solution)/shard_map/ppermute | solution.py:408
  165.1 9.4 %collective-permute-start.39 = (f32[32,192]{1,0:T(8,128)S(1)}, f32[32,192]{1,0:T(8,128)S(1)}, u32[]{:S(2)}, u32[]{:S(2)}) collective-permute-start(f32[32,192]{1,0:T(8,128)S(1)} %get-tuple-element.100.acc_ref), channel_id=1, source_target_pairs={{64,120},{72,96},{80,104},{88,112},{65,121},{73,97},{81,105},{89,1... | collective-permute-start | bytes 73736 | tf_op jit(solution)/shard_map/ppermute | solution.py:408
  167.0 7.5 %collective-permute-start.35 = (f32[4,32,192]{2,1,0:T(8,128)S(1)}, f32[4,32,192]{2,1,0:T(8,128)S(1)}, u32[]{:S(2)}, u32[]{:S(2)}) collective-permute-start(f32[4,32,192]{2,1,0:T(8,128)S(1)} %get-tuple-element.105), channel_id=1, source_target_pairs={{64,96},{72,104},{80,112},{88,120},{65,97},{73,105},{81,113},{89,1... | collective-permute-start | bytes 294920 | tf_op jit(solution)/shard_map/ppermute | solution.py:408
  (20 other events, 85.5 us)
Sparse Core Ops, SparseCore 0:
  10.2 31.9 all-gather.6
  44.3 43.1 all-gather.8
  89.2 28.7 all-gather.10

commit v10 on v7

--- a/solution.py
+++ b/solution.py
@@ -14,7 +14,7 @@
 BLOCK = 768
 PIECE = 96
 CELLS = 24
-LATE = 5
+LATE = 2
 VMEM = 16 * 1024 * 1024
 
 SDS = jax.ShapeDtypeStruct
@@ -434,8 +434,9 @@
         turn_first_kernel,
         [SDS((3 * PIECE, 2 * SLAB), f32)],
         place,
-        [factor1],
-        scratch=[pltpu.VMEM((4 * PIECE, 2 * SLAB), f32)],
+        [],
+        [(factor1, factor1.shape, lambda i, place: (0, 0, 0))],
+        [pltpu.VMEM((4 * PIECE, 2 * SLAB), f32)],
     )
     matrix1 = gather_blocks(turned1)
 
@@ -500,7 +501,7 @@
     )
     sent = plane_send(kept, (2, 3))
     got = plane_spread(acc, 2, 3)
-    weights = load(matrix1, [1, 2], acc)
+    weights = [*weights, *load(matrix1, [2], acc)]
     acc, part = call(
         forward_two_kernel,
         [slab_shape, block_shape],
@@ -508,6 +509,7 @@
         [acc, inverse, sent, *got, *weights],
     )
     got = plane_spread(part, 3, 2)
+    block2 = weights[1]
     weights = load(matrix1, [3], part)
     x3_two, acc, part = call(
         back_three_kernel,
@@ -517,7 +519,7 @@
     )
     x3_one = plane_send(x3_two, (2, 1))
     got = plane_spread(part, 2, 1)
-    weights = load(matrix1, [2, 3], part)
+    weights = [block2, *weights]
     both_one, acc, part = call(
         back_two_kernel,
         [pair_shape, slab_shape, block_shape],
@@ -526,7 +528,7 @@
     )
     later = plane_send(both_one, (1, 0))
     got = plane_spread(part, 1, 0)
-    weights = load(matrix1, [1, 2, 3], part)
+    weights = [*load(matrix1, [1], part), *weights]
     newest, both_zero, part = call(
         back_one_kernel,
         [block_shape, pair_shape, block_shape],
@@ -553,7 +555,7 @@
     )
     passed = plane_send(passing, (1, 2), (0, 3))
     got = plane_spread(acc, 1, 2)
-    weights = load(matrix2, [0, 1], acc, True)
+    weights = [*weights, *load(matrix2, [1], acc, True)]
     acc, kept = call(
         second_one_kernel,
         [slab_shape, SDS((2 * GROUP, ROWS, SLAB), f32)],
@@ -562,7 +564,7 @@
     )
     sent = plane_send(kept, (2, 3), (1, 0))
     got = plane_spread(acc, 2, 3)
-    weights = load(matrix2, [0, 1, 2], acc, True)
+    weights = [*weights, *load(matrix2, [2], acc, True)]
     (acc,) = call(
         second_base_kernel,
         [slab_shape],

time: 182 us -> 177 us (0.973)
  Pallas kernels: 44 us -> 40 us
    pallas_call x24 -> x23, Pallas kernels: 44 us -> 40 us  [call(): pl.pallas_call(body, grid_spec=pltpu.PrefetchScalarGridSpec(num_scalar_pr...]
  transfers between devices with their start and end apart: 43 -> 43, of which waited for: 18 -> 18; matrix products, arithmetic and copies ran while one was open for 2% -> 2% of each run, Pallas kernels for 20% -> 18%
where the time goes in v10:
time: 177 us; the launch traced here: 176 us
  starting transfers between devices  58.3 us (33%)
  waiting for transfers between devices  47.9 us (27%)
  Pallas kernels  40 us (23%)
  between operations  14.5 us (8%)
  blocking collectives  9.95 us (6%)
  local copies, waits for them, and re-layouts  4.33 us (2%)
    ppermute x38, starting transfers between devices, plane_send(): return lax.ppermute(value, 'row', pairs)  45.4 us
    pallas_call x23, Pallas kernels, call(): pl.pallas_call(body, grid_spec=pltpu.PrefetchScalarGridSpec(num_scalar_pr...  40 us
    ppermute x38, waiting for transfers between devices, plane_send(): return lax.ppermute(value, 'row', pairs)  31.2 us
    all_to_all x1, blocking collectives, on_device(): arrived = lax.all_to_all(last, 'col', 0, 0)  9.95 us
    all_to_all x1, starting transfers between devices, on_device(): early = lax.all_to_all(early, 'row', 0, 0).reshape(1024, 128)  7.45 us
    all_to_all x1, waiting for transfers between devices, on_device(): early = lax.all_to_all(early, 'row', 0, 0).reshape(1024, 128)  7.1 us
    all_to_all x1, waiting for transfers between devices, on_device(): packed = lax.all_to_all(packed, 'col', 0, 0)  5.5 us
    all_to_all x1, starting transfers between devices, on_device(): packed = lax.all_to_all(packed, 'col', 0, 0)  5.31 us
  transfers between devices with their start and end apart: 43, of which 18 were waited for; matrix products, arithmetic and copies ran while one was open for 2% of the time, Pallas kernels for 18%

profile of v10, /device:TPU:4, one launch (start us, length us, event | category | flops | bytes accessed | tf_op | source)
XLA Modules:
  0.0 175.6 jit_solution(15547674995154744424)
XLA Ops:
  7.3 2.7 %shard_map.88 = f32[288,384]{1,0:T(8,128)} custom-call(s32[2]{0:T(128)S(1)} %pad_add_fusion.2.place_ref, f32[2,192,384]{2,1,0:T(8,128)} %factor_ref.1), custom_call_target="tpu_custom_call" | custom-call | tf_op jit(solution)/shard_map/pallas_call | solution.py:84
  10.3 1.4 shard_map.86
  11.7 5.3 %all-to-all-start = ((f32[8,16,128]{2,1,0:T(8,128)}), f32[8,16,128]{2,1,0:T(8,128)S(1)}, u32[]{:S(2)}, u32[]{:S(2)}) async-start(f32[8,16,128]{2,1,0:T(8,128)} %shard_map.86), calls=%async_computation | async-start | bytes 131072 | tf_op jit(solution)/shard_map/all_to_all | solution.py:450
  17.1 5.5 %all-to-all-done = f32[8,16,128]{2,1,0:T(8,128)S(1)} async-done(((f32[8,16,128]{2,1,0:T(8,128)}), f32[8,16,128]{2,1,0:T(8,128)S(1)}, u32[]{:S(2)}, u32[]{:S(2)}) %all-to-all-start) | async-done | bytes 65568 | tf_op jit(solution)/shard_map/all_to_all | solution.py:450
  23.5 7.5 %all-to-all-start.1 = ((f32[16,64,128]{2,1,0:T(8,128)}), f32[16,64,128]{2,1,0:T(8,128)S(1)}, u32[]{:S(2)}, u32[]{:S(2)}) async-start(f32[16,64,128]{2,1,0:T(8,128)} %broadcast_in_dim.36), calls=%async_computation.1 | async-start | bytes 1048576 | tf_op jit(solution)/shard_map/all_to_all | solution.py:452
  32.8 7.1 %all-to-all-done.1 = f32[16,64,128]{2,1,0:T(8,128)S(1)} async-done(((f32[16,64,128]{2,1,0:T(8,128)}), f32[16,64,128]{2,1,0:T(8,128)S(1)}, u32[]{:S(2)}, u32[]{:S(2)}) %all-to-all-start.1) | async-done | bytes 524320 | tf_op jit(solution)/shard_map/all_to_all | solution.py:452
  39.9 1.9 %shard_map.87.rhs_ref = f32[32,1024]{1,0:T(8,128)S(1)} custom-call(s32[2048]{0:T(1024)S(1)} %bitcast.35, f32[1024,128]{1,0:T(8,128)S(1)} %bitcast.34, f32[2,1024]{1,0:T(2,128)S(1)} %get-tuple-element.72.mark_ref), custom_call_target="tpu_custom_call" | custom-call | tf_op jit(solution)/shard_map/pallas_call | solution.py:84
  42.2 2.3 %shard_map.89.acc_ref = f32[32,192]{1,0:T(8,128)S(1)} custom-call(s32[2]{0:T(128)S(1)} %pad_add_fusion.2.place_ref, f32[32,1024]{1,0:T(8,128)S(1)} %shard_map.87.rhs_ref, f32[8,3,96,384]{3,2,1,0:T(8,128)} %bitcast.37), custom_call_target="tpu_custom_call" | custom-call | tf_op jit(solution)/shard_map/pallas_call | solution.py:84
  45.2 1.3 collective-permute-start
  46.5 1.3 collective-permute-start.1
  47.8 1.3 collective-permute-start.2
  49.1 1.3 collective-permute-start.3
  50.4 1.9 %shard_map.90.weight_ref.weight1_ref = f32[768,384]{1,0:T(8,128)S(1)} custom-call(s32[2]{0:T(128)S(1)} %pad_add_fusion.2.place_ref, f32[8,3,96,384]{3,2,1,0:T(8,128)} %bitcast.38), custom_call_target="tpu_custom_call" | custom-call | tf_op jit(solution)/shard_map/pallas_call | solution.py:84
  52.3 2.2 %collective-permute-done.1.y1 = f32[32,192]{1,0:T(8,128)S(1)} collective-permute-done((f32[32,192]{1,0:T(8,128)S(1)}, f32[32,192]{1,0:T(8,128)S(1)}, u32[]{:S(2)}, u32[]{:S(2)}) %collective-permute-start.1) | collective-permute-done | bytes 24608 | tf_op jit(solution)/shard_map/ppermute | solution.py:414
  54.5 2.2 %collective-permute-done.2.y2 = f32[32,192]{1,0:T(8,128)S(1)} collective-permute-done((f32[32,192]{1,0:T(8,128)S(1)}, f32[32,192]{1,0:T(8,128)S(1)}, u32[]{:S(2)}, u32[]{:S(2)}) %collective-permute-start.2) | collective-permute-done | bytes 24608 | tf_op jit(solution)/shard_map/ppermute | solution.py:414
  65.3 1.9 %shard_map.92.weight2_ref = f32[768,384]{1,0:T(8,128)S(1)} custom-call(s32[2]{0:T(128)S(1)} %pad_add_fusion.2.place_ref, f32[8,3,96,384]{3,2,1,0:T(8,128)} %bitcast.39), custom_call_target="tpu_custom_call" | custom-call | tf_op jit(solution)/shard_map/pallas_call | solution.py:84
  67.2 1.6 shard_map.93
  68.9 1.3 collective-permute-start.10
  74.1 1.9 %shard_map.94.weight_ref.weight3_ref = f32[768,384]{1,0:T(8,128)S(1)} custom-call(s32[2]{0:T(128)S(1)} %pad_add_fusion.2.place_ref, f32[8,3,96,384]{3,2,1,0:T(8,128)} %bitcast.40), custom_call_target="tpu_custom_call" | custom-call | tf_op jit(solution)/shard_map/pallas_call | solution.py:84
  76.0 2.8 %collective-permute-done.10.p1 = f32[32,768]{1,0:T(8,128)S(1)} collective-permute-done((f32[32,768]{1,0:T(8,128)S(1)}, f32[32,768]{1,0:T(8,128)S(1)}, u32[]{:S(2)}, u32[]{:S(2)}) %collective-permute-start.10) | collective-permute-done | bytes 98336 | tf_op jit(solution)/shard_map/ppermute | solution.py:414
  78.8 5.1 %collective-permute-done.11.p2 = f32[32,768]{1,0:T(8,128)S(1)} collective-permute-done((f32[32,768]{1,0:T(8,128)S(1)}, f32[32,768]{1,0:T(8,128)S(1)}, u32[]{:S(2)}, u32[]{:S(2)}) %collective-permute-start.11) | collective-permute-done | bytes 98336 | tf_op jit(solution)/shard_map/ppermute | solution.py:414
  84.7 1.4 shard_map.95
  86.0 1.3 collective-permute-start.13
  87.3 1.3 collective-permute-start.14
  88.6 1.3 collective-permute-start.15
  89.9 1.3 collective-permute-start.16
  91.2 1.3 collective-permute-start.17
  92.6 2.1 %collective-permute-done.15.p2 = f32[32,768]{1,0:T(8,128)S(1)} collective-permute-done((f32[32,768]{1,0:T(8,128)S(1)}, f32[32,768]{1,0:T(8,128)S(1)}, u32[]{:S(2)}, u32[]{:S(2)}) %collective-permute-start.15) | collective-permute-done | bytes 98336 | tf_op jit(solution)/shard_map/ppermute | solution.py:414
  94.7 1.9 %collective-permute-done.16.p3 = f32[32,768]{1,0:T(8,128)S(1)} collective-permute-done((f32[32,768]{1,0:T(8,128)S(1)}, f32[32,768]{1,0:T(8,128)S(1)}, u32[]{:S(2)}, u32[]{:S(2)}) %collective-permute-start.16) | collective-permute-done | bytes 98336 | tf_op jit(solution)/shard_map/ppermute | solution.py:414
  97.7 1.6 shard_map.96
  102.6 1.9 %shard_map.97.weight1_ref = f32[768,384]{1,0:T(8,128)S(1)} custom-call(s32[2]{0:T(128)S(1)} %pad_add_fusion.2.place_ref, f32[8,3,96,384]{3,2,1,0:T(8,128)} %bitcast.41), custom_call_target="tpu_custom_call" | custom-call | tf_op jit(solution)/shard_map/pallas_call | solution.py:84
  104.6 2.0 %shard_map.98 = (f32[32,768]{1,0:T(8,128)S(1)}, f32[2,32,768]{2,1,0:T(8,128)S(1)}, f32[32,768]{1,0:T(8,128)S(1)}) custom-call(s32[2]{0:T(128)S(1)} %pad_add_fusion.2.place_ref, f32[32,192]{1,0:T(8,128)S(1)} %get-tuple-element.46.acc_ref, f32[192,1536]{1,0:T(8,128)S(1)} %bitcast.33, f32[32,768]{1,0:T(8,128)S(1)} %collective-permute-done.18.p0, ...), custom_call_target="tpu_custom_call" | custom-call | tf_op jit(solution)/shard_map/pallas_call | solution.py:84
  109.3 1.9 %collective-permute-start.27 = (f32[32,768]{1,0:T(8,128)S(1)}, f32[32,768]{1,0:T(8,128)S(1)}, u32[]{:S(2)}, u32[]{:S(2)}) collective-permute-start(f32[32,768]{1,0:T(8,128)S(1)} %get-tuple-element.54.newest_ref), channel_id=1, source_target_pairs={{0,32},{8,40},{16,48},{24,56},{32,64},{40,72},{48,80},{56,88},{64,... | collective-permute-start | bytes 294920 | tf_op jit(solution)/shard_map/ppermute | solution.py:414
  111.2 4.3 %shard_map.99 = (f32[32,1024]{1,0:T(8,128)S(1)}, f32[16,1024]{1,0:T(8,128)S(1)}) custom-call(s32[2048]{0:T(1024)S(1)} %bitcast.36, f32[2,1024]{1,0:T(2,128)S(1)} %get-tuple-element.72.mark_ref, f32[16,64,256]{2,1,0:T(8,128)} %bitcast.47), custom_call_target="tpu_custom_call" | custom-call | tf_op jit(solution)/shard_map/pallas_call | solution.py:84
  115.5 3.0 %all-gather.11.cloned.1.call-done = f32[2304,384]{1,0:T(8,128)} async-done(((f32[288,384]{1,0:T(8,128)}), f32[2304,384]{1,0:T(8,128)}) %all-gather.11.cloned.1.call-update) | async-done | bytes 3538960 | tf_op jit(solution)/shard_map/all_gather | solution.py:431
  118.5 1.9 %shard_map.100.weight_ref.weight0_ref = f32[768,384]{1,0:T(8,128)S(1)} custom-call(s32[2]{0:T(128)S(1)} %pad_add_fusion.2.place_ref, f32[8,3,96,384]{3,2,1,0:T(8,128)} %bitcast.42), custom_call_target="tpu_custom_call" | custom-call | tf_op jit(solution)/shard_map/pallas_call | solution.py:84
  120.5 6.1 %collective-permute-done.27.own_ref = f32[32,768]{1,0:T(8,128)S(1)} collective-permute-done((f32[32,768]{1,0:T(8,128)S(1)}, f32[32,768]{1,0:T(8,128)S(1)}, u32[]{:S(2)}, u32[]{:S(2)}) %collective-permute-start.27) | collective-permute-done | bytes 98336 | tf_op jit(solution)/shard_map/ppermute | solution.py:414
  128.9 1.3 collective-permute-start.29
  134.1 1.9 %shard_map.102.weight1_ref = f32[768,384]{1,0:T(8,128)S(1)} custom-call(s32[2]{0:T(128)S(1)} %pad_add_fusion.2.place_ref, f32[8,3,96,384]{3,2,1,0:T(8,128)} %bitcast.43), custom_call_target="tpu_custom_call" | custom-call | tf_op jit(solution)/shard_map/pallas_call | solution.py:84
  136.0 3.6 %collective-permute-done.29.f0 = f32[32,192]{1,0:T(8,128)S(1)} collective-permute-done((f32[32,192]{1,0:T(8,128)S(1)}, f32[32,192]{1,0:T(8,128)S(1)}, u32[]{:S(2)}, u32[]{:S(2)}) %collective-permute-start.29) | collective-permute-done | bytes 24608 | tf_op jit(solution)/shard_map/ppermute | solution.py:414
  139.7 2.3 %collective-permute-done.30.f1 = f32[32,192]{1,0:T(8,128)S(1)} collective-permute-done((f32[32,192]{1,0:T(8,128)S(1)}, f32[32,192]{1,0:T(8,128)S(1)}, u32[]{:S(2)}, u32[]{:S(2)}) %collective-permute-start.30) | collective-permute-done | bytes 24608 | tf_op jit(solution)/shard_map/ppermute | solution.py:414
  143.3 1.3 collective-permute-start.33
  147.6 1.9 %collective-permute-start.36 = (f32[32,192]{1,0:T(8,128)S(1)}, f32[32,192]{1,0:T(8,128)S(1)}, u32[]{:S(2)}, u32[]{:S(2)}) collective-permute-start(f32[32,192]{1,0:T(8,128)S(1)} %get-tuple-element.61.acc_ref), channel_id=1, source_target_pairs={{64,112},{72,120},{80,96},{88,104},{65,113},{73,121},{81,97},{89,1... | collective-permute-start | bytes 73736 | tf_op jit(solution)/shard_map/ppermute | solution.py:414
  149.6 1.9 %collective-permute-start.37 = (f32[32,192]{1,0:T(8,128)S(1)}, f32[32,192]{1,0:T(8,128)S(1)}, u32[]{:S(2)}, u32[]{:S(2)}) collective-permute-start(f32[32,192]{1,0:T(8,128)S(1)} %get-tuple-element.61.acc_ref), channel_id=1, source_target_pairs={{64,120},{72,96},{80,104},{88,112},{65,121},{73,97},{81,105},{89,1... | collective-permute-start | bytes 73736 | tf_op jit(solution)/shard_map/ppermute | solution.py:414
  151.6 1.9 %shard_map.106.weight2_ref = f32[768,384]{1,0:T(8,128)S(1)} custom-call(s32[2]{0:T(128)S(1)} %pad_add_fusion.2.place_ref, f32[8,3,96,384]{3,2,1,0:T(8,128)} %bitcast.44), custom_call_target="tpu_custom_call" | custom-call | tf_op jit(solution)/shard_map/pallas_call | solution.py:84
  154.5 1.3 shard_map.105.cells_ref
  155.8 1.3 shard_map.107
  157.2 9.9 %all_to_all.15.got_ref = f32[8,32,256]{2,1,0:T(8,128)S(1)} all-to-all(f32[8,32,256]{2,1,0:T(8,128)S(1)} %shard_map.107), channel_id=1, replica_groups=mesh['row'=16,'col'=8] {'col'}, dimensions={0} | all-to-all | bytes 524288 | tf_op jit(solution)/shard_map/all_to_all | solution.py:593
  (105 shorter events, 38.2 us)
Async XLA Ops:
  7.2 2.9 %copy-start.4 = (f32[2,4,6,128]{3,1,2,0:T(4,128)S(1)}, f32[2,4,6,128]{3,1,2,0:T(4,128)}, u32[]{:S(2)}) copy-start(f32[2,4,6,128]{3,1,2,0:T(4,128)} %param.8) | copy-start | bytes 73732
  7.2 2.9 %copy-start.5 = (f32[2,4,6]{2,1,0:T(4,128)S(1)}, f32[2,4,6]{2,1,0:T(4,128)}, u32[]{:S(2)}) copy-start(f32[2,4,6]{2,1,0:T(4,128)} %param.9) | copy-start | bytes 580
  7.2 9.8 %copy-start.2 = (s32[3072]{0:T(1024)S(1)}, s32[3072]{0:T(1024)}, u32[]{:S(2)}) copy-start(s32[3072]{0:T(1024)} %param.13) | copy-start | bytes 36868
  7.2 35.0 %all-gather.7.cloned.1.call-start = ((), (), s32[]{:S(2)}) async-start(), calls=%async_computation.3 | async-start | bytes 3981312 | tf_op jit(solution)/shard_map/all_gather | solution.py:431
  10.1 21.0 %copy-start.1 = (f32[2,192,384]{2,1,0:T(8,128)S(1)}, f32[2,192,384]{2,1,0:T(8,128)}, u32[]{:S(2)}) copy-start(f32[2,192,384]{2,1,0:T(8,128)} %param.11) | copy-start | bytes 1769476
  11.7 10.9 %all-to-all-start = ((f32[8,16,128]{2,1,0:T(8,128)}), f32[8,16,128]{2,1,0:T(8,128)S(1)}, u32[]{:S(2)}, u32[]{:S(2)}) async-start(f32[8,16,128]{2,1,0:T(8,128)} %shard_map.86), calls=%async_computation | async-start | bytes 131072 | tf_op jit(solution)/shard_map/all_to_all | solution.py:450
  23.5 16.5 %all-to-all-start.1 = ((f32[16,64,128]{2,1,0:T(8,128)}), f32[16,64,128]{2,1,0:T(8,128)S(1)}, u32[]{:S(2)}, u32[]{:S(2)}) async-start(f32[16,64,128]{2,1,0:T(8,128)} %broadcast_in_dim.36), calls=%async_computation.1 | async-start | bytes 1048576 | tf_op jit(solution)/shard_map/all_to_all | solution.py:452
  30.9 80.3 %all-gather.9.cloned.1.call-start = ((), (), s32[]{:S(2)}) async-start(), calls=%async_computation.4 | async-start | bytes 1114112 | tf_op jit(solution)/shard_map/all_gather | solution.py:495
  44.5 74.1 %all-gather.11.cloned.1.call-start = ((), (), s32[]{:S(2)}) async-start(), calls=%async_computation.5 | async-start | bytes 3981312 | tf_op jit(solution)/shard_map/all_gather | solution.py:431
  45.2 7.1 %collective-permute-start = (f32[32,192]{1,0:T(8,128)S(1)}, f32[32,192]{1,0:T(8,128)S(1)}, u32[]{:S(2)}, u32[]{:S(2)}) collective-permute-start(f32[32,192]{1,0:T(8,128)S(1)} %shard_map.89.acc_ref), channel_id=1, source_target_pairs={{32,64},{40,72},{48,80},{56,88},{33,65},{41,73},{49,81},{57,89},{3... | collective-permute-start | bytes 73736 | tf_op jit(solution)/shard_map/ppermute | solution.py:414
  46.5 8.0 %collective-permute-start.1 = (f32[32,192]{1,0:T(8,128)S(1)}, f32[32,192]{1,0:T(8,128)S(1)}, u32[]{:S(2)}, u32[]{:S(2)}) collective-permute-start(f32[32,192]{1,0:T(8,128)S(1)} %shard_map.89.acc_ref), channel_id=1, source_target_pairs={{32,72},{40,80},{48,88},{56,64},{33,73},{41,81},{49,89},{57,65},{3... | collective-permute-start | bytes 73736 | tf_op jit(solution)/shard_map/ppermute | solution.py:414
  47.8 8.9 %collective-permute-start.2 = (f32[32,192]{1,0:T(8,128)S(1)}, f32[32,192]{1,0:T(8,128)S(1)}, u32[]{:S(2)}, u32[]{:S(2)}) collective-permute-start(f32[32,192]{1,0:T(8,128)S(1)} %shard_map.89.acc_ref), channel_id=1, source_target_pairs={{32,80},{40,88},{48,64},{56,72},{33,81},{41,89},{49,65},{57,73},{3... | collective-permute-start | bytes 73736 | tf_op jit(solution)/shard_map/ppermute | solution.py:414
  49.1 8.5 %collective-permute-start.3 = (f32[32,192]{1,0:T(8,128)S(1)}, f32[32,192]{1,0:T(8,128)S(1)}, u32[]{:S(2)}, u32[]{:S(2)}) collective-permute-start(f32[32,192]{1,0:T(8,128)S(1)} %shard_map.89.acc_ref), channel_id=1, source_target_pairs={{32,88},{40,64},{48,72},{56,80},{33,89},{41,65},{49,73},{57,81},{3... | collective-permute-start | bytes 73736 | tf_op jit(solution)/shard_map/ppermute | solution.py:414
  52.3 12.9 %copy-start = (f32[2,768,192]{1,2,0:T(8,128)S(1)}, f32[2,768,192]{1,2,0:T(8,128)}, u32[]{:S(2)}) copy-start(f32[2,768,192]{1,2,0:T(8,128)} %param.12) | copy-start | bytes 3538948
  58.6 8.6 %collective-permute-start.4 = (f32[4,32,192]{2,1,0:T(8,128)S(1)}, f32[4,32,192]{2,1,0:T(8,128)S(1)}, u32[]{:S(2)}, u32[]{:S(2)}) collective-permute-start(f32[4,32,192]{2,1,0:T(8,128)S(1)} %get-tuple-element.38), channel_id=1, source_target_pairs={{64,96},{72,104},{80,112},{88,120},{65,97},{73,105},{81,113},{89,1... | collective-permute-start | bytes 294920 | tf_op jit(solution)/shard_map/ppermute | solution.py:414
  59.9 7.2 %collective-permute-start.5 = (f32[32,192]{1,0:T(8,128)S(1)}, f32[32,192]{1,0:T(8,128)S(1)}, u32[]{:S(2)}, u32[]{:S(2)}) collective-permute-start(f32[32,192]{1,0:T(8,128)S(1)} %get-tuple-element.36.acc_ref), channel_id=1, source_target_pairs={{64,96},{72,104},{80,112},{88,120},{65,97},{73,105},{81,113},{89,1... | collective-permute-start | bytes 73736 | tf_op jit(solution)/shard_map/ppermute | solution.py:414
  61.2 5.9 %collective-permute-start.6 = (f32[32,192]{1,0:T(8,128)S(1)}, f32[32,192]{1,0:T(8,128)S(1)}, u32[]{:S(2)}, u32[]{:S(2)}) collective-permute-start(f32[32,192]{1,0:T(8,128)S(1)} %get-tuple-element.36.acc_ref), channel_id=1, source_target_pairs={{64,104},{72,112},{80,120},{88,96},{65,105},{73,113},{81,121},{89,... | collective-permute-start | bytes 73736 | tf_op jit(solution)/shard_map/ppermute | solution.py:414
  62.5 4.7 %collective-permute-start.7 = (f32[32,192]{1,0:T(8,128)S(1)}, f32[32,192]{1,0:T(8,128)S(1)}, u32[]{:S(2)}, u32[]{:S(2)}) collective-permute-start(f32[32,192]{1,0:T(8,128)S(1)} %get-tuple-element.36.acc_ref), channel_id=1, source_target_pairs={{64,112},{72,120},{80,96},{88,104},{65,113},{73,121},{81,97},{89,1... | collective-permute-start | bytes 73736 | tf_op jit(solution)/shard_map/ppermute | solution.py:414
  63.8 3.4 %collective-permute-start.8 = (f32[32,192]{1,0:T(8,128)S(1)}, f32[32,192]{1,0:T(8,128)S(1)}, u32[]{:S(2)}, u32[]{:S(2)}) collective-permute-start(f32[32,192]{1,0:T(8,128)S(1)} %get-tuple-element.36.acc_ref), channel_id=1, source_target_pairs={{64,120},{72,96},{80,104},{88,112},{65,121},{73,97},{81,105},{89,1... | collective-permute-start | bytes 73736 | tf_op jit(solution)/shard_map/ppermute | solution.py:414
  68.9 9.9 %collective-permute-start.10 = (f32[32,768]{1,0:T(8,128)S(1)}, f32[32,768]{1,0:T(8,128)S(1)}, u32[]{:S(2)}, u32[]{:S(2)}) collective-permute-start(f32[32,768]{1,0:T(8,128)S(1)} %get-tuple-element.41), channel_id=1, source_target_pairs={{96,72},{104,80},{112,88},{120,64},{97,73},{105,81},{113,89},{121,... | collective-permute-start | bytes 294920 | tf_op jit(solution)/shard_map/ppermute | solution.py:414
  70.2 13.7 %collective-permute-start.11 = (f32[32,768]{1,0:T(8,128)S(1)}, f32[32,768]{1,0:T(8,128)S(1)}, u32[]{:S(2)}, u32[]{:S(2)}) collective-permute-start(f32[32,768]{1,0:T(8,128)S(1)} %get-tuple-element.41), channel_id=1, source_target_pairs={{96,80},{104,88},{112,64},{120,72},{97,81},{105,89},{113,65},{121,... | collective-permute-start | bytes 294920 | tf_op jit(solution)/shard_map/ppermute | solution.py:414
  71.5 13.1 %collective-permute-start.12 = (f32[32,768]{1,0:T(8,128)S(1)}, f32[32,768]{1,0:T(8,128)S(1)}, u32[]{:S(2)}, u32[]{:S(2)}) collective-permute-start(f32[32,768]{1,0:T(8,128)S(1)} %get-tuple-element.41), channel_id=1, source_target_pairs={{96,88},{104,64},{112,72},{120,80},{97,89},{105,65},{113,73},{121,... | collective-permute-start | bytes 294920 | tf_op jit(solution)/shard_map/ppermute | solution.py:414
  72.8 11.9 %collective-permute-start.9 = (f32[32,768]{1,0:T(8,128)S(1)}, f32[32,768]{1,0:T(8,128)S(1)}, u32[]{:S(2)}, u32[]{:S(2)}) collective-permute-start(f32[32,768]{1,0:T(8,128)S(1)} %get-tuple-element.41), channel_id=1, source_target_pairs={{96,64},{104,72},{112,80},{120,88},{97,65},{105,73},{113,81},{121,... | collective-permute-start | bytes 294920 | tf_op jit(solution)/shard_map/ppermute | solution.py:414
  86.0 6.5 %collective-permute-start.13 = (f32[32,768]{1,0:T(8,128)S(1)}, f32[32,768]{1,0:T(8,128)S(1)}, u32[]{:S(2)}, u32[]{:S(2)}) collective-permute-start(f32[32,768]{1,0:T(8,128)S(1)} %get-tuple-element.44), channel_id=1, source_target_pairs={{64,32},{72,40},{80,48},{88,56},{65,33},{73,41},{81,49},{89,57},{6... | collective-permute-start | bytes 294920 | tf_op jit(solution)/shard_map/ppermute | solution.py:414
  87.3 5.3 %collective-permute-start.14 = (f32[32,768]{1,0:T(8,128)S(1)}, f32[32,768]{1,0:T(8,128)S(1)}, u32[]{:S(2)}, u32[]{:S(2)}) collective-permute-start(f32[32,768]{1,0:T(8,128)S(1)} %get-tuple-element.44), channel_id=1, source_target_pairs={{64,40},{72,48},{80,56},{88,32},{65,41},{73,49},{81,57},{89,33},{6... | collective-permute-start | bytes 294920 | tf_op jit(solution)/shard_map/ppermute | solution.py:414
  88.6 6.1 %collective-permute-start.15 = (f32[32,768]{1,0:T(8,128)S(1)}, f32[32,768]{1,0:T(8,128)S(1)}, u32[]{:S(2)}, u32[]{:S(2)}) collective-permute-start(f32[32,768]{1,0:T(8,128)S(1)} %get-tuple-element.44), channel_id=1, source_target_pairs={{64,48},{72,56},{80,32},{88,40},{65,49},{73,57},{81,33},{89,41},{6... | collective-permute-start | bytes 294920 | tf_op jit(solution)/shard_map/ppermute | solution.py:414
  89.9 6.7 %collective-permute-start.16 = (f32[32,768]{1,0:T(8,128)S(1)}, f32[32,768]{1,0:T(8,128)S(1)}, u32[]{:S(2)}, u32[]{:S(2)}) collective-permute-start(f32[32,768]{1,0:T(8,128)S(1)} %get-tuple-element.44), channel_id=1, source_target_pairs={{64,56},{72,32},{80,40},{88,48},{65,57},{73,33},{81,41},{89,49},{6... | collective-permute-start | bytes 294920 | tf_op jit(solution)/shard_map/ppermute | solution.py:414
  91.2 6.4 %collective-permute-start.17 = (f32[32,768]{1,0:T(8,128)S(1)}, f32[32,768]{1,0:T(8,128)S(1)}, u32[]{:S(2)}, u32[]{:S(2)}) collective-permute-start(f32[32,768]{1,0:T(8,128)S(1)} %get-tuple-element.45.x3_ref), channel_id=1, source_target_pairs={{64,32},{72,40},{80,48},{88,56},{65,33},{73,41},{81,49},{89,57},{6... | collective-permute-start | bytes 294920 | tf_op jit(solution)/shard_map/ppermute | solution.py:414
  99.2 5.3 %collective-permute-start.22 = (f32[2,32,768]{2,1,0:T(8,128)S(1)}, f32[2,32,768]{2,1,0:T(8,128)S(1)}, u32[]{:S(2)}, u32[]{:S(2)}) collective-permute-start(f32[2,32,768]{2,1,0:T(8,128)S(1)} %get-tuple-element.48.x2_ref), channel_id=1, source_target_pairs={{32,0},{40,8},{48,16},{56,24},{33,1},{41,9},{49,17},{57,25},{34,2}... | collective-permute-start | bytes 589832 | tf_op jit(solution)/shard_map/ppermute | solution.py:414
  99.9 4.6 %collective-permute-start.18 = (f32[32,768]{1,0:T(8,128)S(1)}, f32[32,768]{1,0:T(8,128)S(1)}, u32[]{:S(2)}, u32[]{:S(2)}) collective-permute-start(f32[32,768]{1,0:T(8,128)S(1)} %get-tuple-element.47), channel_id=1, source_target_pairs={{32,0},{40,8},{48,16},{56,24},{33,1},{41,9},{49,17},{57,25},{34,2}... | collective-permute-start | bytes 294920 | tf_op jit(solution)/shard_map/ppermute | solution.py:414
  100.6 3.9 %collective-permute-start.19 = (f32[32,768]{1,0:T(8,128)S(1)}, f32[32,768]{1,0:T(8,128)S(1)}, u32[]{:S(2)}, u32[]{:S(2)}) collective-permute-start(f32[32,768]{1,0:T(8,128)S(1)} %get-tuple-element.47), channel_id=1, source_target_pairs={{32,8},{40,16},{48,24},{56,0},{33,9},{41,17},{49,25},{57,1},{34,10... | collective-permute-start | bytes 294920 | tf_op jit(solution)/shard_map/ppermute | solution.py:414
  101.3 3.3 %collective-permute-start.20 = (f32[32,768]{1,0:T(8,128)S(1)}, f32[32,768]{1,0:T(8,128)S(1)}, u32[]{:S(2)}, u32[]{:S(2)}) collective-permute-start(f32[32,768]{1,0:T(8,128)S(1)} %get-tuple-element.47), channel_id=1, source_target_pairs={{32,16},{40,24},{48,0},{56,8},{33,17},{41,25},{49,1},{57,9},{34,18... | collective-permute-start | bytes 294920 | tf_op jit(solution)/shard_map/ppermute | solution.py:414
  102.0 2.6 %collective-permute-start.21 = (f32[32,768]{1,0:T(8,128)S(1)}, f32[32,768]{1,0:T(8,128)S(1)}, u32[]{:S(2)}, u32[]{:S(2)}) collective-permute-start(f32[32,768]{1,0:T(8,128)S(1)} %get-tuple-element.47), channel_id=1, source_target_pairs={{32,24},{40,0},{48,8},{56,16},{33,25},{41,1},{49,9},{57,17},{34,26... | collective-permute-start | bytes 294920 | tf_op jit(solution)/shard_map/ppermute | solution.py:414
  106.6 13.9 %collective-permute-start.23 = (f32[32,768]{1,0:T(8,128)S(1)}, f32[32,768]{1,0:T(8,128)S(1)}, u32[]{:S(2)}, u32[]{:S(2)}) collective-permute-start(f32[32,768]{1,0:T(8,128)S(1)} %get-tuple-element.50), channel_id=1, source_target_pairs={{0,32},{8,40},{16,48},{24,56},{1,33},{9,41},{17,49},{25,57},{2,34}... | collective-permute-start | bytes 294920 | tf_op jit(solution)/shard_map/ppermute | solution.py:414
  107.2 13.2 %collective-permute-start.24 = (f32[32,768]{1,0:T(8,128)S(1)}, f32[32,768]{1,0:T(8,128)S(1)}, u32[]{:S(2)}, u32[]{:S(2)}) collective-permute-start(f32[32,768]{1,0:T(8,128)S(1)} %get-tuple-element.50), channel_id=1, source_target_pairs={{0,40},{8,48},{16,56},{24,32},{1,41},{9,49},{17,57},{25,33},{2,42}... | collective-permute-start | bytes 294920 | tf_op jit(solution)/shard_map/ppermute | solution.py:414
  107.9 12.5 %collective-permute-start.25 = (f32[32,768]{1,0:T(8,128)S(1)}, f32[32,768]{1,0:T(8,128)S(1)}, u32[]{:S(2)}, u32[]{:S(2)}) collective-permute-start(f32[32,768]{1,0:T(8,128)S(1)} %get-tuple-element.50), channel_id=1, source_target_pairs={{0,48},{8,56},{16,32},{24,40},{1,49},{9,57},{17,33},{25,41},{2,50}... | collective-permute-start | bytes 294920 | tf_op jit(solution)/shard_map/ppermute | solution.py:414
  108.6 11.9 %collective-permute-start.26 = (f32[32,768]{1,0:T(8,128)S(1)}, f32[32,768]{1,0:T(8,128)S(1)}, u32[]{:S(2)}, u32[]{:S(2)}) collective-permute-start(f32[32,768]{1,0:T(8,128)S(1)} %get-tuple-element.50), channel_id=1, source_target_pairs={{0,56},{8,32},{16,40},{24,48},{1,57},{9,33},{17,41},{25,49},{2,58}... | collective-permute-start | bytes 294920 | tf_op jit(solution)/shard_map/ppermute | solution.py:414
  109.3 17.3 %collective-permute-start.27 = (f32[32,768]{1,0:T(8,128)S(1)}, f32[32,768]{1,0:T(8,128)S(1)}, u32[]{:S(2)}, u32[]{:S(2)}) collective-permute-start(f32[32,768]{1,0:T(8,128)S(1)} %get-tuple-element.54.newest_ref), channel_id=1, source_target_pairs={{0,32},{8,40},{16,48},{24,56},{32,64},{40,72},{48,80},{56,88},{64,... | collective-permute-start | bytes 294920 | tf_op jit(solution)/shard_map/ppermute | solution.py:414
  127.6 14.4 %collective-permute-start.28 = (f32[2,32,768]{2,1,0:T(8,128)S(1)}, f32[2,32,768]{2,1,0:T(8,128)S(1)}, u32[]{:S(2)}, u32[]{:S(2)}) collective-permute-start(f32[2,32,768]{2,1,0:T(8,128)S(1)} %get-tuple-element.59.sent_ref.pass_ref), channel_id=1, source_target_pairs={{32,64},{40,72},{48,80},{56,88},{0,96},{8,104},{16,112},{24,120},{... | collective-permute-start | bytes 589832 | tf_op jit(solution)/shard_map/ppermute | solution.py:414
  128.9 10.8 %collective-permute-start.29 = (f32[32,192]{1,0:T(8,128)S(1)}, f32[32,192]{1,0:T(8,128)S(1)}, u32[]{:S(2)}, u32[]{:S(2)}) collective-permute-start(f32[32,192]{1,0:T(8,128)S(1)} %get-tuple-element.58.acc_ref), channel_id=1, source_target_pairs={{32,64},{40,72},{48,80},{56,88},{33,65},{41,73},{49,81},{57,89},{3... | collective-permute-start | bytes 73736 | tf_op jit(solution)/shard_map/ppermute | solution.py:414
  130.2 11.8 %collective-permute-start.30 = (f32[32,192]{1,0:T(8,128)S(1)}, f32[32,192]{1,0:T(8,128)S(1)}, u32[]{:S(2)}, u32[]{:S(2)}) collective-permute-start(f32[32,192]{1,0:T(8,128)S(1)} %get-tuple-element.58.acc_ref), channel_id=1, source_target_pairs={{32,72},{40,80},{48,88},{56,64},{33,73},{41,81},{49,89},{57,65},{3... | collective-permute-start | bytes 73736 | tf_op jit(solution)/shard_map/ppermute | solution.py:414
  131.5 10.5 %collective-permute-start.31 = (f32[32,192]{1,0:T(8,128)S(1)}, f32[32,192]{1,0:T(8,128)S(1)}, u32[]{:S(2)}, u32[]{:S(2)}) collective-permute-start(f32[32,192]{1,0:T(8,128)S(1)} %get-tuple-element.58.acc_ref), channel_id=1, source_target_pairs={{32,80},{40,88},{48,64},{56,72},{33,81},{41,89},{49,65},{57,73},{3... | collective-permute-start | bytes 73736 | tf_op jit(solution)/shard_map/ppermute | solution.py:414
  132.8 9.2 %collective-permute-start.32 = (f32[32,192]{1,0:T(8,128)S(1)}, f32[32,192]{1,0:T(8,128)S(1)}, u32[]{:S(2)}, u32[]{:S(2)}) collective-permute-start(f32[32,192]{1,0:T(8,128)S(1)} %get-tuple-element.58.acc_ref), channel_id=1, source_target_pairs={{32,88},{40,64},{48,72},{56,80},{33,89},{41,65},{49,73},{57,81},{3... | collective-permute-start | bytes 73736 | tf_op jit(solution)/shard_map/ppermute | solution.py:414
  143.3 10.2 %collective-permute-start.33 = (f32[8,32,192]{2,1,0:T(8,128)S(1)}, f32[8,32,192]{2,1,0:T(8,128)S(1)}, u32[]{:S(2)}, u32[]{:S(2)}) collective-permute-start(f32[8,32,192]{2,1,0:T(8,128)S(1)} %get-tuple-element.62), channel_id=1, source_target_pairs={{64,96},{72,104},{80,112},{88,120},{32,0},{40,8},{48,16},{56,24},{... | collective-permute-start | bytes 589832 | tf_op jit(solution)/shard_map/ppermute | solution.py:414
  145.0 10.8 %collective-permute-start.34 = (f32[32,192]{1,0:T(8,128)S(1)}, f32[32,192]{1,0:T(8,128)S(1)}, u32[]{:S(2)}, u32[]{:S(2)}) collective-permute-start(f32[32,192]{1,0:T(8,128)S(1)} %get-tuple-element.61.acc_ref), channel_id=1, source_target_pairs={{64,96},{72,104},{80,112},{88,120},{65,97},{73,105},{81,113},{89,1... | collective-permute-start | bytes 73736 | tf_op jit(solution)/shard_map/ppermute | solution.py:414
  146.3 9.5 %collective-permute-start.35 = (f32[32,192]{1,0:T(8,128)S(1)}, f32[32,192]{1,0:T(8,128)S(1)}, u32[]{:S(2)}, u32[]{:S(2)}) collective-permute-start(f32[32,192]{1,0:T(8,128)S(1)} %get-tuple-element.61.acc_ref), channel_id=1, source_target_pairs={{64,104},{72,112},{80,120},{88,96},{65,105},{73,113},{81,121},{89,... | collective-permute-start | bytes 73736 | tf_op jit(solution)/shard_map/ppermute | solution.py:414
  147.6 8.2 %collective-permute-start.36 = (f32[32,192]{1,0:T(8,128)S(1)}, f32[32,192]{1,0:T(8,128)S(1)}, u32[]{:S(2)}, u32[]{:S(2)}) collective-permute-start(f32[32,192]{1,0:T(8,128)S(1)} %get-tuple-element.61.acc_ref), channel_id=1, source_target_pairs={{64,112},{72,120},{80,96},{88,104},{65,113},{73,121},{81,97},{89,1... | collective-permute-start | bytes 73736 | tf_op jit(solution)/shard_map/ppermute | solution.py:414
  149.6 6.3 %collective-permute-start.37 = (f32[32,192]{1,0:T(8,128)S(1)}, f32[32,192]{1,0:T(8,128)S(1)}, u32[]{:S(2)}, u32[]{:S(2)}) collective-permute-start(f32[32,192]{1,0:T(8,128)S(1)} %get-tuple-element.61.acc_ref), channel_id=1, source_target_pairs={{64,120},{72,96},{80,104},{88,112},{65,121},{73,97},{81,105},{89,1... | collective-permute-start | bytes 73736 | tf_op jit(solution)/shard_map/ppermute | solution.py:414
  (1 other events, 2.9 us)
Sparse Core Ops, SparseCore 0:
  10.2 31.9 all-gather.6
  44.9 42.8 all-gather.8
  89.5 29.0 all-gather.10

commit v11 on v10

--- a/solution.py
+++ b/solution.py
@@ -74,23 +74,31 @@
     return total
 
 
-def call(body, out_shape, scalars, inputs, blocks=(), scratch=()):
+def call(body, out_shape, scalars, inputs, blocks=(), scratch=(), last=False):
     vmem = pl.BlockSpec(memory_space=pltpu.VMEM)
     specs = [vmem] * len(inputs)
     for _, shape, at in blocks:
         specs.append(pl.BlockSpec(shape, at, pipeline_mode=pl.Buffered(1)))
     near = [pltpu.with_memory_space_constraint(value, pltpu.VMEM) for value in inputs]
     far = [pltpu.with_memory_space_constraint(array, pltpu.HBM) for array, _, _ in blocks]
+    outs = (vmem,) * len(out_shape)
+    shapes = tuple(pltpu.VMEM(shape.shape, shape.dtype) for shape in out_shape)
+    if last:
+        outs = tuple(
+            pl.BlockSpec(shape.shape, lambda i, place, n=len(shape.shape): (0,) * n)
+            for shape in out_shape
+        )
+        shapes = tuple(pltpu.HBM(shape.shape, shape.dtype) for shape in out_shape)
     return pl.pallas_call(
         body,
         grid_spec=pltpu.PrefetchScalarGridSpec(
             num_scalar_prefetch=1,
             grid=(1,),
             in_specs=specs,
-            out_specs=(vmem,) * len(out_shape),
+            out_specs=outs,
             scratch_shapes=scratch,
         ),
-        out_shape=tuple(pltpu.VMEM(shape.shape, shape.dtype) for shape in out_shape),
+        out_shape=shapes,
         compiler_params=pltpu.CompilerParams(vmem_limit_bytes=VMEM),
     )(scalars, *near, *far)
 
@@ -555,16 +563,15 @@
     )
     passed = plane_send(passing, (1, 2), (0, 3))
     got = plane_spread(acc, 1, 2)
-    weights = [*weights, *load(matrix2, [1], acc, True)]
+    weights = [*weights, *load(matrix2, [1, 2], acc, True)]
     acc, kept = call(
         second_one_kernel,
         [slab_shape, SDS((2 * GROUP, ROWS, SLAB), f32)],
         place,
-        [rhs, link, acc, own, passing, passed, *got, *weights],
+        [rhs, link, acc, own, passing, passed, *got, *weights[:2]],
     )
     sent = plane_send(kept, (2, 3), (1, 0))
     got = plane_spread(acc, 2, 3)
-    weights = [*weights, *load(matrix2, [2], acc, True)]
     (acc,) = call(
         second_base_kernel,
         [slab_shape],
@@ -596,6 +603,7 @@
         [SDS((2, 4, 6, 128), f32), SDS((2, SLAB, 128), f32)],
         place,
         [arrived],
+        last=True,
     )
 
 

time: 177 us -> 176 us (level)
    pallas_call x23 -> x22, Pallas kernels: 40 us -> 39.2 us  [call(): pl.pallas_call(body, grid_spec=pltpu.PrefetchScalarGridSpec(num_scalar_pr...]
  transfers between devices with their start and end apart: 43 -> 43, of which waited for: 18 -> 17; matrix products, arithmetic and copies ran while one was open for 2% -> 2% of each run, Pallas kernels for 18% -> 17%
where the time goes in v11:
time: 176 us; the launch traced here: 174 us
  starting transfers between devices  58.3 us (33%)
  waiting for transfers between devices  47.3 us (27%)
  Pallas kernels  39.2 us (22%)
  between operations  14.5 us (8%)
  blocking collectives  9.95 us (6%)
  local copies, waits for them, and re-layouts  4.4 us (3%)
    ppermute x38, starting transfers between devices, plane_send(): return lax.ppermute(value, 'row', pairs)  45.4 us
    pallas_call x22, Pallas kernels, call(): pl.pallas_call(body, grid_spec=pltpu.PrefetchScalarGridSpec(num_scalar_pr...  39.2 us
    ppermute x38, waiting for transfers between devices, plane_send(): return lax.ppermute(value, 'row', pairs)  30.7 us
    all_to_all x1, blocking collectives, on_device(): arrived = lax.all_to_all(last, 'col', 0, 0)  9.95 us
    all_to_all x1, starting transfers between devices, on_device(): early = lax.all_to_all(early, 'row', 0, 0).reshape(1024, 128)  7.45 us
    all_to_all x1, waiting for transfers between devices, on_device(): early = lax.all_to_all(early, 'row', 0, 0).reshape(1024, 128)  7.1 us
    all_to_all x1, waiting for transfers between devices, on_device(): packed = lax.all_to_all(packed, 'col', 0, 0)  5.5 us
    all_to_all x1, starting transfers between devices, on_device(): packed = lax.all_to_all(packed, 'col', 0, 0)  5.31 us
  transfers between devices with their start and end apart: 43, of which 17 were waited for; matrix products, arithmetic and copies ran while one was open for 2% of the time, Pallas kernels for 17%

profile of v11, /device:TPU:4, one launch (start us, length us, event | category | flops | bytes accessed | tf_op | source)
XLA Modules:
  0.0 174.4 jit_solution(11542219253309663232)
XLA Ops:
  7.3 2.7 %shard_map.88 = f32[288,384]{1,0:T(8,128)} custom-call(s32[2]{0:T(128)S(1)} %pad_add_fusion.2.place_ref, f32[2,192,384]{2,1,0:T(8,128)} %factor_ref.1), custom_call_target="tpu_custom_call" | custom-call | tf_op jit(solution)/shard_map/pallas_call | solution.py:92
  10.3 1.4 shard_map.86
  11.7 5.3 %all-to-all-start = ((f32[8,16,128]{2,1,0:T(8,128)}), f32[8,16,128]{2,1,0:T(8,128)S(1)}, u32[]{:S(2)}, u32[]{:S(2)}) async-start(f32[8,16,128]{2,1,0:T(8,128)} %shard_map.86), calls=%async_computation | async-start | bytes 131072 | tf_op jit(solution)/shard_map/all_to_all | solution.py:458
  17.1 5.5 %all-to-all-done = f32[8,16,128]{2,1,0:T(8,128)S(1)} async-done(((f32[8,16,128]{2,1,0:T(8,128)}), f32[8,16,128]{2,1,0:T(8,128)S(1)}, u32[]{:S(2)}, u32[]{:S(2)}) %all-to-all-start) | async-done | bytes 65568 | tf_op jit(solution)/shard_map/all_to_all | solution.py:458
  23.5 7.5 %all-to-all-start.1 = ((f32[16,64,128]{2,1,0:T(8,128)}), f32[16,64,128]{2,1,0:T(8,128)S(1)}, u32[]{:S(2)}, u32[]{:S(2)}) async-start(f32[16,64,128]{2,1,0:T(8,128)} %broadcast_in_dim.36), calls=%async_computation.1 | async-start | bytes 1048576 | tf_op jit(solution)/shard_map/all_to_all | solution.py:460
  32.8 7.1 %all-to-all-done.1 = f32[16,64,128]{2,1,0:T(8,128)S(1)} async-done(((f32[16,64,128]{2,1,0:T(8,128)}), f32[16,64,128]{2,1,0:T(8,128)S(1)}, u32[]{:S(2)}, u32[]{:S(2)}) %all-to-all-start.1) | async-done | bytes 524320 | tf_op jit(solution)/shard_map/all_to_all | solution.py:460
  39.9 1.9 %shard_map.87.rhs_ref = f32[32,1024]{1,0:T(8,128)S(1)} custom-call(s32[2048]{0:T(1024)S(1)} %bitcast.35, f32[1024,128]{1,0:T(8,128)S(1)} %bitcast.34, f32[2,1024]{1,0:T(2,128)S(1)} %get-tuple-element.74.mark_ref), custom_call_target="tpu_custom_call" | custom-call | tf_op jit(solution)/shard_map/pallas_call | solution.py:92
  42.2 2.3 %shard_map.89.acc_ref = f32[32,192]{1,0:T(8,128)S(1)} custom-call(s32[2]{0:T(128)S(1)} %pad_add_fusion.2.place_ref, f32[32,1024]{1,0:T(8,128)S(1)} %shard_map.87.rhs_ref, f32[8,3,96,384]{3,2,1,0:T(8,128)} %bitcast.37), custom_call_target="tpu_custom_call" | custom-call | tf_op jit(solution)/shard_map/pallas_call | solution.py:92
  45.2 1.3 collective-permute-start
  46.5 1.3 collective-permute-start.1
  47.8 1.3 collective-permute-start.2
  49.1 1.3 collective-permute-start.3
  50.4 1.9 %shard_map.90.weight_ref.weight1_ref = f32[768,384]{1,0:T(8,128)S(1)} custom-call(s32[2]{0:T(128)S(1)} %pad_add_fusion.2.place_ref, f32[8,3,96,384]{3,2,1,0:T(8,128)} %bitcast.38), custom_call_target="tpu_custom_call" | custom-call | tf_op jit(solution)/shard_map/pallas_call | solution.py:92
  52.3 2.2 %collective-permute-done.1.y1 = f32[32,192]{1,0:T(8,128)S(1)} collective-permute-done((f32[32,192]{1,0:T(8,128)S(1)}, f32[32,192]{1,0:T(8,128)S(1)}, u32[]{:S(2)}, u32[]{:S(2)}) %collective-permute-start.1) | collective-permute-done | bytes 24608 | tf_op jit(solution)/shard_map/ppermute | solution.py:422
  54.5 2.2 %collective-permute-done.2.y2 = f32[32,192]{1,0:T(8,128)S(1)} collective-permute-done((f32[32,192]{1,0:T(8,128)S(1)}, f32[32,192]{1,0:T(8,128)S(1)}, u32[]{:S(2)}, u32[]{:S(2)}) %collective-permute-start.2) | collective-permute-done | bytes 24608 | tf_op jit(solution)/shard_map/ppermute | solution.py:422
  65.3 1.9 %shard_map.92.weight2_ref = f32[768,384]{1,0:T(8,128)S(1)} custom-call(s32[2]{0:T(128)S(1)} %pad_add_fusion.2.place_ref, f32[8,3,96,384]{3,2,1,0:T(8,128)} %bitcast.39), custom_call_target="tpu_custom_call" | custom-call | tf_op jit(solution)/shard_map/pallas_call | solution.py:92
  67.2 1.6 shard_map.93
  68.9 1.3 collective-permute-start.10
  70.2 1.3 collective-permute-start.11
  74.1 1.9 %shard_map.94.weight_ref.weight3_ref = f32[768,384]{1,0:T(8,128)S(1)} custom-call(s32[2]{0:T(128)S(1)} %pad_add_fusion.2.place_ref, f32[8,3,96,384]{3,2,1,0:T(8,128)} %bitcast.40), custom_call_target="tpu_custom_call" | custom-call | tf_op jit(solution)/shard_map/pallas_call | solution.py:92
  76.0 2.8 %collective-permute-done.10.p1 = f32[32,768]{1,0:T(8,128)S(1)} collective-permute-done((f32[32,768]{1,0:T(8,128)S(1)}, f32[32,768]{1,0:T(8,128)S(1)}, u32[]{:S(2)}, u32[]{:S(2)}) %collective-permute-start.10) | collective-permute-done | bytes 98336 | tf_op jit(solution)/shard_map/ppermute | solution.py:422
  78.8 5.1 %collective-permute-done.11.p2 = f32[32,768]{1,0:T(8,128)S(1)} collective-permute-done((f32[32,768]{1,0:T(8,128)S(1)}, f32[32,768]{1,0:T(8,128)S(1)}, u32[]{:S(2)}, u32[]{:S(2)}) %collective-permute-start.11) | collective-permute-done | bytes 98336 | tf_op jit(solution)/shard_map/ppermute | solution.py:422
  84.7 1.4 shard_map.95
  87.4 1.3 collective-permute-start.14
  88.7 1.3 collective-permute-start.15
  90.0 1.3 collective-permute-start.16
  91.3 1.3 collective-permute-start.17
  92.6 2.1 %collective-permute-done.15.p2 = f32[32,768]{1,0:T(8,128)S(1)} collective-permute-done((f32[32,768]{1,0:T(8,128)S(1)}, f32[32,768]{1,0:T(8,128)S(1)}, u32[]{:S(2)}, u32[]{:S(2)}) %collective-permute-start.15) | collective-permute-done | bytes 98336 | tf_op jit(solution)/shard_map/ppermute | solution.py:422
  94.7 1.9 %collective-permute-done.16.p3 = f32[32,768]{1,0:T(8,128)S(1)} collective-permute-done((f32[32,768]{1,0:T(8,128)S(1)}, f32[32,768]{1,0:T(8,128)S(1)}, u32[]{:S(2)}, u32[]{:S(2)}) %collective-permute-start.16) | collective-permute-done | bytes 98336 | tf_op jit(solution)/shard_map/ppermute | solution.py:422
  97.7 1.6 shard_map.96
  102.7 1.9 %shard_map.97.weight1_ref = f32[768,384]{1,0:T(8,128)S(1)} custom-call(s32[2]{0:T(128)S(1)} %pad_add_fusion.2.place_ref, f32[8,3,96,384]{3,2,1,0:T(8,128)} %bitcast.41), custom_call_target="tpu_custom_call" | custom-call | tf_op jit(solution)/shard_map/pallas_call | solution.py:92
  104.6 2.0 %shard_map.98 = (f32[32,768]{1,0:T(8,128)S(1)}, f32[2,32,768]{2,1,0:T(8,128)S(1)}, f32[32,768]{1,0:T(8,128)S(1)}) custom-call(s32[2]{0:T(128)S(1)} %pad_add_fusion.2.place_ref, f32[32,192]{1,0:T(8,128)S(1)} %get-tuple-element.47.acc_ref, f32[192,1536]{1,0:T(8,128)S(1)} %bitcast.33, f32[32,768]{1,0:T(8,128)S(1)} %collective-permute-done.18.p0, ...), custom_call_target="tpu_custom_call" | custom-call | tf_op jit(solution)/shard_map/pallas_call | solution.py:92
  109.3 1.9 %collective-permute-start.27 = (f32[32,768]{1,0:T(8,128)S(1)}, f32[32,768]{1,0:T(8,128)S(1)}, u32[]{:S(2)}, u32[]{:S(2)}) collective-permute-start(f32[32,768]{1,0:T(8,128)S(1)} %get-tuple-element.55.newest_ref), channel_id=1, source_target_pairs={{0,32},{8,40},{16,48},{24,56},{32,64},{40,72},{48,80},{56,88},{64,... | collective-permute-start | bytes 294920 | tf_op jit(solution)/shard_map/ppermute | solution.py:422
  111.2 4.3 %shard_map.99 = (f32[32,1024]{1,0:T(8,128)S(1)}, f32[16,1024]{1,0:T(8,128)S(1)}) custom-call(s32[2048]{0:T(1024)S(1)} %bitcast.36, f32[2,1024]{1,0:T(2,128)S(1)} %get-tuple-element.74.mark_ref, f32[16,64,256]{2,1,0:T(8,128)} %bitcast.47), custom_call_target="tpu_custom_call" | custom-call | tf_op jit(solution)/shard_map/pallas_call | solution.py:92
  115.5 3.0 %all-gather.11.cloned.1.call-done = f32[2304,384]{1,0:T(8,128)} async-done(((f32[288,384]{1,0:T(8,128)}), f32[2304,384]{1,0:T(8,128)}) %all-gather.11.cloned.1.call-update) | async-done | bytes 3538960 | tf_op jit(solution)/shard_map/all_gather | solution.py:439
  118.5 1.9 %shard_map.100.weight_ref.weight0_ref = f32[768,384]{1,0:T(8,128)S(1)} custom-call(s32[2]{0:T(128)S(1)} %pad_add_fusion.2.place_ref, f32[8,3,96,384]{3,2,1,0:T(8,128)} %bitcast.42), custom_call_target="tpu_custom_call" | custom-call | tf_op jit(solution)/shard_map/pallas_call | solution.py:92
  120.5 6.1 %collective-permute-done.27.own_ref = f32[32,768]{1,0:T(8,128)S(1)} collective-permute-done((f32[32,768]{1,0:T(8,128)S(1)}, f32[32,768]{1,0:T(8,128)S(1)}, u32[]{:S(2)}, u32[]{:S(2)}) %collective-permute-start.27) | collective-permute-done | bytes 98336 | tf_op jit(solution)/shard_map/ppermute | solution.py:422
  134.1 2.3 %shard_map.102 = (f32[768,384]{1,0:T(8,128)S(1)}, f32[768,384]{1,0:T(8,128)S(1)}) custom-call(s32[2]{0:T(128)S(1)} %pad_add_fusion.2.place_ref, f32[8,3,96,384]{3,2,1,0:T(8,128)} %bitcast.43, f32[8,3,96,384]{3,2,1,0:T(8,128)} %bitcast.44), custom_call_target="tpu_custom_call" | custom-call | tf_op jit(solution)/shard_map/pallas_call | solution.py:92
  136.5 3.1 %collective-permute-done.29.f0 = f32[32,192]{1,0:T(8,128)S(1)} collective-permute-done((f32[32,192]{1,0:T(8,128)S(1)}, f32[32,192]{1,0:T(8,128)S(1)}, u32[]{:S(2)}, u32[]{:S(2)}) %collective-permute-start.29) | collective-permute-done | bytes 24608 | tf_op jit(solution)/shard_map/ppermute | solution.py:422
  139.6 2.1 %collective-permute-done.30.f1 = f32[32,192]{1,0:T(8,128)S(1)} collective-permute-done((f32[32,192]{1,0:T(8,128)S(1)}, f32[32,192]{1,0:T(8,128)S(1)}, u32[]{:S(2)}, u32[]{:S(2)}) %collective-permute-start.30) | collective-permute-done | bytes 24608 | tf_op jit(solution)/shard_map/ppermute | solution.py:422
  143.2 1.3 collective-permute-start.33
  147.5 2.0 %collective-permute-start.36 = (f32[32,192]{1,0:T(8,128)S(1)}, f32[32,192]{1,0:T(8,128)S(1)}, u32[]{:S(2)}, u32[]{:S(2)}) collective-permute-start(f32[32,192]{1,0:T(8,128)S(1)} %get-tuple-element.63.acc_ref), channel_id=1, source_target_pairs={{64,112},{72,120},{80,96},{88,104},{65,113},{73,121},{81,97},{89,1... | collective-permute-start | bytes 73736 | tf_op jit(solution)/shard_map/ppermute | solution.py:422
  149.5 1.9 %collective-permute-start.37 = (f32[32,192]{1,0:T(8,128)S(1)}, f32[32,192]{1,0:T(8,128)S(1)}, u32[]{:S(2)}, u32[]{:S(2)}) collective-permute-start(f32[32,192]{1,0:T(8,128)S(1)} %get-tuple-element.63.acc_ref), channel_id=1, source_target_pairs={{64,120},{72,96},{80,104},{88,112},{65,121},{73,97},{81,105},{89,1... | collective-permute-start | bytes 73736 | tf_op jit(solution)/shard_map/ppermute | solution.py:422
  152.5 1.3 shard_map.105.cells_ref
  153.9 1.3 shard_map.106
  155.2 9.9 %all_to_all.15.got_ref = f32[8,32,256]{2,1,0:T(8,128)S(1)} all-to-all(f32[8,32,256]{2,1,0:T(8,128)S(1)} %shard_map.106), channel_id=1, replica_groups=mesh['row'=16,'col'=8] {'col'}, dimensions={0} | all-to-all | bytes 524288 | tf_op jit(solution)/shard_map/all_to_all | solution.py:600
  165.2 1.3 shard_map.107
  166.5 1.4 copy.18
  (103 shorter events, 37.7 us)
Async XLA Ops:
  7.2 2.9 %copy-start.4 = (f32[2,4,6,128]{3,1,2,0:T(4,128)S(1)}, f32[2,4,6,128]{3,1,2,0:T(4,128)}, u32[]{:S(2)}) copy-start(f32[2,4,6,128]{3,1,2,0:T(4,128)} %param.8) | copy-start | bytes 73732
  7.2 2.9 %copy-start.5 = (f32[2,4,6]{2,1,0:T(4,128)S(1)}, f32[2,4,6]{2,1,0:T(4,128)}, u32[]{:S(2)}) copy-start(f32[2,4,6]{2,1,0:T(4,128)} %param.9) | copy-start | bytes 580
  7.2 9.8 %copy-start.2 = (s32[3072]{0:T(1024)S(1)}, s32[3072]{0:T(1024)}, u32[]{:S(2)}) copy-start(s32[3072]{0:T(1024)} %param.13) | copy-start | bytes 36868
  7.2 35.0 %all-gather.7.cloned.1.call-start = ((), (), s32[]{:S(2)}) async-start(), calls=%async_computation.3 | async-start | bytes 3981312 | tf_op jit(solution)/shard_map/all_gather | solution.py:439
  10.1 21.0 %copy-start.1 = (f32[2,192,384]{2,1,0:T(8,128)S(1)}, f32[2,192,384]{2,1,0:T(8,128)}, u32[]{:S(2)}) copy-start(f32[2,192,384]{2,1,0:T(8,128)} %param.11) | copy-start | bytes 1769476
  11.7 10.9 %all-to-all-start = ((f32[8,16,128]{2,1,0:T(8,128)}), f32[8,16,128]{2,1,0:T(8,128)S(1)}, u32[]{:S(2)}, u32[]{:S(2)}) async-start(f32[8,16,128]{2,1,0:T(8,128)} %shard_map.86), calls=%async_computation | async-start | bytes 131072 | tf_op jit(solution)/shard_map/all_to_all | solution.py:458
  23.5 16.5 %all-to-all-start.1 = ((f32[16,64,128]{2,1,0:T(8,128)}), f32[16,64,128]{2,1,0:T(8,128)S(1)}, u32[]{:S(2)}, u32[]{:S(2)}) async-start(f32[16,64,128]{2,1,0:T(8,128)} %broadcast_in_dim.36), calls=%async_computation.1 | async-start | bytes 1048576 | tf_op jit(solution)/shard_map/all_to_all | solution.py:460
  30.9 80.3 %all-gather.9.cloned.1.call-start = ((), (), s32[]{:S(2)}) async-start(), calls=%async_computation.4 | async-start | bytes 1114112 | tf_op jit(solution)/shard_map/all_gather | solution.py:503
  44.5 74.1 %all-gather.11.cloned.1.call-start = ((), (), s32[]{:S(2)}) async-start(), calls=%async_computation.5 | async-start | bytes 3981312 | tf_op jit(solution)/shard_map/all_gather | solution.py:439
  45.2 7.1 %collective-permute-start = (f32[32,192]{1,0:T(8,128)S(1)}, f32[32,192]{1,0:T(8,128)S(1)}, u32[]{:S(2)}, u32[]{:S(2)}) collective-permute-start(f32[32,192]{1,0:T(8,128)S(1)} %shard_map.89.acc_ref), channel_id=1, source_target_pairs={{32,64},{40,72},{48,80},{56,88},{33,65},{41,73},{49,81},{57,89},{3... | collective-permute-start | bytes 73736 | tf_op jit(solution)/shard_map/ppermute | solution.py:422
  46.5 8.0 %collective-permute-start.1 = (f32[32,192]{1,0:T(8,128)S(1)}, f32[32,192]{1,0:T(8,128)S(1)}, u32[]{:S(2)}, u32[]{:S(2)}) collective-permute-start(f32[32,192]{1,0:T(8,128)S(1)} %shard_map.89.acc_ref), channel_id=1, source_target_pairs={{32,72},{40,80},{48,88},{56,64},{33,73},{41,81},{49,89},{57,65},{3... | collective-permute-start | bytes 73736 | tf_op jit(solution)/shard_map/ppermute | solution.py:422
  47.8 8.9 %collective-permute-start.2 = (f32[32,192]{1,0:T(8,128)S(1)}, f32[32,192]{1,0:T(8,128)S(1)}, u32[]{:S(2)}, u32[]{:S(2)}) collective-permute-start(f32[32,192]{1,0:T(8,128)S(1)} %shard_map.89.acc_ref), channel_id=1, source_target_pairs={{32,80},{40,88},{48,64},{56,72},{33,81},{41,89},{49,65},{57,73},{3... | collective-permute-start | bytes 73736 | tf_op jit(solution)/shard_map/ppermute | solution.py:422
  49.1 8.5 %collective-permute-start.3 = (f32[32,192]{1,0:T(8,128)S(1)}, f32[32,192]{1,0:T(8,128)S(1)}, u32[]{:S(2)}, u32[]{:S(2)}) collective-permute-start(f32[32,192]{1,0:T(8,128)S(1)} %shard_map.89.acc_ref), channel_id=1, source_target_pairs={{32,88},{40,64},{48,72},{56,80},{33,89},{41,65},{49,73},{57,81},{3... | collective-permute-start | bytes 73736 | tf_op jit(solution)/shard_map/ppermute | solution.py:422
  52.3 12.9 %copy-start = (f32[2,768,192]{1,2,0:T(8,128)S(1)}, f32[2,768,192]{1,2,0:T(8,128)}, u32[]{:S(2)}) copy-start(f32[2,768,192]{1,2,0:T(8,128)} %param.12) | copy-start | bytes 3538948
  58.7 8.6 %collective-permute-start.4 = (f32[4,32,192]{2,1,0:T(8,128)S(1)}, f32[4,32,192]{2,1,0:T(8,128)S(1)}, u32[]{:S(2)}, u32[]{:S(2)}) collective-permute-start(f32[4,32,192]{2,1,0:T(8,128)S(1)} %get-tuple-element.39), channel_id=1, source_target_pairs={{64,96},{72,104},{80,112},{88,120},{65,97},{73,105},{81,113},{89,1... | collective-permute-start | bytes 294920 | tf_op jit(solution)/shard_map/ppermute | solution.py:422
  60.0 7.2 %collective-permute-start.5 = (f32[32,192]{1,0:T(8,128)S(1)}, f32[32,192]{1,0:T(8,128)S(1)}, u32[]{:S(2)}, u32[]{:S(2)}) collective-permute-start(f32[32,192]{1,0:T(8,128)S(1)} %get-tuple-element.37.acc_ref), channel_id=1, source_target_pairs={{64,96},{72,104},{80,112},{88,120},{65,97},{73,105},{81,113},{89,1... | collective-permute-start | bytes 73736 | tf_op jit(solution)/shard_map/ppermute | solution.py:422
  61.2 5.9 %collective-permute-start.6 = (f32[32,192]{1,0:T(8,128)S(1)}, f32[32,192]{1,0:T(8,128)S(1)}, u32[]{:S(2)}, u32[]{:S(2)}) collective-permute-start(f32[32,192]{1,0:T(8,128)S(1)} %get-tuple-element.37.acc_ref), channel_id=1, source_target_pairs={{64,104},{72,112},{80,120},{88,96},{65,105},{73,113},{81,121},{89,... | collective-permute-start | bytes 73736 | tf_op jit(solution)/shard_map/ppermute | solution.py:422
  62.5 4.7 %collective-permute-start.7 = (f32[32,192]{1,0:T(8,128)S(1)}, f32[32,192]{1,0:T(8,128)S(1)}, u32[]{:S(2)}, u32[]{:S(2)}) collective-permute-start(f32[32,192]{1,0:T(8,128)S(1)} %get-tuple-element.37.acc_ref), channel_id=1, source_target_pairs={{64,112},{72,120},{80,96},{88,104},{65,113},{73,121},{81,97},{89,1... | collective-permute-start | bytes 73736 | tf_op jit(solution)/shard_map/ppermute | solution.py:422
  63.8 3.4 %collective-permute-start.8 = (f32[32,192]{1,0:T(8,128)S(1)}, f32[32,192]{1,0:T(8,128)S(1)}, u32[]{:S(2)}, u32[]{:S(2)}) collective-permute-start(f32[32,192]{1,0:T(8,128)S(1)} %get-tuple-element.37.acc_ref), channel_id=1, source_target_pairs={{64,120},{72,96},{80,104},{88,112},{65,121},{73,97},{81,105},{89,1... | collective-permute-start | bytes 73736 | tf_op jit(solution)/shard_map/ppermute | solution.py:422
  68.9 9.9 %collective-permute-start.10 = (f32[32,768]{1,0:T(8,128)S(1)}, f32[32,768]{1,0:T(8,128)S(1)}, u32[]{:S(2)}, u32[]{:S(2)}) collective-permute-start(f32[32,768]{1,0:T(8,128)S(1)} %get-tuple-element.42), channel_id=1, source_target_pairs={{96,72},{104,80},{112,88},{120,64},{97,73},{105,81},{113,89},{121,... | collective-permute-start | bytes 294920 | tf_op jit(solution)/shard_map/ppermute | solution.py:422
  70.2 13.7 %collective-permute-start.11 = (f32[32,768]{1,0:T(8,128)S(1)}, f32[32,768]{1,0:T(8,128)S(1)}, u32[]{:S(2)}, u32[]{:S(2)}) collective-permute-start(f32[32,768]{1,0:T(8,128)S(1)} %get-tuple-element.42), channel_id=1, source_target_pairs={{96,80},{104,88},{112,64},{120,72},{97,81},{105,89},{113,65},{121,... | collective-permute-start | bytes 294920 | tf_op jit(solution)/shard_map/ppermute | solution.py:422
  71.5 13.2 %collective-permute-start.12 = (f32[32,768]{1,0:T(8,128)S(1)}, f32[32,768]{1,0:T(8,128)S(1)}, u32[]{:S(2)}, u32[]{:S(2)}) collective-permute-start(f32[32,768]{1,0:T(8,128)S(1)} %get-tuple-element.42), channel_id=1, source_target_pairs={{96,88},{104,64},{112,72},{120,80},{97,89},{105,65},{113,73},{121,... | collective-permute-start | bytes 294920 | tf_op jit(solution)/shard_map/ppermute | solution.py:422
  72.8 11.9 %collective-permute-start.9 = (f32[32,768]{1,0:T(8,128)S(1)}, f32[32,768]{1,0:T(8,128)S(1)}, u32[]{:S(2)}, u32[]{:S(2)}) collective-permute-start(f32[32,768]{1,0:T(8,128)S(1)} %get-tuple-element.42), channel_id=1, source_target_pairs={{96,64},{104,72},{112,80},{120,88},{97,65},{105,73},{113,81},{121,... | collective-permute-start | bytes 294920 | tf_op jit(solution)/shard_map/ppermute | solution.py:422
  86.1 6.5 %collective-permute-start.13 = (f32[32,768]{1,0:T(8,128)S(1)}, f32[32,768]{1,0:T(8,128)S(1)}, u32[]{:S(2)}, u32[]{:S(2)}) collective-permute-start(f32[32,768]{1,0:T(8,128)S(1)} %get-tuple-element.45), channel_id=1, source_target_pairs={{64,32},{72,40},{80,48},{88,56},{65,33},{73,41},{81,49},{89,57},{6... | collective-permute-start | bytes 294920 | tf_op jit(solution)/shard_map/ppermute | solution.py:422
  87.4 5.3 %collective-permute-start.14 = (f32[32,768]{1,0:T(8,128)S(1)}, f32[32,768]{1,0:T(8,128)S(1)}, u32[]{:S(2)}, u32[]{:S(2)}) collective-permute-start(f32[32,768]{1,0:T(8,128)S(1)} %get-tuple-element.45), channel_id=1, source_target_pairs={{64,40},{72,48},{80,56},{88,32},{65,41},{73,49},{81,57},{89,33},{6... | collective-permute-start | bytes 294920 | tf_op jit(solution)/shard_map/ppermute | solution.py:422
  88.7 6.1 %collective-permute-start.15 = (f32[32,768]{1,0:T(8,128)S(1)}, f32[32,768]{1,0:T(8,128)S(1)}, u32[]{:S(2)}, u32[]{:S(2)}) collective-permute-start(f32[32,768]{1,0:T(8,128)S(1)} %get-tuple-element.45), channel_id=1, source_target_pairs={{64,48},{72,56},{80,32},{88,40},{65,49},{73,57},{81,33},{89,41},{6... | collective-permute-start | bytes 294920 | tf_op jit(solution)/shard_map/ppermute | solution.py:422
  90.0 6.7 %collective-permute-start.16 = (f32[32,768]{1,0:T(8,128)S(1)}, f32[32,768]{1,0:T(8,128)S(1)}, u32[]{:S(2)}, u32[]{:S(2)}) collective-permute-start(f32[32,768]{1,0:T(8,128)S(1)} %get-tuple-element.45), channel_id=1, source_target_pairs={{64,56},{72,32},{80,40},{88,48},{65,57},{73,33},{81,41},{89,49},{6... | collective-permute-start | bytes 294920 | tf_op jit(solution)/shard_map/ppermute | solution.py:422
  91.3 6.4 %collective-permute-start.17 = (f32[32,768]{1,0:T(8,128)S(1)}, f32[32,768]{1,0:T(8,128)S(1)}, u32[]{:S(2)}, u32[]{:S(2)}) collective-permute-start(f32[32,768]{1,0:T(8,128)S(1)} %get-tuple-element.46.x3_ref), channel_id=1, source_target_pairs={{64,32},{72,40},{80,48},{88,56},{65,33},{73,41},{81,49},{89,57},{6... | collective-permute-start | bytes 294920 | tf_op jit(solution)/shard_map/ppermute | solution.py:422
  99.3 5.3 %collective-permute-start.22 = (f32[2,32,768]{2,1,0:T(8,128)S(1)}, f32[2,32,768]{2,1,0:T(8,128)S(1)}, u32[]{:S(2)}, u32[]{:S(2)}) collective-permute-start(f32[2,32,768]{2,1,0:T(8,128)S(1)} %get-tuple-element.49.x2_ref), channel_id=1, source_target_pairs={{32,0},{40,8},{48,16},{56,24},{33,1},{41,9},{49,17},{57,25},{34,2}... | collective-permute-start | bytes 589832 | tf_op jit(solution)/shard_map/ppermute | solution.py:422
  100.0 4.6 %collective-permute-start.18 = (f32[32,768]{1,0:T(8,128)S(1)}, f32[32,768]{1,0:T(8,128)S(1)}, u32[]{:S(2)}, u32[]{:S(2)}) collective-permute-start(f32[32,768]{1,0:T(8,128)S(1)} %get-tuple-element.48), channel_id=1, source_target_pairs={{32,0},{40,8},{48,16},{56,24},{33,1},{41,9},{49,17},{57,25},{34,2}... | collective-permute-start | bytes 294920 | tf_op jit(solution)/shard_map/ppermute | solution.py:422
  100.6 3.9 %collective-permute-start.19 = (f32[32,768]{1,0:T(8,128)S(1)}, f32[32,768]{1,0:T(8,128)S(1)}, u32[]{:S(2)}, u32[]{:S(2)}) collective-permute-start(f32[32,768]{1,0:T(8,128)S(1)} %get-tuple-element.48), channel_id=1, source_target_pairs={{32,8},{40,16},{48,24},{56,0},{33,9},{41,17},{49,25},{57,1},{34,10... | collective-permute-start | bytes 294920 | tf_op jit(solution)/shard_map/ppermute | solution.py:422
  101.3 3.3 %collective-permute-start.20 = (f32[32,768]{1,0:T(8,128)S(1)}, f32[32,768]{1,0:T(8,128)S(1)}, u32[]{:S(2)}, u32[]{:S(2)}) collective-permute-start(f32[32,768]{1,0:T(8,128)S(1)} %get-tuple-element.48), channel_id=1, source_target_pairs={{32,16},{40,24},{48,0},{56,8},{33,17},{41,25},{49,1},{57,9},{34,18... | collective-permute-start | bytes 294920 | tf_op jit(solution)/shard_map/ppermute | solution.py:422
  102.0 2.6 %collective-permute-start.21 = (f32[32,768]{1,0:T(8,128)S(1)}, f32[32,768]{1,0:T(8,128)S(1)}, u32[]{:S(2)}, u32[]{:S(2)}) collective-permute-start(f32[32,768]{1,0:T(8,128)S(1)} %get-tuple-element.48), channel_id=1, source_target_pairs={{32,24},{40,0},{48,8},{56,16},{33,25},{41,1},{49,9},{57,17},{34,26... | collective-permute-start | bytes 294920 | tf_op jit(solution)/shard_map/ppermute | solution.py:422
  106.6 13.9 %collective-permute-start.23 = (f32[32,768]{1,0:T(8,128)S(1)}, f32[32,768]{1,0:T(8,128)S(1)}, u32[]{:S(2)}, u32[]{:S(2)}) collective-permute-start(f32[32,768]{1,0:T(8,128)S(1)} %get-tuple-element.51), channel_id=1, source_target_pairs={{0,32},{8,40},{16,48},{24,56},{1,33},{9,41},{17,49},{25,57},{2,34}... | collective-permute-start | bytes 294920 | tf_op jit(solution)/shard_map/ppermute | solution.py:422
  107.3 13.2 %collective-permute-start.24 = (f32[32,768]{1,0:T(8,128)S(1)}, f32[32,768]{1,0:T(8,128)S(1)}, u32[]{:S(2)}, u32[]{:S(2)}) collective-permute-start(f32[32,768]{1,0:T(8,128)S(1)} %get-tuple-element.51), channel_id=1, source_target_pairs={{0,40},{8,48},{16,56},{24,32},{1,41},{9,49},{17,57},{25,33},{2,42}... | collective-permute-start | bytes 294920 | tf_op jit(solution)/shard_map/ppermute | solution.py:422
  107.9 12.5 %collective-permute-start.25 = (f32[32,768]{1,0:T(8,128)S(1)}, f32[32,768]{1,0:T(8,128)S(1)}, u32[]{:S(2)}, u32[]{:S(2)}) collective-permute-start(f32[32,768]{1,0:T(8,128)S(1)} %get-tuple-element.51), channel_id=1, source_target_pairs={{0,48},{8,56},{16,32},{24,40},{1,49},{9,57},{17,33},{25,41},{2,50}... | collective-permute-start | bytes 294920 | tf_op jit(solution)/shard_map/ppermute | solution.py:422
  108.6 11.9 %collective-permute-start.26 = (f32[32,768]{1,0:T(8,128)S(1)}, f32[32,768]{1,0:T(8,128)S(1)}, u32[]{:S(2)}, u32[]{:S(2)}) collective-permute-start(f32[32,768]{1,0:T(8,128)S(1)} %get-tuple-element.51), channel_id=1, source_target_pairs={{0,56},{8,32},{16,40},{24,48},{1,57},{9,33},{17,41},{25,49},{2,58}... | collective-permute-start | bytes 294920 | tf_op jit(solution)/shard_map/ppermute | solution.py:422
  109.3 17.3 %collective-permute-start.27 = (f32[32,768]{1,0:T(8,128)S(1)}, f32[32,768]{1,0:T(8,128)S(1)}, u32[]{:S(2)}, u32[]{:S(2)}) collective-permute-start(f32[32,768]{1,0:T(8,128)S(1)} %get-tuple-element.55.newest_ref), channel_id=1, source_target_pairs={{0,32},{8,40},{16,48},{24,56},{32,64},{40,72},{48,80},{56,88},{64,... | collective-permute-start | bytes 294920 | tf_op jit(solution)/shard_map/ppermute | solution.py:422
  127.6 14.3 %collective-permute-start.28 = (f32[2,32,768]{2,1,0:T(8,128)S(1)}, f32[2,32,768]{2,1,0:T(8,128)S(1)}, u32[]{:S(2)}, u32[]{:S(2)}) collective-permute-start(f32[2,32,768]{2,1,0:T(8,128)S(1)} %get-tuple-element.60.sent_ref.pass_ref), channel_id=1, source_target_pairs={{32,64},{40,72},{48,80},{56,88},{0,96},{8,104},{16,112},{24,120},{... | collective-permute-start | bytes 589832 | tf_op jit(solution)/shard_map/ppermute | solution.py:422
  128.9 10.7 %collective-permute-start.29 = (f32[32,192]{1,0:T(8,128)S(1)}, f32[32,192]{1,0:T(8,128)S(1)}, u32[]{:S(2)}, u32[]{:S(2)}) collective-permute-start(f32[32,192]{1,0:T(8,128)S(1)} %get-tuple-element.59.acc_ref), channel_id=1, source_target_pairs={{32,64},{40,72},{48,80},{56,88},{33,65},{41,73},{49,81},{57,89},{3... | collective-permute-start | bytes 73736 | tf_op jit(solution)/shard_map/ppermute | solution.py:422
  130.2 11.5 %collective-permute-start.30 = (f32[32,192]{1,0:T(8,128)S(1)}, f32[32,192]{1,0:T(8,128)S(1)}, u32[]{:S(2)}, u32[]{:S(2)}) collective-permute-start(f32[32,192]{1,0:T(8,128)S(1)} %get-tuple-element.59.acc_ref), channel_id=1, source_target_pairs={{32,72},{40,80},{48,88},{56,64},{33,73},{41,81},{49,89},{57,65},{3... | collective-permute-start | bytes 73736 | tf_op jit(solution)/shard_map/ppermute | solution.py:422
  131.5 10.4 %collective-permute-start.31 = (f32[32,192]{1,0:T(8,128)S(1)}, f32[32,192]{1,0:T(8,128)S(1)}, u32[]{:S(2)}, u32[]{:S(2)}) collective-permute-start(f32[32,192]{1,0:T(8,128)S(1)} %get-tuple-element.59.acc_ref), channel_id=1, source_target_pairs={{32,80},{40,88},{48,64},{56,72},{33,81},{41,89},{49,65},{57,73},{3... | collective-permute-start | bytes 73736 | tf_op jit(solution)/shard_map/ppermute | solution.py:422
  132.8 9.1 %collective-permute-start.32 = (f32[32,192]{1,0:T(8,128)S(1)}, f32[32,192]{1,0:T(8,128)S(1)}, u32[]{:S(2)}, u32[]{:S(2)}) collective-permute-start(f32[32,192]{1,0:T(8,128)S(1)} %get-tuple-element.59.acc_ref), channel_id=1, source_target_pairs={{32,88},{40,64},{48,72},{56,80},{33,89},{41,65},{49,73},{57,81},{3... | collective-permute-start | bytes 73736 | tf_op jit(solution)/shard_map/ppermute | solution.py:422
  143.2 8.3 %collective-permute-start.33 = (f32[8,32,192]{2,1,0:T(8,128)S(1)}, f32[8,32,192]{2,1,0:T(8,128)S(1)}, u32[]{:S(2)}, u32[]{:S(2)}) collective-permute-start(f32[8,32,192]{2,1,0:T(8,128)S(1)} %get-tuple-element.64), channel_id=1, source_target_pairs={{64,96},{72,104},{80,112},{88,120},{32,0},{40,8},{48,16},{56,24},{... | collective-permute-start | bytes 589832 | tf_op jit(solution)/shard_map/ppermute | solution.py:422
  144.9 8.9 %collective-permute-start.34 = (f32[32,192]{1,0:T(8,128)S(1)}, f32[32,192]{1,0:T(8,128)S(1)}, u32[]{:S(2)}, u32[]{:S(2)}) collective-permute-start(f32[32,192]{1,0:T(8,128)S(1)} %get-tuple-element.63.acc_ref), channel_id=1, source_target_pairs={{64,96},{72,104},{80,112},{88,120},{65,97},{73,105},{81,113},{89,1... | collective-permute-start | bytes 73736 | tf_op jit(solution)/shard_map/ppermute | solution.py:422
  146.2 7.7 %collective-permute-start.35 = (f32[32,192]{1,0:T(8,128)S(1)}, f32[32,192]{1,0:T(8,128)S(1)}, u32[]{:S(2)}, u32[]{:S(2)}) collective-permute-start(f32[32,192]{1,0:T(8,128)S(1)} %get-tuple-element.63.acc_ref), channel_id=1, source_target_pairs={{64,104},{72,112},{80,120},{88,96},{65,105},{73,113},{81,121},{89,... | collective-permute-start | bytes 73736 | tf_op jit(solution)/shard_map/ppermute | solution.py:422
  147.5 6.4 %collective-permute-start.36 = (f32[32,192]{1,0:T(8,128)S(1)}, f32[32,192]{1,0:T(8,128)S(1)}, u32[]{:S(2)}, u32[]{:S(2)}) collective-permute-start(f32[32,192]{1,0:T(8,128)S(1)} %get-tuple-element.63.acc_ref), channel_id=1, source_target_pairs={{64,112},{72,120},{80,96},{88,104},{65,113},{73,121},{81,97},{89,1... | collective-permute-start | bytes 73736 | tf_op jit(solution)/shard_map/ppermute | solution.py:422
  149.5 4.4 %collective-permute-start.37 = (f32[32,192]{1,0:T(8,128)S(1)}, f32[32,192]{1,0:T(8,128)S(1)}, u32[]{:S(2)}, u32[]{:S(2)}) collective-permute-start(f32[32,192]{1,0:T(8,128)S(1)} %get-tuple-element.63.acc_ref), channel_id=1, source_target_pairs={{64,120},{72,96},{80,104},{88,112},{65,121},{73,97},{81,105},{89,1... | collective-permute-start | bytes 73736 | tf_op jit(solution)/shard_map/ppermute | solution.py:422
  (1 other events, 2.9 us)
Sparse Core Ops, SparseCore 0:
  10.2 31.9 all-gather.6
  44.9 42.8 all-gather.8
  89.5 29.0 all-gather.10

commit v12 on v11

--- a/solution.py
+++ b/solution.py
@@ -423,7 +423,8 @@
 
 
 def plane_spread(value, source, target):
-    return [plane_send(value, (source, target), turn=d) for d in range(GROUP)]
+    sent = {d: plane_send(value, (source, target), turn=d) for d in (2, 1, 3, 0)}
+    return [sent[d] for d in range(GROUP)]
 
 
 def after(value, arrived):

time: 176 us -> 176 us (level)
  no operation moved by 1% of the time
where the time goes in v12:
time: 176 us; the launch traced here: 174 us
  starting transfers between devices  58.3 us (33%)
  waiting for transfers between devices  47.3 us (27%)
  Pallas kernels  39.2 us (22%)
  between operations  14.5 us (8%)
  blocking collectives  9.95 us (6%)
  local copies, waits for them, and re-layouts  4.4 us (3%)
    ppermute x38, starting transfers between devices, plane_send(): return lax.ppermute(value, 'row', pairs)  45.4 us
    pallas_call x22, Pallas kernels, call(): pl.pallas_call(body, grid_spec=pltpu.PrefetchScalarGridSpec(num_scalar_pr...  39.2 us
    ppermute x38, waiting for transfers between devices, plane_send(): return lax.ppermute(value, 'row', pairs)  30.7 us
    all_to_all x1, blocking collectives, on_device(): arrived = lax.all_to_all(last, 'col', 0, 0)  9.95 us
    all_to_all x1, starting transfers between devices, on_device(): early = lax.all_to_all(early, 'row', 0, 0).reshape(1024, 128)  7.45 us
    all_to_all x1, waiting for transfers between devices, on_device(): early = lax.all_to_all(early, 'row', 0, 0).reshape(1024, 128)  7.1 us
    all_to_all x1, waiting for transfers between devices, on_device(): packed = lax.all_to_all(packed, 'col', 0, 0)  5.5 us
    all_to_all x1, starting transfers between devices, on_device(): packed = lax.all_to_all(packed, 'col', 0, 0)  5.31 us
  transfers between devices with their start and end apart: 43, of which 17 were waited for; matrix products, arithmetic and copies ran while one was open for 2% of the time, Pallas kernels for 17%

profile of v12, /device:TPU:4, one launch (start us, length us, event | category | flops | bytes accessed | tf_op | source)
XLA Modules:
  0.0 174.4 jit_solution(11542219253309663232)
XLA Ops:
  7.3 2.7 %shard_map.88 = f32[288,384]{1,0:T(8,128)} custom-call(s32[2]{0:T(128)S(1)} %pad_add_fusion.2.place_ref, f32[2,192,384]{2,1,0:T(8,128)} %factor_ref.1), custom_call_target="tpu_custom_call" | custom-call | tf_op jit(solution)/shard_map/pallas_call | solution.py:92
  10.3 1.4 shard_map.86
  11.7 5.3 %all-to-all-start = ((f32[8,16,128]{2,1,0:T(8,128)}), f32[8,16,128]{2,1,0:T(8,128)S(1)}, u32[]{:S(2)}, u32[]{:S(2)}) async-start(f32[8,16,128]{2,1,0:T(8,128)} %shard_map.86), calls=%async_computation | async-start | bytes 131072 | tf_op jit(solution)/shard_map/all_to_all | solution.py:459
  17.1 5.5 %all-to-all-done = f32[8,16,128]{2,1,0:T(8,128)S(1)} async-done(((f32[8,16,128]{2,1,0:T(8,128)}), f32[8,16,128]{2,1,0:T(8,128)S(1)}, u32[]{:S(2)}, u32[]{:S(2)}) %all-to-all-start) | async-done | bytes 65568 | tf_op jit(solution)/shard_map/all_to_all | solution.py:459
  23.5 7.5 %all-to-all-start.1 = ((f32[16,64,128]{2,1,0:T(8,128)}), f32[16,64,128]{2,1,0:T(8,128)S(1)}, u32[]{:S(2)}, u32[]{:S(2)}) async-start(f32[16,64,128]{2,1,0:T(8,128)} %broadcast_in_dim.36), calls=%async_computation.1 | async-start | bytes 1048576 | tf_op jit(solution)/shard_map/all_to_all | solution.py:461
  32.8 7.1 %all-to-all-done.1 = f32[16,64,128]{2,1,0:T(8,128)S(1)} async-done(((f32[16,64,128]{2,1,0:T(8,128)}), f32[16,64,128]{2,1,0:T(8,128)S(1)}, u32[]{:S(2)}, u32[]{:S(2)}) %all-to-all-start.1) | async-done | bytes 524320 | tf_op jit(solution)/shard_map/all_to_all | solution.py:461
  39.9 1.9 %shard_map.87.rhs_ref = f32[32,1024]{1,0:T(8,128)S(1)} custom-call(s32[2048]{0:T(1024)S(1)} %bitcast.35, f32[1024,128]{1,0:T(8,128)S(1)} %bitcast.34, f32[2,1024]{1,0:T(2,128)S(1)} %get-tuple-element.74.mark_ref), custom_call_target="tpu_custom_call" | custom-call | tf_op jit(solution)/shard_map/pallas_call | solution.py:92
  42.2 2.3 %shard_map.89.acc_ref = f32[32,192]{1,0:T(8,128)S(1)} custom-call(s32[2]{0:T(128)S(1)} %pad_add_fusion.2.place_ref, f32[32,1024]{1,0:T(8,128)S(1)} %shard_map.87.rhs_ref, f32[8,3,96,384]{3,2,1,0:T(8,128)} %bitcast.37), custom_call_target="tpu_custom_call" | custom-call | tf_op jit(solution)/shard_map/pallas_call | solution.py:92
  45.2 1.3 collective-permute-start
  46.5 1.3 collective-permute-start.1
  47.8 1.3 collective-permute-start.2
  49.1 1.3 collective-permute-start.3
  50.4 1.9 %shard_map.90.weight_ref.weight1_ref = f32[768,384]{1,0:T(8,128)S(1)} custom-call(s32[2]{0:T(128)S(1)} %pad_add_fusion.2.place_ref, f32[8,3,96,384]{3,2,1,0:T(8,128)} %bitcast.38), custom_call_target="tpu_custom_call" | custom-call | tf_op jit(solution)/shard_map/pallas_call | solution.py:92
  52.3 2.2 %collective-permute-done.1.y1 = f32[32,192]{1,0:T(8,128)S(1)} collective-permute-done((f32[32,192]{1,0:T(8,128)S(1)}, f32[32,192]{1,0:T(8,128)S(1)}, u32[]{:S(2)}, u32[]{:S(2)}) %collective-permute-start.1) | collective-permute-done | bytes 24608 | tf_op jit(solution)/shard_map/ppermute | solution.py:422
  54.5 2.2 %collective-permute-done.2.y2 = f32[32,192]{1,0:T(8,128)S(1)} collective-permute-done((f32[32,192]{1,0:T(8,128)S(1)}, f32[32,192]{1,0:T(8,128)S(1)}, u32[]{:S(2)}, u32[]{:S(2)}) %collective-permute-start.2) | collective-permute-done | bytes 24608 | tf_op jit(solution)/shard_map/ppermute | solution.py:422
  65.3 1.9 %shard_map.92.weight2_ref = f32[768,384]{1,0:T(8,128)S(1)} custom-call(s32[2]{0:T(128)S(1)} %pad_add_fusion.2.place_ref, f32[8,3,96,384]{3,2,1,0:T(8,128)} %bitcast.39), custom_call_target="tpu_custom_call" | custom-call | tf_op jit(solution)/shard_map/pallas_call | solution.py:92
  67.2 1.6 shard_map.93
  68.9 1.3 collective-permute-start.10
  70.2 1.3 collective-permute-start.11
  74.1 1.9 %shard_map.94.weight_ref.weight3_ref = f32[768,384]{1,0:T(8,128)S(1)} custom-call(s32[2]{0:T(128)S(1)} %pad_add_fusion.2.place_ref, f32[8,3,96,384]{3,2,1,0:T(8,128)} %bitcast.40), custom_call_target="tpu_custom_call" | custom-call | tf_op jit(solution)/shard_map/pallas_call | solution.py:92
  76.0 2.8 %collective-permute-done.10.p1 = f32[32,768]{1,0:T(8,128)S(1)} collective-permute-done((f32[32,768]{1,0:T(8,128)S(1)}, f32[32,768]{1,0:T(8,128)S(1)}, u32[]{:S(2)}, u32[]{:S(2)}) %collective-permute-start.10) | collective-permute-done | bytes 98336 | tf_op jit(solution)/shard_map/ppermute | solution.py:422
  78.8 5.1 %collective-permute-done.11.p2 = f32[32,768]{1,0:T(8,128)S(1)} collective-permute-done((f32[32,768]{1,0:T(8,128)S(1)}, f32[32,768]{1,0:T(8,128)S(1)}, u32[]{:S(2)}, u32[]{:S(2)}) %collective-permute-start.11) | collective-permute-done | bytes 98336 | tf_op jit(solution)/shard_map/ppermute | solution.py:422
  84.7 1.4 shard_map.95
  87.4 1.3 collective-permute-start.14
  88.7 1.3 collective-permute-start.15
  90.0 1.3 collective-permute-start.16
  91.3 1.3 collective-permute-start.17
  92.6 2.1 %collective-permute-done.15.p2 = f32[32,768]{1,0:T(8,128)S(1)} collective-permute-done((f32[32,768]{1,0:T(8,128)S(1)}, f32[32,768]{1,0:T(8,128)S(1)}, u32[]{:S(2)}, u32[]{:S(2)}) %collective-permute-start.15) | collective-permute-done | bytes 98336 | tf_op jit(solution)/shard_map/ppermute | solution.py:422
  94.7 1.9 %collective-permute-done.16.p3 = f32[32,768]{1,0:T(8,128)S(1)} collective-permute-done((f32[32,768]{1,0:T(8,128)S(1)}, f32[32,768]{1,0:T(8,128)S(1)}, u32[]{:S(2)}, u32[]{:S(2)}) %collective-permute-start.16) | collective-permute-done | bytes 98336 | tf_op jit(solution)/shard_map/ppermute | solution.py:422
  97.7 1.6 shard_map.96
  102.7 1.9 %shard_map.97.weight1_ref = f32[768,384]{1,0:T(8,128)S(1)} custom-call(s32[2]{0:T(128)S(1)} %pad_add_fusion.2.place_ref, f32[8,3,96,384]{3,2,1,0:T(8,128)} %bitcast.41), custom_call_target="tpu_custom_call" | custom-call | tf_op jit(solution)/shard_map/pallas_call | solution.py:92
  104.6 2.0 %shard_map.98 = (f32[32,768]{1,0:T(8,128)S(1)}, f32[2,32,768]{2,1,0:T(8,128)S(1)}, f32[32,768]{1,0:T(8,128)S(1)}) custom-call(s32[2]{0:T(128)S(1)} %pad_add_fusion.2.place_ref, f32[32,192]{1,0:T(8,128)S(1)} %get-tuple-element.47.acc_ref, f32[192,1536]{1,0:T(8,128)S(1)} %bitcast.33, f32[32,768]{1,0:T(8,128)S(1)} %collective-permute-done.18.p0, ...), custom_call_target="tpu_custom_call" | custom-call | tf_op jit(solution)/shard_map/pallas_call | solution.py:92
  109.3 1.9 %collective-permute-start.27 = (f32[32,768]{1,0:T(8,128)S(1)}, f32[32,768]{1,0:T(8,128)S(1)}, u32[]{:S(2)}, u32[]{:S(2)}) collective-permute-start(f32[32,768]{1,0:T(8,128)S(1)} %get-tuple-element.55.newest_ref), channel_id=1, source_target_pairs={{0,32},{8,40},{16,48},{24,56},{32,64},{40,72},{48,80},{56,88},{64,... | collective-permute-start | bytes 294920 | tf_op jit(solution)/shard_map/ppermute | solution.py:422
  111.2 4.3 %shard_map.99 = (f32[32,1024]{1,0:T(8,128)S(1)}, f32[16,1024]{1,0:T(8,128)S(1)}) custom-call(s32[2048]{0:T(1024)S(1)} %bitcast.36, f32[2,1024]{1,0:T(2,128)S(1)} %get-tuple-element.74.mark_ref, f32[16,64,256]{2,1,0:T(8,128)} %bitcast.47), custom_call_target="tpu_custom_call" | custom-call | tf_op jit(solution)/shard_map/pallas_call | solution.py:92
  115.5 3.0 %all-gather.11.cloned.1.call-done = f32[2304,384]{1,0:T(8,128)} async-done(((f32[288,384]{1,0:T(8,128)}), f32[2304,384]{1,0:T(8,128)}) %all-gather.11.cloned.1.call-update) | async-done | bytes 3538960 | tf_op jit(solution)/shard_map/all_gather | solution.py:440
  118.5 1.9 %shard_map.100.weight_ref.weight0_ref = f32[768,384]{1,0:T(8,128)S(1)} custom-call(s32[2]{0:T(128)S(1)} %pad_add_fusion.2.place_ref, f32[8,3,96,384]{3,2,1,0:T(8,128)} %bitcast.42), custom_call_target="tpu_custom_call" | custom-call | tf_op jit(solution)/shard_map/pallas_call | solution.py:92
  120.5 6.1 %collective-permute-done.27.own_ref = f32[32,768]{1,0:T(8,128)S(1)} collective-permute-done((f32[32,768]{1,0:T(8,128)S(1)}, f32[32,768]{1,0:T(8,128)S(1)}, u32[]{:S(2)}, u32[]{:S(2)}) %collective-permute-start.27) | collective-permute-done | bytes 98336 | tf_op jit(solution)/shard_map/ppermute | solution.py:422
  134.1 2.3 %shard_map.102 = (f32[768,384]{1,0:T(8,128)S(1)}, f32[768,384]{1,0:T(8,128)S(1)}) custom-call(s32[2]{0:T(128)S(1)} %pad_add_fusion.2.place_ref, f32[8,3,96,384]{3,2,1,0:T(8,128)} %bitcast.43, f32[8,3,96,384]{3,2,1,0:T(8,128)} %bitcast.44), custom_call_target="tpu_custom_call" | custom-call | tf_op jit(solution)/shard_map/pallas_call | solution.py:92
  136.5 3.1 %collective-permute-done.29.f0 = f32[32,192]{1,0:T(8,128)S(1)} collective-permute-done((f32[32,192]{1,0:T(8,128)S(1)}, f32[32,192]{1,0:T(8,128)S(1)}, u32[]{:S(2)}, u32[]{:S(2)}) %collective-permute-start.29) | collective-permute-done | bytes 24608 | tf_op jit(solution)/shard_map/ppermute | solution.py:422
  139.6 2.1 %collective-permute-done.30.f1 = f32[32,192]{1,0:T(8,128)S(1)} collective-permute-done((f32[32,192]{1,0:T(8,128)S(1)}, f32[32,192]{1,0:T(8,128)S(1)}, u32[]{:S(2)}, u32[]{:S(2)}) %collective-permute-start.30) | collective-permute-done | bytes 24608 | tf_op jit(solution)/shard_map/ppermute | solution.py:422
  143.2 1.3 collective-permute-start.33
  147.5 2.0 %collective-permute-start.36 = (f32[32,192]{1,0:T(8,128)S(1)}, f32[32,192]{1,0:T(8,128)S(1)}, u32[]{:S(2)}, u32[]{:S(2)}) collective-permute-start(f32[32,192]{1,0:T(8,128)S(1)} %get-tuple-element.63.acc_ref), channel_id=1, source_target_pairs={{64,112},{72,120},{80,96},{88,104},{65,113},{73,121},{81,97},{89,1... | collective-permute-start | bytes 73736 | tf_op jit(solution)/shard_map/ppermute | solution.py:422
  149.5 1.9 %collective-permute-start.37 = (f32[32,192]{1,0:T(8,128)S(1)}, f32[32,192]{1,0:T(8,128)S(1)}, u32[]{:S(2)}, u32[]{:S(2)}) collective-permute-start(f32[32,192]{1,0:T(8,128)S(1)} %get-tuple-element.63.acc_ref), channel_id=1, source_target_pairs={{64,120},{72,96},{80,104},{88,112},{65,121},{73,97},{81,105},{89,1... | collective-permute-start | bytes 73736 | tf_op jit(solution)/shard_map/ppermute | solution.py:422
  152.5 1.3 shard_map.105.cells_ref
  153.9 1.3 shard_map.106
  155.2 9.9 %all_to_all.15.got_ref = f32[8,32,256]{2,1,0:T(8,128)S(1)} all-to-all(f32[8,32,256]{2,1,0:T(8,128)S(1)} %shard_map.106), channel_id=1, replica_groups=mesh['row'=16,'col'=8] {'col'}, dimensions={0} | all-to-all | bytes 524288 | tf_op jit(solution)/shard_map/all_to_all | solution.py:601
  165.2 1.3 shard_map.107
  166.5 1.4 copy.18
  (103 shorter events, 37.7 us)
Async XLA Ops:
  7.2 2.9 %copy-start.4 = (f32[2,4,6,128]{3,1,2,0:T(4,128)S(1)}, f32[2,4,6,128]{3,1,2,0:T(4,128)}, u32[]{:S(2)}) copy-start(f32[2,4,6,128]{3,1,2,0:T(4,128)} %param.8) | copy-start | bytes 73732
  7.2 2.9 %copy-start.5 = (f32[2,4,6]{2,1,0:T(4,128)S(1)}, f32[2,4,6]{2,1,0:T(4,128)}, u32[]{:S(2)}) copy-start(f32[2,4,6]{2,1,0:T(4,128)} %param.9) | copy-start | bytes 580
  7.2 9.8 %copy-start.2 = (s32[3072]{0:T(1024)S(1)}, s32[3072]{0:T(1024)}, u32[]{:S(2)}) copy-start(s32[3072]{0:T(1024)} %param.13) | copy-start | bytes 36868
  7.2 35.0 %all-gather.7.cloned.1.call-start = ((), (), s32[]{:S(2)}) async-start(), calls=%async_computation.3 | async-start | bytes 3981312 | tf_op jit(solution)/shard_map/all_gather | solution.py:440
  10.1 21.0 %copy-start.1 = (f32[2,192,384]{2,1,0:T(8,128)S(1)}, f32[2,192,384]{2,1,0:T(8,128)}, u32[]{:S(2)}) copy-start(f32[2,192,384]{2,1,0:T(8,128)} %param.11) | copy-start | bytes 1769476
  11.7 10.9 %all-to-all-start = ((f32[8,16,128]{2,1,0:T(8,128)}), f32[8,16,128]{2,1,0:T(8,128)S(1)}, u32[]{:S(2)}, u32[]{:S(2)}) async-start(f32[8,16,128]{2,1,0:T(8,128)} %shard_map.86), calls=%async_computation | async-start | bytes 131072 | tf_op jit(solution)/shard_map/all_to_all | solution.py:459
  23.5 16.5 %all-to-all-start.1 = ((f32[16,64,128]{2,1,0:T(8,128)}), f32[16,64,128]{2,1,0:T(8,128)S(1)}, u32[]{:S(2)}, u32[]{:S(2)}) async-start(f32[16,64,128]{2,1,0:T(8,128)} %broadcast_in_dim.36), calls=%async_computation.1 | async-start | bytes 1048576 | tf_op jit(solution)/shard_map/all_to_all | solution.py:461
  30.9 80.3 %all-gather.9.cloned.1.call-start = ((), (), s32[]{:S(2)}) async-start(), calls=%async_computation.4 | async-start | bytes 1114112 | tf_op jit(solution)/shard_map/all_gather | solution.py:504
  44.5 74.1 %all-gather.11.cloned.1.call-start = ((), (), s32[]{:S(2)}) async-start(), calls=%async_computation.5 | async-start | bytes 3981312 | tf_op jit(solution)/shard_map/all_gather | solution.py:440
  45.2 7.1 %collective-permute-start = (f32[32,192]{1,0:T(8,128)S(1)}, f32[32,192]{1,0:T(8,128)S(1)}, u32[]{:S(2)}, u32[]{:S(2)}) collective-permute-start(f32[32,192]{1,0:T(8,128)S(1)} %shard_map.89.acc_ref), channel_id=1, source_target_pairs={{32,64},{40,72},{48,80},{56,88},{33,65},{41,73},{49,81},{57,89},{3... | collective-permute-start | bytes 73736 | tf_op jit(solution)/shard_map/ppermute | solution.py:422
  46.5 8.0 %collective-permute-start.1 = (f32[32,192]{1,0:T(8,128)S(1)}, f32[32,192]{1,0:T(8,128)S(1)}, u32[]{:S(2)}, u32[]{:S(2)}) collective-permute-start(f32[32,192]{1,0:T(8,128)S(1)} %shard_map.89.acc_ref), channel_id=1, source_target_pairs={{32,72},{40,80},{48,88},{56,64},{33,73},{41,81},{49,89},{57,65},{3... | collective-permute-start | bytes 73736 | tf_op jit(solution)/shard_map/ppermute | solution.py:422
  47.8 8.9 %collective-permute-start.2 = (f32[32,192]{1,0:T(8,128)S(1)}, f32[32,192]{1,0:T(8,128)S(1)}, u32[]{:S(2)}, u32[]{:S(2)}) collective-permute-start(f32[32,192]{1,0:T(8,128)S(1)} %shard_map.89.acc_ref), channel_id=1, source_target_pairs={{32,80},{40,88},{48,64},{56,72},{33,81},{41,89},{49,65},{57,73},{3... | collective-permute-start | bytes 73736 | tf_op jit(solution)/shard_map/ppermute | solution.py:422
  49.1 8.5 %collective-permute-start.3 = (f32[32,192]{1,0:T(8,128)S(1)}, f32[32,192]{1,0:T(8,128)S(1)}, u32[]{:S(2)}, u32[]{:S(2)}) collective-permute-start(f32[32,192]{1,0:T(8,128)S(1)} %shard_map.89.acc_ref), channel_id=1, source_target_pairs={{32,88},{40,64},{48,72},{56,80},{33,89},{41,65},{49,73},{57,81},{3... | collective-permute-start | bytes 73736 | tf_op jit(solution)/shard_map/ppermute | solution.py:422
  52.3 12.9 %copy-start = (f32[2,768,192]{1,2,0:T(8,128)S(1)}, f32[2,768,192]{1,2,0:T(8,128)}, u32[]{:S(2)}) copy-start(f32[2,768,192]{1,2,0:T(8,128)} %param.12) | copy-start | bytes 3538948
  58.7 8.6 %collective-permute-start.4 = (f32[4,32,192]{2,1,0:T(8,128)S(1)}, f32[4,32,192]{2,1,0:T(8,128)S(1)}, u32[]{:S(2)}, u32[]{:S(2)}) collective-permute-start(f32[4,32,192]{2,1,0:T(8,128)S(1)} %get-tuple-element.39), channel_id=1, source_target_pairs={{64,96},{72,104},{80,112},{88,120},{65,97},{73,105},{81,113},{89,1... | collective-permute-start | bytes 294920 | tf_op jit(solution)/shard_map/ppermute | solution.py:422
  60.0 7.2 %collective-permute-start.5 = (f32[32,192]{1,0:T(8,128)S(1)}, f32[32,192]{1,0:T(8,128)S(1)}, u32[]{:S(2)}, u32[]{:S(2)}) collective-permute-start(f32[32,192]{1,0:T(8,128)S(1)} %get-tuple-element.37.acc_ref), channel_id=1, source_target_pairs={{64,96},{72,104},{80,112},{88,120},{65,97},{73,105},{81,113},{89,1... | collective-permute-start | bytes 73736 | tf_op jit(solution)/shard_map/ppermute | solution.py:422
  61.2 5.9 %collective-permute-start.6 = (f32[32,192]{1,0:T(8,128)S(1)}, f32[32,192]{1,0:T(8,128)S(1)}, u32[]{:S(2)}, u32[]{:S(2)}) collective-permute-start(f32[32,192]{1,0:T(8,128)S(1)} %get-tuple-element.37.acc_ref), channel_id=1, source_target_pairs={{64,104},{72,112},{80,120},{88,96},{65,105},{73,113},{81,121},{89,... | collective-permute-start | bytes 73736 | tf_op jit(solution)/shard_map/ppermute | solution.py:422
  62.5 4.7 %collective-permute-start.7 = (f32[32,192]{1,0:T(8,128)S(1)}, f32[32,192]{1,0:T(8,128)S(1)}, u32[]{:S(2)}, u32[]{:S(2)}) collective-permute-start(f32[32,192]{1,0:T(8,128)S(1)} %get-tuple-element.37.acc_ref), channel_id=1, source_target_pairs={{64,112},{72,120},{80,96},{88,104},{65,113},{73,121},{81,97},{89,1... | collective-permute-start | bytes 73736 | tf_op jit(solution)/shard_map/ppermute | solution.py:422
  63.8 3.4 %collective-permute-start.8 = (f32[32,192]{1,0:T(8,128)S(1)}, f32[32,192]{1,0:T(8,128)S(1)}, u32[]{:S(2)}, u32[]{:S(2)}) collective-permute-start(f32[32,192]{1,0:T(8,128)S(1)} %get-tuple-element.37.acc_ref), channel_id=1, source_target_pairs={{64,120},{72,96},{80,104},{88,112},{65,121},{73,97},{81,105},{89,1... | collective-permute-start | bytes 73736 | tf_op jit(solution)/shard_map/ppermute | solution.py:422
  68.9 9.9 %collective-permute-start.10 = (f32[32,768]{1,0:T(8,128)S(1)}, f32[32,768]{1,0:T(8,128)S(1)}, u32[]{:S(2)}, u32[]{:S(2)}) collective-permute-start(f32[32,768]{1,0:T(8,128)S(1)} %get-tuple-element.42), channel_id=1, source_target_pairs={{96,72},{104,80},{112,88},{120,64},{97,73},{105,81},{113,89},{121,... | collective-permute-start | bytes 294920 | tf_op jit(solution)/shard_map/ppermute | solution.py:422
  70.2 13.7 %collective-permute-start.11 = (f32[32,768]{1,0:T(8,128)S(1)}, f32[32,768]{1,0:T(8,128)S(1)}, u32[]{:S(2)}, u32[]{:S(2)}) collective-permute-start(f32[32,768]{1,0:T(8,128)S(1)} %get-tuple-element.42), channel_id=1, source_target_pairs={{96,80},{104,88},{112,64},{120,72},{97,81},{105,89},{113,65},{121,... | collective-permute-start | bytes 294920 | tf_op jit(solution)/shard_map/ppermute | solution.py:422
  71.5 13.2 %collective-permute-start.12 = (f32[32,768]{1,0:T(8,128)S(1)}, f32[32,768]{1,0:T(8,128)S(1)}, u32[]{:S(2)}, u32[]{:S(2)}) collective-permute-start(f32[32,768]{1,0:T(8,128)S(1)} %get-tuple-element.42), channel_id=1, source_target_pairs={{96,88},{104,64},{112,72},{120,80},{97,89},{105,65},{113,73},{121,... | collective-permute-start | bytes 294920 | tf_op jit(solution)/shard_map/ppermute | solution.py:422
  72.8 11.9 %collective-permute-start.9 = (f32[32,768]{1,0:T(8,128)S(1)}, f32[32,768]{1,0:T(8,128)S(1)}, u32[]{:S(2)}, u32[]{:S(2)}) collective-permute-start(f32[32,768]{1,0:T(8,128)S(1)} %get-tuple-element.42), channel_id=1, source_target_pairs={{96,64},{104,72},{112,80},{120,88},{97,65},{105,73},{113,81},{121,... | collective-permute-start | bytes 294920 | tf_op jit(solution)/shard_map/ppermute | solution.py:422
  86.1 6.5 %collective-permute-start.13 = (f32[32,768]{1,0:T(8,128)S(1)}, f32[32,768]{1,0:T(8,128)S(1)}, u32[]{:S(2)}, u32[]{:S(2)}) collective-permute-start(f32[32,768]{1,0:T(8,128)S(1)} %get-tuple-element.45), channel_id=1, source_target_pairs={{64,32},{72,40},{80,48},{88,56},{65,33},{73,41},{81,49},{89,57},{6... | collective-permute-start | bytes 294920 | tf_op jit(solution)/shard_map/ppermute | solution.py:422
  87.4 5.3 %collective-permute-start.14 = (f32[32,768]{1,0:T(8,128)S(1)}, f32[32,768]{1,0:T(8,128)S(1)}, u32[]{:S(2)}, u32[]{:S(2)}) collective-permute-start(f32[32,768]{1,0:T(8,128)S(1)} %get-tuple-element.45), channel_id=1, source_target_pairs={{64,40},{72,48},{80,56},{88,32},{65,41},{73,49},{81,57},{89,33},{6... | collective-permute-start | bytes 294920 | tf_op jit(solution)/shard_map/ppermute | solution.py:422
  88.7 6.1 %collective-permute-start.15 = (f32[32,768]{1,0:T(8,128)S(1)}, f32[32,768]{1,0:T(8,128)S(1)}, u32[]{:S(2)}, u32[]{:S(2)}) collective-permute-start(f32[32,768]{1,0:T(8,128)S(1)} %get-tuple-element.45), channel_id=1, source_target_pairs={{64,48},{72,56},{80,32},{88,40},{65,49},{73,57},{81,33},{89,41},{6... | collective-permute-start | bytes 294920 | tf_op jit(solution)/shard_map/ppermute | solution.py:422
  90.0 6.7 %collective-permute-start.16 = (f32[32,768]{1,0:T(8,128)S(1)}, f32[32,768]{1,0:T(8,128)S(1)}, u32[]{:S(2)}, u32[]{:S(2)}) collective-permute-start(f32[32,768]{1,0:T(8,128)S(1)} %get-tuple-element.45), channel_id=1, source_target_pairs={{64,56},{72,32},{80,40},{88,48},{65,57},{73,33},{81,41},{89,49},{6... | collective-permute-start | bytes 294920 | tf_op jit(solution)/shard_map/ppermute | solution.py:422
  91.3 6.4 %collective-permute-start.17 = (f32[32,768]{1,0:T(8,128)S(1)}, f32[32,768]{1,0:T(8,128)S(1)}, u32[]{:S(2)}, u32[]{:S(2)}) collective-permute-start(f32[32,768]{1,0:T(8,128)S(1)} %get-tuple-element.46.x3_ref), channel_id=1, source_target_pairs={{64,32},{72,40},{80,48},{88,56},{65,33},{73,41},{81,49},{89,57},{6... | collective-permute-start | bytes 294920 | tf_op jit(solution)/shard_map/ppermute | solution.py:422
  99.3 5.3 %collective-permute-start.22 = (f32[2,32,768]{2,1,0:T(8,128)S(1)}, f32[2,32,768]{2,1,0:T(8,128)S(1)}, u32[]{:S(2)}, u32[]{:S(2)}) collective-permute-start(f32[2,32,768]{2,1,0:T(8,128)S(1)} %get-tuple-element.49.x2_ref), channel_id=1, source_target_pairs={{32,0},{40,8},{48,16},{56,24},{33,1},{41,9},{49,17},{57,25},{34,2}... | collective-permute-start | bytes 589832 | tf_op jit(solution)/shard_map/ppermute | solution.py:422
  100.0 4.6 %collective-permute-start.18 = (f32[32,768]{1,0:T(8,128)S(1)}, f32[32,768]{1,0:T(8,128)S(1)}, u32[]{:S(2)}, u32[]{:S(2)}) collective-permute-start(f32[32,768]{1,0:T(8,128)S(1)} %get-tuple-element.48), channel_id=1, source_target_pairs={{32,0},{40,8},{48,16},{56,24},{33,1},{41,9},{49,17},{57,25},{34,2}... | collective-permute-start | bytes 294920 | tf_op jit(solution)/shard_map/ppermute | solution.py:422
  100.6 3.9 %collective-permute-start.19 = (f32[32,768]{1,0:T(8,128)S(1)}, f32[32,768]{1,0:T(8,128)S(1)}, u32[]{:S(2)}, u32[]{:S(2)}) collective-permute-start(f32[32,768]{1,0:T(8,128)S(1)} %get-tuple-element.48), channel_id=1, source_target_pairs={{32,8},{40,16},{48,24},{56,0},{33,9},{41,17},{49,25},{57,1},{34,10... | collective-permute-start | bytes 294920 | tf_op jit(solution)/shard_map/ppermute | solution.py:422
  101.3 3.3 %collective-permute-start.20 = (f32[32,768]{1,0:T(8,128)S(1)}, f32[32,768]{1,0:T(8,128)S(1)}, u32[]{:S(2)}, u32[]{:S(2)}) collective-permute-start(f32[32,768]{1,0:T(8,128)S(1)} %get-tuple-element.48), channel_id=1, source_target_pairs={{32,16},{40,24},{48,0},{56,8},{33,17},{41,25},{49,1},{57,9},{34,18... | collective-permute-start | bytes 294920 | tf_op jit(solution)/shard_map/ppermute | solution.py:422
  102.0 2.6 %collective-permute-start.21 = (f32[32,768]{1,0:T(8,128)S(1)}, f32[32,768]{1,0:T(8,128)S(1)}, u32[]{:S(2)}, u32[]{:S(2)}) collective-permute-start(f32[32,768]{1,0:T(8,128)S(1)} %get-tuple-element.48), channel_id=1, source_target_pairs={{32,24},{40,0},{48,8},{56,16},{33,25},{41,1},{49,9},{57,17},{34,26... | collective-permute-start | bytes 294920 | tf_op jit(solution)/shard_map/ppermute | solution.py:422
  106.6 13.9 %collective-permute-start.23 = (f32[32,768]{1,0:T(8,128)S(1)}, f32[32,768]{1,0:T(8,128)S(1)}, u32[]{:S(2)}, u32[]{:S(2)}) collective-permute-start(f32[32,768]{1,0:T(8,128)S(1)} %get-tuple-element.51), channel_id=1, source_target_pairs={{0,32},{8,40},{16,48},{24,56},{1,33},{9,41},{17,49},{25,57},{2,34}... | collective-permute-start | bytes 294920 | tf_op jit(solution)/shard_map/ppermute | solution.py:422
  107.3 13.2 %collective-permute-start.24 = (f32[32,768]{1,0:T(8,128)S(1)}, f32[32,768]{1,0:T(8,128)S(1)}, u32[]{:S(2)}, u32[]{:S(2)}) collective-permute-start(f32[32,768]{1,0:T(8,128)S(1)} %get-tuple-element.51), channel_id=1, source_target_pairs={{0,40},{8,48},{16,56},{24,32},{1,41},{9,49},{17,57},{25,33},{2,42}... | collective-permute-start | bytes 294920 | tf_op jit(solution)/shard_map/ppermute | solution.py:422
  107.9 12.5 %collective-permute-start.25 = (f32[32,768]{1,0:T(8,128)S(1)}, f32[32,768]{1,0:T(8,128)S(1)}, u32[]{:S(2)}, u32[]{:S(2)}) collective-permute-start(f32[32,768]{1,0:T(8,128)S(1)} %get-tuple-element.51), channel_id=1, source_target_pairs={{0,48},{8,56},{16,32},{24,40},{1,49},{9,57},{17,33},{25,41},{2,50}... | collective-permute-start | bytes 294920 | tf_op jit(solution)/shard_map/ppermute | solution.py:422
  108.6 11.9 %collective-permute-start.26 = (f32[32,768]{1,0:T(8,128)S(1)}, f32[32,768]{1,0:T(8,128)S(1)}, u32[]{:S(2)}, u32[]{:S(2)}) collective-permute-start(f32[32,768]{1,0:T(8,128)S(1)} %get-tuple-element.51), channel_id=1, source_target_pairs={{0,56},{8,32},{16,40},{24,48},{1,57},{9,33},{17,41},{25,49},{2,58}... | collective-permute-start | bytes 294920 | tf_op jit(solution)/shard_map/ppermute | solution.py:422
  109.3 17.3 %collective-permute-start.27 = (f32[32,768]{1,0:T(8,128)S(1)}, f32[32,768]{1,0:T(8,128)S(1)}, u32[]{:S(2)}, u32[]{:S(2)}) collective-permute-start(f32[32,768]{1,0:T(8,128)S(1)} %get-tuple-element.55.newest_ref), channel_id=1, source_target_pairs={{0,32},{8,40},{16,48},{24,56},{32,64},{40,72},{48,80},{56,88},{64,... | collective-permute-start | bytes 294920 | tf_op jit(solution)/shard_map/ppermute | solution.py:422
  127.6 14.3 %collective-permute-start.28 = (f32[2,32,768]{2,1,0:T(8,128)S(1)}, f32[2,32,768]{2,1,0:T(8,128)S(1)}, u32[]{:S(2)}, u32[]{:S(2)}) collective-permute-start(f32[2,32,768]{2,1,0:T(8,128)S(1)} %get-tuple-element.60.sent_ref.pass_ref), channel_id=1, source_target_pairs={{32,64},{40,72},{48,80},{56,88},{0,96},{8,104},{16,112},{24,120},{... | collective-permute-start | bytes 589832 | tf_op jit(solution)/shard_map/ppermute | solution.py:422
  128.9 10.7 %collective-permute-start.29 = (f32[32,192]{1,0:T(8,128)S(1)}, f32[32,192]{1,0:T(8,128)S(1)}, u32[]{:S(2)}, u32[]{:S(2)}) collective-permute-start(f32[32,192]{1,0:T(8,128)S(1)} %get-tuple-element.59.acc_ref), channel_id=1, source_target_pairs={{32,64},{40,72},{48,80},{56,88},{33,65},{41,73},{49,81},{57,89},{3... | collective-permute-start | bytes 73736 | tf_op jit(solution)/shard_map/ppermute | solution.py:422
  130.2 11.5 %collective-permute-start.30 = (f32[32,192]{1,0:T(8,128)S(1)}, f32[32,192]{1,0:T(8,128)S(1)}, u32[]{:S(2)}, u32[]{:S(2)}) collective-permute-start(f32[32,192]{1,0:T(8,128)S(1)} %get-tuple-element.59.acc_ref), channel_id=1, source_target_pairs={{32,72},{40,80},{48,88},{56,64},{33,73},{41,81},{49,89},{57,65},{3... | collective-permute-start | bytes 73736 | tf_op jit(solution)/shard_map/ppermute | solution.py:422
  131.5 10.4 %collective-permute-start.31 = (f32[32,192]{1,0:T(8,128)S(1)}, f32[32,192]{1,0:T(8,128)S(1)}, u32[]{:S(2)}, u32[]{:S(2)}) collective-permute-start(f32[32,192]{1,0:T(8,128)S(1)} %get-tuple-element.59.acc_ref), channel_id=1, source_target_pairs={{32,80},{40,88},{48,64},{56,72},{33,81},{41,89},{49,65},{57,73},{3... | collective-permute-start | bytes 73736 | tf_op jit(solution)/shard_map/ppermute | solution.py:422
  132.8 9.1 %collective-permute-start.32 = (f32[32,192]{1,0:T(8,128)S(1)}, f32[32,192]{1,0:T(8,128)S(1)}, u32[]{:S(2)}, u32[]{:S(2)}) collective-permute-start(f32[32,192]{1,0:T(8,128)S(1)} %get-tuple-element.59.acc_ref), channel_id=1, source_target_pairs={{32,88},{40,64},{48,72},{56,80},{33,89},{41,65},{49,73},{57,81},{3... | collective-permute-start | bytes 73736 | tf_op jit(solution)/shard_map/ppermute | solution.py:422
  143.2 8.3 %collective-permute-start.33 = (f32[8,32,192]{2,1,0:T(8,128)S(1)}, f32[8,32,192]{2,1,0:T(8,128)S(1)}, u32[]{:S(2)}, u32[]{:S(2)}) collective-permute-start(f32[8,32,192]{2,1,0:T(8,128)S(1)} %get-tuple-element.64), channel_id=1, source_target_pairs={{64,96},{72,104},{80,112},{88,120},{32,0},{40,8},{48,16},{56,24},{... | collective-permute-start | bytes 589832 | tf_op jit(solution)/shard_map/ppermute | solution.py:422
  144.9 8.9 %collective-permute-start.34 = (f32[32,192]{1,0:T(8,128)S(1)}, f32[32,192]{1,0:T(8,128)S(1)}, u32[]{:S(2)}, u32[]{:S(2)}) collective-permute-start(f32[32,192]{1,0:T(8,128)S(1)} %get-tuple-element.63.acc_ref), channel_id=1, source_target_pairs={{64,96},{72,104},{80,112},{88,120},{65,97},{73,105},{81,113},{89,1... | collective-permute-start | bytes 73736 | tf_op jit(solution)/shard_map/ppermute | solution.py:422
  146.2 7.7 %collective-permute-start.35 = (f32[32,192]{1,0:T(8,128)S(1)}, f32[32,192]{1,0:T(8,128)S(1)}, u32[]{:S(2)}, u32[]{:S(2)}) collective-permute-start(f32[32,192]{1,0:T(8,128)S(1)} %get-tuple-element.63.acc_ref), channel_id=1, source_target_pairs={{64,104},{72,112},{80,120},{88,96},{65,105},{73,113},{81,121},{89,... | collective-permute-start | bytes 73736 | tf_op jit(solution)/shard_map/ppermute | solution.py:422
  147.5 6.4 %collective-permute-start.36 = (f32[32,192]{1,0:T(8,128)S(1)}, f32[32,192]{1,0:T(8,128)S(1)}, u32[]{:S(2)}, u32[]{:S(2)}) collective-permute-start(f32[32,192]{1,0:T(8,128)S(1)} %get-tuple-element.63.acc_ref), channel_id=1, source_target_pairs={{64,112},{72,120},{80,96},{88,104},{65,113},{73,121},{81,97},{89,1... | collective-permute-start | bytes 73736 | tf_op jit(solution)/shard_map/ppermute | solution.py:422
  149.5 4.4 %collective-permute-start.37 = (f32[32,192]{1,0:T(8,128)S(1)}, f32[32,192]{1,0:T(8,128)S(1)}, u32[]{:S(2)}, u32[]{:S(2)}) collective-permute-start(f32[32,192]{1,0:T(8,128)S(1)} %get-tuple-element.63.acc_ref), channel_id=1, source_target_pairs={{64,120},{72,96},{80,104},{88,112},{65,121},{73,97},{81,105},{89,1... | collective-permute-start | bytes 73736 | tf_op jit(solution)/shard_map/ppermute | solution.py:422
  (1 other events, 2.9 us)
Sparse Core Ops, SparseCore 0:
  10.2 31.9 all-gather.6
  44.9 42.8 all-gather.8
  89.5 29.0 all-gather.10
